TPU v7x, 256 devices: a whole 4x4x8 slice. The times are simulated.
256 devices in a mesh: clip: 2 (over z_hi), tm: 16 (over y, z_lo), space: 8 (over x, core).
Axes of the slice: x: 4, y: 4, z: 8 (z_hi: 2, z_lo: 4; z = z_hi * 4 + z_lo), core: 2. Of those that a mesh axis runs over, the one named last changes fastest.
Arguments:
- frames_in: bfloat16 [2, 32, 64, 128, 256], P('clip', 'tm', 'space'), may hold values from -6 to 6
- cotangent: bfloat16 [2, 32, 64, 128, 256], P('clip', 'tm', 'space'), may hold values from -6 to 6
- spatial_weight: bfloat16 [3, 3, 256, 256], replicated, may hold values from -0.125 to 0.125
- temporal_weight: bfloat16 [3, 256, 256], replicated, may hold values from -0.21875 to 0.21875
Outputs:
- block_out: bfloat16 [2, 32, 64, 128, 256], P('clip', 'tm', 'space')
- input_grad: bfloat16 [2, 32, 64, 128, 256], P('clip', 'tm', 'space')
- spatial_grad: float32 [3, 3, 256, 256], replicated
- temporal_grad: float32 [3, 256, 256], replicated
All inputs are finite; a program needn't handle non-finite values.
Results may differ from a plain program's by a relative error of at most 0.0054.
Values may be sent and summed in bfloat16 or wider, within the bound.
No kernel may reach another device: no remote copies, remote signals or barrier semaphores. Data moves between devices by JAX's collectives and lax.ppermute only.
A program may use at most 64 MiB of HBM per device.

v0:
```python
import jax
import jax.numpy as jnp
from jax import lax
from jax.sharding import PartitionSpec as P


def padded_2(block, sides, width):
    for axis, dim in sides:
        count = lax.axis_size(axis)
        forward = [(i, i + 1) for i in range(count - 1)]
        backward = [(target, source) for source, target in forward]
        low = lax.ppermute(
            lax.slice_in_dim(block, block.shape[dim] - width, None, axis=dim), axis, forward
        )
        high = lax.ppermute(lax.slice_in_dim(block, 0, width, axis=dim), axis, backward)
        block = jnp.concatenate([low, block, high], axis=dim)
    return block


def spatial_conv(padded, kernel, height, width):
    chans = padded.shape[-1]
    total = jnp.zeros((padded.shape[0] * height * width, kernel.shape[-1]), jnp.float32)
    for i in range(3):
        for j in range(3):
            window = padded[:, i : i + height, j : j + width, :].reshape(-1, chans)
            total = total + jnp.dot(window, kernel[i, j], preferred_element_type=jnp.float32)
    return total.reshape(padded.shape[0], height, width, kernel.shape[-1])


def causal_mix(extended, lead, kernel):
    count = extended.shape[0] - lead
    chans = extended.shape[-1]
    total = jnp.zeros((count * extended.shape[1] * extended.shape[2], chans), jnp.float32)
    for k in range(3):
        past = extended[lead - k : lead - k + count].reshape(-1, chans)
        total = total + jnp.dot(past, kernel[k], preferred_element_type=jnp.float32)
    return total.astype(jnp.bfloat16).reshape((count,) + extended.shape[1:])


def reverse_mix(extended, count, kernel):
    chans = extended.shape[-1]
    total = jnp.zeros((count * extended.shape[1] * extended.shape[2], chans), jnp.float32)
    for k in range(3):
        ahead = extended[k : k + count].reshape(-1, chans)
        total = total + jnp.dot(ahead, kernel[k].T, preferred_element_type=jnp.float32)
    return total.astype(jnp.bfloat16).reshape((count,) + extended.shape[1:])


def kernel_terms(extended, lead, upstream):
    count = upstream.shape[0]
    chans = upstream.shape[-1]
    flat_up = upstream.reshape(-1, chans)
    terms = []
    for k in range(3):
        past = extended[lead - k : lead - k + count].reshape(-1, chans)
        terms.append(jnp.dot(past.T, flat_up, preferred_element_type=jnp.float32))
    return jnp.stack(terms)


def local(frames_in, cotangent, spatial_weight, temporal_weight):
    xin = frames_in[0]
    dyv = cotangent[0]
    nfr, height, width, chans = xin.shape
    rimmed = padded_2(xin, (("space", 1),), 1)
    xpad = jnp.pad(rimmed, ((0, 0), (0, 0), (1, 1), (0, 0)))
    pre = spatial_conv(xpad, spatial_weight, height, width)
    act = jax.nn.silu(pre).astype(jnp.bfloat16)
    act_time, dy_time = (
        lax.all_to_all(act, "tm", split_axis=2, concat_axis=0, tiled=True),
        lax.all_to_all(dyv, "tm", split_axis=2, concat_axis=0, tiled=True),
    )
    total_frames = act_time.shape[0]
    act_ext = jnp.pad(act_time, ((2, 0), (0, 0), (0, 0), (0, 0)))
    dy_ext = jnp.pad(dy_time, ((0, 2), (0, 0), (0, 0), (0, 0)))
    mixed_time = causal_mix(act_ext, 2, temporal_weight)
    agrad_time = reverse_mix(dy_ext, total_frames, temporal_weight)
    temporal_terms = kernel_terms(act_ext, 2, dy_time)
    mixed, agrad = (
        lax.all_to_all(mixed_time, "tm", split_axis=0, concat_axis=2, tiled=True),
        lax.all_to_all(agrad_time, "tm", split_axis=0, concat_axis=2, tiled=True),
    )
    block_out = (xin.astype(jnp.float32) + mixed.astype(jnp.float32)).astype(jnp.bfloat16)
    sigma = jax.nn.sigmoid(pre)
    pgrad = (agrad.astype(jnp.float32) * sigma * (1.0 + pre * (1.0 - sigma))).astype(jnp.bfloat16)
    pflat = pgrad.reshape(-1, chans)
    spatial_terms = []
    for i in range(3):
        for j in range(3):
            window = xpad[:, i : i + height, j : j + width, :].reshape(-1, chans)
            spatial_terms.append(jnp.dot(window.T, pflat, preferred_element_type=jnp.float32))
    spatial_terms = jnp.stack(spatial_terms).reshape(3, 3, chans, chans)
    grad_rimmed = padded_2(pgrad, (("space", 1),), 1)
    grad_pad = jnp.pad(grad_rimmed, ((0, 0), (0, 0), (1, 1), (0, 0)))
    flipped = jnp.transpose(spatial_weight, (0, 1, 3, 2))[::-1, ::-1]
    back = spatial_conv(grad_pad, flipped, height, width)
    input_grad = (dyv.astype(jnp.float32) + back).astype(jnp.bfloat16)
    spatial_sum, temporal_sum = lax.psum((spatial_terms, temporal_terms), ("clip", "tm", "space"))
    positions = (
        lax.axis_size("clip") * lax.axis_size("tm") * nfr * lax.axis_size("space") * height * width
    )
    scale = 1.0 / jnp.sqrt(jnp.float32(positions))
    return (block_out[None], input_grad[None], spatial_sum * scale, temporal_sum * scale)


def solution(mesh):
    in_specs = (
        P("clip", "tm", "space", None, None),
        P("clip", "tm", "space", None, None),
        P(),
        P(),
    )
    out_specs = (
        P("clip", "tm", "space", None, None),
        P("clip", "tm", "space", None, None),
        P(),
        P(),
    )
    return jax.shard_map(local, mesh=mesh, in_specs=in_specs, out_specs=out_specs, check_vma=False)
```

profile of v0, /device:TPU:1, one launch (start us, length us, event | category | flops | bytes accessed | tf_op | source)
XLA Modules:
  0.0 425.4 jit_solution(2361727054454158863)
XLA Ops:
  7.2 2.9 copy.131
  10.0 9.2 %all-to-all-start.2 = ((bf16[2,8,128,256]{3,1,0,2:T(8,128)(2,1)}), bf16[2,8,128,256]{3,1,0,2:T(8,128)(2,1)}, u32[]{:S(2)}, u32[]{:S(2)}) async-start(bf16[2,8,128,256]{3,1,0,2:T(8,128)(2,1)} %bitcast.271), calls=%async_computation.2 | async-start | bytes 2097152 | tf_op jit(solution)/shard_map/all_to_all | solution.py:70
  20.0 4.0 collective-permute-start
  25.9 4.7 %collective-permute-done.1 = bf16[2,1,128,256]{2,3,1,0:T(8,128)(2,1)S(1)} collective-permute-done((bf16[2,1,128,256]{2,3,1,0:T(8,128)(2,1)S(1)}, bf16[2,1,128,256]{2,3,1,0:T(8,128)(2,1)S(1)}, u32[]{:S(2)}, u32[]{:S(2)}) %collective-permute-start.1) | collective-permute-done | bytes 131104 | tf_op jit(solution)/shard_map/ppermute | solution.py:15
  30.7 2.8 fusion.7
  33.5 3.8 fusion.97
  39.6 3.0 pad_maximum_fusion.2
  48.9 2.7 convolution_add_fusion.18
  56.9 6.9 %all-to-all-start.3 = ((bf16[32,8,8,256]{3,2,1,0:T(8,128)(2,1)}), bf16[32,8,8,256]{3,2,1,0:T(8,128)(2,1)}, u32[]{:S(2)}, u32[]{:S(2)}) async-start(bf16[32,8,8,256]{3,2,1,0:T(8,128)(2,1)} %bitcast.309), calls=%async_computation.3 | async-start | bytes 2097152 | tf_op jit(solution)/shard_map/all_to_all | solution.py:80
  63.9 3.7 convolution_add_fusion.17
  76.7 2.3 copy.78
  79.0 2.5 convolution_add_fusion.16
  85.9 2.7 convolution_add_fusion.12
  92.8 2.9 fusion.12
  95.7 2.9 fusion.14
  102.1 6.0 %all-to-all-start = ((bf16[2,8,128,256]{3,1,0,2:T(8,128)(2,1)}), bf16[2,8,128,256]{3,1,0,2:T(8,128)(2,1)}, u32[]{:S(2)}, u32[]{:S(2)}) async-start(bf16[2,8,128,256]{3,1,0,2:T(8,128)(2,1)} %copy.79), calls=%async_computation | async-start | bytes 2097152 | tf_op jit(solution)/shard_map/all_to_all | solution.py:69
  108.1 2.7 fusion.37
  113.3 3.0 fusion.40
  118.7 3.4 collective-permute-start.2
  129.1 2.3 fusion.98
  139.2 2.3 convolution_bitcast_fusion.3
  147.0 7.2 %all-to-all-start.1 = ((bf16[32,8,8,256]{3,2,1,0:T(8,128)(2,1)}), bf16[32,8,8,256]{3,2,1,0:T(8,128)(2,1)S(1)}, u32[]{:S(2)}, u32[]{:S(2)}) async-start(bf16[32,8,8,256]{3,2,1,0:T(8,128)(2,1)} %bitcast.310), calls=%async_computation.1 | async-start | bytes 2097152 | tf_op jit(solution)/shard_map/all_to_all | solution.py:79
  160.6 251.3 %all-reduce.7.cloned.1.call-done = (f32[3,3,256,256]{3,2,1,0:T(8,128)}, f32[3,256,256]{2,1,0:T(8,128)}) async-done(((f32[3,3,256,256]{3,2,1,0:T(8,128)}, f32[3,256,256]{2,1,0:T(8,128)}), (f32[3,3,256,256]{3,2,1,0:T(8,128)}, f32[3,256,256]{2,1,0:T(8,128)})) %all-reduce.7.cloned.1.call-update) | async-done | bytes 3145744 | tf_op jit(solution)/shard_map/psum | solution.py:97
  413.9 3.4 broadcast_multiply_fusion
  (114 shorter events, 72.1 us)
Async XLA Ops:
  7.2 12.1 %copy-start.6 = (bf16[1,2,8,128,256]{4,3,2,1,0:T(8,128)(2,1)S(1)}, bf16[1,2,8,128,256]{4,3,2,1,0:T(8,128)(2,1)}, u32[]{:S(2)}) copy-start(bf16[1,2,8,128,256]{4,3,2,1,0:T(8,128)(2,1)} %param.4) | copy-start | bytes 3145732
  10.0 41.5 %all-to-all-start.2 = ((bf16[2,8,128,256]{3,1,0,2:T(8,128)(2,1)}), bf16[2,8,128,256]{3,1,0,2:T(8,128)(2,1)}, u32[]{:S(2)}, u32[]{:S(2)}) async-start(bf16[2,8,128,256]{3,1,0,2:T(8,128)(2,1)} %bitcast.271), calls=%async_computation.2 | async-start | bytes 2097152 | tf_op jit(solution)/shard_map/all_to_all | solution.py:70
  20.0 5.9 %copy-start.4 = (bf16[1,2,8,128,256]{3,4,2,1,0:T(8,128)(2,1)}, bf16[1,2,8,128,256]{3,4,2,1,0:T(8,128)(2,1)S(1)}, u32[]{:S(2)}) copy-start(bf16[1,2,8,128,256]{3,4,2,1,0:T(8,128)(2,1)S(1)} %copy.70) | copy-start | bytes 3145732
  20.0 5.9 %collective-permute-start = (bf16[2,1,128,256]{2,3,1,0:T(8,128)(2,1)S(1)}, bf16[2,1,128,256]{2,3,1,0:T(8,128)(2,1)S(1)}, u32[]{:S(2)}, u32[]{:S(2)}) collective-permute-start(bf16[2,1,128,256]{2,3,1,0:T(8,128)(2,1)S(1)} %get-tuple-element.30), channel_id=1, source_target_pairs={{0,1},{1,2},{2,3},{3,4},{4,5},{5,6},{6,7},{8,9},{9,10},{10,11},{11... | collective-permute-start | bytes 393224 | tf_op jit(solution)/shard_map/ppermute | solution.py:12
  24.0 6.7 %collective-permute-start.1 = (bf16[2,1,128,256]{2,3,1,0:T(8,128)(2,1)S(1)}, bf16[2,1,128,256]{2,3,1,0:T(8,128)(2,1)S(1)}, u32[]{:S(2)}, u32[]{:S(2)}) collective-permute-start(bf16[2,1,128,256]{2,3,1,0:T(8,128)(2,1)S(1)} %get-tuple-element.31), channel_id=1, source_target_pairs={{1,0},{2,1},{3,2},{4,3},{5,4},{6,5},{7,6},{9,8},{10,9},{11,10},{12... | collective-permute-start | bytes 393224 | tf_op jit(solution)/shard_map/ppermute | solution.py:15
  47.1 1.8 copy-start.19
  53.2 1.8 copy-start
  56.9 32.6 %all-to-all-start.3 = ((bf16[32,8,8,256]{3,2,1,0:T(8,128)(2,1)}), bf16[32,8,8,256]{3,2,1,0:T(8,128)(2,1)}, u32[]{:S(2)}, u32[]{:S(2)}) async-start(bf16[32,8,8,256]{3,2,1,0:T(8,128)(2,1)} %bitcast.309), calls=%async_computation.3 | async-start | bytes 2097152 | tf_op jit(solution)/shard_map/all_to_all | solution.py:80
  79.0 2.5 copy-start.7
  91.0 1.8 copy-start.24
  95.7 3.0 copy-start.20
  102.1 35.5 %all-to-all-start = ((bf16[2,8,128,256]{3,1,0,2:T(8,128)(2,1)}), bf16[2,8,128,256]{3,1,0,2:T(8,128)(2,1)}, u32[]{:S(2)}, u32[]{:S(2)}) async-start(bf16[2,8,128,256]{3,1,0,2:T(8,128)(2,1)} %copy.79), calls=%async_computation | async-start | bytes 2097152 | tf_op jit(solution)/shard_map/all_to_all | solution.py:69
  108.1 303.8 %all-reduce.7.cloned.1.call-start = ((), (), s32[]{:S(2)}) async-start(), calls=%async_computation.4 | async-start | bytes 6291456 | tf_op jit(solution)/shard_map/psum | solution.py:97
  108.1 2.7 copy-start.3
  110.9 2.4 copy-start.8
  110.9 2.4 copy-start.21
  116.3 7.9 %copy-start.5 = (bf16[1,2,8,128,256]{3,4,2,1,0:T(8,128)(2,1)S(1)}, bf16[1,2,8,128,256]{3,4,2,1,0:T(8,128)(2,1)}, u32[]{:S(2)}) copy-start(bf16[1,2,8,128,256]{3,4,2,1,0:T(8,128)(2,1)} %copy-done.4) | copy-start | bytes 3145732
  118.7 8.0 %collective-permute-start.2 = (bf16[2,1,128,256]{3,2,1,0:T(8,128)(2,1)}, bf16[2,1,128,256]{3,2,1,0:T(8,128)(2,1)S(1)}, u32[]{:S(2)}, u32[]{:S(2)}) collective-permute-start(bf16[2,1,128,256]{3,2,1,0:T(8,128)(2,1)} %get-tuple-element.22), channel_id=1, source_target_pairs={{0,1},{1,2},{2,3},{3,4},{4,5},{5,6},{6,7},{8,9},{9,10},{10,11},{11... | collective-permute-start | bytes 393224 | tf_op jit(solution)/shard_map/ppermute | solution.py:12
  122.0 6.3 %collective-permute-start.3 = (bf16[2,1,128,256]{3,2,1,0:T(8,128)(2,1)S(1)}, bf16[2,1,128,256]{3,2,1,0:T(8,128)(2,1)S(1)}, u32[]{:S(2)}, u32[]{:S(2)}) collective-permute-start(bf16[2,1,128,256]{3,2,1,0:T(8,128)(2,1)S(1)} %get-tuple-element.23), channel_id=1, source_target_pairs={{1,0},{2,1},{3,2},{4,3},{5,4},{6,5},{7,6},{9,8},{10,9},{11,10},{12... | collective-permute-start | bytes 393224 | tf_op jit(solution)/shard_map/ppermute | solution.py:15
  129.0 2.4 copy-start.11
  147.0 7.3 %copy-start.12 = (bf16[2,8,128,256]{3,2,1,0:T(8,128)(2,1)S(1)}, bf16[2,8,128,256]{3,2,1,0:T(8,128)(2,1)}, u32[]{:S(2)}) copy-start(bf16[2,8,128,256]{3,2,1,0:T(8,128)(2,1)} %get-tuple-element.19) | copy-start | bytes 3145732
  147.0 270.3 %all-to-all-start.1 = ((bf16[32,8,8,256]{3,2,1,0:T(8,128)(2,1)}), bf16[32,8,8,256]{3,2,1,0:T(8,128)(2,1)S(1)}, u32[]{:S(2)}, u32[]{:S(2)}) async-start(bf16[32,8,8,256]{3,2,1,0:T(8,128)(2,1)} %bitcast.310), calls=%async_computation.1 | async-start | bytes 2097152 | tf_op jit(solution)/shard_map/all_to_all | solution.py:79
  154.3 2.0 copy-start.14
  413.9 3.4 copy-start.9
  (11 other events, 15.4 us)
Sparse Core Ops, SparseCore 0:
  145.7 266.0 all-reduce.6
where the time goes:
time: 428 us; the launch traced here: 425 us
  waiting for transfers between devices  259 us (61%)
  matrix products  51.2 us (12%)
  starting transfers between devices  40.8 us (10%)
  local copies, waits for them, and re-layouts  39.1 us (9%)
  other arithmetic  21.1 us (5%)
  between operations  14.5 us (3%)
    psum x1, waiting for transfers between devices, local(): lax.psum((spatial_terms, temporal_terms), ('clip', 'tm', 'space'))  251 us
    dot_general x18, matrix products, spatial_conv(): jnp.dot(window, kernel[i, j], preferred_element_type=jnp.float32)  29.1 us
    slice x10, local copies, waits for them, and re-layouts, spatial_conv(): window = padded[:, i:i + height, j:j + width, :].reshape(-1, chans)  24.4 us
    dot_general x9, matrix products, local(): jnp.dot(window.T, pflat, preferred_element_type=jnp.float32)  14.1 us
    all_to_all x1, starting transfers between devices, local(): lax.all_to_all(dyv, 'tm', split_axis=2, concat_axis=0, tiled=True)  9.24 us
  transfers between devices with their start and end apart: 9, of which 4 were waited for; matrix products, arithmetic and copies ran while one was open for 19% of the time, Pallas kernels for 0%

commit v1 on v0

v1 whole, which is shorter than its diff:
```python
import functools

import jax
import jax.numpy as jnp
from jax import lax
from jax.experimental import pallas as pl
from jax.experimental.pallas import tpu as pltpu
from jax.sharding import Mesh, PartitionSpec as P

BF = jnp.bfloat16
F32 = jnp.float32
TM = ("y", "zl")
SPACE = ("x", "core")
PLANE = ("y", "x")
COLUMN = ("clip", "zl")
COLS = 128
NT = (((1,), (1,)), ((), ()))


def call(kernel, outs, ins, scratch=(), flops=0, moved=0, limit=32, smem=()):
    vmem = pl.BlockSpec(memory_space=pltpu.VMEM)
    specs = [pl.BlockSpec(memory_space=pltpu.SMEM) if i in smem else vmem for i in range(len(ins))]
    return pl.pallas_call(
        kernel,
        out_shape=outs,
        in_specs=specs,
        out_specs=jax.tree.map(lambda _: vmem, outs),
        scratch_shapes=list(scratch),
        cost_estimate=pl.CostEstimate(flops=flops, bytes_accessed=moved, transcendentals=0),
        compiler_params=pltpu.CompilerParams(vmem_limit_bytes=limit << 20),
    )(*ins)


def shape(dims, kind=BF):
    return jax.ShapeDtypeStruct(dims, kind)


def shifted(value, column, step):
    edge = 0 if step == 1 else COLS - 1
    rolled = pltpu.roll(value, step % value.shape[0], 0)
    return jnp.where(column == edge, 0.0, rolled)


def columns_of(rows, width):
    return lax.broadcasted_iota(jnp.int32, (rows, width), 0) % COLS


def window(ref, frame, start, rows, offsets):
    parts = [ref[frame, pl.ds(start + off * COLS, rows), :] for off in offsets]
    return jnp.concatenate(parts, axis=1)


CHUNK = 512


def fill(padded, block, top, bottom, frame):
    size = block.shape[1]
    padded[frame, 0:COLS, :] = top[frame]
    padded[frame, COLS : COLS + size, :] = block[frame]
    padded[frame, COLS + size :, :] = bottom[frame]


def forward_kernel(x, top, bottom, weight, act, slope, x_t, act_t, padded):
    frames, size, chans = x.shape
    for f in range(frames):
        fill(padded, x, top, bottom, f)

    @pl.loop(0, frames * (size // CHUNK))
    def _(step):
        f = step // (size // CHUNK)
        start = pl.multiple_of((step % (size // CHUNK)) * CHUNK, CHUNK)
        rows = window(padded, f, start, CHUNK, (0, 1, 2))
        column = columns_of(CHUNK, chans)
        z = [
            jnp.dot(rows, weight[:, j].reshape(3 * chans, chans), preferred_element_type=F32)
            for j in range(3)
        ]
        pre = shifted(z[0], column, 1) + z[1] + shifted(z[2], column, -1)
        sigma = 1.0 / (1.0 + jnp.exp(-pre))
        active = (pre * sigma).astype(BF)
        act[f, pl.ds(start, CHUNK), :] = active
        slope[f, pl.ds(start, CHUNK), :] = sigma * (1.0 + pre * (1.0 - sigma))
        act_t[f, :, pl.ds(start, CHUNK)] = active.T

    for f in range(frames):
        x_t[f] = padded[f].T


def gradient_kernel(core, dy, ahead, weight, slope, x_t, act_t, pgrad, keep, send, dyx, wide, terms):
    frames, size, chans = dy.shape
    for f in range(frames):
        dyx[f * size : (f + 1) * size, :] = dy[f]
        dyx[(frames + f) * size : (frames + f + 1) * size, :] = ahead[f]

    @pl.loop(0, frames * (size // CHUNK))
    def _(step):
        start = pl.multiple_of(step * CHUNK, CHUNK)
        rows = jnp.concatenate([dyx[pl.ds(start + k * size, CHUNK), :] for k in range(3)], axis=1)
        taps = jnp.concatenate([weight[k] for k in range(3)], axis=1)
        agrad = lax.dot_general(rows, taps, NT, preferred_element_type=F32).astype(BF)
        grad = (agrad.astype(F32) * slope[pl.ds(start, CHUNK), :]).astype(BF)
        pgrad[pl.ds(start, CHUNK), :] = grad
        full = grad.astype(F32)
        column = columns_of(CHUNK, chans)
        wide[0, pl.ds(start, CHUNK), :] = shifted(full, column, -1).astype(BF)
        wide[1, pl.ds(start, CHUNK), :] = grad
        wide[2, pl.ds(start, CHUNK), :] = shifted(full, column, 1).astype(BF)

    left = jnp.concatenate(
        [
            jnp.concatenate([x_t[f, :, i * COLS : i * COLS + size] for f in range(frames)], axis=1)
            for i in range(3)
        ],
        axis=0,
    )
    for j in range(3):
        out = jnp.dot(left, wide[j], preferred_element_type=F32).astype(BF)
        for i in range(3):
            for h in range(2):
                at = ((3 * i + j) * 2 + h) * chans
                terms[at : at + chans, :] = out[i * chans : (i + 1) * chans, h * 128 : (h + 1) * 128]
    left_t = jnp.concatenate([act_t[f] for f in range(frames)], axis=1)
    for k in range(3):
        right = dyx[k * size : (k + frames) * size, :]
        out = jnp.dot(left_t, right, preferred_element_type=F32).astype(BF)
        for h in range(2):
            at = ((9 + k) * 2 + h) * chans
            terms[at : at + chans, :] = out[:, h * 128 : (h + 1) * 128]
    half = terms.shape[0] // 2
    for c in range(2):

        @pl.when(core[0] == c)
        def _():
            keep[...] = terms[c * half : (c + 1) * half, :]
            send[...] = terms[(1 - c) * half : (2 - c) * half, :]


def add_kernel(a, b, out):
    out[...] = (a[...].astype(F32) + b[...].astype(F32)).astype(BF)


def sum_kernel(scale, parts, out):
    total = parts[0].astype(F32)
    for i in range(1, parts.shape[0]):
        total = total + parts[i].astype(F32)
    out[...] = (total * scale).astype(out.dtype)


def spread_kernel(value, out):
    for i in range(out.shape[0]):
        out[i] = value[...].astype(out.dtype)


def final_kernel(core, own, other, spatial, temporal):
    half = own.shape[0] // 2
    for c in range(2):

        @pl.when(core[0] == c)
        def _():
            for t in range(12):
                source = own if t // 6 == c else other
                at = (t % 6) * 512
                for h in range(2):
                    part = source[at + h * 256 : at + (h + 1) * 256, :].astype(F32)
                    if t < 9:
                        spatial[t, :, h * 128 : (h + 1) * 128] = part
                    else:
                        temporal[t - 9, :, h * 128 : (h + 1) * 128] = part


def back_kernel(grad, top, bottom, weight, dy, out, padded):
    frames, size, chans = dy.shape
    for f in range(frames):
        fill(padded, grad, top, bottom, f)

    @pl.loop(0, frames * (size // CHUNK))
    def _(step):
        f = step // (size // CHUNK)
        start = pl.multiple_of((step % (size // CHUNK)) * CHUNK, CHUNK)
        rows = window(padded, f, start, CHUNK, (2, 1, 0))
        column = columns_of(CHUNK, chans)
        z = [
            lax.dot_general(
                rows,
                jnp.concatenate([weight[i, j] for i in range(3)], axis=1),
                NT,
                preferred_element_type=F32,
            )
            for j in range(3)
        ]
        back = shifted(z[0], column, -1) + z[1] + shifted(z[2], column, 1)
        out[f, pl.ds(start, CHUNK), :] = (dy[f, pl.ds(start, CHUNK), :].astype(F32) + back).astype(BF)


def mix_kernel(act, behind, weight, x, out, ext):
    frames, size, chans = act.shape
    for f in range(frames):
        ext[f * size : (f + 1) * size, :] = behind[f]
        ext[(frames + f) * size : (frames + f + 1) * size, :] = act[f]

    @pl.loop(0, frames * (size // CHUNK))
    def _(step):
        start = pl.multiple_of(step * CHUNK, CHUNK)
        rows = jnp.concatenate(
            [ext[pl.ds(start + (2 - k) * size, CHUNK), :] for k in range(3)], axis=1
        )
        mixed = jnp.dot(rows, weight[...].reshape(3 * chans, chans), preferred_element_type=F32)
        own = x[pl.ds(start, CHUNK), :].astype(F32)
        out[pl.ds(start, CHUNK), :] = (own + mixed.astype(BF).astype(F32)).astype(BF)


def steps(axes, by):
    count = lax.axis_size(axes)
    return [(i, i + by) for i in range(count) if 0 <= i + by < count]


def exchange(value, axes):
    return lax.all_to_all(value, axes, split_axis=0, concat_axis=0, tiled=True)


def rims(block):
    size = block.shape[1]
    top = lax.ppermute(block[:, size - COLS :, :], SPACE, steps(SPACE, 1))
    bottom = lax.ppermute(block[:, :COLS, :], SPACE, steps(SPACE, -1))
    return top, bottom


def local(scale, frames_in, cotangent, spatial_weight, temporal_weight):
    dims = frames_in.shape
    frames, chans = dims[1], dims[4]
    size = dims[2] * dims[3]
    x = frames_in.reshape(frames, size, chans)
    dy = cotangent.reshape(frames, size, chans)
    work = 2 * frames * size * chans * chans
    core = lax.axis_index("core").astype(jnp.int32).reshape(1)
    top, bottom = rims(x)
    ahead = lax.ppermute(dy, TM, steps(TM, -1))
    act, slope, x_t, act_t = call(
        forward_kernel,
        [
            shape((frames, size, chans)),
            shape((frames, size, chans), F32),
            shape((frames, chans, size + 2 * COLS)),
            shape((frames, chans, size)),
        ],
        (x, top, bottom, spatial_weight),
        [pltpu.VMEM((frames, size + 2 * COLS, chans), BF)],
        flops=9 * work,
        moved=9 << 20,
    )
    act_later, ahead = lax.optimization_barrier((act, ahead))
    behind = lax.ppermute(act_later, TM, steps(TM, 1))
    flat = frames * size
    rows = 12 * chans
    pgrad, keep, send = call(
        gradient_kernel,
        [shape((flat, chans)), shape((rows, 128)), shape((rows, 128))],
        (core, dy, ahead, temporal_weight, slope.reshape(flat, chans), x_t, act_t),
        [
            pltpu.VMEM((2 * flat, chans), BF),
            pltpu.VMEM((3, flat, chans), BF),
            pltpu.VMEM((2 * rows, 128), BF),
        ],
        flops=15 * work,
        moved=11 << 20,
        smem=(0,),
    )
    got = lax.ppermute(send, "core", [(0, 1), (1, 0)])
    pgrad = pgrad.reshape(frames, size, chans)
    half = call(add_kernel, shape((rows, 128)), (keep, got), moved=3 << 20)
    plane, column = lax.axis_size(PLANE), lax.axis_size(COLUMN)
    share = rows // plane
    piece = share // column
    first = exchange(half.reshape(plane, share, 128), PLANE)
    grad_top, grad_bottom = rims(pgrad)
    part = call(functools.partial(sum_kernel, 1.0), shape((share, 128), F32), (first,), moved=1 << 20)
    second = exchange(part.reshape(column, piece, 128), COLUMN)
    total = call(functools.partial(sum_kernel, scale), shape((piece, 128), F32), (second,), moved=1 << 17)
    spread = call(spread_kernel, shape((column, piece, 128), F32), (total,), moved=1 << 17)
    third = exchange(spread, COLUMN).reshape(share, 128)
    wider = call(spread_kernel, shape((plane, share, 128)), (third,), moved=1 << 20)
    own = exchange(wider, PLANE).reshape(rows, 128)
    other = lax.ppermute(own, "core", [(0, 1), (1, 0)])
    spatial, temporal = call(
        final_kernel,
        [shape((9, chans, chans), F32), shape((3, chans, chans), F32)],
        (core, own, other),
        moved=5 << 20,
        smem=(0,),
    )
    input_grad = call(
        back_kernel,
        shape((frames, size, chans)),
        (pgrad, grad_top, grad_bottom, spatial_weight, dy),
        [pltpu.VMEM((frames, size + 2 * COLS, chans), BF)],
        flops=9 * work,
        moved=5 << 20,
    )
    block_out = call(
        mix_kernel,
        shape((flat, chans)),
        (act, behind, temporal_weight, x.reshape(flat, chans)),
        [pltpu.VMEM((2 * flat, chans), BF)],
        flops=3 * work,
        moved=4 << 20,
    )
    return (
        block_out.reshape(dims),
        input_grad.reshape(dims),
        spatial.reshape(3, 3, chans, chans),
        temporal,
    )


def solution(mesh):
    fine = Mesh(mesh.devices.reshape(2, 4, 4, 4, 2), ("clip", "y", "zl", "x", "core"))
    blocks = P("clip", TM, SPACE, None, None)

    def run(frames_in, cotangent, spatial_weight, temporal_weight):
        clips, frames, height, width, _ = frames_in.shape
        scale = (clips * frames * height * width) ** -0.5
        return jax.shard_map(
            functools.partial(local, scale),
            mesh=fine,
            in_specs=(blocks, blocks, P(), P()),
            out_specs=(blocks, blocks, P(), P()),
            check_vma=False,
        )(frames_in, cotangent, spatial_weight, temporal_weight)

    return run
```

time: 428 us -> 149 us (0.35)
  waiting for transfers between devices: 259 us -> 24.4 us
  matrix products: 51.2 us -> 0 us
  blocking collectives: 0 us -> 47.2 us
  local copies, waits for them, and re-layouts: 39.1 us -> 8.21 us
  other arithmetic: 21.1 us -> 0 us
  Pallas kernels: 0 us -> 19.8 us
  between operations: 14.5 us -> 0.78 us
  starting transfers between devices: 40.8 us -> 47.6 us
    psum x1 -> x0, waiting for transfers between devices: 251 us -> none  [local(): lax.psum((spatial_terms, temporal_terms), ('clip', 'tm', 'space'))]
    dot_general x36 -> x0, matrix products: 51.2 us -> none  [the longest x18 29.1 us: spatial_conv(): jnp.dot(window, kernel[i, j], preferred_element_type=jnp.float32)]
    all_to_all x0 -> x3, blocking collectives: none -> 47.2 us  [exchange(): return lax.all_to_all(value, axes, split_axis=0, concat_axis=0, tiled=True)]
    ppermute x4 -> x8, starting transfers between devices: 11.4 us -> 44 us  [the longest x1 26.2 us: local(): other = lax.ppermute(own, 'core', [(0, 1), (1, 0)])]
    all_to_all x4 -> x1, starting transfers between devices: 29.4 us -> 3.61 us  [exchange(): return lax.all_to_all(value, axes, split_axis=0, concat_axis=0, tiled=True)]
    slice x14 -> x2, local copies, waits for them, and re-layouts: 25.4 us -> 1.98 us  [rims(): bottom = lax.ppermute(block[:, :COLS, :], SPACE, steps(SPACE, -1))]
    pallas_call x0 -> x10, Pallas kernels: none -> 19.8 us  [call(): pl.pallas_call(kernel, out_shape=outs, in_specs=specs, out_specs=jax.tree...]
    ppermute x4 -> x8, waiting for transfers between devices: 6.46 us -> 16.2 us  [the longest x2 8.97 us: rims(): bottom = lax.ppermute(block[:, :COLS, :], SPACE, steps(SPACE, -1))]
  transfers between devices with their start and end apart: 9 -> 9, of which waited for: 4 -> 5; matrix products, arithmetic and copies ran while one was open for 19% -> 1% of each run, Pallas kernels for 0% -> 8%
where the time goes in v1:
time: 149 us; the launch traced here: 148 us
  starting transfers between devices  47.6 us (32%)
  blocking collectives  47.2 us (32%)
  waiting for transfers between devices  24.4 us (16%)
  Pallas kernels  19.8 us (13%)
  local copies, waits for them, and re-layouts  8.21 us (6%)
    all_to_all x3, blocking collectives, exchange(): return lax.all_to_all(value, axes, split_axis=0, concat_axis=0, tiled=True)  47.2 us
    ppermute x1, starting transfers between devices, local(): other = lax.ppermute(own, 'core', [(0, 1), (1, 0)])  26.2 us
    pallas_call x10, Pallas kernels, call(): pl.pallas_call(kernel, out_shape=outs, in_specs=specs, out_specs=jax.tree...  19.8 us
    ppermute x2, waiting for transfers between devices, rims(): bottom = lax.ppermute(block[:, :COLS, :], SPACE, steps(SPACE, -1))  8.97 us
    all_to_all x1, waiting for transfers between devices, exchange(): return lax.all_to_all(value, axes, split_axis=0, concat_axis=0, tiled=True)  8.25 us
    ppermute x2, starting transfers between devices, rims(): top = lax.ppermute(block[:, size - COLS:, :], SPACE, steps(SPACE, 1))  7.12 us
    unnamed x18, local copies, waits for them, and re-layouts  6.23 us
    ppermute x1, waiting for transfers between devices, local(): ahead = lax.ppermute(dy, TM, steps(TM, -1))  5.26 us
  transfers between devices with their start and end apart: 9, of which 5 were waited for; matrix products, arithmetic and copies ran while one was open for 1% of the time, Pallas kernels for 8%

profile of v1, /device:TPU:1, one launch (start us, length us, event | category | flops | bytes accessed | tf_op | source)
XLA Modules:
  0.0 148.0 jit_solution(5563652262961037068)
XLA Ops:
  0.6 1.3 collective-permute-start.2
  2.9 4.5 %collective-permute-start = (bf16[2,128,256]{2,1,0:T(8,128)(2,1)S(1)}, bf16[2,128,256]{2,1,0:T(8,128)(2,1)S(1)}, u32[]{:S(2)}, u32[]{:S(2)}) collective-permute-start(bf16[2,128,256]{2,1,0:T(8,128)(2,1)S(1)} %get-tuple-element.29), channel_id=1, source_target_pairs={{0,1},{1,2},{2,3},{3,4},{4,5},{5,6},{6,7},{8,9},{9,10},{10,11},{11... | collective-permute-start | bytes 393224 | tf_op jit(solution)/shard_map/ppermute | solution.py:223
  7.4 1.9 %collective-permute-start.1 = (bf16[2,128,256]{2,1,0:T(8,128)(2,1)S(1)}, bf16[2,128,256]{2,1,0:T(8,128)(2,1)S(1)}, u32[]{:S(2)}, u32[]{:S(2)}) collective-permute-start(bf16[2,128,256]{2,1,0:T(8,128)(2,1)S(1)} %get-tuple-element.28), channel_id=1, source_target_pairs={{1,0},{2,1},{3,2},{4,3},{5,4},{6,5},{7,6},{9,8},{10,9},{11,10},{12... | collective-permute-start | bytes 393224 | tf_op jit(solution)/shard_map/ppermute | solution.py:224
  9.4 4.6 %collective-permute-done.1.bottom = bf16[2,128,256]{2,1,0:T(8,128)(2,1)S(1)} collective-permute-done((bf16[2,128,256]{2,1,0:T(8,128)(2,1)S(1)}, bf16[2,128,256]{2,1,0:T(8,128)(2,1)S(1)}, u32[]{:S(2)}, u32[]{:S(2)}) %collective-permute-start.1) | collective-permute-done | bytes 131104 | tf_op jit(solution)/shard_map/ppermute | solution.py:224
  15.3 1.3 copy-done.5
  16.5 4.4 %shard_map.75 = (bf16[2,1024,256]{2,1,0:T(8,128)(2,1)S(1)}, f32[2,1024,256]{2,1,0:T(8,128)S(1)}, bf16[2,256,1280]{2,1,0:T(8,128)(2,1)S(1)}, bf16[2,256,1024]{2,1,0:T(8,128)(2,1)S(1)}) custom-call(bf16[2,1024,256]{2,1,0:T(8,128)(2,1)S(1)} %bitcast.17, bf16[2,128,256]{2,1,0:T(8,128)(2,1)S(1)} %collective-permute-done.top, ...), custom_call_target="tpu_custom_call" | custom-call | flops 2415919104 | bytes 9437184 | tf_op jit(solution)/shard_map/pallas_call | solution.py:23
  20.9 5.3 %collective-permute-done.2.ahead = bf16[2,1024,256]{2,1,0:T(8,128)(2,1)S(1)} collective-permute-done((bf16[2,1024,256]{2,1,0:T(8,128)(2,1)}, bf16[2,1024,256]{2,1,0:T(8,128)(2,1)S(1)}, u32[]{:S(2)}, u32[]{:S(2)}) %collective-permute-start.2) | collective-permute-done | bytes 1048608 | tf_op jit(solution)/shard_map/ppermute | solution.py:237
  26.2 5.4 %shard_map.77 = (bf16[2048,256]{1,0:T(8,128)(2,1)S(1)}, bf16[3072,128]{1,0:T(8,128)(2,1)S(1)}, bf16[3072,128]{1,0:T(8,128)(2,1)S(1)}) custom-call(s32[1]{0:T(128)} %bitcast.4.core, bf16[2,1024,256]{2,1,0:T(8,128)(2,1)S(1)} %bitcast.24, bf16[2,1024,256]{2,1,0:T(8,128)(2,1)S(1)} %collective-permute-done.2.ahead, bf16[3,256,256]{2,1,0:T(8,128)(2,1)S(1)} %copy-done.2, ...), custom_call_target="tpu_custom_call" | custom-call | flops 4026531840 | bytes 11534336 | tf_op jit(solution)/shard_map/pallas_call | solution.py:23
  31.6 3.2 %collective-permute-start.6 = (bf16[3072,128]{1,0:T(8,128)(2,1)S(1)}, bf16[3072,128]{1,0:T(8,128)(2,1)S(1)}, u32[]{:S(2)}, u32[]{:S(2)}) collective-permute-start(bf16[3072,128]{1,0:T(8,128)(2,1)S(1)} %get-tuple-element.23), channel_id=1, source_target_pairs={{0,1},{1,0},{2,3},{3,2},{4,5},{5,4},{6,7},{7,6},{8,9},{9,8},{10,11... | collective-permute-start | bytes 2359304 | tf_op jit(solution)/shard_map/ppermute | solution.py:268
  34.8 1.9 %collective-permute-done.6.b = bf16[3072,128]{1,0:T(8,128)(2,1)S(1)} collective-permute-done((bf16[3072,128]{1,0:T(8,128)(2,1)S(1)}, bf16[3072,128]{1,0:T(8,128)(2,1)S(1)}, u32[]{:S(2)}, u32[]{:S(2)}) %collective-permute-start.6) | collective-permute-done | bytes 786464 | tf_op jit(solution)/shard_map/ppermute | solution.py:268
  36.9 22.4 %all_to_all.20.parts = bf16[16,192,128]{2,1,0:T(8,128)(2,1)S(1)} all-to-all(bf16[16,192,128]{2,1,0:T(8,128)(2,1)S(1)} %bitcast.15), channel_id=1, replica_groups=mesh['clip'=2,'y'=4,'zl'=4,'x'=4,'core'=2] {'y','x'}, dimensions={0} | all-to-all | bytes 1572864 | tf_op jit(solution)/shard_map/all_to_all | solution.py:218
  59.5 14.7 %all_to_all.21.parts = f32[8,24,128]{2,1,0:T(8,128)S(1)} all-to-all(f32[8,24,128]{2,1,0:T(8,128)S(1)} %bitcast.19), channel_id=1, replica_groups=mesh['clip'=2,'y'=4,'zl'=4,'x'=4,'core'=2] {'clip','zl'}, dimensions={0} | all-to-all | bytes 196608 | tf_op jit(solution)/shard_map/all_to_all | solution.py:218
  74.2 10.1 %all_to_all.22 = f32[8,24,128]{2,1,0:T(8,128)S(1)} all-to-all(f32[8,24,128]{2,1,0:T(8,128)S(1)} %shard_map.82), channel_id=1, replica_groups=mesh['clip'=2,'y'=4,'zl'=4,'x'=4,'core'=2] {'clip','zl'}, dimensions={0} | all-to-all | bytes 196608 | tf_op jit(solution)/shard_map/all_to_all | solution.py:218
  85.2 3.6 %all-to-all-start.3 = ((bf16[16,192,128]{2,1,0:T(8,128)(2,1)}), bf16[16,192,128]{2,1,0:T(8,128)(2,1)S(1)}, u32[]{:S(2)}, u32[]{:S(2)}) async-start(bf16[16,192,128]{2,1,0:T(8,128)(2,1)} %shard_map.83), calls=%async_computation.3 | async-start | bytes 1572864 | tf_op jit(solution)/shard_map/all_to_all | solution.py:218
  88.8 2.2 %collective-permute-start.3 = (bf16[2,1024,256]{2,1,0:T(8,128)(2,1)S(1)}, bf16[2,1024,256]{2,1,0:T(8,128)(2,1)S(1)}, u32[]{:S(2)}, u32[]{:S(2)}) collective-permute-start(bf16[2,1024,256]{2,1,0:T(8,128)(2,1)S(1)} %get-tuple-element.16.act), channel_id=1, source_target_pairs={{0,8},{8,16},{16,24},{24,32},{32,40},{40,48},{48,56},{56,64},{64,7... | collective-permute-start | bytes 3145736 | tf_op jit(solution)/shard_map/ppermute | solution.py:252
  91.0 8.2 %all-to-all-done.3 = bf16[16,192,128]{2,1,0:T(8,128)(2,1)S(1)} async-done(((bf16[16,192,128]{2,1,0:T(8,128)(2,1)}), bf16[16,192,128]{2,1,0:T(8,128)(2,1)S(1)}, u32[]{:S(2)}, u32[]{:S(2)}) %all-to-all-start.3) | async-done | bytes 786464 | tf_op jit(solution)/shard_map/all_to_all | solution.py:218
  99.2 26.2 %collective-permute-start.7 = (bf16[3072,128]{1,0:T(8,128)(2,1)S(1)}, bf16[3072,128]{1,0:T(8,128)(2,1)S(1)}, u32[]{:S(2)}, u32[]{:S(2)}) collective-permute-start(bf16[3072,128]{1,0:T(8,128)(2,1)S(1)} %bitcast.13), channel_id=1, source_target_pairs={{0,1},{1,0},{2,3},{3,2},{4,5},{5,4},{6,7},{7,6},{8,9},{9,8},{10,11... | collective-permute-start | bytes 2359304 | tf_op jit(solution)/shard_map/ppermute | solution.py:283
  126.4 2.6 %collective-permute-start.4 = (bf16[2,128,256]{2,1,0:T(8,128)(2,1)S(1)}, bf16[2,128,256]{2,1,0:T(8,128)(2,1)S(1)}, u32[]{:S(2)}, u32[]{:S(2)}) collective-permute-start(bf16[2,128,256]{2,1,0:T(8,128)(2,1)S(1)} %get-tuple-element.27), channel_id=1, source_target_pairs={{0,1},{1,2},{2,3},{3,4},{4,5},{5,6},{6,7},{8,9},{9,10},{10,11},{11... | collective-permute-start | bytes 393224 | tf_op jit(solution)/shard_map/ppermute | solution.py:223
  129.1 2.1 %collective-permute-start.5 = (bf16[2,128,256]{2,1,0:T(8,128)(2,1)S(1)}, bf16[2,128,256]{2,1,0:T(8,128)(2,1)S(1)}, u32[]{:S(2)}, u32[]{:S(2)}) collective-permute-start(bf16[2,128,256]{2,1,0:T(8,128)(2,1)S(1)} %get-tuple-element.26), channel_id=1, source_target_pairs={{1,0},{2,1},{3,2},{4,3},{5,4},{6,5},{7,6},{9,8},{10,9},{11,10},{12... | collective-permute-start | bytes 393224 | tf_op jit(solution)/shard_map/ppermute | solution.py:224
  131.1 4.3 %collective-permute-done.5.bottom = bf16[2,128,256]{2,1,0:T(8,128)(2,1)S(1)} collective-permute-done((bf16[2,128,256]{2,1,0:T(8,128)(2,1)S(1)}, bf16[2,128,256]{2,1,0:T(8,128)(2,1)S(1)}, u32[]{:S(2)}, u32[]{:S(2)}) %collective-permute-start.5) | collective-permute-done | bytes 131104 | tf_op jit(solution)/shard_map/ppermute | solution.py:224
  136.7 1.3 copy-done.6
  139.2 4.3 %shard_map.78 = bf16[2,1024,256]{2,1,0:T(8,128)(2,1)} custom-call(bf16[2,1024,256]{2,1,0:T(8,128)(2,1)S(1)} %bitcast.22, bf16[2,128,256]{2,1,0:T(8,128)(2,1)S(1)} %collective-permute-done.4.top, bf16[2,128,256]{2,1,0:T(8,128)(2,1)S(1)} %collective-permute-done.5.bottom, bf16[3,3,256,256]{3,2,1,0:T(8,128)(2,1)S(1)} %copy-done.6, ...), custom_call_target="tpu_custom_call" | custom-call | flops 2415919104 | bytes 5242880 | tf_op jit(solution)/shard_map/pallas_call | solution.py:23
  143.5 2.6 %shard_map.76 = bf16[2048,256]{1,0:T(8,128)(2,1)} custom-call(bf16[2,1024,256]{2,1,0:T(8,128)(2,1)S(1)} %get-tuple-element.16.act, bf16[2,1024,256]{2,1,0:T(8,128)(2,1)S(1)} %collective-permute-done.3.behind, bf16[3,256,256]{2,1,0:T(8,128)(2,1)S(1)} %copy-done.2, bf16[2048,256]{1,0:T(8,128)(2,1)S(1)} %bitcast.18), custom_call_target="tpu_custom_call" | custom-call | flops 805306368 | bytes 4194304 | tf_op jit(solution)/shard_map/pallas_call | solution.py:23
  146.2 1.9 %shard_map.84 = (f32[9,256,256]{2,1,0:T(8,128)}, f32[3,256,256]{2,1,0:T(8,128)}) custom-call(s32[1]{0:T(128)} %bitcast.4.core, bf16[3072,128]{1,0:T(8,128)(2,1)S(1)} %bitcast.14, bf16[3072,128]{1,0:T(8,128)(2,1)S(1)} %collective-permute-done.7.other), custom_call_target="tpu_custom_call" | custom-call | bytes 5242880 | tf_op jit(solution)/shard_map/pallas_call | solution.py:23
  (27 shorter events, 6.9 us)
Async XLA Ops:
  0.6 25.5 %collective-permute-start.2 = (bf16[2,1024,256]{2,1,0:T(8,128)(2,1)}, bf16[2,1024,256]{2,1,0:T(8,128)(2,1)S(1)}, u32[]{:S(2)}, u32[]{:S(2)}) collective-permute-start(bf16[2,1024,256]{2,1,0:T(8,128)(2,1)} %bitcast.23), channel_id=1, source_target_pairs={{8,0},{16,8},{24,16},{32,24},{40,32},{48,40},{56,48},{64,56},{72,6... | collective-permute-start | bytes 3145736 | tf_op jit(solution)/shard_map/ppermute | solution.py:237
  2.9 6.5 %collective-permute-start = (bf16[2,128,256]{2,1,0:T(8,128)(2,1)S(1)}, bf16[2,128,256]{2,1,0:T(8,128)(2,1)S(1)}, u32[]{:S(2)}, u32[]{:S(2)}) collective-permute-start(bf16[2,128,256]{2,1,0:T(8,128)(2,1)S(1)} %get-tuple-element.29), channel_id=1, source_target_pairs={{0,1},{1,2},{2,3},{3,4},{4,5},{5,6},{6,7},{8,9},{9,10},{10,11},{11... | collective-permute-start | bytes 393224 | tf_op jit(solution)/shard_map/ppermute | solution.py:223
  7.4 6.6 %collective-permute-start.1 = (bf16[2,128,256]{2,1,0:T(8,128)(2,1)S(1)}, bf16[2,128,256]{2,1,0:T(8,128)(2,1)S(1)}, u32[]{:S(2)}, u32[]{:S(2)}) collective-permute-start(bf16[2,128,256]{2,1,0:T(8,128)(2,1)S(1)} %get-tuple-element.28), channel_id=1, source_target_pairs={{1,0},{2,1},{3,2},{4,3},{5,4},{6,5},{7,6},{9,8},{10,9},{11,10},{12... | collective-permute-start | bytes 393224 | tf_op jit(solution)/shard_map/ppermute | solution.py:224
  14.0 1.2 copy-start
  15.3 1.3 copy-start.5
  16.5 9.7 %copy-start.2 = (bf16[3,256,256]{2,1,0:T(8,128)(2,1)S(1)}, bf16[3,256,256]{2,1,0:T(8,128)(2,1)}, u32[]{:S(2)}) copy-start(bf16[3,256,256]{2,1,0:T(8,128)(2,1)} %weight.6) | copy-start | bytes 1179652
  16.5 9.7 %copy-start.7 = (bf16[1,2,8,128,256]{4,3,2,1,0:T(8,128)(2,1)S(1)}, bf16[1,2,8,128,256]{4,3,2,1,0:T(8,128)(2,1)}, u32[]{:S(2)}) copy-start(bf16[1,2,8,128,256]{4,3,2,1,0:T(8,128)(2,1)} %param.5) | copy-start | bytes 3145732
  31.6 27.9 %copy-start.3 = (bf16[2048,256]{1,0:T(8,128)(2,1)}, bf16[2048,256]{1,0:T(8,128)(2,1)S(1)}, u32[]{:S(2)}) copy-start(bf16[2048,256]{1,0:T(8,128)(2,1)S(1)} %get-tuple-element.21) | copy-start | bytes 3145732
  31.6 5.1 %collective-permute-start.6 = (bf16[3072,128]{1,0:T(8,128)(2,1)S(1)}, bf16[3072,128]{1,0:T(8,128)(2,1)S(1)}, u32[]{:S(2)}, u32[]{:S(2)}) collective-permute-start(bf16[3072,128]{1,0:T(8,128)(2,1)S(1)} %get-tuple-element.23), channel_id=1, source_target_pairs={{0,1},{1,0},{2,3},{3,2},{4,5},{5,4},{6,7},{7,6},{8,9},{9,8},{10,11... | collective-permute-start | bytes 2359304 | tf_op jit(solution)/shard_map/ppermute | solution.py:268
  85.2 14.0 %all-to-all-start.3 = ((bf16[16,192,128]{2,1,0:T(8,128)(2,1)}), bf16[16,192,128]{2,1,0:T(8,128)(2,1)S(1)}, u32[]{:S(2)}, u32[]{:S(2)}) async-start(bf16[16,192,128]{2,1,0:T(8,128)(2,1)} %shard_map.83), calls=%async_computation.3 | async-start | bytes 1572864 | tf_op jit(solution)/shard_map/all_to_all | solution.py:218
  88.8 54.7 %collective-permute-start.3 = (bf16[2,1024,256]{2,1,0:T(8,128)(2,1)S(1)}, bf16[2,1024,256]{2,1,0:T(8,128)(2,1)S(1)}, u32[]{:S(2)}, u32[]{:S(2)}) collective-permute-start(bf16[2,1024,256]{2,1,0:T(8,128)(2,1)S(1)} %get-tuple-element.16.act), channel_id=1, source_target_pairs={{0,8},{8,16},{16,24},{24,32},{32,40},{40,48},{48,56},{56,64},{64,7... | collective-permute-start | bytes 3145736 | tf_op jit(solution)/shard_map/ppermute | solution.py:252
  99.2 46.9 %collective-permute-start.7 = (bf16[3072,128]{1,0:T(8,128)(2,1)S(1)}, bf16[3072,128]{1,0:T(8,128)(2,1)S(1)}, u32[]{:S(2)}, u32[]{:S(2)}) collective-permute-start(bf16[3072,128]{1,0:T(8,128)(2,1)S(1)} %bitcast.13), channel_id=1, source_target_pairs={{0,1},{1,0},{2,3},{3,2},{4,5},{5,4},{6,7},{7,6},{8,9},{9,8},{10,11... | collective-permute-start | bytes 2359304 | tf_op jit(solution)/shard_map/ppermute | solution.py:283
  126.4 4.7 %collective-permute-start.4 = (bf16[2,128,256]{2,1,0:T(8,128)(2,1)S(1)}, bf16[2,128,256]{2,1,0:T(8,128)(2,1)S(1)}, u32[]{:S(2)}, u32[]{:S(2)}) collective-permute-start(bf16[2,128,256]{2,1,0:T(8,128)(2,1)S(1)} %get-tuple-element.27), channel_id=1, source_target_pairs={{0,1},{1,2},{2,3},{3,4},{4,5},{5,6},{6,7},{8,9},{9,10},{10,11},{11... | collective-permute-start | bytes 393224 | tf_op jit(solution)/shard_map/ppermute | solution.py:223
  129.1 14.5 %copy-start.1 = (bf16[1,2,8,128,256]{4,3,2,1,0:T(8,128)(2,1)S(1)}, bf16[1,2,8,128,256]{4,3,2,1,0:T(8,128)(2,1)}, u32[]{:S(2)}) copy-start(bf16[1,2,8,128,256]{4,3,2,1,0:T(8,128)(2,1)} %param.4) | copy-start | bytes 3145732
  129.1 6.4 %collective-permute-start.5 = (bf16[2,128,256]{2,1,0:T(8,128)(2,1)S(1)}, bf16[2,128,256]{2,1,0:T(8,128)(2,1)S(1)}, u32[]{:S(2)}, u32[]{:S(2)}) collective-permute-start(bf16[2,128,256]{2,1,0:T(8,128)(2,1)S(1)} %get-tuple-element.26), channel_id=1, source_target_pairs={{1,0},{2,1},{3,2},{4,3},{5,4},{6,5},{7,6},{9,8},{10,9},{11,10},{12... | collective-permute-start | bytes 393224 | tf_op jit(solution)/shard_map/ppermute | solution.py:224
  135.5 1.2 copy-start.4
  136.7 1.3 copy-start.6
  138.0 1.2 copy-start.8

commit v2 on v1

--- a/solution.py
+++ b/solution.py
@@ -11,8 +11,7 @@
 F32 = jnp.float32
 TM = ("y", "zl")
 SPACE = ("x", "core")
-PLANE = ("y", "x")
-COLUMN = ("clip", "zl")
+PLANE = ("x", "y")
 COLS = 128
 NT = (((1,), (1,)), ((), ()))
 
@@ -86,25 +85,51 @@
         x_t[f] = padded[f].T
 
 
-def gradient_kernel(core, dy, ahead, weight, slope, x_t, act_t, pgrad, keep, send, dyx, wide, terms):
+def early_kernel(dy, weight, act_t, partial, terms):
     frames, size, chans = dy.shape
-    for f in range(frames):
-        dyx[f * size : (f + 1) * size, :] = dy[f]
-        dyx[(frames + f) * size : (frames + f + 1) * size, :] = ahead[f]
-
-    @pl.loop(0, frames * (size // CHUNK))
-    def _(step):
-        start = pl.multiple_of(step * CHUNK, CHUNK)
-        rows = jnp.concatenate([dyx[pl.ds(start + k * size, CHUNK), :] for k in range(3)], axis=1)
-        taps = jnp.concatenate([weight[k] for k in range(3)], axis=1)
-        agrad = lax.dot_general(rows, taps, NT, preferred_element_type=F32).astype(BF)
-        grad = (agrad.astype(F32) * slope[pl.ds(start, CHUNK), :]).astype(BF)
-        pgrad[pl.ds(start, CHUNK), :] = grad
+
+    @pl.loop(0, size // CHUNK)
+    def _(step):
+        at = pl.ds(pl.multiple_of(step * CHUNK, CHUNK), CHUNK)
+        second = dy[1, at, :]
+        both = jnp.concatenate([dy[0, at, :], second], axis=1)
+        taps = jnp.concatenate([weight[0], weight[1]], axis=1)
+        partial[0, at, :] = lax.dot_general(both, taps, NT, preferred_element_type=F32)
+        partial[1, at, :] = lax.dot_general(second, weight[0], NT, preferred_element_type=F32)
+
+    left = jnp.concatenate([act_t[0], act_t[1]], axis=1)
+    right = dy[...].reshape(frames * size, chans)
+    terms[0] = jnp.dot(left, right, preferred_element_type=F32)
+    terms[1] = jnp.dot(act_t[0], dy[1], preferred_element_type=F32)
+
+
+def gradient_kernel(
+    core, ahead, weight, slope, x_t, act_t, partial, early, pgrad, keep, send, wide, terms
+):
+    frames, size, chans = ahead.shape
+
+    def finish(f, start, agrad):
+        at = pl.ds(start, CHUNK)
+        grad = (agrad.astype(BF).astype(F32) * slope[f, at, :]).astype(BF)
+        pgrad[f, at, :] = grad
         full = grad.astype(F32)
         column = columns_of(CHUNK, chans)
-        wide[0, pl.ds(start, CHUNK), :] = shifted(full, column, -1).astype(BF)
-        wide[1, pl.ds(start, CHUNK), :] = grad
-        wide[2, pl.ds(start, CHUNK), :] = shifted(full, column, 1).astype(BF)
+        into = pl.ds(f * size + start, CHUNK)
+        wide[0, into, :] = shifted(full, column, -1).astype(BF)
+        wide[1, into, :] = grad
+        wide[2, into, :] = shifted(full, column, 1).astype(BF)
+
+    @pl.loop(0, size // CHUNK)
+    def _(step):
+        start = pl.multiple_of(step * CHUNK, CHUNK)
+        at = pl.ds(start, CHUNK)
+        first = ahead[0, at, :]
+        more = lax.dot_general(first, weight[2], NT, preferred_element_type=F32)
+        finish(0, start, partial[0, at, :] + more)
+        both = jnp.concatenate([first, ahead[1, at, :]], axis=1)
+        taps = jnp.concatenate([weight[1], weight[2]], axis=1)
+        more = lax.dot_general(both, taps, NT, preferred_element_type=F32)
+        finish(1, start, partial[1, at, :] + more)
 
     left = jnp.concatenate(
         [
@@ -113,19 +138,21 @@
         ],
         axis=0,
     )
+
+    def put(tap, value):
+        for h in range(2):
+            at = (tap * 2 + h) * chans
+            terms[at : at + chans, :] = value[:, h * 128 : (h + 1) * 128].astype(BF)
+
     for j in range(3):
-        out = jnp.dot(left, wide[j], preferred_element_type=F32).astype(BF)
+        out = jnp.dot(left, wide[j], preferred_element_type=F32)
         for i in range(3):
-            for h in range(2):
-                at = ((3 * i + j) * 2 + h) * chans
-                terms[at : at + chans, :] = out[i * chans : (i + 1) * chans, h * 128 : (h + 1) * 128]
-    left_t = jnp.concatenate([act_t[f] for f in range(frames)], axis=1)
-    for k in range(3):
-        right = dyx[k * size : (k + frames) * size, :]
-        out = jnp.dot(left_t, right, preferred_element_type=F32).astype(BF)
-        for h in range(2):
-            at = ((9 + k) * 2 + h) * chans
-            terms[at : at + chans, :] = out[:, h * 128 : (h + 1) * 128]
+            put(3 * i + j, out[i * chans : (i + 1) * chans])
+    put(9, early[0])
+    put(10, early[1] + jnp.dot(act_t[1], ahead[0], preferred_element_type=F32))
+    left_t = jnp.concatenate([act_t[0], act_t[1]], axis=1)
+    right = ahead[...].reshape(frames * size, chans)
+    put(11, jnp.dot(left_t, right, preferred_element_type=F32))
     half = terms.shape[0] // 2
     for c in range(2):
 
@@ -139,16 +166,22 @@
     out[...] = (a[...].astype(F32) + b[...].astype(F32)).astype(BF)
 
 
-def sum_kernel(scale, parts, out):
+def sum_kernel(parts, out):
     total = parts[0].astype(F32)
     for i in range(1, parts.shape[0]):
         total = total + parts[i].astype(F32)
-    out[...] = (total * scale).astype(out.dtype)
+    out[...] = total.astype(out.dtype)
+
+
+def last_kernel(scale, a, b, out):
+    total = ((a[...] + b[...]) * scale).astype(out.dtype)
+    for i in range(out.shape[0]):
+        out[i] = total
 
 
 def spread_kernel(value, out):
     for i in range(out.shape[0]):
-        out[i] = value[...].astype(out.dtype)
+        out[i] = value[...]
 
 
 def final_kernel(core, own, other, spatial, temporal):
@@ -248,46 +281,27 @@
         flops=9 * work,
         moved=9 << 20,
     )
+    partial, early = call(
+        early_kernel,
+        [shape((frames, size, chans), F32), shape((2, chans, chans), F32)],
+        (dy, temporal_weight, act_t),
+        flops=6 * work,
+        moved=6 << 20,
+    )
     act_later, ahead = lax.optimization_barrier((act, ahead))
     behind = lax.ppermute(act_later, TM, steps(TM, 1))
     flat = frames * size
     rows = 12 * chans
     pgrad, keep, send = call(
         gradient_kernel,
-        [shape((flat, chans)), shape((rows, 128)), shape((rows, 128))],
-        (core, dy, ahead, temporal_weight, slope.reshape(flat, chans), x_t, act_t),
-        [
-            pltpu.VMEM((2 * flat, chans), BF),
-            pltpu.VMEM((3, flat, chans), BF),
-            pltpu.VMEM((2 * rows, 128), BF),
-        ],
-        flops=15 * work,
+        [shape((frames, size, chans)), shape((rows, 128)), shape((rows, 128))],
+        (core, ahead, temporal_weight, slope, x_t, act_t, partial, early),
+        [pltpu.VMEM((3, flat, chans), BF), pltpu.VMEM((2 * rows, 128), BF)],
+        flops=12 * work,
         moved=11 << 20,
         smem=(0,),
     )
-    got = lax.ppermute(send, "core", [(0, 1), (1, 0)])
-    pgrad = pgrad.reshape(frames, size, chans)
-    half = call(add_kernel, shape((rows, 128)), (keep, got), moved=3 << 20)
-    plane, column = lax.axis_size(PLANE), lax.axis_size(COLUMN)
-    share = rows // plane
-    piece = share // column
-    first = exchange(half.reshape(plane, share, 128), PLANE)
     grad_top, grad_bottom = rims(pgrad)
-    part = call(functools.partial(sum_kernel, 1.0), shape((share, 128), F32), (first,), moved=1 << 20)
-    second = exchange(part.reshape(column, piece, 128), COLUMN)
-    total = call(functools.partial(sum_kernel, scale), shape((piece, 128), F32), (second,), moved=1 << 17)
-    spread = call(spread_kernel, shape((column, piece, 128), F32), (total,), moved=1 << 17)
-    third = exchange(spread, COLUMN).reshape(share, 128)
-    wider = call(spread_kernel, shape((plane, share, 128)), (third,), moved=1 << 20)
-    own = exchange(wider, PLANE).reshape(rows, 128)
-    other = lax.ppermute(own, "core", [(0, 1), (1, 0)])
-    spatial, temporal = call(
-        final_kernel,
-        [shape((9, chans, chans), F32), shape((3, chans, chans), F32)],
-        (core, own, other),
-        moved=5 << 20,
-        smem=(0,),
-    )
     input_grad = call(
         back_kernel,
         shape((frames, size, chans)),
@@ -303,6 +317,34 @@
         [pltpu.VMEM((2 * flat, chans), BF)],
         flops=3 * work,
         moved=4 << 20,
+    )
+    pair = [(0, 1), (1, 0)]
+    got = lax.ppermute(send, "core", pair)
+    half = call(add_kernel, shape((rows, 128)), (keep, got), moved=3 << 20)
+    line, ring = lax.axis_size("x"), lax.axis_size(TM)
+    share, piece = rows // line, rows // line // ring
+    first = exchange(half.reshape(line, share, 128), "x")
+    first, input_grad = lax.optimization_barrier((first, input_grad))
+    part = call(sum_kernel, shape((share, 128)), (first,), moved=1 << 20)
+    second = exchange(part.reshape(ring, piece, 128), TM)
+    mine = call(sum_kernel, shape((piece, 128), F32), (second,), moved=1 << 18)
+    theirs = lax.ppermute(mine, "clip", pair)
+    near = lax.axis_size("zl")
+    spread = call(
+        functools.partial(last_kernel, scale), shape((near, piece, 128)), (mine, theirs), moved=1 << 17
+    )
+    third = exchange(spread, "zl").reshape(near * piece, 128)
+    third, block_out = lax.optimization_barrier((third, block_out))
+    plane = lax.axis_size(PLANE)
+    wider = call(spread_kernel, shape((plane, near * piece, 128)), (third,), moved=1 << 20)
+    own = exchange(wider, PLANE).reshape(rows, 128)
+    other = lax.ppermute(own, "core", pair)
+    spatial, temporal = call(
+        final_kernel,
+        [shape((9, chans, chans), F32), shape((3, chans, chans), F32)],
+        (core, own, other),
+        moved=5 << 20,
+        smem=(0,),
     )
     return (
         block_out.reshape(dims),

time: 149 us -> 122 us (0.82)
  blocking collectives: 47.2 us -> 32.2 us
  starting transfers between devices: 47.6 us -> 38.6 us
  waiting for transfers between devices: 24.4 us -> 19.4 us
  Pallas kernels: 19.8 us -> 21.9 us
    ppermute x2 -> x3, starting transfers between devices: 29.4 us -> 12.4 us  [the longest x1 4.74 us: local(): other = lax.ppermute(own, 'core', pair)]
    all_to_all x3 -> x2, blocking collectives: 47.2 us -> 32.2 us  [exchange(): return lax.all_to_all(value, axes, split_axis=0, concat_axis=0, tiled=True)]
    all_to_all x1 -> x2, waiting for transfers between devices: 8.25 us -> 0.66 us  [exchange(): return lax.all_to_all(value, axes, split_axis=0, concat_axis=0, tiled=True)]
    all_to_all x1 -> x2, starting transfers between devices: 3.61 us -> 7.28 us  [exchange(): return lax.all_to_all(value, axes, split_axis=0, concat_axis=0, tiled=True)]
    ppermute x2, starting transfers between devices: 3.99 us -> 7.64 us  [rims(): bottom = lax.ppermute(block[:, :COLS, :], SPACE, steps(SPACE, -1))]
    ppermute x1, starting transfers between devices: 2.16 us -> 4.55 us  [local(): behind = lax.ppermute(act_later, TM, steps(TM, 1))]
    ppermute x2 -> x3, waiting for transfers between devices: 1.91 us -> 4.19 us  [the longest x1 2.27 us: local(): theirs = lax.ppermute(mine, 'clip', pair)]
    pallas_call x10 -> x11, Pallas kernels: 19.8 us -> 21.9 us  [call(): pl.pallas_call(kernel, out_shape=outs, in_specs=specs, out_specs=jax.tree...]
  transfers between devices with their start and end apart: 9 -> 11, of which waited for: 5 -> 7; matrix products, arithmetic and copies ran while one was open for 1% -> 1% of each run, Pallas kernels for 8% -> 13%
where the time goes in v2:
time: 122 us; the launch traced here: 121 us
  starting transfers between devices  38.6 us (32%)
  blocking collectives  32.2 us (26%)
  Pallas kernels  21.9 us (18%)
  waiting for transfers between devices  19.4 us (16%)
  local copies, waits for them, and re-layouts  8.21 us (7%)
    all_to_all x2, blocking collectives, exchange(): return lax.all_to_all(value, axes, split_axis=0, concat_axis=0, tiled=True)  32.2 us
    pallas_call x11, Pallas kernels, call(): pl.pallas_call(kernel, out_shape=outs, in_specs=specs, out_specs=jax.tree...  21.9 us
    ppermute x2, starting transfers between devices, rims(): bottom = lax.ppermute(block[:, :COLS, :], SPACE, steps(SPACE, -1))  7.64 us
    all_to_all x2, starting transfers between devices, exchange(): return lax.all_to_all(value, axes, split_axis=0, concat_axis=0, tiled=True)  7.28 us
    unnamed x18, local copies, waits for them, and re-layouts  7.19 us
    ppermute x2, waiting for transfers between devices, rims(): bottom = lax.ppermute(block[:, :COLS, :], SPACE, steps(SPACE, -1))  7.03 us
    ppermute x1, waiting for transfers between devices, local(): ahead = lax.ppermute(dy, TM, steps(TM, -1))  5.97 us
    ppermute x2, starting transfers between devices, rims(): top = lax.ppermute(block[:, size - COLS:, :], SPACE, steps(SPACE, 1))  5.47 us
  transfers between devices with their start and end apart: 11, of which 7 were waited for; matrix products, arithmetic and copies ran while one was open for 1% of the time, Pallas kernels for 13%

profile of v2, /device:TPU:1, one launch (start us, length us, event | category | flops | bytes accessed | tf_op | source)
XLA Modules:
  0.0 121.2 jit_solution(6721022038042747577)
XLA Ops:
  0.6 1.3 %collective-permute-start.2 = (bf16[2,1024,256]{2,1,0:T(8,128)(2,1)}, bf16[2,1024,256]{2,1,0:T(8,128)(2,1)S(1)}, u32[]{:S(2)}, u32[]{:S(2)}) collective-permute-start(bf16[2,1024,256]{2,1,0:T(8,128)(2,1)} %bitcast.18), channel_id=1, source_target_pairs={{8,0},{16,8},{24,16},{32,24},{40,32},{48,40},{56,48},{64,56},{72,6... | collective-permute-start | bytes 3145736 | tf_op jit(solution)/shard_map/ppermute | solution.py:270
  2.9 5.1 %collective-permute-start.1 = (bf16[2,128,256]{2,1,0:T(8,128)(2,1)S(1)}, bf16[2,128,256]{2,1,0:T(8,128)(2,1)S(1)}, u32[]{:S(2)}, u32[]{:S(2)}) collective-permute-start(bf16[2,128,256]{2,1,0:T(8,128)(2,1)S(1)} %get-tuple-element.40), channel_id=1, source_target_pairs={{1,0},{2,1},{3,2},{4,3},{5,4},{6,5},{7,6},{9,8},{10,9},{11,10},{12... | collective-permute-start | bytes 393224 | tf_op jit(solution)/shard_map/ppermute | solution.py:257
  8.1 1.9 %collective-permute-start = (bf16[2,128,256]{2,1,0:T(8,128)(2,1)S(1)}, bf16[2,128,256]{2,1,0:T(8,128)(2,1)S(1)}, u32[]{:S(2)}, u32[]{:S(2)}) collective-permute-start(bf16[2,128,256]{2,1,0:T(8,128)(2,1)S(1)} %get-tuple-element.41), channel_id=1, source_target_pairs={{0,1},{1,2},{2,3},{3,4},{4,5},{5,6},{6,7},{8,9},{9,10},{10,11},{11... | collective-permute-start | bytes 393224 | tf_op jit(solution)/shard_map/ppermute | solution.py:256
  10.4 1.6 %collective-permute-done.top = bf16[2,128,256]{2,1,0:T(8,128)(2,1)S(1)} collective-permute-done((bf16[2,128,256]{2,1,0:T(8,128)(2,1)S(1)}, bf16[2,128,256]{2,1,0:T(8,128)(2,1)S(1)}, u32[]{:S(2)}, u32[]{:S(2)}) %collective-permute-start) | collective-permute-done | bytes 131104 | tf_op jit(solution)/shard_map/ppermute | solution.py:256
  14.4 4.4 %shard_map.75 = (bf16[2,1024,256]{2,1,0:T(8,128)(2,1)S(1)}, f32[2,1024,256]{2,1,0:T(8,128)S(1)}, bf16[2,256,1280]{2,1,0:T(8,128)(2,1)S(1)}, bf16[2,256,1024]{2,1,0:T(8,128)(2,1)S(1)}) custom-call(bf16[2,1024,256]{2,1,0:T(8,128)(2,1)S(1)} %bitcast.14, bf16[2,128,256]{2,1,0:T(8,128)(2,1)S(1)} %collective-permute-done.top, ...), custom_call_target="tpu_custom_call" | custom-call | flops 2415919104 | bytes 9437184 | tf_op jit(solution)/shard_map/pallas_call | solution.py:22
  18.8 1.4 %shard_map.76 = (f32[2,1024,256]{2,1,0:T(8,128)S(1)}, f32[2,256,256]{2,1,0:T(8,128)S(1)}) custom-call(bf16[2,1024,256]{2,1,0:T(8,128)(2,1)S(1)} %bitcast.19, bf16[3,256,256]{2,1,0:T(8,128)(2,1)S(1)} %copy-done.2, bf16[2,256,1024]{2,1,0:T(8,128)(2,1)S(1)} %get-tuple-element.25.act_t), custom_call_target="tpu_custom_call" | custom-call | flops 1610612736 | bytes 6291456 | tf_op jit(solution)/shard_map/pallas_call | solution.py:22
  20.2 6.0 %collective-permute-done.2.ahead = bf16[2,1024,256]{2,1,0:T(8,128)(2,1)S(1)} collective-permute-done((bf16[2,1024,256]{2,1,0:T(8,128)(2,1)}, bf16[2,1024,256]{2,1,0:T(8,128)(2,1)S(1)}, u32[]{:S(2)}, u32[]{:S(2)}) %collective-permute-start.2) | collective-permute-done | bytes 1048608 | tf_op jit(solution)/shard_map/ppermute | solution.py:270
  28.4 4.3 %shard_map.77 = (bf16[2,1024,256]{2,1,0:T(8,128)(2,1)S(1)}, bf16[3072,128]{1,0:T(8,128)(2,1)S(1)}, bf16[3072,128]{1,0:T(8,128)(2,1)S(1)}) custom-call(s32[1]{0:T(128)} %bitcast.core, bf16[2,1024,256]{2,1,0:T(8,128)(2,1)S(1)} %copy-done.8, bf16[3,256,256]{2,1,0:T(8,128)(2,1)S(1)} %copy-done.2, f32[2,1024,256]{2,1,0:T(8,128)S(1)} %get-tuple-element.23.slope, ...), custom_call_target="tpu_custom_call" | custom-call | flops 3221225472 | bytes 11534336 | tf_op jit(solution)/shard_map/pallas_call | solution.py:22
  32.7 3.2 %collective-permute-start.3 = (bf16[3072,128]{1,0:T(8,128)(2,1)S(1)}, bf16[3072,128]{1,0:T(8,128)(2,1)S(1)}, u32[]{:S(2)}, u32[]{:S(2)}) collective-permute-start(bf16[3072,128]{1,0:T(8,128)(2,1)S(1)} %get-tuple-element.29), channel_id=1, source_target_pairs={{0,1},{1,0},{2,3},{3,2},{4,5},{5,4},{6,7},{7,6},{8,9},{9,8},{10,11... | collective-permute-start | bytes 2359304 | tf_op jit(solution)/shard_map/ppermute | solution.py:322
  35.9 4.6 %collective-permute-start.7 = (bf16[2,1024,256]{2,1,0:T(8,128)(2,1)S(1)}, bf16[2,1024,256]{2,1,0:T(8,128)(2,1)}, u32[]{:S(2)}, u32[]{:S(2)}) collective-permute-start(bf16[2,1024,256]{2,1,0:T(8,128)(2,1)S(1)} %get-tuple-element.32.act), channel_id=1, source_target_pairs={{0,8},{8,16},{16,24},{24,32},{32,40},{40,48},{48,56},{56,64},{64,7... | collective-permute-start | bytes 3145736 | tf_op jit(solution)/shard_map/ppermute | solution.py:292
  41.5 4.0 %all-to-all-start = ((bf16[4,768,128]{2,1,0:T(8,128)(2,1)}), bf16[4,768,128]{2,1,0:T(8,128)(2,1)S(1)}, u32[]{:S(2)}, u32[]{:S(2)}) async-start(bf16[4,768,128]{2,1,0:T(8,128)(2,1)} %bitcast.3), calls=%async_computation | async-start | bytes 1572864 | tf_op jit(solution)/shard_map/all_to_all | solution.py:251
  45.5 2.5 %collective-permute-start.5 = (bf16[2,128,256]{2,1,0:T(8,128)(2,1)S(1)}, bf16[2,128,256]{2,1,0:T(8,128)(2,1)S(1)}, u32[]{:S(2)}, u32[]{:S(2)}) collective-permute-start(bf16[2,128,256]{2,1,0:T(8,128)(2,1)S(1)} %get-tuple-element.38), channel_id=1, source_target_pairs={{1,0},{2,1},{3,2},{4,3},{5,4},{6,5},{7,6},{9,8},{10,9},{11,10},{12... | collective-permute-start | bytes 393224 | tf_op jit(solution)/shard_map/ppermute | solution.py:257
  48.0 3.5 %collective-permute-start.4 = (bf16[2,128,256]{2,1,0:T(8,128)(2,1)S(1)}, bf16[2,128,256]{2,1,0:T(8,128)(2,1)S(1)}, u32[]{:S(2)}, u32[]{:S(2)}) collective-permute-start(bf16[2,128,256]{2,1,0:T(8,128)(2,1)S(1)} %get-tuple-element.39), channel_id=1, source_target_pairs={{0,1},{1,2},{2,3},{3,4},{4,5},{5,6},{6,7},{8,9},{9,10},{10,11},{11... | collective-permute-start | bytes 393224 | tf_op jit(solution)/shard_map/ppermute | solution.py:256
  51.6 6.7 %collective-permute-done.5.bottom = bf16[2,128,256]{2,1,0:T(8,128)(2,1)S(1)} collective-permute-done((bf16[2,128,256]{2,1,0:T(8,128)(2,1)S(1)}, bf16[2,128,256]{2,1,0:T(8,128)(2,1)S(1)}, u32[]{:S(2)}, u32[]{:S(2)}) %collective-permute-start.5) | collective-permute-done | bytes 131104 | tf_op jit(solution)/shard_map/ppermute | solution.py:257
  60.7 4.3 %shard_map.79 = bf16[2,1024,256]{2,1,0:T(8,128)(2,1)} custom-call(bf16[2,1024,256]{2,1,0:T(8,128)(2,1)S(1)} %get-tuple-element.30.grad, bf16[2,128,256]{2,1,0:T(8,128)(2,1)S(1)} %collective-permute-done.4.top, bf16[2,128,256]{2,1,0:T(8,128)(2,1)S(1)} %collective-permute-done.5.bottom, bf16[3,3,256,256]{3,2,1,0:T(8,128)(2,1)S(1)} %copy-done.4, ...), custom_call_target="tpu_custom_call" | custom-call | flops 2415919104 | bytes 5242880 | tf_op jit(solution)/shard_map/pallas_call | solution.py:22
  65.2 16.1 %all_to_all.20.parts = bf16[16,48,128]{2,1,0:T(8,128)(2,1)S(1)} all-to-all(bf16[16,48,128]{2,1,0:T(8,128)(2,1)S(1)} %bitcast.16), channel_id=1, replica_groups=mesh['clip'=2,'y'=4,'zl'=4,'x'=4,'core'=2] {'y','zl'}, dimensions={0} | all-to-all | bytes 393216 | tf_op jit(solution)/shard_map/all_to_all | solution.py:251
  81.3 4.4 %collective-permute-start.6 = (f32[48,128]{1,0:T(8,128)S(1)}, f32[48,128]{1,0:T(8,128)S(1)}, u32[]{:S(2)}, u32[]{:S(2)}) collective-permute-start(f32[48,128]{1,0:T(8,128)S(1)} %shard_map.81.a), channel_id=1, source_target_pairs={{0,128},{128,0},{1,129},{129,1},{2,130},{130,2},{3,131},{131,3},{4... | collective-permute-start | bytes 73736 | tf_op jit(solution)/shard_map/ppermute | solution.py:331
  85.7 2.3 %collective-permute-done.6.b = f32[48,128]{1,0:T(8,128)S(1)} collective-permute-done((f32[48,128]{1,0:T(8,128)S(1)}, f32[48,128]{1,0:T(8,128)S(1)}, u32[]{:S(2)}, u32[]{:S(2)}) %collective-permute-start.6) | collective-permute-done | bytes 24608 | tf_op jit(solution)/shard_map/ppermute | solution.py:331
  88.6 3.3 %all-to-all-start.2 = ((bf16[4,48,128]{2,1,0:T(8,128)(2,1)}), bf16[4,48,128]{2,1,0:T(8,128)(2,1)S(1)}, u32[]{:S(2)}, u32[]{:S(2)}) async-start(bf16[4,48,128]{2,1,0:T(8,128)(2,1)} %shard_map.82), calls=%async_computation.2 | async-start | bytes 98304 | tf_op jit(solution)/shard_map/all_to_all | solution.py:251
  91.9 3.8 %shard_map.83 = bf16[2048,256]{1,0:T(8,128)(2,1)} custom-call(bf16[2,1024,256]{2,1,0:T(8,128)(2,1)S(1)} %get-tuple-element.32.act, bf16[2,1024,256]{2,1,0:T(8,128)(2,1)} %collective-permute-done.7.behind, bf16[3,256,256]{2,1,0:T(8,128)(2,1)S(1)} %copy-done.2, bf16[2048,256]{1,0:T(8,128)(2,1)S(1)} %bitcast.15), custom_call_target="tpu_custom_call" | custom-call | flops 805306368 | bytes 4194304 | tf_op jit(solution)/shard_map/pallas_call | solution.py:22
  96.5 16.2 %all_to_all.21 = bf16[16,192,128]{2,1,0:T(8,128)(2,1)S(1)} all-to-all(bf16[16,192,128]{2,1,0:T(8,128)(2,1)S(1)} %shard_map.84), channel_id=1, replica_groups=mesh['clip'=2,'y'=4,'zl'=4,'x'=4,'core'=2] {'x','y'}, dimensions={0} | all-to-all | bytes 1572864 | tf_op jit(solution)/shard_map/all_to_all | solution.py:251
  112.6 4.7 %collective-permute-start.8 = (bf16[3072,128]{1,0:T(8,128)(2,1)S(1)}, bf16[3072,128]{1,0:T(8,128)(2,1)S(1)}, u32[]{:S(2)}, u32[]{:S(2)}) collective-permute-start(bf16[3072,128]{1,0:T(8,128)(2,1)S(1)} %bitcast.11), channel_id=1, source_target_pairs={{0,1},{1,0},{2,3},{3,2},{4,5},{5,4},{6,7},{7,6},{8,9},{9,8},{10,11... | collective-permute-start | bytes 2359304 | tf_op jit(solution)/shard_map/ppermute | solution.py:341
  117.4 1.9 %collective-permute-done.8.other = bf16[3072,128]{1,0:T(8,128)(2,1)S(1)} collective-permute-done((bf16[3072,128]{1,0:T(8,128)(2,1)S(1)}, bf16[3072,128]{1,0:T(8,128)(2,1)S(1)}, u32[]{:S(2)}, u32[]{:S(2)}) %collective-permute-start.8) | collective-permute-done | bytes 786464 | tf_op jit(solution)/shard_map/ppermute | solution.py:341
  119.3 1.9 %shard_map.85 = (f32[9,256,256]{2,1,0:T(8,128)}, f32[3,256,256]{2,1,0:T(8,128)}) custom-call(s32[1]{0:T(128)} %bitcast.core, bf16[3072,128]{1,0:T(8,128)(2,1)S(1)} %bitcast.12, bf16[3072,128]{1,0:T(8,128)(2,1)S(1)} %collective-permute-done.8.other), custom_call_target="tpu_custom_call" | custom-call | bytes 5242880 | tf_op jit(solution)/shard_map/pallas_call | solution.py:22
  (31 shorter events, 11.2 us)
Async XLA Ops:
  0.6 25.5 %collective-permute-start.2 = (bf16[2,1024,256]{2,1,0:T(8,128)(2,1)}, bf16[2,1024,256]{2,1,0:T(8,128)(2,1)S(1)}, u32[]{:S(2)}, u32[]{:S(2)}) collective-permute-start(bf16[2,1024,256]{2,1,0:T(8,128)(2,1)} %bitcast.18), channel_id=1, source_target_pairs={{8,0},{16,8},{24,16},{32,24},{40,32},{48,40},{56,48},{64,56},{72,6... | collective-permute-start | bytes 3145736 | tf_op jit(solution)/shard_map/ppermute | solution.py:270
  2.9 7.4 %collective-permute-start.1 = (bf16[2,128,256]{2,1,0:T(8,128)(2,1)S(1)}, bf16[2,128,256]{2,1,0:T(8,128)(2,1)S(1)}, u32[]{:S(2)}, u32[]{:S(2)}) collective-permute-start(bf16[2,128,256]{2,1,0:T(8,128)(2,1)S(1)} %get-tuple-element.40), channel_id=1, source_target_pairs={{1,0},{2,1},{3,2},{4,3},{5,4},{6,5},{7,6},{9,8},{10,9},{11,10},{12... | collective-permute-start | bytes 393224 | tf_op jit(solution)/shard_map/ppermute | solution.py:257
  8.1 3.9 %collective-permute-start = (bf16[2,128,256]{2,1,0:T(8,128)(2,1)S(1)}, bf16[2,128,256]{2,1,0:T(8,128)(2,1)S(1)}, u32[]{:S(2)}, u32[]{:S(2)}) collective-permute-start(bf16[2,128,256]{2,1,0:T(8,128)(2,1)S(1)} %get-tuple-element.41), channel_id=1, source_target_pairs={{0,1},{1,2},{2,3},{3,4},{4,5},{5,6},{6,7},{8,9},{9,10},{10,11},{11... | collective-permute-start | bytes 393224 | tf_op jit(solution)/shard_map/ppermute | solution.py:256
  11.9 1.2 %copy-start = (bf16[1,2,8,128,256]{4,3,2,1,0:T(8,128)(2,1)S(1)}, bf16[1,2,8,128,256]{4,3,2,1,0:T(8,128)(2,1)}, u32[]{:S(2)}) copy-start(bf16[1,2,8,128,256]{4,3,2,1,0:T(8,128)(2,1)} %param.4) | copy-start | bytes 3145732
  13.2 1.3 %copy-start.3 = (bf16[3,3,256,256]{3,2,1,0:T(8,128)(2,1)S(1)}, bf16[3,3,256,256]{3,2,1,0:T(8,128)(2,1)}, u32[]{:S(2)}) copy-start(bf16[3,3,256,256]{3,2,1,0:T(8,128)(2,1)} %weight.8) | copy-start | bytes 3538948
  14.4 4.4 %copy-start.2 = (bf16[3,256,256]{2,1,0:T(8,128)(2,1)S(1)}, bf16[3,256,256]{2,1,0:T(8,128)(2,1)}, u32[]{:S(2)}) copy-start(bf16[3,256,256]{2,1,0:T(8,128)(2,1)} %weight.9) | copy-start | bytes 1179652
  14.4 4.4 %copy-start.5 = (bf16[1,2,8,128,256]{4,3,2,1,0:T(8,128)(2,1)S(1)}, bf16[1,2,8,128,256]{4,3,2,1,0:T(8,128)(2,1)}, u32[]{:S(2)}) copy-start(bf16[1,2,8,128,256]{4,3,2,1,0:T(8,128)(2,1)} %param.5) | copy-start | bytes 3145732
  26.2 1.0 copy-start.7
  27.1 1.2 %copy-start.8 = (bf16[2,1024,256]{2,1,0:T(8,128)(2,1)S(1)}, bf16[2,1024,256]{2,1,0:T(8,128)(2,1)}, u32[]{:S(2)}) copy-start(bf16[2,1024,256]{2,1,0:T(8,128)(2,1)} %copy-done.7) | copy-start | bytes 3145732
  32.7 7.8 %collective-permute-start.3 = (bf16[3072,128]{1,0:T(8,128)(2,1)S(1)}, bf16[3072,128]{1,0:T(8,128)(2,1)S(1)}, u32[]{:S(2)}, u32[]{:S(2)}) collective-permute-start(bf16[3072,128]{1,0:T(8,128)(2,1)S(1)} %get-tuple-element.29), channel_id=1, source_target_pairs={{0,1},{1,0},{2,3},{3,2},{4,5},{5,4},{6,7},{7,6},{8,9},{9,8},{10,11... | collective-permute-start | bytes 2359304 | tf_op jit(solution)/shard_map/ppermute | solution.py:322
  35.9 56.0 %collective-permute-start.7 = (bf16[2,1024,256]{2,1,0:T(8,128)(2,1)S(1)}, bf16[2,1024,256]{2,1,0:T(8,128)(2,1)}, u32[]{:S(2)}, u32[]{:S(2)}) collective-permute-start(bf16[2,1024,256]{2,1,0:T(8,128)(2,1)S(1)} %get-tuple-element.32.act), channel_id=1, source_target_pairs={{0,8},{8,16},{16,24},{24,32},{32,40},{40,48},{48,56},{56,64},{64,7... | collective-permute-start | bytes 3145736 | tf_op jit(solution)/shard_map/ppermute | solution.py:292
  41.5 23.6 %all-to-all-start = ((bf16[4,768,128]{2,1,0:T(8,128)(2,1)}), bf16[4,768,128]{2,1,0:T(8,128)(2,1)S(1)}, u32[]{:S(2)}, u32[]{:S(2)}) async-start(bf16[4,768,128]{2,1,0:T(8,128)(2,1)} %bitcast.3), calls=%async_computation | async-start | bytes 1572864 | tf_op jit(solution)/shard_map/all_to_all | solution.py:251
  45.5 12.7 %collective-permute-start.5 = (bf16[2,128,256]{2,1,0:T(8,128)(2,1)S(1)}, bf16[2,128,256]{2,1,0:T(8,128)(2,1)S(1)}, u32[]{:S(2)}, u32[]{:S(2)}) collective-permute-start(bf16[2,128,256]{2,1,0:T(8,128)(2,1)S(1)} %get-tuple-element.38), channel_id=1, source_target_pairs={{1,0},{2,1},{3,2},{4,3},{5,4},{6,5},{7,6},{9,8},{10,9},{11,10},{12... | collective-permute-start | bytes 393224 | tf_op jit(solution)/shard_map/ppermute | solution.py:257
  48.0 10.2 %collective-permute-start.4 = (bf16[2,128,256]{2,1,0:T(8,128)(2,1)S(1)}, bf16[2,128,256]{2,1,0:T(8,128)(2,1)S(1)}, u32[]{:S(2)}, u32[]{:S(2)}) collective-permute-start(bf16[2,128,256]{2,1,0:T(8,128)(2,1)S(1)} %get-tuple-element.39), channel_id=1, source_target_pairs={{0,1},{1,2},{2,3},{3,4},{4,5},{5,6},{6,7},{8,9},{9,10},{10,11},{11... | collective-permute-start | bytes 393224 | tf_op jit(solution)/shard_map/ppermute | solution.py:256
  58.2 1.3 %copy-start.4 = (bf16[3,3,256,256]{3,2,1,0:T(8,128)(2,1)S(1)}, bf16[3,3,256,256]{3,2,1,0:T(8,128)(2,1)}, u32[]{:S(2)}) copy-start(bf16[3,3,256,256]{3,2,1,0:T(8,128)(2,1)} %weight.8) | copy-start | bytes 3538948
  59.5 1.2 %copy-start.6 = (bf16[1,2,8,128,256]{4,3,2,1,0:T(8,128)(2,1)S(1)}, bf16[1,2,8,128,256]{4,3,2,1,0:T(8,128)(2,1)}, u32[]{:S(2)}) copy-start(bf16[1,2,8,128,256]{4,3,2,1,0:T(8,128)(2,1)} %param.5) | copy-start | bytes 3145732
  65.1 26.8 %copy-start.1 = (bf16[1,2,8,128,256]{4,3,2,1,0:T(8,128)(2,1)S(1)}, bf16[1,2,8,128,256]{4,3,2,1,0:T(8,128)(2,1)}, u32[]{:S(2)}) copy-start(bf16[1,2,8,128,256]{4,3,2,1,0:T(8,128)(2,1)} %param.4) | copy-start | bytes 3145732
  81.3 6.7 %collective-permute-start.6 = (f32[48,128]{1,0:T(8,128)S(1)}, f32[48,128]{1,0:T(8,128)S(1)}, u32[]{:S(2)}, u32[]{:S(2)}) collective-permute-start(f32[48,128]{1,0:T(8,128)S(1)} %shard_map.81.a), channel_id=1, source_target_pairs={{0,128},{128,0},{1,129},{129,1},{2,130},{130,2},{3,131},{131,3},{4... | collective-permute-start | bytes 73736 | tf_op jit(solution)/shard_map/ppermute | solution.py:331
  88.6 7.8 %all-to-all-start.2 = ((bf16[4,48,128]{2,1,0:T(8,128)(2,1)}), bf16[4,48,128]{2,1,0:T(8,128)(2,1)S(1)}, u32[]{:S(2)}, u32[]{:S(2)}) async-start(bf16[4,48,128]{2,1,0:T(8,128)(2,1)} %shard_map.82), calls=%async_computation.2 | async-start | bytes 98304 | tf_op jit(solution)/shard_map/all_to_all | solution.py:251
  112.6 6.7 %collective-permute-start.8 = (bf16[3072,128]{1,0:T(8,128)(2,1)S(1)}, bf16[3072,128]{1,0:T(8,128)(2,1)S(1)}, u32[]{:S(2)}, u32[]{:S(2)}) collective-permute-start(bf16[3072,128]{1,0:T(8,128)(2,1)S(1)} %bitcast.11), channel_id=1, source_target_pairs={{0,1},{1,0},{2,3},{3,2},{4,5},{5,4},{6,7},{7,6},{8,9},{9,8},{10,11... | collective-permute-start | bytes 2359304 | tf_op jit(solution)/shard_map/ppermute | solution.py:341

commit v3 on v2

--- a/solution.py
+++ b/solution.py
@@ -12,22 +12,30 @@
 TM = ("y", "zl")
 SPACE = ("x", "core")
 PLANE = ("x", "y")
+REST = ("y", "clip", "zl")
+COLUMN = ("clip", "zl")
 COLS = 128
 NT = (((1,), (1,)), ((), ()))
 
 
-def call(kernel, outs, ins, scratch=(), flops=0, moved=0, limit=32, smem=()):
+def call(kernel, outs, ins, scratch=(), flops=0, moved=0, limit=32, smem=(), after=()):
     vmem = pl.BlockSpec(memory_space=pltpu.VMEM)
     specs = [pl.BlockSpec(memory_space=pltpu.SMEM) if i in smem else vmem for i in range(len(ins))]
+    specs += [pl.BlockSpec(memory_space=pltpu.HBM)] * len(after)
+    count = len(ins)
+
+    def body(*refs):
+        kernel(*refs[:count], *refs[count + len(after) :])
+
     return pl.pallas_call(
-        kernel,
+        body,
         out_shape=outs,
         in_specs=specs,
         out_specs=jax.tree.map(lambda _: vmem, outs),
         scratch_shapes=list(scratch),
         cost_estimate=pl.CostEstimate(flops=flops, bytes_accessed=moved, transcendentals=0),
         compiler_params=pltpu.CompilerParams(vmem_limit_bytes=limit << 20),
-    )(*ins)
+    )(*ins, *after)
 
 
 def shape(dims, kind=BF):
@@ -173,8 +181,11 @@
     out[...] = total.astype(out.dtype)
 
 
-def last_kernel(scale, a, b, out):
-    total = ((a[...] + b[...]) * scale).astype(out.dtype)
+def last_kernel(scale, parts, out):
+    total = parts[0].astype(F32)
+    for i in range(1, parts.shape[0]):
+        total = total + parts[i].astype(F32)
+    total = (total * scale).astype(out.dtype)
     for i in range(out.shape[0]):
         out[i] = total
 
@@ -288,8 +299,7 @@
         flops=6 * work,
         moved=6 << 20,
     )
-    act_later, ahead = lax.optimization_barrier((act, ahead))
-    behind = lax.ppermute(act_later, TM, steps(TM, 1))
+    behind = lax.ppermute(act, TM, steps(TM, 1))
     flat = frames * size
     rows = 12 * chans
     pgrad, keep, send = call(
@@ -297,8 +307,8 @@
         [shape((frames, size, chans)), shape((rows, 128)), shape((rows, 128))],
         (core, ahead, temporal_weight, slope, x_t, act_t, partial, early),
         [pltpu.VMEM((3, flat, chans), BF), pltpu.VMEM((2 * rows, 128), BF)],
-        flops=12 * work,
-        moved=11 << 20,
+        flops=work // 16,
+        moved=1 << 18,
         smem=(0,),
     )
     grad_top, grad_bottom = rims(pgrad)
@@ -310,6 +320,25 @@
         flops=9 * work,
         moved=5 << 20,
     )
+    pair = [(0, 1), (1, 0)]
+    got = lax.ppermute(send, "core", pair)
+    half = call(add_kernel, shape((rows, 128)), (keep, got), moved=3 << 20)
+    line, ring = lax.axis_size("x"), lax.axis_size(REST)
+    share, piece = rows // line, rows // line // ring
+    first = exchange(half.reshape(line, share, 128), "x")
+    part = call(sum_kernel, shape((share, 128)), (first,), moved=1 << 18)
+    second = exchange(part.reshape(ring, piece, 128), REST)
+    column, plane = lax.axis_size(COLUMN), lax.axis_size(PLANE)
+    spread = call(
+        functools.partial(last_kernel, scale),
+        shape((column, piece, 128)),
+        (second,),
+        moved=1 << 18,
+        after=(input_grad, behind),
+    )
+    third = exchange(spread, COLUMN).reshape(column * piece, 128)
+    wider = call(spread_kernel, shape((plane, column * piece, 128)), (third,), moved=1 << 18)
+    own = exchange(wider, PLANE).reshape(rows, 128)
     block_out = call(
         mix_kernel,
         shape((flat, chans)),
@@ -318,26 +347,7 @@
         flops=3 * work,
         moved=4 << 20,
     )
-    pair = [(0, 1), (1, 0)]
-    got = lax.ppermute(send, "core", pair)
-    half = call(add_kernel, shape((rows, 128)), (keep, got), moved=3 << 20)
-    line, ring = lax.axis_size("x"), lax.axis_size(TM)
-    share, piece = rows // line, rows // line // ring
-    first = exchange(half.reshape(line, share, 128), "x")
-    first, input_grad = lax.optimization_barrier((first, input_grad))
-    part = call(sum_kernel, shape((share, 128)), (first,), moved=1 << 20)
-    second = exchange(part.reshape(ring, piece, 128), TM)
-    mine = call(sum_kernel, shape((piece, 128), F32), (second,), moved=1 << 18)
-    theirs = lax.ppermute(mine, "clip", pair)
-    near = lax.axis_size("zl")
-    spread = call(
-        functools.partial(last_kernel, scale), shape((near, piece, 128)), (mine, theirs), moved=1 << 17
-    )
-    third = exchange(spread, "zl").reshape(near * piece, 128)
-    third, block_out = lax.optimization_barrier((third, block_out))
-    plane = lax.axis_size(PLANE)
-    wider = call(spread_kernel, shape((plane, near * piece, 128)), (third,), moved=1 << 20)
-    own = exchange(wider, PLANE).reshape(rows, 128)
+    own, block_out = lax.optimization_barrier((own, block_out))
     other = lax.ppermute(own, "core", pair)
     spatial, temporal = call(
         final_kernel,

time: 122 us -> 124 us (1.016)
  blocking collectives: 32.2 us -> 13.5 us
  waiting for transfers between devices: 19.4 us -> 34.4 us
  starting transfers between devices: 38.6 us -> 44.2 us
  Pallas kernels: 21.9 us -> 23.4 us
    all_to_all x2 -> x1, blocking collectives: 32.2 us -> 13.5 us  [exchange(): return lax.all_to_all(value, axes, split_axis=0, concat_axis=0, tiled=True)]
    all_to_all x2 -> x3, waiting for transfers between devices: 0.66 us -> 18 us  [exchange(): return lax.all_to_all(value, axes, split_axis=0, concat_axis=0, tiled=True)]
    all_to_all x2 -> x3, starting transfers between devices: 7.28 us -> 22 us  [exchange(): return lax.all_to_all(value, axes, split_axis=0, concat_axis=0, tiled=True)]
    ppermute x2 -> x1, starting transfers between devices: 8.95 us -> 3.6 us  [local(): behind = lax.ppermute(act, TM, steps(TM, 1))]
    ppermute x2, starting transfers between devices: 7.64 us -> 3.86 us  [rims(): bottom = lax.ppermute(block[:, :COLS, :], SPACE, steps(SPACE, -1))]
    ppermute x2, starting transfers between devices: 5.47 us -> 8.39 us  [rims(): top = lax.ppermute(block[:, size - COLS:, :], SPACE, steps(SPACE, 1))]
    ppermute x1, starting transfers between devices: 4.74 us -> 1.86 us  [local(): other = lax.ppermute(own, 'core', pair)]
    ppermute x1, waiting for transfers between devices: 5.97 us -> 3.36 us  [local(): ahead = lax.ppermute(dy, TM, steps(TM, -1))]
  transfers between devices with their start and end apart: 11 -> 11, of which waited for: 7 -> 7; matrix products, arithmetic and copies ran while one was open for 1% -> 1% of each run, Pallas kernels for 13% -> 12%
where the time goes in v3:
time: 124 us
  starting transfers between devices  44.2 us (36%)
  waiting for transfers between devices  34.4 us (28%)
  Pallas kernels  23.4 us (19%)
  blocking collectives  13.5 us (11%)
  local copies, waits for them, and re-layouts  7.32 us (6%)
    pallas_call x10, Pallas kernels, call(): pl.pallas_call(body, out_shape=outs, in_specs=specs, out_specs=jax.tree.m...  23.4 us
    all_to_all x3, starting transfers between devices, exchange(): return lax.all_to_all(value, axes, split_axis=0, concat_axis=0, tiled=True)  22 us
    all_to_all x3, waiting for transfers between devices, exchange(): return lax.all_to_all(value, axes, split_axis=0, concat_axis=0, tiled=True)  18 us
    all_to_all x1, blocking collectives, exchange(): return lax.all_to_all(value, axes, split_axis=0, concat_axis=0, tiled=True)  13.5 us
    ppermute x2, waiting for transfers between devices, rims(): bottom = lax.ppermute(block[:, :COLS, :], SPACE, steps(SPACE, -1))  9.26 us
    ppermute x2, starting transfers between devices, rims(): top = lax.ppermute(block[:, size - COLS:, :], SPACE, steps(SPACE, 1))  8.39 us
    unnamed x16, local copies, waits for them, and re-layouts  6.31 us
    ppermute x2, starting transfers between devices, rims(): bottom = lax.ppermute(block[:, :COLS, :], SPACE, steps(SPACE, -1))  3.86 us
  transfers between devices with their start and end apart: 11, of which 7 were waited for; matrix products, arithmetic and copies ran while one was open for 1% of the time, Pallas kernels for 12%

profile of v3, /device:TPU:1, one launch (start us, length us, event | category | flops | bytes accessed | tf_op | source)
XLA Modules:
  0.0 123.7 jit_solution(6787625165118988222)
XLA Ops:
  2.9 4.5 %collective-permute-start.1 = (bf16[2,128,256]{2,1,0:T(8,128)(2,1)S(1)}, bf16[2,128,256]{2,1,0:T(8,128)(2,1)S(1)}, u32[]{:S(2)}, u32[]{:S(2)}) collective-permute-start(bf16[2,128,256]{2,1,0:T(8,128)(2,1)S(1)} %get-tuple-element.33), channel_id=1, source_target_pairs={{0,1},{1,2},{2,3},{3,4},{4,5},{5,6},{6,7},{8,9},{9,10},{10,11},{11... | collective-permute-start | bytes 393224 | tf_op jit(solution)/shard_map/ppermute | solution.py:267
  7.4 1.9 %collective-permute-start.2 = (bf16[2,128,256]{2,1,0:T(8,128)(2,1)S(1)}, bf16[2,128,256]{2,1,0:T(8,128)(2,1)S(1)}, u32[]{:S(2)}, u32[]{:S(2)}) collective-permute-start(bf16[2,128,256]{2,1,0:T(8,128)(2,1)S(1)} %get-tuple-element.32), channel_id=1, source_target_pairs={{1,0},{2,1},{3,2},{4,3},{5,4},{6,5},{7,6},{9,8},{10,9},{11,10},{12... | collective-permute-start | bytes 393224 | tf_op jit(solution)/shard_map/ppermute | solution.py:268
  9.4 4.6 %collective-permute-done.2.refs_2_ = bf16[2,128,256]{2,1,0:T(8,128)(2,1)S(1)} collective-permute-done((bf16[2,128,256]{2,1,0:T(8,128)(2,1)S(1)}, bf16[2,128,256]{2,1,0:T(8,128)(2,1)S(1)}, u32[]{:S(2)}, u32[]{:S(2)}) %collective-permute-start.2) | collective-permute-done | bytes 131104 | tf_op jit(solution)/shard_map/ppermute | solution.py:268
  16.5 4.9 %shard_map.75 = (bf16[2,1024,256]{2,1,0:T(8,128)(2,1)}, f32[2,1024,256]{2,1,0:T(8,128)S(1)}, bf16[2,256,1280]{2,1,0:T(8,128)(2,1)S(1)}, bf16[2,256,1024]{2,1,0:T(8,128)(2,1)S(1)}) custom-call(bf16[2,1024,256]{2,1,0:T(8,128)(2,1)S(1)} %bitcast.14, bf16[2,128,256]{2,1,0:T(8,128)(2,1)S(1)} %collective-permute-done.1.refs_1_, ...), custom_call_target="tpu_custom_call" | custom-call | flops 2415919104 | bytes 9437184 | tf_op jit(solution)/shard_map/pallas_call | solution.py:30
  21.5 1.4 %shard_map.76 = (f32[2,1024,256]{2,1,0:T(8,128)S(1)}, f32[2,256,256]{2,1,0:T(8,128)S(1)}) custom-call(bf16[2,1024,256]{2,1,0:T(8,128)(2,1)S(1)} %bitcast.19, bf16[3,256,256]{2,1,0:T(8,128)(2,1)S(1)} %copy-done.2, bf16[2,256,1024]{2,1,0:T(8,128)(2,1)S(1)} %get-tuple-element.19.refs_2_.refs_5_), custom_call_target="tpu_custom_call" | custom-call | flops 1610612736 | bytes 6291456 | tf_op jit(solution)/shard_map/pallas_call | solution.py:30
  22.8 3.4 %collective-permute-done.refs_1_ = bf16[2,1024,256]{2,1,0:T(8,128)(2,1)S(1)} collective-permute-done((bf16[2,1024,256]{2,1,0:T(8,128)(2,1)}, bf16[2,1024,256]{2,1,0:T(8,128)(2,1)S(1)}, u32[]{:S(2)}, u32[]{:S(2)}) %collective-permute-start) | collective-permute-done | bytes 1048608 | tf_op jit(solution)/shard_map/ppermute | solution.py:281
  26.2 4.3 %shard_map.77 = (bf16[2,1024,256]{2,1,0:T(8,128)(2,1)S(1)}, bf16[3072,128]{1,0:T(8,128)(2,1)S(1)}, bf16[3072,128]{1,0:T(8,128)(2,1)S(1)}) custom-call(s32[1]{0:T(128)} %bitcast.refs_0_, bf16[2,1024,256]{2,1,0:T(8,128)(2,1)S(1)} %collective-permute-done.refs_1_, bf16[3,256,256]{2,1,0:T(8,128)(2,1)S(1)} %copy-done.2, ...), custom_call_target="tpu_custom_call" | custom-call | flops 16777216 | bytes 262144 | tf_op jit(solution)/shard_map/pallas_call | solution.py:30
  30.5 3.2 %collective-permute-start.3 = (bf16[3072,128]{1,0:T(8,128)(2,1)S(1)}, bf16[3072,128]{1,0:T(8,128)(2,1)S(1)}, u32[]{:S(2)}, u32[]{:S(2)}) collective-permute-start(bf16[3072,128]{1,0:T(8,128)(2,1)S(1)} %get-tuple-element.23), channel_id=1, source_target_pairs={{0,1},{1,0},{2,3},{3,2},{4,5},{5,4},{6,7},{7,6},{8,9},{9,8},{10,11... | collective-permute-start | bytes 2359304 | tf_op jit(solution)/shard_map/ppermute | solution.py:324
  33.7 1.9 %collective-permute-done.3.refs_1_ = bf16[3072,128]{1,0:T(8,128)(2,1)S(1)} collective-permute-done((bf16[3072,128]{1,0:T(8,128)(2,1)S(1)}, bf16[3072,128]{1,0:T(8,128)(2,1)S(1)}, u32[]{:S(2)}, u32[]{:S(2)}) %collective-permute-start.3) | collective-permute-done | bytes 786464 | tf_op jit(solution)/shard_map/ppermute | solution.py:324
  36.7 4.0 %all-to-all-start = ((bf16[4,768,128]{2,1,0:T(8,128)(2,1)}), bf16[4,768,128]{2,1,0:T(8,128)(2,1)S(1)}, u32[]{:S(2)}, u32[]{:S(2)}) async-start(bf16[4,768,128]{2,1,0:T(8,128)(2,1)} %bitcast.3), calls=%async_computation | async-start | bytes 1572864 | tf_op jit(solution)/shard_map/all_to_all | solution.py:262
  40.7 3.6 %collective-permute-start.6 = (bf16[2,1024,256]{2,1,0:T(8,128)(2,1)}, bf16[2,1024,256]{2,1,0:T(8,128)(2,1)S(1)}, u32[]{:S(2)}, u32[]{:S(2)}) collective-permute-start(bf16[2,1024,256]{2,1,0:T(8,128)(2,1)} %get-tuple-element.25.refs_0_), channel_id=1, source_target_pairs={{0,8},{8,16},{16,24},{24,32},{32,40},{40,48},{48,56},{56,64},{64,7... | collective-permute-start | bytes 3145736 | tf_op jit(solution)/shard_map/ppermute | solution.py:302
  44.3 8.1 %all-to-all-done.refs_0_ = bf16[4,768,128]{2,1,0:T(8,128)(2,1)S(1)} async-done(((bf16[4,768,128]{2,1,0:T(8,128)(2,1)}), bf16[4,768,128]{2,1,0:T(8,128)(2,1)S(1)}, u32[]{:S(2)}, u32[]{:S(2)}) %all-to-all-start) | async-done | bytes 786464 | tf_op jit(solution)/shard_map/all_to_all | solution.py:262
  53.2 12.4 %all-to-all-start.1 = ((bf16[32,24,128]{2,1,0:T(8,128)(2,1)}), bf16[32,24,128]{2,1,0:T(8,128)(2,1)S(1)}, u32[]{:S(2)}, u32[]{:S(2)}) async-start(bf16[32,24,128]{2,1,0:T(8,128)(2,1)} %bitcast.4), calls=%async_computation.1 | async-start | bytes 393216 | tf_op jit(solution)/shard_map/all_to_all | solution.py:262
  65.6 3.9 %collective-permute-start.4 = (bf16[2,128,256]{2,1,0:T(8,128)(2,1)S(1)}, bf16[2,128,256]{2,1,0:T(8,128)(2,1)S(1)}, u32[]{:S(2)}, u32[]{:S(2)}) collective-permute-start(bf16[2,128,256]{2,1,0:T(8,128)(2,1)S(1)} %get-tuple-element.31), channel_id=1, source_target_pairs={{0,1},{1,2},{2,3},{3,4},{4,5},{5,6},{6,7},{8,9},{9,10},{10,11},{11... | collective-permute-start | bytes 393224 | tf_op jit(solution)/shard_map/ppermute | solution.py:267
  69.5 1.9 %collective-permute-start.5 = (bf16[2,128,256]{2,1,0:T(8,128)(2,1)S(1)}, bf16[2,128,256]{2,1,0:T(8,128)(2,1)S(1)}, u32[]{:S(2)}, u32[]{:S(2)}) collective-permute-start(bf16[2,128,256]{2,1,0:T(8,128)(2,1)S(1)} %get-tuple-element.30), channel_id=1, source_target_pairs={{1,0},{2,1},{3,2},{4,3},{5,4},{6,5},{7,6},{9,8},{10,9},{11,10},{12... | collective-permute-start | bytes 393224 | tf_op jit(solution)/shard_map/ppermute | solution.py:268
  71.4 4.6 %collective-permute-done.5.refs_2_ = bf16[2,128,256]{2,1,0:T(8,128)(2,1)S(1)} collective-permute-done((bf16[2,128,256]{2,1,0:T(8,128)(2,1)S(1)}, bf16[2,128,256]{2,1,0:T(8,128)(2,1)S(1)}, u32[]{:S(2)}, u32[]{:S(2)}) %collective-permute-start.5) | collective-permute-done | bytes 131104 | tf_op jit(solution)/shard_map/ppermute | solution.py:268
  78.6 4.3 %shard_map.80.refs_1_ = bf16[2,1024,256]{2,1,0:T(8,128)(2,1)} custom-call(bf16[2,1024,256]{2,1,0:T(8,128)(2,1)S(1)} %get-tuple-element.24.refs_0_, bf16[2,128,256]{2,1,0:T(8,128)(2,1)S(1)} %collective-permute-done.4.refs_1_, bf16[2,128,256]{2,1,0:T(8,128)(2,1)S(1)} %collective-permute-done.5.refs_2_, bf16[3,3,256,256]{3,2,1,0:T(8,128)(2,1)S(1)} %copy-done.5, ...), custom_call_target="tpu_custom_call" | custom-call | flops 2415919104 | bytes 5242880 | tf_op jit(solution)/shard_map/pallas_call | solution.py:30
  84.3 13.5 %all_to_all.20 = bf16[8,24,128]{2,1,0:T(8,128)(2,1)S(1)} all-to-all(bf16[8,24,128]{2,1,0:T(8,128)(2,1)S(1)} %shard_map.81), channel_id=1, replica_groups=mesh['clip'=2,'y'=4,'zl'=4,'x'=4,'core'=2] {'clip','zl'}, dimensions={0} | all-to-all | bytes 98304 | tf_op jit(solution)/shard_map/all_to_all | solution.py:262
  98.8 5.6 %all-to-all-start.3 = ((bf16[16,192,128]{2,1,0:T(8,128)(2,1)}), bf16[16,192,128]{2,1,0:T(8,128)(2,1)S(1)}, u32[]{:S(2)}, u32[]{:S(2)}) async-start(bf16[16,192,128]{2,1,0:T(8,128)(2,1)} %shard_map.82), calls=%async_computation.3 | async-start | bytes 1572864 | tf_op jit(solution)/shard_map/all_to_all | solution.py:262
  104.4 3.8 %shard_map.83 = bf16[2048,256]{1,0:T(8,128)(2,1)} custom-call(bf16[2,1024,256]{2,1,0:T(8,128)(2,1)} %get-tuple-element.25.refs_0_, bf16[2,1024,256]{2,1,0:T(8,128)(2,1)S(1)} %collective-permute-done.6.refs_2_.refs_1_, bf16[3,256,256]{2,1,0:T(8,128)(2,1)S(1)} %copy-done.2, bf16[2048,256]{1,0:T(8,128)(2,1)S(1)} %bitcast.15), custom_call_target="tpu_custom_call" | custom-call | flops 805306368 | bytes 4194304 | tf_op jit(solution)/shard_map/pallas_call | solution.py:30
  108.2 9.9 %all-to-all-done.3 = bf16[16,192,128]{2,1,0:T(8,128)(2,1)S(1)} async-done(((bf16[16,192,128]{2,1,0:T(8,128)(2,1)}), bf16[16,192,128]{2,1,0:T(8,128)(2,1)S(1)}, u32[]{:S(2)}, u32[]{:S(2)}) %all-to-all-start.3) | async-done | bytes 786464 | tf_op jit(solution)/shard_map/all_to_all | solution.py:262
  118.1 1.9 %collective-permute-start.7 = (bf16[3072,128]{1,0:T(8,128)(2,1)S(1)}, bf16[3072,128]{1,0:T(8,128)(2,1)S(1)}, u32[]{:S(2)}, u32[]{:S(2)}) collective-permute-start(bf16[3072,128]{1,0:T(8,128)(2,1)S(1)} %bitcast.11), channel_id=1, source_target_pairs={{0,1},{1,0},{2,3},{3,2},{4,5},{5,4},{6,7},{7,6},{8,9},{9,8},{10,11... | collective-permute-start | bytes 2359304 | tf_op jit(solution)/shard_map/ppermute | solution.py:351
  119.9 1.9 %collective-permute-done.7.refs_2_ = bf16[3072,128]{1,0:T(8,128)(2,1)S(1)} collective-permute-done((bf16[3072,128]{1,0:T(8,128)(2,1)S(1)}, bf16[3072,128]{1,0:T(8,128)(2,1)S(1)}, u32[]{:S(2)}, u32[]{:S(2)}) %collective-permute-start.7) | collective-permute-done | bytes 786464 | tf_op jit(solution)/shard_map/ppermute | solution.py:351
  121.9 1.9 %shard_map.84 = (f32[9,256,256]{2,1,0:T(8,128)}, f32[3,256,256]{2,1,0:T(8,128)}) custom-call(s32[1]{0:T(128)} %bitcast.refs_0_, bf16[3072,128]{1,0:T(8,128)(2,1)S(1)} %bitcast.12, bf16[3072,128]{1,0:T(8,128)(2,1)S(1)} %collective-permute-done.7.refs_2_), custom_call_target="tpu_custom_call" | custom-call | bytes 5242880 | tf_op jit(solution)/shard_map/pallas_call | solution.py:30
  (27 shorter events, 11.5 us)
Async XLA Ops:
  0.6 25.5 %collective-permute-start = (bf16[2,1024,256]{2,1,0:T(8,128)(2,1)}, bf16[2,1024,256]{2,1,0:T(8,128)(2,1)S(1)}, u32[]{:S(2)}, u32[]{:S(2)}) collective-permute-start(bf16[2,1024,256]{2,1,0:T(8,128)(2,1)} %bitcast.18), channel_id=1, source_target_pairs={{8,0},{16,8},{24,16},{32,24},{40,32},{48,40},{56,48},{64,56},{72,6... | collective-permute-start | bytes 3145736 | tf_op jit(solution)/shard_map/ppermute | solution.py:281
  2.9 6.5 %collective-permute-start.1 = (bf16[2,128,256]{2,1,0:T(8,128)(2,1)S(1)}, bf16[2,128,256]{2,1,0:T(8,128)(2,1)S(1)}, u32[]{:S(2)}, u32[]{:S(2)}) collective-permute-start(bf16[2,128,256]{2,1,0:T(8,128)(2,1)S(1)} %get-tuple-element.33), channel_id=1, source_target_pairs={{0,1},{1,2},{2,3},{3,4},{4,5},{5,6},{6,7},{8,9},{9,10},{10,11},{11... | collective-permute-start | bytes 393224 | tf_op jit(solution)/shard_map/ppermute | solution.py:267
  7.4 6.6 %collective-permute-start.2 = (bf16[2,128,256]{2,1,0:T(8,128)(2,1)S(1)}, bf16[2,128,256]{2,1,0:T(8,128)(2,1)S(1)}, u32[]{:S(2)}, u32[]{:S(2)}) collective-permute-start(bf16[2,128,256]{2,1,0:T(8,128)(2,1)S(1)} %get-tuple-element.32), channel_id=1, source_target_pairs={{1,0},{2,1},{3,2},{4,3},{5,4},{6,5},{7,6},{9,8},{10,9},{11,10},{12... | collective-permute-start | bytes 393224 | tf_op jit(solution)/shard_map/ppermute | solution.py:268
  14.0 1.2 copy-start
  15.3 1.3 %copy-start.4 = (bf16[3,3,256,256]{3,2,1,0:T(8,128)(2,1)S(1)}, bf16[3,3,256,256]{3,2,1,0:T(8,128)(2,1)}, u32[]{:S(2)}) copy-start(bf16[3,3,256,256]{3,2,1,0:T(8,128)(2,1)} %refs_3_.3) | copy-start | bytes 3538948
  16.5 4.9 %copy-start.2 = (bf16[3,256,256]{2,1,0:T(8,128)(2,1)S(1)}, bf16[3,256,256]{2,1,0:T(8,128)(2,1)}, u32[]{:S(2)}) copy-start(bf16[3,256,256]{2,1,0:T(8,128)(2,1)} %refs_2_.3) | copy-start | bytes 1179652
  16.5 4.9 %copy-start.6 = (bf16[1,2,8,128,256]{4,3,2,1,0:T(8,128)(2,1)S(1)}, bf16[1,2,8,128,256]{4,3,2,1,0:T(8,128)(2,1)}, u32[]{:S(2)}) copy-start(bf16[1,2,8,128,256]{4,3,2,1,0:T(8,128)(2,1)} %param.5) | copy-start | bytes 3145732
  30.5 5.1 %collective-permute-start.3 = (bf16[3072,128]{1,0:T(8,128)(2,1)S(1)}, bf16[3072,128]{1,0:T(8,128)(2,1)S(1)}, u32[]{:S(2)}, u32[]{:S(2)}) collective-permute-start(bf16[3072,128]{1,0:T(8,128)(2,1)S(1)} %get-tuple-element.23), channel_id=1, source_target_pairs={{0,1},{1,0},{2,3},{3,2},{4,5},{5,4},{6,7},{7,6},{8,9},{9,8},{10,11... | collective-permute-start | bytes 2359304 | tf_op jit(solution)/shard_map/ppermute | solution.py:324
  36.7 15.7 %all-to-all-start = ((bf16[4,768,128]{2,1,0:T(8,128)(2,1)}), bf16[4,768,128]{2,1,0:T(8,128)(2,1)S(1)}, u32[]{:S(2)}, u32[]{:S(2)}) async-start(bf16[4,768,128]{2,1,0:T(8,128)(2,1)} %bitcast.3), calls=%async_computation | async-start | bytes 1572864 | tf_op jit(solution)/shard_map/all_to_all | solution.py:262
  40.7 42.2 %collective-permute-start.6 = (bf16[2,1024,256]{2,1,0:T(8,128)(2,1)}, bf16[2,1024,256]{2,1,0:T(8,128)(2,1)S(1)}, u32[]{:S(2)}, u32[]{:S(2)}) collective-permute-start(bf16[2,1024,256]{2,1,0:T(8,128)(2,1)} %get-tuple-element.25.refs_0_), channel_id=1, source_target_pairs={{0,8},{8,16},{16,24},{24,32},{32,40},{40,48},{48,56},{56,64},{64,7... | collective-permute-start | bytes 3145736 | tf_op jit(solution)/shard_map/ppermute | solution.py:302
  53.2 29.7 %all-to-all-start.1 = ((bf16[32,24,128]{2,1,0:T(8,128)(2,1)}), bf16[32,24,128]{2,1,0:T(8,128)(2,1)S(1)}, u32[]{:S(2)}, u32[]{:S(2)}) async-start(bf16[32,24,128]{2,1,0:T(8,128)(2,1)} %bitcast.4), calls=%async_computation.1 | async-start | bytes 393216 | tf_op jit(solution)/shard_map/all_to_all | solution.py:262
  65.6 5.8 %collective-permute-start.4 = (bf16[2,128,256]{2,1,0:T(8,128)(2,1)S(1)}, bf16[2,128,256]{2,1,0:T(8,128)(2,1)S(1)}, u32[]{:S(2)}, u32[]{:S(2)}) collective-permute-start(bf16[2,128,256]{2,1,0:T(8,128)(2,1)S(1)} %get-tuple-element.31), channel_id=1, source_target_pairs={{0,1},{1,2},{2,3},{3,4},{4,5},{5,6},{6,7},{8,9},{9,10},{10,11},{11... | collective-permute-start | bytes 393224 | tf_op jit(solution)/shard_map/ppermute | solution.py:267
  69.5 6.6 %collective-permute-start.5 = (bf16[2,128,256]{2,1,0:T(8,128)(2,1)S(1)}, bf16[2,128,256]{2,1,0:T(8,128)(2,1)S(1)}, u32[]{:S(2)}, u32[]{:S(2)}) collective-permute-start(bf16[2,128,256]{2,1,0:T(8,128)(2,1)S(1)} %get-tuple-element.30), channel_id=1, source_target_pairs={{1,0},{2,1},{3,2},{4,3},{5,4},{6,5},{7,6},{9,8},{10,9},{11,10},{12... | collective-permute-start | bytes 393224 | tf_op jit(solution)/shard_map/ppermute | solution.py:268
  76.1 1.3 %copy-start.5 = (bf16[3,3,256,256]{3,2,1,0:T(8,128)(2,1)S(1)}, bf16[3,3,256,256]{3,2,1,0:T(8,128)(2,1)}, u32[]{:S(2)}) copy-start(bf16[3,3,256,256]{3,2,1,0:T(8,128)(2,1)} %refs_3_.3) | copy-start | bytes 3538948
  77.3 1.2 copy-start.7
  82.9 21.5 %copy-start.1 = (bf16[1,2,8,128,256]{4,3,2,1,0:T(8,128)(2,1)S(1)}, bf16[1,2,8,128,256]{4,3,2,1,0:T(8,128)(2,1)}, u32[]{:S(2)}) copy-start(bf16[1,2,8,128,256]{4,3,2,1,0:T(8,128)(2,1)} %param.4) | copy-start | bytes 3145732
  82.9 1.3 %copy-start.3 = (bf16[2,1024,256]{2,1,0:T(8,128)(2,1)S(1)}, bf16[2,1024,256]{2,1,0:T(8,128)(2,1)}, u32[]{:S(2)}) copy-start(bf16[2,1024,256]{2,1,0:T(8,128)(2,1)} %shard_map.80.refs_1_) | copy-start | bytes 3145732
  98.8 19.3 %all-to-all-start.3 = ((bf16[16,192,128]{2,1,0:T(8,128)(2,1)}), bf16[16,192,128]{2,1,0:T(8,128)(2,1)S(1)}, u32[]{:S(2)}, u32[]{:S(2)}) async-start(bf16[16,192,128]{2,1,0:T(8,128)(2,1)} %shard_map.82), calls=%async_computation.3 | async-start | bytes 1572864 | tf_op jit(solution)/shard_map/all_to_all | solution.py:262
  118.1 3.8 %collective-permute-start.7 = (bf16[3072,128]{1,0:T(8,128)(2,1)S(1)}, bf16[3072,128]{1,0:T(8,128)(2,1)S(1)}, u32[]{:S(2)}, u32[]{:S(2)}) collective-permute-start(bf16[3072,128]{1,0:T(8,128)(2,1)S(1)} %bitcast.11), channel_id=1, source_target_pairs={{0,1},{1,0},{2,3},{3,2},{4,5},{5,4},{6,7},{7,6},{8,9},{9,8},{10,11... | collective-permute-start | bytes 2359304 | tf_op jit(solution)/shard_map/ppermute | solution.py:351

commit v4 on v3

--- a/solution.py
+++ b/solution.py
@@ -12,7 +12,6 @@
 TM = ("y", "zl")
 SPACE = ("x", "core")
 PLANE = ("x", "y")
-REST = ("y", "clip", "zl")
 COLUMN = ("clip", "zl")
 COLS = 128
 NT = (((1,), (1,)), ((), ()))
@@ -323,21 +322,25 @@
     pair = [(0, 1), (1, 0)]
     got = lax.ppermute(send, "core", pair)
     half = call(add_kernel, shape((rows, 128)), (keep, got), moved=3 << 20)
-    line, ring = lax.axis_size("x"), lax.axis_size(REST)
-    share, piece = rows // line, rows // line // ring
+    line, rank = lax.axis_size("x"), lax.axis_size("y")
+    column, plane = lax.axis_size(COLUMN), lax.axis_size(PLANE)
+    share, piece = rows // line, rows // plane // column
     first = exchange(half.reshape(line, share, 128), "x")
     part = call(sum_kernel, shape((share, 128)), (first,), moved=1 << 18)
-    second = exchange(part.reshape(ring, piece, 128), REST)
-    column, plane = lax.axis_size(COLUMN), lax.axis_size(PLANE)
+    second = exchange(part.reshape(rank, share // rank, 128), "y")
+    part = call(
+        sum_kernel, shape((share // rank, 128), F32), (second,), moved=1 << 18, after=(behind,)
+    )
+    third = exchange(part.reshape(column, piece, 128), COLUMN)
     spread = call(
         functools.partial(last_kernel, scale),
         shape((column, piece, 128)),
-        (second,),
+        (third,),
         moved=1 << 18,
-        after=(input_grad, behind),
-    )
-    third = exchange(spread, COLUMN).reshape(column * piece, 128)
-    wider = call(spread_kernel, shape((plane, column * piece, 128)), (third,), moved=1 << 18)
+        after=(grad_top, grad_bottom),
+    )
+    fourth = exchange(spread, COLUMN).reshape(column * piece, 128)
+    wider = call(spread_kernel, shape((plane, column * piece, 128)), (fourth,), moved=1 << 18)
     own = exchange(wider, PLANE).reshape(rows, 128)
     block_out = call(
         mix_kernel,
@@ -347,7 +350,7 @@
         flops=3 * work,
         moved=4 << 20,
     )
-    own, block_out = lax.optimization_barrier((own, block_out))
+    own, block_out, input_grad = lax.optimization_barrier((own, block_out, input_grad))
     other = lax.ppermute(own, "core", pair)
     spatial, temporal = call(
         final_kernel,

time: 124 us -> 127 us (1.024)
  blocking collectives: 13.5 us -> 29.1 us
  starting transfers between devices: 44.2 us -> 37.8 us
  waiting for transfers between devices: 34.4 us -> 31.7 us
  Pallas kernels: 23.4 us -> 21.4 us
  local copies, waits for them, and re-layouts: 7.32 us -> 5.73 us
    all_to_all x1 -> x2, blocking collectives: 13.5 us -> 29.1 us  [exchange(): return lax.all_to_all(value, axes, split_axis=0, concat_axis=0, tiled=True)]
    all_to_all x3, starting transfers between devices: 22 us -> 14.8 us  [exchange(): return lax.all_to_all(value, axes, split_axis=0, concat_axis=0, tiled=True)]
    unnamed x16 -> x22, local copies, waits for them, and re-layouts: 6.31 us -> 3.75 us
    all_to_all x3, waiting for transfers between devices: 18 us -> 15.6 us  [exchange(): return lax.all_to_all(value, axes, split_axis=0, concat_axis=0, tiled=True)]
    pallas_call x10 -> x11, Pallas kernels: 23.4 us -> 21.4 us  [call(): pl.pallas_call(body, out_shape=outs, in_specs=specs, out_specs=jax.tree.m...]
    ppermute x1, waiting for transfers between devices: 1.91 us -> 0.01 us  [local(): got = lax.ppermute(send, 'core', pair)]
    ppermute x1, waiting for transfers between devices: 0.01 us -> 1.38 us  [local(): behind = lax.ppermute(act, TM, steps(TM, 1))]
  transfers between devices with their start and end apart: 11 -> 11, of which waited for: 7 -> 7; matrix products, arithmetic and copies ran while one was open for 1% -> 2% of each run, Pallas kernels for 12% -> 11%
where the time goes in v4:
time: 127 us
  starting transfers between devices  37.8 us (30%)
  waiting for transfers between devices  31.7 us (25%)
  blocking collectives  29.1 us (23%)
  Pallas kernels  21.4 us (17%)
  local copies, waits for them, and re-layouts  5.73 us (5%)
    all_to_all x2, blocking collectives, exchange(): return lax.all_to_all(value, axes, split_axis=0, concat_axis=0, tiled=True)  29.1 us
    pallas_call x11, Pallas kernels, call(): pl.pallas_call(body, out_shape=outs, in_specs=specs, out_specs=jax.tree.m...  21.4 us
    all_to_all x3, waiting for transfers between devices, exchange(): return lax.all_to_all(value, axes, split_axis=0, concat_axis=0, tiled=True)  15.6 us
    all_to_all x3, starting transfers between devices, exchange(): return lax.all_to_all(value, axes, split_axis=0, concat_axis=0, tiled=True)  14.8 us
    ppermute x2, waiting for transfers between devices, rims(): bottom = lax.ppermute(block[:, :COLS, :], SPACE, steps(SPACE, -1))  8.97 us
    ppermute x2, starting transfers between devices, rims(): top = lax.ppermute(block[:, size - COLS:, :], SPACE, steps(SPACE, 1))  8.29 us
    ppermute x2, starting transfers between devices, rims(): bottom = lax.ppermute(block[:, :COLS, :], SPACE, steps(SPACE, -1))  3.86 us
    ppermute x1, waiting for transfers between devices, local(): ahead = lax.ppermute(dy, TM, steps(TM, -1))  3.85 us
  transfers between devices with their start and end apart: 11, of which 7 were waited for; matrix products, arithmetic and copies ran while one was open for 2% of the time, Pallas kernels for 11%

profile of v4, /device:TPU:1, one launch (start us, length us, event | category | flops | bytes accessed | tf_op | source)
XLA Modules:
  0.0 126.5 jit_solution(18426725824391024093)
XLA Ops:
  2.9 4.5 %collective-permute-start.1 = (bf16[2,128,256]{2,1,0:T(8,128)(2,1)S(1)}, bf16[2,128,256]{2,1,0:T(8,128)(2,1)S(1)}, u32[]{:S(2)}, u32[]{:S(2)}) collective-permute-start(bf16[2,128,256]{2,1,0:T(8,128)(2,1)S(1)} %get-tuple-element.35), channel_id=1, source_target_pairs={{0,1},{1,2},{2,3},{3,4},{4,5},{5,6},{6,7},{8,9},{9,10},{10,11},{11... | collective-permute-start | bytes 393224 | tf_op jit(solution)/shard_map/ppermute | solution.py:266
  7.4 1.9 %collective-permute-start.2 = (bf16[2,128,256]{2,1,0:T(8,128)(2,1)S(1)}, bf16[2,128,256]{2,1,0:T(8,128)(2,1)S(1)}, u32[]{:S(2)}, u32[]{:S(2)}) collective-permute-start(bf16[2,128,256]{2,1,0:T(8,128)(2,1)S(1)} %get-tuple-element.34), channel_id=1, source_target_pairs={{1,0},{2,1},{3,2},{4,3},{5,4},{6,5},{7,6},{9,8},{10,9},{11,10},{12... | collective-permute-start | bytes 393224 | tf_op jit(solution)/shard_map/ppermute | solution.py:267
  9.4 4.6 %collective-permute-done.2.refs_2_ = bf16[2,128,256]{2,1,0:T(8,128)(2,1)S(1)} collective-permute-done((bf16[2,128,256]{2,1,0:T(8,128)(2,1)S(1)}, bf16[2,128,256]{2,1,0:T(8,128)(2,1)S(1)}, u32[]{:S(2)}, u32[]{:S(2)}) %collective-permute-start.2) | collective-permute-done | bytes 131104 | tf_op jit(solution)/shard_map/ppermute | solution.py:267
  16.5 4.4 %shard_map.75 = (bf16[2,1024,256]{2,1,0:T(8,128)(2,1)S(1)}, f32[2,1024,256]{2,1,0:T(8,128)S(1)}, bf16[2,256,1280]{2,1,0:T(8,128)(2,1)S(1)}, bf16[2,256,1024]{2,1,0:T(8,128)(2,1)S(1)}) custom-call(bf16[2,1024,256]{2,1,0:T(8,128)(2,1)S(1)} %bitcast.16, bf16[2,128,256]{2,1,0:T(8,128)(2,1)S(1)} %collective-permute-done.1.refs_1_, ...), custom_call_target="tpu_custom_call" | custom-call | flops 2415919104 | bytes 9437184 | tf_op jit(solution)/shard_map/pallas_call | solution.py:29
  22.3 3.9 %collective-permute-done.refs_1_ = bf16[2,1024,256]{2,1,0:T(8,128)(2,1)S(1)} collective-permute-done((bf16[2,1024,256]{2,1,0:T(8,128)(2,1)}, bf16[2,1024,256]{2,1,0:T(8,128)(2,1)S(1)}, u32[]{:S(2)}, u32[]{:S(2)}) %collective-permute-start) | collective-permute-done | bytes 1048608 | tf_op jit(solution)/shard_map/ppermute | solution.py:280
  26.2 4.2 %shard_map.77 = (bf16[2,1024,256]{2,1,0:T(8,128)(2,1)S(1)}, bf16[3072,128]{1,0:T(8,128)(2,1)S(1)}, bf16[3072,128]{1,0:T(8,128)(2,1)S(1)}) custom-call(s32[1]{0:T(128)} %bitcast.refs_0_, bf16[2,1024,256]{2,1,0:T(8,128)(2,1)S(1)} %collective-permute-done.refs_1_, bf16[3,256,256]{2,1,0:T(8,128)(2,1)S(1)} %copy-done.2, ...), custom_call_target="tpu_custom_call" | custom-call | flops 16777216 | bytes 262144 | tf_op jit(solution)/shard_map/pallas_call | solution.py:29
  30.4 3.2 %collective-permute-start.3 = (bf16[3072,128]{1,0:T(8,128)(2,1)S(1)}, bf16[3072,128]{1,0:T(8,128)(2,1)S(1)}, u32[]{:S(2)}, u32[]{:S(2)}) collective-permute-start(bf16[3072,128]{1,0:T(8,128)(2,1)S(1)} %get-tuple-element.24), channel_id=1, source_target_pairs={{0,1},{1,0},{2,3},{3,2},{4,5},{5,4},{6,7},{7,6},{8,9},{9,8},{10,11... | collective-permute-start | bytes 2359304 | tf_op jit(solution)/shard_map/ppermute | solution.py:323
  33.6 3.6 %collective-permute-start.4 = (bf16[2,1024,256]{2,1,0:T(8,128)(2,1)S(1)}, bf16[2,1024,256]{2,1,0:T(8,128)(2,1)S(1)}, u32[]{:S(2)}, u32[]{:S(2)}) collective-permute-start(bf16[2,1024,256]{2,1,0:T(8,128)(2,1)S(1)} %get-tuple-element.25.refs_0_), channel_id=1, source_target_pairs={{0,8},{8,16},{16,24},{24,32},{32,40},{40,48},{48,56},{56,64},{64,7... | collective-permute-start | bytes 3145736 | tf_op jit(solution)/shard_map/ppermute | solution.py:301
  37.4 15.3 %all_to_all.25.refs_0_ = bf16[4,768,128]{2,1,0:T(8,128)(2,1)S(1)} all-to-all(bf16[4,768,128]{2,1,0:T(8,128)(2,1)S(1)} %bitcast.14), channel_id=1, replica_groups=mesh['clip'=2,'y'=4,'zl'=4,'x'=4,'core'=2] {'x'}, dimensions={0} | all-to-all | bytes 1572864 | tf_op jit(solution)/shard_map/all_to_all | solution.py:261
  53.5 4.8 %all-to-all-start.1 = ((bf16[4,192,128]{2,1,0:T(8,128)(2,1)}), bf16[4,192,128]{2,1,0:T(8,128)(2,1)S(1)}, u32[]{:S(2)}, u32[]{:S(2)}) async-start(bf16[4,192,128]{2,1,0:T(8,128)(2,1)} %bitcast.4), calls=%async_computation.1 | async-start | bytes 393216 | tf_op jit(solution)/shard_map/all_to_all | solution.py:261
  58.3 1.4 %collective-permute-done.4.refs_1_ = bf16[2,1024,256]{2,1,0:T(8,128)(2,1)S(1)} collective-permute-done((bf16[2,1024,256]{2,1,0:T(8,128)(2,1)S(1)}, bf16[2,1024,256]{2,1,0:T(8,128)(2,1)S(1)}, u32[]{:S(2)}, u32[]{:S(2)}) %collective-permute-start.4) | collective-permute-done | bytes 1048608 | tf_op jit(solution)/shard_map/ppermute | solution.py:301
  59.7 11.0 %all-to-all-done.1.refs_0_ = bf16[4,192,128]{2,1,0:T(8,128)(2,1)S(1)} async-done(((bf16[4,192,128]{2,1,0:T(8,128)(2,1)}), bf16[4,192,128]{2,1,0:T(8,128)(2,1)S(1)}, u32[]{:S(2)}, u32[]{:S(2)}) %all-to-all-start.1) | async-done | bytes 196640 | tf_op jit(solution)/shard_map/all_to_all | solution.py:261
  71.4 5.6 %all-to-all-start.2 = ((f32[8,24,128]{2,1,0:T(8,128)}), f32[8,24,128]{2,1,0:T(8,128)S(1)}, u32[]{:S(2)}, u32[]{:S(2)}) async-start(f32[8,24,128]{2,1,0:T(8,128)} %bitcast.5), calls=%async_computation.2 | async-start | bytes 196608 | tf_op jit(solution)/shard_map/all_to_all | solution.py:261
  78.0 3.8 %collective-permute-start.5 = (bf16[2,128,256]{2,1,0:T(8,128)(2,1)S(1)}, bf16[2,128,256]{2,1,0:T(8,128)(2,1)S(1)}, u32[]{:S(2)}, u32[]{:S(2)}) collective-permute-start(bf16[2,128,256]{2,1,0:T(8,128)(2,1)S(1)} %get-tuple-element.33), channel_id=1, source_target_pairs={{0,1},{1,2},{2,3},{3,4},{4,5},{5,6},{6,7},{8,9},{9,10},{10,11},{11... | collective-permute-start | bytes 393224 | tf_op jit(solution)/shard_map/ppermute | solution.py:266
  81.8 1.9 %collective-permute-start.6 = (bf16[2,128,256]{2,1,0:T(8,128)(2,1)S(1)}, bf16[2,128,256]{2,1,0:T(8,128)(2,1)S(1)}, u32[]{:S(2)}, u32[]{:S(2)}) collective-permute-start(bf16[2,128,256]{2,1,0:T(8,128)(2,1)S(1)} %get-tuple-element.32), channel_id=1, source_target_pairs={{1,0},{2,1},{3,2},{4,3},{5,4},{6,5},{7,6},{9,8},{10,9},{11,10},{12... | collective-permute-start | bytes 393224 | tf_op jit(solution)/shard_map/ppermute | solution.py:267
  83.7 4.3 %collective-permute-done.6.refs_2_ = bf16[2,128,256]{2,1,0:T(8,128)(2,1)S(1)} collective-permute-done((bf16[2,128,256]{2,1,0:T(8,128)(2,1)S(1)}, bf16[2,128,256]{2,1,0:T(8,128)(2,1)S(1)}, u32[]{:S(2)}, u32[]{:S(2)}) %collective-permute-start.6) | collective-permute-done | bytes 131104 | tf_op jit(solution)/shard_map/ppermute | solution.py:267
  88.1 13.8 %all_to_all.26 = bf16[8,24,128]{2,1,0:T(8,128)(2,1)S(1)} all-to-all(bf16[8,24,128]{2,1,0:T(8,128)(2,1)S(1)} %shard_map.81), channel_id=1, replica_groups=mesh['clip'=2,'y'=4,'zl'=4,'x'=4,'core'=2] {'clip','zl'}, dimensions={0} | all-to-all | bytes 98304 | tf_op jit(solution)/shard_map/all_to_all | solution.py:261
  102.9 4.4 %all-to-all-start.4 = ((bf16[16,192,128]{2,1,0:T(8,128)(2,1)}), bf16[16,192,128]{2,1,0:T(8,128)(2,1)S(1)}, u32[]{:S(2)}, u32[]{:S(2)}) async-start(bf16[16,192,128]{2,1,0:T(8,128)(2,1)} %shard_map.82), calls=%async_computation.4 | async-start | bytes 1572864 | tf_op jit(solution)/shard_map/all_to_all | solution.py:261
  108.5 2.6 %shard_map.83 = bf16[2048,256]{1,0:T(8,128)(2,1)} custom-call(bf16[2,1024,256]{2,1,0:T(8,128)(2,1)S(1)} %copy-done.4, bf16[2,1024,256]{2,1,0:T(8,128)(2,1)S(1)} %collective-permute-done.4.refs_1_, bf16[3,256,256]{2,1,0:T(8,128)(2,1)S(1)} %copy-done.2, bf16[2048,256]{1,0:T(8,128)(2,1)S(1)} %bitcast.17), custom_call_target="tpu_custom_call" | custom-call | flops 805306368 | bytes 4194304 | tf_op jit(solution)/shard_map/pallas_call | solution.py:29
  111.1 4.3 %shard_map.84 = bf16[2,1024,256]{2,1,0:T(8,128)(2,1)} custom-call(bf16[2,1024,256]{2,1,0:T(8,128)(2,1)S(1)} %copy-done.6, bf16[2,128,256]{2,1,0:T(8,128)(2,1)S(1)} %collective-permute-done.5.refs_1_, bf16[2,128,256]{2,1,0:T(8,128)(2,1)S(1)} %collective-permute-done.6.refs_2_, bf16[3,3,256,256]{3,2,1,0:T(8,128)(2,1)S(1)} %copy-done.8, ...), custom_call_target="tpu_custom_call" | custom-call | flops 2415919104 | bytes 5242880 | tf_op jit(solution)/shard_map/pallas_call | solution.py:29
  115.4 4.5 %all-to-all-done.4 = bf16[16,192,128]{2,1,0:T(8,128)(2,1)S(1)} async-done(((bf16[16,192,128]{2,1,0:T(8,128)(2,1)}), bf16[16,192,128]{2,1,0:T(8,128)(2,1)S(1)}, u32[]{:S(2)}, u32[]{:S(2)}) %all-to-all-start.4) | async-done | bytes 786464 | tf_op jit(solution)/shard_map/all_to_all | solution.py:261
  120.0 2.8 %collective-permute-start.7 = (bf16[3072,128]{1,0:T(8,128)(2,1)S(1)}, bf16[3072,128]{1,0:T(8,128)(2,1)S(1)}, u32[]{:S(2)}, u32[]{:S(2)}) collective-permute-start(bf16[3072,128]{1,0:T(8,128)(2,1)S(1)} %bitcast.12), channel_id=1, source_target_pairs={{0,1},{1,0},{2,3},{3,2},{4,5},{5,4},{6,7},{7,6},{8,9},{9,8},{10,11... | collective-permute-start | bytes 2359304 | tf_op jit(solution)/shard_map/ppermute | solution.py:354
  122.7 1.9 %collective-permute-done.7.refs_2_ = bf16[3072,128]{1,0:T(8,128)(2,1)S(1)} collective-permute-done((bf16[3072,128]{1,0:T(8,128)(2,1)S(1)}, bf16[3072,128]{1,0:T(8,128)(2,1)S(1)}, u32[]{:S(2)}, u32[]{:S(2)}) %collective-permute-start.7) | collective-permute-done | bytes 786464 | tf_op jit(solution)/shard_map/ppermute | solution.py:354
  124.7 1.9 %shard_map.85 = (f32[9,256,256]{2,1,0:T(8,128)}, f32[3,256,256]{2,1,0:T(8,128)}) custom-call(s32[1]{0:T(128)} %bitcast.refs_0_, bf16[3072,128]{1,0:T(8,128)(2,1)S(1)} %bitcast.13, bf16[3072,128]{1,0:T(8,128)(2,1)S(1)} %collective-permute-done.7.refs_2_), custom_call_target="tpu_custom_call" | custom-call | bytes 5242880 | tf_op jit(solution)/shard_map/pallas_call | solution.py:29
  (35 shorter events, 11.0 us)
Async XLA Ops:
  0.6 25.5 %collective-permute-start = (bf16[2,1024,256]{2,1,0:T(8,128)(2,1)}, bf16[2,1024,256]{2,1,0:T(8,128)(2,1)S(1)}, u32[]{:S(2)}, u32[]{:S(2)}) collective-permute-start(bf16[2,1024,256]{2,1,0:T(8,128)(2,1)} %bitcast.19), channel_id=1, source_target_pairs={{8,0},{16,8},{24,16},{32,24},{40,32},{48,40},{56,48},{64,56},{72,6... | collective-permute-start | bytes 3145736 | tf_op jit(solution)/shard_map/ppermute | solution.py:280
  2.9 6.5 %collective-permute-start.1 = (bf16[2,128,256]{2,1,0:T(8,128)(2,1)S(1)}, bf16[2,128,256]{2,1,0:T(8,128)(2,1)S(1)}, u32[]{:S(2)}, u32[]{:S(2)}) collective-permute-start(bf16[2,128,256]{2,1,0:T(8,128)(2,1)S(1)} %get-tuple-element.35), channel_id=1, source_target_pairs={{0,1},{1,2},{2,3},{3,4},{4,5},{5,6},{6,7},{8,9},{9,10},{10,11},{11... | collective-permute-start | bytes 393224 | tf_op jit(solution)/shard_map/ppermute | solution.py:266
  7.4 6.6 %collective-permute-start.2 = (bf16[2,128,256]{2,1,0:T(8,128)(2,1)S(1)}, bf16[2,128,256]{2,1,0:T(8,128)(2,1)S(1)}, u32[]{:S(2)}, u32[]{:S(2)}) collective-permute-start(bf16[2,128,256]{2,1,0:T(8,128)(2,1)S(1)} %get-tuple-element.34), channel_id=1, source_target_pairs={{1,0},{2,1},{3,2},{4,3},{5,4},{6,5},{7,6},{9,8},{10,9},{11,10},{12... | collective-permute-start | bytes 393224 | tf_op jit(solution)/shard_map/ppermute | solution.py:267
  14.0 1.2 copy-start
  15.3 1.3 %copy-start.7 = (bf16[3,3,256,256]{3,2,1,0:T(8,128)(2,1)S(1)}, bf16[3,3,256,256]{3,2,1,0:T(8,128)(2,1)}, u32[]{:S(2)}) copy-start(bf16[3,3,256,256]{3,2,1,0:T(8,128)(2,1)} %refs_3_.3) | copy-start | bytes 3538948
  16.5 4.4 %copy-start.2 = (bf16[3,256,256]{2,1,0:T(8,128)(2,1)S(1)}, bf16[3,256,256]{2,1,0:T(8,128)(2,1)}, u32[]{:S(2)}) copy-start(bf16[3,256,256]{2,1,0:T(8,128)(2,1)} %refs_2_.3) | copy-start | bytes 1179652
  16.5 4.4 %copy-start.9 = (bf16[1,2,8,128,256]{4,3,2,1,0:T(8,128)(2,1)S(1)}, bf16[1,2,8,128,256]{4,3,2,1,0:T(8,128)(2,1)}, u32[]{:S(2)}) copy-start(bf16[1,2,8,128,256]{4,3,2,1,0:T(8,128)(2,1)} %param.5) | copy-start | bytes 3145732
  20.9 12.7 %copy-start.3 = (bf16[2,1024,256]{2,1,0:T(8,128)(2,1)}, bf16[2,1024,256]{2,1,0:T(8,128)(2,1)S(1)}, u32[]{:S(2)}) copy-start(bf16[2,1024,256]{2,1,0:T(8,128)(2,1)S(1)} %get-tuple-element.25.refs_0_) | copy-start | bytes 3145732
  30.4 23.1 %copy-start.5 = (bf16[2,1024,256]{2,1,0:T(8,128)(2,1)}, bf16[2,1024,256]{2,1,0:T(8,128)(2,1)S(1)}, u32[]{:S(2)}) copy-start(bf16[2,1024,256]{2,1,0:T(8,128)(2,1)S(1)} %get-tuple-element.26.refs_0_) | copy-start | bytes 3145732
  30.4 6.8 %collective-permute-start.3 = (bf16[3072,128]{1,0:T(8,128)(2,1)S(1)}, bf16[3072,128]{1,0:T(8,128)(2,1)S(1)}, u32[]{:S(2)}, u32[]{:S(2)}) collective-permute-start(bf16[3072,128]{1,0:T(8,128)(2,1)S(1)} %get-tuple-element.24), channel_id=1, source_target_pairs={{0,1},{1,0},{2,3},{3,2},{4,5},{5,4},{6,7},{7,6},{8,9},{9,8},{10,11... | collective-permute-start | bytes 2359304 | tf_op jit(solution)/shard_map/ppermute | solution.py:323
  33.6 26.1 %collective-permute-start.4 = (bf16[2,1024,256]{2,1,0:T(8,128)(2,1)S(1)}, bf16[2,1024,256]{2,1,0:T(8,128)(2,1)S(1)}, u32[]{:S(2)}, u32[]{:S(2)}) collective-permute-start(bf16[2,1024,256]{2,1,0:T(8,128)(2,1)S(1)} %get-tuple-element.25.refs_0_), channel_id=1, source_target_pairs={{0,8},{8,16},{16,24},{24,32},{32,40},{40,48},{48,56},{56,64},{64,7... | collective-permute-start | bytes 3145736 | tf_op jit(solution)/shard_map/ppermute | solution.py:301
  53.5 17.2 %all-to-all-start.1 = ((bf16[4,192,128]{2,1,0:T(8,128)(2,1)}), bf16[4,192,128]{2,1,0:T(8,128)(2,1)S(1)}, u32[]{:S(2)}, u32[]{:S(2)}) async-start(bf16[4,192,128]{2,1,0:T(8,128)(2,1)} %bitcast.4), calls=%async_computation.1 | async-start | bytes 393216 | tf_op jit(solution)/shard_map/all_to_all | solution.py:261
  71.4 35.8 %copy-start.1 = (bf16[1,2,8,128,256]{4,3,2,1,0:T(8,128)(2,1)S(1)}, bf16[1,2,8,128,256]{4,3,2,1,0:T(8,128)(2,1)}, u32[]{:S(2)}) copy-start(bf16[1,2,8,128,256]{4,3,2,1,0:T(8,128)(2,1)} %param.4) | copy-start | bytes 3145732
  71.4 16.7 %all-to-all-start.2 = ((f32[8,24,128]{2,1,0:T(8,128)}), f32[8,24,128]{2,1,0:T(8,128)S(1)}, u32[]{:S(2)}, u32[]{:S(2)}) async-start(f32[8,24,128]{2,1,0:T(8,128)} %bitcast.5), calls=%async_computation.2 | async-start | bytes 196608 | tf_op jit(solution)/shard_map/all_to_all | solution.py:261
  78.0 5.7 %collective-permute-start.5 = (bf16[2,128,256]{2,1,0:T(8,128)(2,1)S(1)}, bf16[2,128,256]{2,1,0:T(8,128)(2,1)S(1)}, u32[]{:S(2)}, u32[]{:S(2)}) collective-permute-start(bf16[2,128,256]{2,1,0:T(8,128)(2,1)S(1)} %get-tuple-element.33), channel_id=1, source_target_pairs={{0,1},{1,2},{2,3},{3,4},{4,5},{5,6},{6,7},{8,9},{9,10},{10,11},{11... | collective-permute-start | bytes 393224 | tf_op jit(solution)/shard_map/ppermute | solution.py:266
  81.8 6.3 %collective-permute-start.6 = (bf16[2,128,256]{2,1,0:T(8,128)(2,1)S(1)}, bf16[2,128,256]{2,1,0:T(8,128)(2,1)S(1)}, u32[]{:S(2)}, u32[]{:S(2)}) collective-permute-start(bf16[2,128,256]{2,1,0:T(8,128)(2,1)S(1)} %get-tuple-element.32), channel_id=1, source_target_pairs={{1,0},{2,1},{3,2},{4,3},{5,4},{6,5},{7,6},{9,8},{10,9},{11,10},{12... | collective-permute-start | bytes 393224 | tf_op jit(solution)/shard_map/ppermute | solution.py:267
  102.9 17.1 %all-to-all-start.4 = ((bf16[16,192,128]{2,1,0:T(8,128)(2,1)}), bf16[16,192,128]{2,1,0:T(8,128)(2,1)S(1)}, u32[]{:S(2)}, u32[]{:S(2)}) async-start(bf16[16,192,128]{2,1,0:T(8,128)(2,1)} %shard_map.82), calls=%async_computation.4 | async-start | bytes 1572864 | tf_op jit(solution)/shard_map/all_to_all | solution.py:261
  107.3 1.2 copy-start.4
  108.5 2.6 %copy-start.6 = (bf16[2,1024,256]{2,1,0:T(8,128)(2,1)S(1)}, bf16[2,1024,256]{2,1,0:T(8,128)(2,1)}, u32[]{:S(2)}) copy-start(bf16[2,1024,256]{2,1,0:T(8,128)(2,1)} %copy-done.5) | copy-start | bytes 3145732
  108.5 2.6 %copy-start.8 = (bf16[3,3,256,256]{3,2,1,0:T(8,128)(2,1)S(1)}, bf16[3,3,256,256]{3,2,1,0:T(8,128)(2,1)}, u32[]{:S(2)}) copy-start(bf16[3,3,256,256]{3,2,1,0:T(8,128)(2,1)} %refs_3_.3) | copy-start | bytes 3538948
  108.5 2.6 %copy-start.10 = (bf16[1,2,8,128,256]{4,3,2,1,0:T(8,128)(2,1)S(1)}, bf16[1,2,8,128,256]{4,3,2,1,0:T(8,128)(2,1)}, u32[]{:S(2)}) copy-start(bf16[1,2,8,128,256]{4,3,2,1,0:T(8,128)(2,1)} %param.5) | copy-start | bytes 3145732
  120.0 4.7 %collective-permute-start.7 = (bf16[3072,128]{1,0:T(8,128)(2,1)S(1)}, bf16[3072,128]{1,0:T(8,128)(2,1)S(1)}, u32[]{:S(2)}, u32[]{:S(2)}) collective-permute-start(bf16[3072,128]{1,0:T(8,128)(2,1)S(1)} %bitcast.12), channel_id=1, source_target_pairs={{0,1},{1,0},{2,3},{3,2},{4,5},{5,4},{6,7},{7,6},{8,9},{9,8},{10,11... | collective-permute-start | bytes 2359304 | tf_op jit(solution)/shard_map/ppermute | solution.py:354

commit v5 on v4

--- a/solution.py
+++ b/solution.py
@@ -17,10 +17,12 @@
 NT = (((1,), (1,)), ((), ()))
 
 
-def call(kernel, outs, ins, scratch=(), flops=0, moved=0, limit=32, smem=(), after=()):
+def call(kernel, outs, ins, scratch=(), flops=0, moved=0, limit=20, smem=(), after=(), hbm=(), out_hbm=False, alias=None):
     vmem = pl.BlockSpec(memory_space=pltpu.VMEM)
     specs = [pl.BlockSpec(memory_space=pltpu.SMEM) if i in smem else vmem for i in range(len(ins))]
+    specs = [pl.BlockSpec(memory_space=pltpu.HBM) if i in hbm else p for i, p in enumerate(specs)]
     specs += [pl.BlockSpec(memory_space=pltpu.HBM)] * len(after)
+    placed = pl.BlockSpec(memory_space=pltpu.HBM) if out_hbm else vmem
     count = len(ins)
 
     def body(*refs):
@@ -30,7 +32,8 @@
         body,
         out_shape=outs,
         in_specs=specs,
-        out_specs=jax.tree.map(lambda _: vmem, outs),
+        out_specs=jax.tree.map(lambda _: placed, outs),
+        input_output_aliases=alias or {},
         scratch_shapes=list(scratch),
         cost_estimate=pl.CostEstimate(flops=flops, bytes_accessed=moved, transcendentals=0),
         compiler_params=pltpu.CompilerParams(vmem_limit_bytes=limit << 20),
@@ -110,56 +113,93 @@
     terms[1] = jnp.dot(act_t[0], dy[1], preferred_element_type=F32)
 
 
-def gradient_kernel(
-    core, ahead, weight, slope, x_t, act_t, partial, early, pgrad, keep, send, wide, terms
+def finish(f, start, agrad, slope, pgrad, wide):
+    at = pl.ds(start, CHUNK)
+    grad = (agrad.astype(BF).astype(F32) * slope[f, at, :]).astype(BF)
+    pgrad[at, :] = grad
+    full = grad.astype(F32)
+    column = columns_of(CHUNK, full.shape[1])
+    wide[0, at, :] = shifted(full, column, -1).astype(BF)
+    wide[1, at, :] = grad
+    wide[2, at, :] = shifted(full, column, 1).astype(BF)
+
+
+def windows_of(x_t, f, size):
+    return jnp.concatenate([x_t[f, :, i * COLS : i * COLS + size] for i in range(3)], axis=0)
+
+
+def first_kernel(
+    ahead, weight, slope, x_t, act_t, partial, early, pgrad, rest, spatial, temporal, last, first, wide
 ):
-    frames, size, chans = ahead.shape
-
-    def finish(f, start, agrad):
-        at = pl.ds(start, CHUNK)
-        grad = (agrad.astype(BF).astype(F32) * slope[f, at, :]).astype(BF)
-        pgrad[f, at, :] = grad
-        full = grad.astype(F32)
-        column = columns_of(CHUNK, chans)
-        into = pl.ds(f * size + start, CHUNK)
-        wide[0, into, :] = shifted(full, column, -1).astype(BF)
-        wide[1, into, :] = grad
-        wide[2, into, :] = shifted(full, column, 1).astype(BF)
+    size = ahead.shape[0]
 
     @pl.loop(0, size // CHUNK)
     def _(step):
         start = pl.multiple_of(step * CHUNK, CHUNK)
         at = pl.ds(start, CHUNK)
-        first = ahead[0, at, :]
-        more = lax.dot_general(first, weight[2], NT, preferred_element_type=F32)
-        finish(0, start, partial[0, at, :] + more)
-        both = jnp.concatenate([first, ahead[1, at, :]], axis=1)
-        taps = jnp.concatenate([weight[1], weight[2]], axis=1)
-        more = lax.dot_general(both, taps, NT, preferred_element_type=F32)
-        finish(1, start, partial[1, at, :] + more)
-
-    left = jnp.concatenate(
-        [
-            jnp.concatenate([x_t[f, :, i * COLS : i * COLS + size] for f in range(frames)], axis=1)
-            for i in range(3)
-        ],
-        axis=0,
-    )
+        block = ahead[at, :]
+        more = lax.dot_general(block, weight[2], NT, preferred_element_type=F32)
+        finish(0, start, partial[0, at, :] + more, slope, pgrad, wide)
+        more = lax.dot_general(block, weight[1], NT, preferred_element_type=F32)
+        rest[at, :] = partial[1, at, :] + more
+
+    last[...] = pgrad[size - COLS :, :]
+    first[...] = pgrad[:COLS, :]
+    left = windows_of(x_t, 0, size)
+    for j in range(3):
+        spatial[j] = jnp.dot(left, wide[j], preferred_element_type=F32)
+    temporal[0] = early[1] + jnp.dot(act_t[1], ahead[...], preferred_element_type=F32)
+    temporal[1] = jnp.dot(act_t[0], ahead[...], preferred_element_type=F32)
+
+
+def second_kernel(
+    core,
+    ahead,
+    weight,
+    slope,
+    x_t,
+    act_t,
+    rest,
+    early,
+    spatial,
+    temporal,
+    last_0,
+    first_0,
+    pgrad,
+    keep,
+    send,
+    last,
+    first,
+    wide,
+    terms,
+):
+    size, chans = ahead.shape
+
+    @pl.loop(0, size // CHUNK)
+    def _(step):
+        start = pl.multiple_of(step * CHUNK, CHUNK)
+        at = pl.ds(start, CHUNK)
+        more = lax.dot_general(ahead[at, :], weight[2], NT, preferred_element_type=F32)
+        finish(1, start, rest[at, :] + more, slope, pgrad, wide)
+
+    last[0] = last_0[...]
+    first[0] = first_0[...]
+    last[1] = pgrad[size - COLS :, :]
+    first[1] = pgrad[:COLS, :]
 
     def put(tap, value):
         for h in range(2):
             at = (tap * 2 + h) * chans
             terms[at : at + chans, :] = value[:, h * 128 : (h + 1) * 128].astype(BF)
 
+    left = windows_of(x_t, 1, size)
     for j in range(3):
-        out = jnp.dot(left, wide[j], preferred_element_type=F32)
+        out = spatial[j] + jnp.dot(left, wide[j], preferred_element_type=F32)
         for i in range(3):
             put(3 * i + j, out[i * chans : (i + 1) * chans])
     put(9, early[0])
-    put(10, early[1] + jnp.dot(act_t[1], ahead[0], preferred_element_type=F32))
-    left_t = jnp.concatenate([act_t[0], act_t[1]], axis=1)
-    right = ahead[...].reshape(frames * size, chans)
-    put(11, jnp.dot(left_t, right, preferred_element_type=F32))
+    put(10, temporal[0])
+    put(11, temporal[1] + jnp.dot(act_t[1], ahead[...], preferred_element_type=F32))
     half = terms.shape[0] // 2
     for c in range(2):
 
@@ -194,27 +234,43 @@
         out[i] = value[...]
 
 
-def final_kernel(core, own, other, spatial, temporal):
-    half = own.shape[0] // 2
+def write_half(first, source, spatial, temporal, wide, sems):
+    copies = []
+    for n in range(6):
+        t = n if first else n + 6
+        for h in range(2):
+            at = (n * 2 + h) * 256
+            wide[n, :, h * 128 : (h + 1) * 128] = source[at : at + 256, :].astype(F32)
+        target = spatial.at[t] if t < 9 else temporal.at[t - 9]
+        copy = pltpu.make_async_copy(wide.at[n], target, sems.at[n])
+        copy.start()
+        copies.append(copy)
+    for copy in copies:
+        copy.wait()
+
+
+def own_kernel(core, own, spatial, temporal, wide, sems):
     for c in range(2):
 
         @pl.when(core[0] == c)
         def _():
-            for t in range(12):
-                source = own if t // 6 == c else other
-                at = (t % 6) * 512
-                for h in range(2):
-                    part = source[at + h * 256 : at + (h + 1) * 256, :].astype(F32)
-                    if t < 9:
-                        spatial[t, :, h * 128 : (h + 1) * 128] = part
-                    else:
-                        temporal[t - 9, :, h * 128 : (h + 1) * 128] = part
-
-
-def back_kernel(grad, top, bottom, weight, dy, out, padded):
+            write_half(c == 0, own, spatial, temporal, wide, sems)
+
+
+def other_kernel(core, other, spatial_in, temporal_in, spatial, temporal, wide, sems):
+    for c in range(2):
+
+        @pl.when(core[0] == c)
+        def _():
+            write_half(c == 1, other, spatial, temporal, wide, sems)
+
+
+def back_kernel(grad_0, grad_1, top, bottom, weight, dy, out, padded):
     frames, size, chans = dy.shape
-    for f in range(frames):
-        fill(padded, grad, top, bottom, f)
+    for f, grad in enumerate((grad_0, grad_1)):
+        padded[f, 0:COLS, :] = top[f]
+        padded[f, COLS : COLS + size, :] = grad[...]
+        padded[f, COLS + size :, :] = bottom[f]
 
     @pl.loop(0, frames * (size // CHUNK))
     def _(step):
@@ -261,11 +317,8 @@
     return lax.all_to_all(value, axes, split_axis=0, concat_axis=0, tiled=True)
 
 
-def rims(block):
-    size = block.shape[1]
-    top = lax.ppermute(block[:, size - COLS :, :], SPACE, steps(SPACE, 1))
-    bottom = lax.ppermute(block[:, :COLS, :], SPACE, steps(SPACE, -1))
-    return top, bottom
+def swap_rims(last, first):
+    return lax.ppermute(last, SPACE, steps(SPACE, 1)), lax.ppermute(first, SPACE, steps(SPACE, -1))
 
 
 def local(scale, frames_in, cotangent, spatial_weight, temporal_weight):
@@ -276,8 +329,8 @@
     dy = cotangent.reshape(frames, size, chans)
     work = 2 * frames * size * chans * chans
     core = lax.axis_index("core").astype(jnp.int32).reshape(1)
-    top, bottom = rims(x)
-    ahead = lax.ppermute(dy, TM, steps(TM, -1))
+    ahead = [lax.ppermute(dy[f], TM, steps(TM, -1)) for f in range(frames)]
+    top, bottom = swap_rims(x[:, size - COLS :, :], x[:, :COLS, :])
     act, slope, x_t, act_t = call(
         forward_kernel,
         [
@@ -301,20 +354,51 @@
     behind = lax.ppermute(act, TM, steps(TM, 1))
     flat = frames * size
     rows = 12 * chans
-    pgrad, keep, send = call(
-        gradient_kernel,
-        [shape((frames, size, chans)), shape((rows, 128)), shape((rows, 128))],
-        (core, ahead, temporal_weight, slope, x_t, act_t, partial, early),
-        [pltpu.VMEM((3, flat, chans), BF), pltpu.VMEM((2 * rows, 128), BF)],
+    wide = pltpu.VMEM((3, size, chans), BF)
+    edge = shape((COLS, chans))
+    pgrad_0, rest, spatial, temporal, last_0, first_0 = call(
+        first_kernel,
+        [
+            shape((size, chans)),
+            shape((size, chans), F32),
+            shape((3, 3 * chans, chans), F32),
+            shape((2, chans, chans), F32),
+            edge,
+            edge,
+        ],
+        (ahead[0], temporal_weight, slope, x_t, act_t, partial, early),
+        [wide],
+        flops=work // 16,
+        moved=1 << 18,
+    )
+    edges = shape((frames, COLS, chans))
+    pgrad_1, keep, send, last, first = call(
+        second_kernel,
+        [shape((size, chans)), shape((rows, 128)), shape((rows, 128)), edges, edges],
+        (
+            core,
+            ahead[1],
+            temporal_weight,
+            slope,
+            x_t,
+            act_t,
+            rest,
+            early,
+            spatial,
+            temporal,
+            last_0,
+            first_0,
+        ),
+        [wide, pltpu.VMEM((2 * rows, 128), BF)],
         flops=work // 16,
         moved=1 << 18,
         smem=(0,),
     )
-    grad_top, grad_bottom = rims(pgrad)
+    grad_top, grad_bottom = swap_rims(last, first)
     input_grad = call(
         back_kernel,
         shape((frames, size, chans)),
-        (pgrad, grad_top, grad_bottom, spatial_weight, dy),
+        (pgrad_0, pgrad_1, grad_top, grad_bottom, spatial_weight, dy),
         [pltpu.VMEM((frames, size + 2 * COLS, chans), BF)],
         flops=9 * work,
         moved=5 << 20,
@@ -329,19 +413,9 @@
     part = call(sum_kernel, shape((share, 128)), (first,), moved=1 << 18)
     second = exchange(part.reshape(rank, share // rank, 128), "y")
     part = call(
-        sum_kernel, shape((share // rank, 128), F32), (second,), moved=1 << 18, after=(behind,)
+        sum_kernel, shape((share // rank, 128), F32), (second,), moved=1 << 18, after=(behind, grad_top, grad_bottom)
     )
     third = exchange(part.reshape(column, piece, 128), COLUMN)
-    spread = call(
-        functools.partial(last_kernel, scale),
-        shape((column, piece, 128)),
-        (third,),
-        moved=1 << 18,
-        after=(grad_top, grad_bottom),
-    )
-    fourth = exchange(spread, COLUMN).reshape(column * piece, 128)
-    wider = call(spread_kernel, shape((plane, column * piece, 128)), (fourth,), moved=1 << 18)
-    own = exchange(wider, PLANE).reshape(rows, 128)
     block_out = call(
         mix_kernel,
         shape((flat, chans)),
@@ -350,14 +424,32 @@
         flops=3 * work,
         moved=4 << 20,
     )
+    spread = call(
+        functools.partial(last_kernel, scale),
+        shape((column, piece, 128)),
+        (third,),
+        moved=1 << 18,
+    )
+    fourth = exchange(spread, COLUMN).reshape(column * piece, 128)
+    wider = call(spread_kernel, shape((plane, column * piece, 128)), (fourth,), moved=1 << 18)
+    own = exchange(wider, PLANE).reshape(rows, 128)
     own, block_out, input_grad = lax.optimization_barrier((own, block_out, input_grad))
     other = lax.ppermute(own, "core", pair)
+    grads = [shape((9, chans, chans), F32), shape((3, chans, chans), F32)]
+    room = [pltpu.VMEM((6, chans, chans), F32), pltpu.SemaphoreType.DMA((6,))]
     spatial, temporal = call(
-        final_kernel,
-        [shape((9, chans, chans), F32), shape((3, chans, chans), F32)],
-        (core, own, other),
-        moved=5 << 20,
+        own_kernel, grads, (core, own), room, moved=3 << 20, smem=(0,), out_hbm=True
+    )
+    spatial, temporal = call(
+        other_kernel,
+        grads,
+        (core, other, spatial, temporal),
+        room,
+        moved=3 << 20,
         smem=(0,),
+        hbm=(2, 3),
+        out_hbm=True,
+        alias={2: 0, 3: 1},
     )
     return (
         block_out.reshape(dims),

time: 127 us -> 120 us (0.945)
  waiting for transfers between devices: 31.7 us -> 13.1 us
  blocking collectives: 29.1 us -> 38.4 us
  local copies, waits for them, and re-layouts: 5.73 us -> 8.05 us
  Pallas kernels: 21.4 us -> 23.6 us
  starting transfers between devices: 37.8 us -> 35.6 us
    all_to_all x3 -> x2, waiting for transfers between devices: 15.6 us -> 1.88 us  [exchange(): return lax.all_to_all(value, axes, split_axis=0, concat_axis=0, tiled=True)]
    all_to_all x2 -> x3, blocking collectives: 29.1 us -> 38.4 us  [exchange(): return lax.all_to_all(value, axes, split_axis=0, concat_axis=0, tiled=True)]
    all_to_all x3 -> x2, starting transfers between devices: 14.8 us -> 11 us  [exchange(): return lax.all_to_all(value, axes, split_axis=0, concat_axis=0, tiled=True)]
    ppermute x5 -> x6, waiting for transfers between devices: 12.8 us -> 10.5 us  [the longest x2 8.95 us: swap_rims(): lax.ppermute(first, SPACE, steps(SPACE, -1))]
    pallas_call x11 -> x13, Pallas kernels: 21.4 us -> 23.6 us  [call(): pl.pallas_call(body, out_shape=outs, in_specs=specs, out_specs=jax.tree.m...]
    unnamed x22 -> x20, local copies, waits for them, and re-layouts: 3.75 us -> 5.87 us
    ppermute x5 -> x6, starting transfers between devices: 13.4 us -> 15.3 us  [the longest x2 8.83 us: swap_rims(): lax.ppermute(last, SPACE, steps(SPACE, 1))]
    ppermute x1, waiting for transfers between devices: 1.38 us -> 0.01 us  [local(): behind = lax.ppermute(act, TM, steps(TM, 1))]
  transfers between devices with their start and end apart: 11 -> 11, of which waited for: 7 -> 5; matrix products, arithmetic and copies ran while one was open for 2% -> 0% of each run, Pallas kernels for 11% -> 16%
where the time goes in v5:
time: 120 us
  blocking collectives  38.4 us (32%)
  starting transfers between devices  35.6 us (30%)
  Pallas kernels  23.6 us (20%)
  waiting for transfers between devices  13.1 us (11%)
  local copies, waits for them, and re-layouts  8.05 us (7%)
    all_to_all x3, blocking collectives, exchange(): return lax.all_to_all(value, axes, split_axis=0, concat_axis=0, tiled=True)  38.4 us
    pallas_call x13, Pallas kernels, call(): pl.pallas_call(body, out_shape=outs, in_specs=specs, out_specs=jax.tree.m...  23.6 us
    all_to_all x2, starting transfers between devices, exchange(): return lax.all_to_all(value, axes, split_axis=0, concat_axis=0, tiled=True)  11 us
    ppermute x2, waiting for transfers between devices, swap_rims(): lax.ppermute(first, SPACE, steps(SPACE, -1))  8.95 us
    ppermute x2, starting transfers between devices, swap_rims(): lax.ppermute(last, SPACE, steps(SPACE, 1))  8.83 us
    unnamed x20, local copies, waits for them, and re-layouts  5.87 us
    ppermute x2, starting transfers between devices, swap_rims(): lax.ppermute(first, SPACE, steps(SPACE, -1))  3.86 us
    ppermute x1, starting transfers between devices, local(): behind = lax.ppermute(act, TM, steps(TM, 1))  3.6 us
  transfers between devices with their start and end apart: 11, of which 5 were waited for; matrix products, arithmetic and copies ran while one was open for 0% of the time, Pallas kernels for 16%

profile of v5, /device:TPU:1, one launch (start us, length us, event | category | flops | bytes accessed | tf_op | source)
XLA Modules:
  0.0 119.6 jit_solution(3560032401700382797)
XLA Ops:
  0.6 2.2 %fusion = (bf16[1,1,8,128,256]{4,3,2,1,0:T(8,128)(2,1)S(1)}, bf16[1,1,8,128,256]{4,3,2,1,0:T(8,128)(2,1)}) fusion(bf16[1,2,8,128,256]{4,3,2,1,0:T(8,128)(2,1)} %param.5), kind=kLoop, calls=%fused_computation | loop fusion | bytes 2097152 | tf_op jit(solution)/shard_map/slice | solution.py:332
  4.1 1.3 %collective-permute-start = (bf16[1024,256]{1,0:T(8,128)(2,1)}, bf16[1024,256]{1,0:T(8,128)(2,1)S(1)}, u32[]{:S(2)}, u32[]{:S(2)}) collective-permute-start(bf16[1024,256]{1,0:T(8,128)(2,1)} %bitcast.1), channel_id=1, source_target_pairs={{8,0},{16,8},{24,16},{32,24},{40,32},{48,40},{56,48},{64,56},{72,6... | collective-permute-start | bytes 1572872 | tf_op jit(solution)/shard_map/ppermute | solution.py:332
  5.4 4.5 %collective-permute-start.1 = (bf16[2,128,256]{2,1,0:T(8,128)(2,1)S(1)}, bf16[2,128,256]{2,1,0:T(8,128)(2,1)S(1)}, u32[]{:S(2)}, u32[]{:S(2)}) collective-permute-start(bf16[2,128,256]{2,1,0:T(8,128)(2,1)S(1)} %get-tuple-element.55), channel_id=1, source_target_pairs={{0,1},{1,2},{2,3},{3,4},{4,5},{5,6},{6,7},{8,9},{9,10},{10,11},{11... | collective-permute-start | bytes 393224 | tf_op jit(solution)/shard_map/ppermute | solution.py:321
  9.9 1.9 %collective-permute-start.2 = (bf16[2,128,256]{2,1,0:T(8,128)(2,1)S(1)}, bf16[2,128,256]{2,1,0:T(8,128)(2,1)S(1)}, u32[]{:S(2)}, u32[]{:S(2)}) collective-permute-start(bf16[2,128,256]{2,1,0:T(8,128)(2,1)S(1)} %get-tuple-element.54), channel_id=1, source_target_pairs={{1,0},{2,1},{3,2},{4,3},{5,4},{6,5},{7,6},{9,8},{10,9},{11,10},{12... | collective-permute-start | bytes 393224 | tf_op jit(solution)/shard_map/ppermute | solution.py:321
  11.9 4.6 %collective-permute-done.2.refs_2_ = bf16[2,128,256]{2,1,0:T(8,128)(2,1)S(1)} collective-permute-done((bf16[2,128,256]{2,1,0:T(8,128)(2,1)S(1)}, bf16[2,128,256]{2,1,0:T(8,128)(2,1)S(1)}, u32[]{:S(2)}, u32[]{:S(2)}) %collective-permute-start.2) | collective-permute-done | bytes 131104 | tf_op jit(solution)/shard_map/ppermute | solution.py:321
  17.8 4.9 %shard_map.75 = (bf16[2,1024,256]{2,1,0:T(8,128)(2,1)}, f32[2,1024,256]{2,1,0:T(8,128)S(1)}, bf16[2,256,1280]{2,1,0:T(8,128)(2,1)S(1)}, bf16[2,256,1024]{2,1,0:T(8,128)(2,1)S(1)}) custom-call(bf16[2,1024,256]{2,1,0:T(8,128)(2,1)S(1)} %bitcast.18, bf16[2,128,256]{2,1,0:T(8,128)(2,1)S(1)} %collective-permute-done.1.refs_1_, ...), custom_call_target="tpu_custom_call" | custom-call | flops 2415919104 | bytes 9437184 | tf_op jit(solution)/shard_map/pallas_call | solution.py:31
  22.7 1.4 %shard_map.76 = (f32[2,1024,256]{2,1,0:T(8,128)S(1)}, f32[2,256,256]{2,1,0:T(8,128)S(1)}) custom-call(bf16[2,1024,256]{2,1,0:T(8,128)(2,1)S(1)} %bitcast.20, bf16[3,256,256]{2,1,0:T(8,128)(2,1)S(1)} %copy-done, bf16[2,256,1024]{2,1,0:T(8,128)(2,1)S(1)} %get-tuple-element.30.refs_2_.refs_4_.refs_5_), custom_call_target="tpu_custom_call" | custom-call | flops 1610612736 | bytes 6291456 | tf_op jit(solution)/shard_map/pallas_call | solution.py:31
  24.1 2.4 %shard_map.77 = (bf16[1024,256]{1,0:T(8,128)(2,1)S(1)}, f32[1024,256]{1,0:T(8,128)S(1)}, f32[3,768,256]{2,1,0:T(8,128)S(1)}, f32[2,256,256]{2,1,0:T(8,128)S(1)},...) custom-call(bf16[1024,256]{1,0:T(8,128)(2,1)S(1)} %collective-permute-done.3.refs_0_, ...), custom_call_target="tpu_custom_call" | custom-call | flops 16777216 | bytes 262144 | tf_op jit(solution)/shard_map/pallas_call | solution.py:31
  26.6 1.6 %collective-permute-done.refs_1_ = bf16[1024,256]{1,0:T(8,128)(2,1)S(1)} collective-permute-done((bf16[1024,256]{1,0:T(8,128)(2,1)}, bf16[1024,256]{1,0:T(8,128)(2,1)S(1)}, u32[]{:S(2)}, u32[]{:S(2)}) %collective-permute-start) | collective-permute-done | bytes 524320 | tf_op jit(solution)/shard_map/ppermute | solution.py:332
  28.1 2.4 %shard_map.78 = (bf16[1024,256]{1,0:T(8,128)(2,1)S(1)}, bf16[3072,128]{1,0:T(8,128)(2,1)S(1)}, bf16[3072,128]{1,0:T(8,128)(2,1)S(1)}, bf16[2,128,256]{2,1,0:T(8,128)(2,1)S(1)}, bf16[2,128,256]{2,1,0:T(8,128)(2,1)S(1)}) custom-call(s32[1]{0:T(128)} %bitcast.refs_0_, bf16[1024,256]{1,0:T(8,128)(2,1)S(1)} %collective-permute-done.refs_1_, ...), custom_call_target="tpu_custom_call" | custom-call | flops 16777216 | bytes 262144 | tf_op jit(solution)/shard_map/pallas_call | solution.py:31
  30.5 3.2 %collective-permute-start.4 = (bf16[3072,128]{1,0:T(8,128)(2,1)S(1)}, bf16[3072,128]{1,0:T(8,128)(2,1)S(1)}, u32[]{:S(2)}, u32[]{:S(2)}) collective-permute-start(bf16[3072,128]{1,0:T(8,128)(2,1)S(1)} %get-tuple-element.39), channel_id=1, source_target_pairs={{0,1},{1,0},{2,3},{3,2},{4,5},{5,4},{6,7},{7,6},{8,9},{9,8},{10,11... | collective-permute-start | bytes 2359304 | tf_op jit(solution)/shard_map/ppermute | solution.py:407
  33.8 3.6 %collective-permute-start.5 = (bf16[2,1024,256]{2,1,0:T(8,128)(2,1)}, bf16[2,1024,256]{2,1,0:T(8,128)(2,1)S(1)}, u32[]{:S(2)}, u32[]{:S(2)}) collective-permute-start(bf16[2,1024,256]{2,1,0:T(8,128)(2,1)} %get-tuple-element.40.refs_0_), channel_id=1, source_target_pairs={{0,8},{8,16},{16,24},{24,32},{32,40},{40,48},{48,56},{56,64},{64,7... | collective-permute-start | bytes 3145736 | tf_op jit(solution)/shard_map/ppermute | solution.py:354
  37.6 15.3 %all_to_all.25.refs_0_ = bf16[4,768,128]{2,1,0:T(8,128)(2,1)S(1)} all-to-all(bf16[4,768,128]{2,1,0:T(8,128)(2,1)S(1)} %bitcast.16), channel_id=1, replica_groups=mesh['clip'=2,'y'=4,'zl'=4,'x'=4,'core'=2] {'x'}, dimensions={0} | all-to-all | bytes 1572864 | tf_op jit(solution)/shard_map/all_to_all | solution.py:317
  53.6 4.9 %all-to-all-start.1 = ((bf16[4,192,128]{2,1,0:T(8,128)(2,1)}), bf16[4,192,128]{2,1,0:T(8,128)(2,1)S(1)}, u32[]{:S(2)}, u32[]{:S(2)}) async-start(bf16[4,192,128]{2,1,0:T(8,128)(2,1)} %bitcast.6), calls=%async_computation.1 | async-start | bytes 393216 | tf_op jit(solution)/shard_map/all_to_all | solution.py:317
  58.6 4.3 %collective-permute-start.6 = (bf16[2,128,256]{2,1,0:T(8,128)(2,1)S(1)}, bf16[2,128,256]{2,1,0:T(8,128)(2,1)S(1)}, u32[]{:S(2)}, u32[]{:S(2)}) collective-permute-start(bf16[2,128,256]{2,1,0:T(8,128)(2,1)S(1)} %get-tuple-element.41), channel_id=1, source_target_pairs={{0,1},{1,2},{2,3},{3,4},{4,5},{5,6},{6,7},{8,9},{9,10},{10,11},{11... | collective-permute-start | bytes 393224 | tf_op jit(solution)/shard_map/ppermute | solution.py:321
  62.9 1.9 %collective-permute-start.7 = (bf16[2,128,256]{2,1,0:T(8,128)(2,1)S(1)}, bf16[2,128,256]{2,1,0:T(8,128)(2,1)S(1)}, u32[]{:S(2)}, u32[]{:S(2)}) collective-permute-start(bf16[2,128,256]{2,1,0:T(8,128)(2,1)S(1)} %get-tuple-element.42), channel_id=1, source_target_pairs={{1,0},{2,1},{3,2},{4,3},{5,4},{6,5},{7,6},{9,8},{10,9},{11,10},{12... | collective-permute-start | bytes 393224 | tf_op jit(solution)/shard_map/ppermute | solution.py:321
  64.8 4.3 %collective-permute-done.7.refs_3_ = bf16[2,128,256]{2,1,0:T(8,128)(2,1)S(1)} collective-permute-done((bf16[2,128,256]{2,1,0:T(8,128)(2,1)S(1)}, bf16[2,128,256]{2,1,0:T(8,128)(2,1)S(1)}, u32[]{:S(2)}, u32[]{:S(2)}) %collective-permute-start.7) | collective-permute-done | bytes 131104 | tf_op jit(solution)/shard_map/ppermute | solution.py:321
  69.2 1.9 %all-to-all-done.1.refs_0_ = bf16[4,192,128]{2,1,0:T(8,128)(2,1)S(1)} async-done(((bf16[4,192,128]{2,1,0:T(8,128)(2,1)}), bf16[4,192,128]{2,1,0:T(8,128)(2,1)S(1)}, u32[]{:S(2)}, u32[]{:S(2)}) %all-to-all-start.1) | async-done | bytes 196640 | tf_op jit(solution)/shard_map/all_to_all | solution.py:317
  71.1 13.6 %all_to_all.26.refs_0_ = f32[8,24,128]{2,1,0:T(8,128)S(1)} all-to-all(f32[8,24,128]{2,1,0:T(8,128)S(1)} %bitcast.22), channel_id=1, replica_groups=mesh['clip'=2,'y'=4,'zl'=4,'x'=4,'core'=2] {'clip','zl'}, dimensions={0} | all-to-all | bytes 196608 | tf_op jit(solution)/shard_map/all_to_all | solution.py:317
  84.7 9.4 %all_to_all.27 = bf16[8,24,128]{2,1,0:T(8,128)(2,1)S(1)} all-to-all(bf16[8,24,128]{2,1,0:T(8,128)(2,1)S(1)} %shard_map.82), channel_id=1, replica_groups=mesh['clip'=2,'y'=4,'zl'=4,'x'=4,'core'=2] {'clip','zl'}, dimensions={0} | all-to-all | bytes 98304 | tf_op jit(solution)/shard_map/all_to_all | solution.py:317
  95.1 6.1 %all-to-all-start.4 = ((bf16[16,192,128]{2,1,0:T(8,128)(2,1)}), bf16[16,192,128]{2,1,0:T(8,128)(2,1)S(1)}, u32[]{:S(2)}, u32[]{:S(2)}) async-start(bf16[16,192,128]{2,1,0:T(8,128)(2,1)} %shard_map.83), calls=%async_computation.4 | async-start | bytes 1572864 | tf_op jit(solution)/shard_map/all_to_all | solution.py:317
  105.8 4.3 %shard_map.85 = bf16[2,1024,256]{2,1,0:T(8,128)(2,1)} custom-call(bf16[1024,256]{1,0:T(8,128)(2,1)S(1)} %copy-done.7, bf16[1024,256]{1,0:T(8,128)(2,1)S(1)} %copy-done.9, bf16[2,128,256]{2,1,0:T(8,128)(2,1)S(1)} %collective-permute-done.6.refs_2_, bf16[2,128,256]{2,1,0:T(8,128)(2,1)S(1)} %collective-permute-done.7.refs_3_, ...), custom_call_target="tpu_custom_call" | custom-call | flops 2415919104 | bytes 5242880 | tf_op jit(solution)/shard_map/pallas_call | solution.py:31
  110.1 3.8 %shard_map.84 = bf16[2048,256]{1,0:T(8,128)(2,1)} custom-call(bf16[2,1024,256]{2,1,0:T(8,128)(2,1)} %get-tuple-element.40.refs_0_, bf16[2,1024,256]{2,1,0:T(8,128)(2,1)S(1)} %collective-permute-done.5.refs_1_, bf16[3,256,256]{2,1,0:T(8,128)(2,1)S(1)} %copy-done, bf16[2048,256]{1,0:T(8,128)(2,1)S(1)} %bitcast.19), custom_call_target="tpu_custom_call" | custom-call | flops 805306368 | bytes 4194304 | tf_op jit(solution)/shard_map/pallas_call | solution.py:31
  114.0 2.5 %collective-permute-start.8 = (bf16[3072,128]{1,0:T(8,128)(2,1)S(1)}, bf16[3072,128]{1,0:T(8,128)(2,1)S(1)}, u32[]{:S(2)}, u32[]{:S(2)}) collective-permute-start(bf16[3072,128]{1,0:T(8,128)(2,1)S(1)} %bitcast.14), channel_id=1, source_target_pairs={{0,1},{1,0},{2,3},{3,2},{4,5},{5,4},{6,7},{7,6},{8,9},{9,8},{10,11... | collective-permute-start | bytes 2359304 | tf_op jit(solution)/shard_map/ppermute | solution.py:437
  (36 shorter events, 12.3 us)
Async XLA Ops:
  0.6 4.8 %copy-start.1 = (bf16[1,2,8,128,256]{4,3,2,1,0:T(8,128)(2,1)S(1)}, bf16[1,2,8,128,256]{4,3,2,1,0:T(8,128)(2,1)}, u32[]{:S(2)}) copy-start(bf16[1,2,8,128,256]{4,3,2,1,0:T(8,128)(2,1)} %param.4) | copy-start | bytes 3145732
  2.8 21.3 %collective-permute-start.3 = (bf16[1024,256]{1,0:T(8,128)(2,1)S(1)}, bf16[1024,256]{1,0:T(8,128)(2,1)S(1)}, u32[]{:S(2)}, u32[]{:S(2)}) collective-permute-start(bf16[1024,256]{1,0:T(8,128)(2,1)S(1)} %bitcast.26), channel_id=1, source_target_pairs={{8,0},{16,8},{24,16},{32,24},{40,32},{48,40},{56,48},{64,56},{72,6... | collective-permute-start | bytes 1572872 | tf_op jit(solution)/shard_map/ppermute | solution.py:332
  4.1 24.0 %collective-permute-start = (bf16[1024,256]{1,0:T(8,128)(2,1)}, bf16[1024,256]{1,0:T(8,128)(2,1)S(1)}, u32[]{:S(2)}, u32[]{:S(2)}) collective-permute-start(bf16[1024,256]{1,0:T(8,128)(2,1)} %bitcast.1), channel_id=1, source_target_pairs={{8,0},{16,8},{24,16},{32,24},{40,32},{48,40},{56,48},{64,56},{72,6... | collective-permute-start | bytes 1572872 | tf_op jit(solution)/shard_map/ppermute | solution.py:332
  5.4 6.5 %collective-permute-start.1 = (bf16[2,128,256]{2,1,0:T(8,128)(2,1)S(1)}, bf16[2,128,256]{2,1,0:T(8,128)(2,1)S(1)}, u32[]{:S(2)}, u32[]{:S(2)}) collective-permute-start(bf16[2,128,256]{2,1,0:T(8,128)(2,1)S(1)} %get-tuple-element.55), channel_id=1, source_target_pairs={{0,1},{1,2},{2,3},{3,4},{4,5},{5,6},{6,7},{8,9},{9,10},{10,11},{11... | collective-permute-start | bytes 393224 | tf_op jit(solution)/shard_map/ppermute | solution.py:321
  9.9 6.6 %collective-permute-start.2 = (bf16[2,128,256]{2,1,0:T(8,128)(2,1)S(1)}, bf16[2,128,256]{2,1,0:T(8,128)(2,1)S(1)}, u32[]{:S(2)}, u32[]{:S(2)}) collective-permute-start(bf16[2,128,256]{2,1,0:T(8,128)(2,1)S(1)} %get-tuple-element.54), channel_id=1, source_target_pairs={{1,0},{2,1},{3,2},{4,3},{5,4},{6,5},{7,6},{9,8},{10,9},{11,10},{12... | collective-permute-start | bytes 393224 | tf_op jit(solution)/shard_map/ppermute | solution.py:321
  11.9 10.8 %copy-start = (bf16[3,256,256]{2,1,0:T(8,128)(2,1)S(1)}, bf16[3,256,256]{2,1,0:T(8,128)(2,1)}, u32[]{:S(2)}) copy-start(bf16[3,256,256]{2,1,0:T(8,128)(2,1)} %refs_2_.3) | copy-start | bytes 1179652
  11.9 10.8 %copy-start.2 = (bf16[1,2,8,128,256]{4,3,2,1,0:T(8,128)(2,1)S(1)}, bf16[1,2,8,128,256]{4,3,2,1,0:T(8,128)(2,1)}, u32[]{:S(2)}) copy-start(bf16[1,2,8,128,256]{4,3,2,1,0:T(8,128)(2,1)} %param.5) | copy-start | bytes 3145732
  16.5 1.3 %copy-start.4 = (bf16[3,3,256,256]{3,2,1,0:T(8,128)(2,1)S(1)}, bf16[3,3,256,256]{3,2,1,0:T(8,128)(2,1)}, u32[]{:S(2)}) copy-start(bf16[3,3,256,256]{3,2,1,0:T(8,128)(2,1)} %refs_4_.1) | copy-start | bytes 3538948
  26.6 3.9 %copy-start.6 = (bf16[1024,256]{1,0:T(8,128)(2,1)}, bf16[1024,256]{1,0:T(8,128)(2,1)S(1)}, u32[]{:S(2)}) copy-start(bf16[1024,256]{1,0:T(8,128)(2,1)S(1)} %get-tuple-element.43.refs_0_) | copy-start | bytes 1572868
  30.5 23.1 %copy-start.8 = (bf16[1024,256]{1,0:T(8,128)(2,1)}, bf16[1024,256]{1,0:T(8,128)(2,1)S(1)}, u32[]{:S(2)}) copy-start(bf16[1024,256]{1,0:T(8,128)(2,1)S(1)} %get-tuple-element.44.refs_1_) | copy-start | bytes 1572868
  30.5 6.8 %collective-permute-start.4 = (bf16[3072,128]{1,0:T(8,128)(2,1)S(1)}, bf16[3072,128]{1,0:T(8,128)(2,1)S(1)}, u32[]{:S(2)}, u32[]{:S(2)}) collective-permute-start(bf16[3072,128]{1,0:T(8,128)(2,1)S(1)} %get-tuple-element.39), channel_id=1, source_target_pairs={{0,1},{1,0},{2,3},{3,2},{4,5},{5,4},{6,7},{7,6},{8,9},{9,8},{10,11... | collective-permute-start | bytes 2359304 | tf_op jit(solution)/shard_map/ppermute | solution.py:407
  33.8 35.4 %collective-permute-start.5 = (bf16[2,1024,256]{2,1,0:T(8,128)(2,1)}, bf16[2,1024,256]{2,1,0:T(8,128)(2,1)S(1)}, u32[]{:S(2)}, u32[]{:S(2)}) collective-permute-start(bf16[2,1024,256]{2,1,0:T(8,128)(2,1)} %get-tuple-element.40.refs_0_), channel_id=1, source_target_pairs={{0,8},{8,16},{16,24},{24,32},{32,40},{40,48},{48,56},{56,64},{64,7... | collective-permute-start | bytes 3145736 | tf_op jit(solution)/shard_map/ppermute | solution.py:354
  53.6 17.4 %all-to-all-start.1 = ((bf16[4,192,128]{2,1,0:T(8,128)(2,1)}), bf16[4,192,128]{2,1,0:T(8,128)(2,1)S(1)}, u32[]{:S(2)}, u32[]{:S(2)}) async-start(bf16[4,192,128]{2,1,0:T(8,128)(2,1)} %bitcast.6), calls=%async_computation.1 | async-start | bytes 393216 | tf_op jit(solution)/shard_map/all_to_all | solution.py:317
  58.6 6.3 %collective-permute-start.6 = (bf16[2,128,256]{2,1,0:T(8,128)(2,1)S(1)}, bf16[2,128,256]{2,1,0:T(8,128)(2,1)S(1)}, u32[]{:S(2)}, u32[]{:S(2)}) collective-permute-start(bf16[2,128,256]{2,1,0:T(8,128)(2,1)S(1)} %get-tuple-element.41), channel_id=1, source_target_pairs={{0,1},{1,2},{2,3},{3,4},{4,5},{5,6},{6,7},{8,9},{9,10},{10,11},{11... | collective-permute-start | bytes 393224 | tf_op jit(solution)/shard_map/ppermute | solution.py:321
  62.9 6.3 %collective-permute-start.7 = (bf16[2,128,256]{2,1,0:T(8,128)(2,1)S(1)}, bf16[2,128,256]{2,1,0:T(8,128)(2,1)S(1)}, u32[]{:S(2)}, u32[]{:S(2)}) collective-permute-start(bf16[2,128,256]{2,1,0:T(8,128)(2,1)S(1)} %get-tuple-element.42), channel_id=1, source_target_pairs={{1,0},{2,1},{3,2},{4,3},{5,4},{6,5},{7,6},{9,8},{10,9},{11,10},{12... | collective-permute-start | bytes 393224 | tf_op jit(solution)/shard_map/ppermute | solution.py:321
  95.1 18.8 %all-to-all-start.4 = ((bf16[16,192,128]{2,1,0:T(8,128)(2,1)}), bf16[16,192,128]{2,1,0:T(8,128)(2,1)S(1)}, u32[]{:S(2)}, u32[]{:S(2)}) async-start(bf16[16,192,128]{2,1,0:T(8,128)(2,1)} %shard_map.83), calls=%async_computation.4 | async-start | bytes 1572864 | tf_op jit(solution)/shard_map/all_to_all | solution.py:317
  101.2 1.2 %copy-start.3 = (bf16[1,2,8,128,256]{4,3,2,1,0:T(8,128)(2,1)S(1)}, bf16[1,2,8,128,256]{4,3,2,1,0:T(8,128)(2,1)}, u32[]{:S(2)}) copy-start(bf16[1,2,8,128,256]{4,3,2,1,0:T(8,128)(2,1)} %param.5) | copy-start | bytes 3145732
  102.4 1.3 %copy-start.5 = (bf16[3,3,256,256]{3,2,1,0:T(8,128)(2,1)S(1)}, bf16[3,3,256,256]{3,2,1,0:T(8,128)(2,1)}, u32[]{:S(2)}) copy-start(bf16[3,3,256,256]{3,2,1,0:T(8,128)(2,1)} %refs_4_.1) | copy-start | bytes 3538948
  103.7 1.0 copy-start.7
  104.8 1.0 copy-start.9
  114.0 4.4 %collective-permute-start.8 = (bf16[3072,128]{1,0:T(8,128)(2,1)S(1)}, bf16[3072,128]{1,0:T(8,128)(2,1)S(1)}, u32[]{:S(2)}, u32[]{:S(2)}) collective-permute-start(bf16[3072,128]{1,0:T(8,128)(2,1)S(1)} %bitcast.14), channel_id=1, source_target_pairs={{0,1},{1,0},{2,3},{3,2},{4,5},{5,4},{6,7},{7,6},{8,9},{9,8},{10,11... | collective-permute-start | bytes 2359304 | tf_op jit(solution)/shard_map/ppermute | solution.py:437

commit v6 on v5

--- a/solution.py
+++ b/solution.py
@@ -20,9 +20,13 @@
 def call(kernel, outs, ins, scratch=(), flops=0, moved=0, limit=20, smem=(), after=(), hbm=(), out_hbm=False, alias=None):
     vmem = pl.BlockSpec(memory_space=pltpu.VMEM)
     specs = [pl.BlockSpec(memory_space=pltpu.SMEM) if i in smem else vmem for i in range(len(ins))]
-    specs = [pl.BlockSpec(memory_space=pltpu.HBM) if i in hbm else p for i, p in enumerate(specs)]
+    specs = [pl.BlockSpec(memory_space=pl.ANY) if i in hbm else p for i, p in enumerate(specs)]
     specs += [pl.BlockSpec(memory_space=pltpu.HBM)] * len(after)
-    placed = pl.BlockSpec(memory_space=pltpu.HBM) if out_hbm else vmem
+    many = isinstance(outs, list)
+    placed = [
+        pl.BlockSpec(memory_space=pltpu.HBM) if out_hbm is True or i in (out_hbm or ()) else vmem
+        for i in range(len(outs) if many else 1)
+    ]
     count = len(ins)
 
     def body(*refs):
@@ -32,7 +36,7 @@
         body,
         out_shape=outs,
         in_specs=specs,
-        out_specs=jax.tree.map(lambda _: placed, outs),
+        out_specs=placed if many else placed[0],
         input_output_aliases=alias or {},
         scratch_shapes=list(scratch),
         cost_estimate=pl.CostEstimate(flops=flops, bytes_accessed=moved, transcendentals=0),
@@ -113,10 +117,9 @@
     terms[1] = jnp.dot(act_t[0], dy[1], preferred_element_type=F32)
 
 
-def finish(f, start, agrad, slope, pgrad, wide):
+def finish(f, start, agrad, slope, wide):
     at = pl.ds(start, CHUNK)
     grad = (agrad.astype(BF).astype(F32) * slope[f, at, :]).astype(BF)
-    pgrad[at, :] = grad
     full = grad.astype(F32)
     column = columns_of(CHUNK, full.shape[1])
     wide[0, at, :] = shifted(full, column, -1).astype(BF)
@@ -129,7 +132,7 @@
 
 
 def first_kernel(
-    ahead, weight, slope, x_t, act_t, partial, early, pgrad, rest, spatial, temporal, last, first, wide
+    ahead, weight, slope, x_t, act_t, partial, early, pgrad, rest, spatial, temporal, last, first, wide, sem
 ):
     size = ahead.shape[0]
 
@@ -139,17 +142,20 @@
         at = pl.ds(start, CHUNK)
         block = ahead[at, :]
         more = lax.dot_general(block, weight[2], NT, preferred_element_type=F32)
-        finish(0, start, partial[0, at, :] + more, slope, pgrad, wide)
+        finish(0, start, partial[0, at, :] + more, slope, wide)
         more = lax.dot_general(block, weight[1], NT, preferred_element_type=F32)
         rest[at, :] = partial[1, at, :] + more
 
-    last[...] = pgrad[size - COLS :, :]
-    first[...] = pgrad[:COLS, :]
+    store = pltpu.make_async_copy(wide.at[1], pgrad, sem)
+    store.start()
+    last[...] = wide[1, size - COLS :, :]
+    first[...] = wide[1, :COLS, :]
     left = windows_of(x_t, 0, size)
     for j in range(3):
         spatial[j] = jnp.dot(left, wide[j], preferred_element_type=F32)
     temporal[0] = early[1] + jnp.dot(act_t[1], ahead[...], preferred_element_type=F32)
     temporal[1] = jnp.dot(act_t[0], ahead[...], preferred_element_type=F32)
+    store.wait()
 
 
 def second_kernel(
@@ -172,6 +178,7 @@
     first,
     wide,
     terms,
+    sem,
 ):
     size, chans = ahead.shape
 
@@ -180,12 +187,14 @@
         start = pl.multiple_of(step * CHUNK, CHUNK)
         at = pl.ds(start, CHUNK)
         more = lax.dot_general(ahead[at, :], weight[2], NT, preferred_element_type=F32)
-        finish(1, start, rest[at, :] + more, slope, pgrad, wide)
-
+        finish(1, start, rest[at, :] + more, slope, wide)
+
+    store = pltpu.make_async_copy(wide.at[1], pgrad, sem)
+    store.start()
     last[0] = last_0[...]
     first[0] = first_0[...]
-    last[1] = pgrad[size - COLS :, :]
-    first[1] = pgrad[:COLS, :]
+    last[1] = wide[1, size - COLS :, :]
+    first[1] = wide[1, :COLS, :]
 
     def put(tap, value):
         for h in range(2):
@@ -208,6 +217,8 @@
             keep[...] = terms[c * half : (c + 1) * half, :]
             send[...] = terms[(1 - c) * half : (2 - c) * half, :]
 
+    store.wait()
+
 
 def add_kernel(a, b, out):
     out[...] = (a[...].astype(F32) + b[...].astype(F32)).astype(BF)
@@ -220,18 +231,13 @@
     out[...] = total.astype(out.dtype)
 
 
-def last_kernel(scale, parts, out):
+def spread_sum_kernel(scale, parts, out):
     total = parts[0].astype(F32)
     for i in range(1, parts.shape[0]):
         total = total + parts[i].astype(F32)
     total = (total * scale).astype(out.dtype)
     for i in range(out.shape[0]):
         out[i] = total
-
-
-def spread_kernel(value, out):
-    for i in range(out.shape[0]):
-        out[i] = value[...]
 
 
 def write_half(first, source, spatial, temporal, wide, sems):
@@ -265,47 +271,85 @@
             write_half(c == 1, other, spatial, temporal, wide, sems)
 
 
-def back_kernel(grad_0, grad_1, top, bottom, weight, dy, out, padded):
-    frames, size, chans = dy.shape
+def back_kernel(
+    grad_0, grad_1, top, bottom, weight, dy, out, padded, taps, own, result, sems
+):
+    frames, size, chans = own.shape
+    whole = pltpu.make_async_copy(weight, taps, sems.at[0])
+    whole.start()
+    loads = []
     for f, grad in enumerate((grad_0, grad_1)):
-        padded[f, 0:COLS, :] = top[f]
-        padded[f, COLS : COLS + size, :] = grad[...]
-        padded[f, COLS + size :, :] = bottom[f]
-
-    @pl.loop(0, frames * (size // CHUNK))
-    def _(step):
-        f = step // (size // CHUNK)
-        start = pl.multiple_of((step % (size // CHUNK)) * CHUNK, CHUNK)
-        rows = window(padded, f, start, CHUNK, (2, 1, 0))
-        column = columns_of(CHUNK, chans)
-        z = [
-            lax.dot_general(
-                rows,
-                jnp.concatenate([weight[i, j] for i in range(3)], axis=1),
-                NT,
-                preferred_element_type=F32,
-            )
-            for j in range(3)
-        ]
-        back = shifted(z[0], column, -1) + z[1] + shifted(z[2], column, 1)
-        out[f, pl.ds(start, CHUNK), :] = (dy[f, pl.ds(start, CHUNK), :].astype(F32) + back).astype(BF)
-
-
-def mix_kernel(act, behind, weight, x, out, ext):
-    frames, size, chans = act.shape
+        base = 1 + 5 * f
+        loads.append(
+            [
+                pltpu.make_async_copy(top.at[f], padded.at[f, pl.ds(0, COLS)], sems.at[base]),
+                pltpu.make_async_copy(grad, padded.at[f, pl.ds(COLS, size)], sems.at[base + 1]),
+                pltpu.make_async_copy(
+                    bottom.at[f], padded.at[f, pl.ds(COLS + size, COLS)], sems.at[base + 2]
+                ),
+                pltpu.make_async_copy(dy.at[f], own.at[f], sems.at[base + 3]),
+            ]
+        )
+        for load in loads[f]:
+            load.start()
+    whole.wait()
+    stores = []
     for f in range(frames):
-        ext[f * size : (f + 1) * size, :] = behind[f]
-        ext[(frames + f) * size : (frames + f + 1) * size, :] = act[f]
-
-    @pl.loop(0, frames * (size // CHUNK))
-    def _(step):
-        start = pl.multiple_of(step * CHUNK, CHUNK)
-        rows = jnp.concatenate(
-            [ext[pl.ds(start + (2 - k) * size, CHUNK), :] for k in range(3)], axis=1
-        )
-        mixed = jnp.dot(rows, weight[...].reshape(3 * chans, chans), preferred_element_type=F32)
-        own = x[pl.ds(start, CHUNK), :].astype(F32)
-        out[pl.ds(start, CHUNK), :] = (own + mixed.astype(BF).astype(F32)).astype(BF)
+        for load in loads[f]:
+            load.wait()
+
+        @pl.loop(0, size // CHUNK)
+        def _(step):
+            start = pl.multiple_of(step * CHUNK, CHUNK)
+            at = pl.ds(start, CHUNK)
+            rows = window(padded, f, start, CHUNK, (2, 1, 0))
+            column = columns_of(CHUNK, chans)
+            z = [
+                lax.dot_general(
+                    rows,
+                    jnp.concatenate([taps[i, j] for i in range(3)], axis=1),
+                    NT,
+                    preferred_element_type=F32,
+                )
+                for j in range(3)
+            ]
+            back = shifted(z[0], column, -1) + z[1] + shifted(z[2], column, 1)
+            result[f, at, :] = (own[f, at, :].astype(F32) + back).astype(BF)
+
+        store = pltpu.make_async_copy(result.at[f], out.at[f], sems.at[5 + 5 * f])
+        store.start()
+        stores.append(store)
+    for store in stores:
+        store.wait()
+
+
+def mix_kernel(act, behind, weight, x, out, ext, own, result, sems):
+    frames, size, chans = own.shape
+    loads = []
+    for f in range(frames):
+        loads.append(pltpu.make_async_copy(behind.at[f], ext.at[f], sems.at[f]))
+        loads.append(pltpu.make_async_copy(act.at[f], ext.at[frames + f], sems.at[frames + f]))
+        loads.append(pltpu.make_async_copy(x.at[f], own.at[f], sems.at[2 * frames + f]))
+    for load in loads:
+        load.start()
+    for load in loads:
+        load.wait()
+    stores = []
+    for f in range(frames):
+
+        @pl.loop(0, size // CHUNK)
+        def _(step):
+            at = pl.ds(pl.multiple_of(step * CHUNK, CHUNK), CHUNK)
+            rows = jnp.concatenate([ext[f + 2 - k, at, :] for k in range(3)], axis=1)
+            taps = weight[...].reshape(3 * chans, chans)
+            mixed = jnp.dot(rows, taps, preferred_element_type=F32).astype(BF)
+            result[f, at, :] = (own[f, at, :].astype(F32) + mixed.astype(F32)).astype(BF)
+
+        store = pltpu.make_async_copy(result.at[f], out.at[f], sems.at[3 * frames + f])
+        store.start()
+        stores.append(store)
+    for store in stores:
+        store.wait()
 
 
 def steps(axes, by):
@@ -329,7 +373,8 @@
     dy = cotangent.reshape(frames, size, chans)
     work = 2 * frames * size * chans * chans
     core = lax.axis_index("core").astype(jnp.int32).reshape(1)
-    ahead = [lax.ppermute(dy[f], TM, steps(TM, -1)) for f in range(frames)]
+    dy_0, later = lax.optimization_barrier((dy[0], dy))
+    ahead = [lax.ppermute(frame, TM, steps(TM, -1)) for frame in (dy_0, later[1])]
     top, bottom = swap_rims(x[:, size - COLS :, :], x[:, :COLS, :])
     act, slope, x_t, act_t = call(
         forward_kernel,
@@ -367,9 +412,10 @@
             edge,
         ],
         (ahead[0], temporal_weight, slope, x_t, act_t, partial, early),
-        [wide],
+        [wide, pltpu.SemaphoreType.DMA],
         flops=work // 16,
         moved=1 << 18,
+        out_hbm=(0,),
     )
     edges = shape((frames, COLS, chans))
     pgrad_1, keep, send, last, first = call(
@@ -389,49 +435,71 @@
             last_0,
             first_0,
         ),
-        [wide, pltpu.VMEM((2 * rows, 128), BF)],
+        [wide, pltpu.VMEM((2 * rows, 128), BF), pltpu.SemaphoreType.DMA],
         flops=work // 16,
         moved=1 << 18,
+        out_hbm=(0,),
         smem=(0,),
     )
     grad_top, grad_bottom = swap_rims(last, first)
+    pair = [(0, 1), (1, 0)]
+    got = lax.ppermute(send, "core", pair)
+    half = call(add_kernel, shape((rows, 128)), (keep, got), moved=3 << 20)
+    block = pltpu.VMEM((frames, size, chans), BF)
+    line, rank = lax.axis_size("x"), lax.axis_size("y")
+    column, plane = lax.axis_size(COLUMN), lax.axis_size(PLANE)
+    share = rows // line
+    first = exchange(half.reshape(line, share, 128), "x")
+    part = call(sum_kernel, shape((share, 128)), (first,), moved=1 << 18)
+    second = exchange(part.reshape(rank, share // rank, 128), "y")
+    spread = call(
+        functools.partial(spread_sum_kernel, 1.0),
+        shape((column, share // rank, 128)),
+        (second,),
+        moved=1 << 18,
+        after=(behind,),
+    )
+    third = exchange(spread, COLUMN)
+    block_out = call(
+        mix_kernel,
+        shape((frames, size, chans)),
+        (act, behind, temporal_weight, x),
+        [
+            pltpu.VMEM((2 * frames, size, chans), BF),
+            block,
+            block,
+            pltpu.SemaphoreType.DMA((4 * frames,)),
+        ],
+        flops=3 * work,
+        moved=4 << 20,
+        hbm=(0, 1, 3),
+        out_hbm=True,
+        limit=58,
+    )
+    third, grad_top, grad_bottom = lax.optimization_barrier((third, grad_top, grad_bottom))
     input_grad = call(
         back_kernel,
         shape((frames, size, chans)),
         (pgrad_0, pgrad_1, grad_top, grad_bottom, spatial_weight, dy),
-        [pltpu.VMEM((frames, size + 2 * COLS, chans), BF)],
+        [
+            pltpu.VMEM((frames, size + 2 * COLS, chans), BF),
+            pltpu.VMEM((3, 3, chans, chans), BF),
+            block,
+            block,
+            pltpu.SemaphoreType.DMA((11,)),
+        ],
         flops=9 * work,
         moved=5 << 20,
-    )
-    pair = [(0, 1), (1, 0)]
-    got = lax.ppermute(send, "core", pair)
-    half = call(add_kernel, shape((rows, 128)), (keep, got), moved=3 << 20)
-    line, rank = lax.axis_size("x"), lax.axis_size("y")
-    column, plane = lax.axis_size(COLUMN), lax.axis_size(PLANE)
-    share, piece = rows // line, rows // plane // column
-    first = exchange(half.reshape(line, share, 128), "x")
-    part = call(sum_kernel, shape((share, 128)), (first,), moved=1 << 18)
-    second = exchange(part.reshape(rank, share // rank, 128), "y")
-    part = call(
-        sum_kernel, shape((share // rank, 128), F32), (second,), moved=1 << 18, after=(behind, grad_top, grad_bottom)
-    )
-    third = exchange(part.reshape(column, piece, 128), COLUMN)
-    block_out = call(
-        mix_kernel,
-        shape((flat, chans)),
-        (act, behind, temporal_weight, x.reshape(flat, chans)),
-        [pltpu.VMEM((2 * flat, chans), BF)],
-        flops=3 * work,
-        moved=4 << 20,
-    )
-    spread = call(
-        functools.partial(last_kernel, scale),
-        shape((column, piece, 128)),
+        hbm=range(6),
+        out_hbm=True,
+        limit=58,
+    )
+    wider = call(
+        functools.partial(spread_sum_kernel, scale),
+        shape((plane, share // rank, 128)),
         (third,),
         moved=1 << 18,
     )
-    fourth = exchange(spread, COLUMN).reshape(column * piece, 128)
-    wider = call(spread_kernel, shape((plane, column * piece, 128)), (fourth,), moved=1 << 18)
     own = exchange(wider, PLANE).reshape(rows, 128)
     own, block_out, input_grad = lax.optimization_barrier((own, block_out, input_grad))
     other = lax.ppermute(own, "core", pair)

time: 120 us -> 118 us (0.983)
  blocking collectives: 38.4 us -> 15.6 us
  waiting for transfers between devices: 13.1 us -> 27.6 us
  starting transfers between devices: 35.6 us -> 40.4 us
  Pallas kernels: 23.6 us -> 27.3 us
  local copies, waits for them, and re-layouts: 8.05 us -> 5.97 us
    all_to_all x3 -> x1, blocking collectives: 38.4 us -> 15.6 us  [exchange(): return lax.all_to_all(value, axes, split_axis=0, concat_axis=0, tiled=True)]
    all_to_all x2 -> x3, waiting for transfers between devices: 1.88 us -> 17.6 us  [exchange(): return lax.all_to_all(value, axes, split_axis=0, concat_axis=0, tiled=True)]
    all_to_all x2 -> x3, starting transfers between devices: 11 us -> 16.5 us  [exchange(): return lax.all_to_all(value, axes, split_axis=0, concat_axis=0, tiled=True)]
    pallas_call x13 -> x12, Pallas kernels: 23.6 us -> 27.3 us  [call(): pl.pallas_call(body, out_shape=outs, in_specs=specs, out_specs=placed if...]
    unnamed x20 -> x18, local copies, waits for them, and re-layouts: 5.87 us -> 2.91 us
    ppermute x2, waiting for transfers between devices: 1.56 us -> 0.01 us  [local(): lax.ppermute(frame, TM, steps(TM, -1))]
  transfers between devices with their start and end apart: 11 -> 12, of which waited for: 5 -> 6; matrix products, arithmetic and copies ran while one was open for 0% -> 1% of each run, Pallas kernels for 16% -> 19%
where the time goes in v6:
time: 118 us
  starting transfers between devices  40.4 us (34%)
  waiting for transfers between devices  27.6 us (23%)
  Pallas kernels  27.3 us (23%)
  blocking collectives  15.6 us (13%)
  local copies, waits for them, and re-layouts  5.97 us (5%)
    pallas_call x12, Pallas kernels, call(): pl.pallas_call(body, out_shape=outs, in_specs=specs, out_specs=placed if...  27.3 us
    all_to_all x3, waiting for transfers between devices, exchange(): return lax.all_to_all(value, axes, split_axis=0, concat_axis=0, tiled=True)  17.6 us
    all_to_all x3, starting transfers between devices, exchange(): return lax.all_to_all(value, axes, split_axis=0, concat_axis=0, tiled=True)  16.5 us
    all_to_all x1, blocking collectives, exchange(): return lax.all_to_all(value, axes, split_axis=0, concat_axis=0, tiled=True)  15.6 us
    ppermute x2, waiting for transfers between devices, swap_rims(): lax.ppermute(first, SPACE, steps(SPACE, -1))  9.23 us
    ppermute x2, starting transfers between devices, swap_rims(): lax.ppermute(last, SPACE, steps(SPACE, 1))  8.28 us
    ppermute x2, starting transfers between devices, swap_rims(): lax.ppermute(first, SPACE, steps(SPACE, -1))  3.86 us
    ppermute x1, starting transfers between devices, local(): behind = lax.ppermute(act, TM, steps(TM, 1))  3.6 us
  transfers between devices with their start and end apart: 12, of which 6 were waited for; matrix products, arithmetic and copies ran while one was open for 1% of the time, Pallas kernels for 19%

profile of v6, /device:TPU:1, one launch (start us, length us, event | category | flops | bytes accessed | tf_op | source)
XLA Modules:
  0.0 117.7 jit_solution(3453972115342728829)
XLA Ops:
  0.6 2.0 %slice.13 = bf16[1,1,8,128,256]{4,3,2,1,0:T(8,128)(2,1)} slice(bf16[1,2,8,128,256]{4,3,2,1,0:T(8,128)(2,1)} %param.5), slice={[0:1], [0:1], [0:8], [0:128], [0:256]} | slice | bytes 1048576 | tf_op jit(solution)/shard_map/slice | solution.py:376
  5.0 1.3 %collective-permute-start = (bf16[1024,256]{1,0:T(8,128)(2,1)S(1)}, bf16[1024,256]{1,0:T(8,128)(2,1)S(1)}, u32[]{:S(2)}, u32[]{:S(2)}) collective-permute-start(bf16[1024,256]{1,0:T(8,128)(2,1)S(1)} %slice_bitcast_fusion), channel_id=1, source_target_pairs={{8,0},{16,8},{24,16},{32,24},{40,32},{48,40},{56,48},{64,56},{72,6... | collective-permute-start | bytes 1572872 | tf_op jit(solution)/shard_map/ppermute | solution.py:377
  6.3 4.5 %collective-permute-start.1 = (bf16[2,128,256]{2,1,0:T(8,128)(2,1)S(1)}, bf16[2,128,256]{2,1,0:T(8,128)(2,1)S(1)}, u32[]{:S(2)}, u32[]{:S(2)}) collective-permute-start(bf16[2,128,256]{2,1,0:T(8,128)(2,1)S(1)} %get-tuple-element.63), channel_id=1, source_target_pairs={{0,1},{1,2},{2,3},{3,4},{4,5},{5,6},{6,7},{8,9},{9,10},{10,11},{11... | collective-permute-start | bytes 393224 | tf_op jit(solution)/shard_map/ppermute | solution.py:365
  10.8 1.9 %collective-permute-start.2 = (bf16[2,128,256]{2,1,0:T(8,128)(2,1)S(1)}, bf16[2,128,256]{2,1,0:T(8,128)(2,1)S(1)}, u32[]{:S(2)}, u32[]{:S(2)}) collective-permute-start(bf16[2,128,256]{2,1,0:T(8,128)(2,1)S(1)} %get-tuple-element.62), channel_id=1, source_target_pairs={{1,0},{2,1},{3,2},{4,3},{5,4},{6,5},{7,6},{9,8},{10,9},{11,10},{12... | collective-permute-start | bytes 393224 | tf_op jit(solution)/shard_map/ppermute | solution.py:365
  12.8 4.6 %collective-permute-done.2.refs_2_ = bf16[2,128,256]{2,1,0:T(8,128)(2,1)S(1)} collective-permute-done((bf16[2,128,256]{2,1,0:T(8,128)(2,1)S(1)}, bf16[2,128,256]{2,1,0:T(8,128)(2,1)S(1)}, u32[]{:S(2)}, u32[]{:S(2)}) %collective-permute-start.2) | collective-permute-done | bytes 131104 | tf_op jit(solution)/shard_map/ppermute | solution.py:365
  18.7 4.9 %shard_map.75 = (bf16[2,1024,256]{2,1,0:T(8,128)(2,1)}, f32[2,1024,256]{2,1,0:T(8,128)S(1)}, bf16[2,256,1280]{2,1,0:T(8,128)(2,1)S(1)}, bf16[2,256,1024]{2,1,0:T(8,128)(2,1)S(1)}) custom-call(bf16[2,1024,256]{2,1,0:T(8,128)(2,1)S(1)} %bitcast.17, bf16[2,128,256]{2,1,0:T(8,128)(2,1)S(1)} %collective-permute-done.1.refs_1_, ...), custom_call_target="tpu_custom_call" | custom-call | flops 2415919104 | bytes 9437184 | tf_op jit(solution)/shard_map/pallas_call | solution.py:35
  23.6 1.4 %shard_map.76 = (f32[2,1024,256]{2,1,0:T(8,128)S(1)}, f32[2,256,256]{2,1,0:T(8,128)S(1)}) custom-call(bf16[2,1024,256]{2,1,0:T(8,128)(2,1)S(1)} %bitcast.20, bf16[3,256,256]{2,1,0:T(8,128)(2,1)S(1)} %copy-done.1, bf16[2,256,1024]{2,1,0:T(8,128)(2,1)S(1)} %get-tuple-element.36.refs_2_.refs_4_.refs_5_), custom_call_target="tpu_custom_call" | custom-call | flops 1610612736 | bytes 6291456 | tf_op jit(solution)/shard_map/pallas_call | solution.py:35
  25.0 2.5 %shard_map.77 = (bf16[1024,256]{1,0:T(8,128)(2,1)S(1)}, f32[1024,256]{1,0:T(8,128)S(1)}, f32[3,768,256]{2,1,0:T(8,128)S(1)}, f32[2,256,256]{2,1,0:T(8,128)S(1)},...) custom-call(bf16[1024,256]{1,0:T(8,128)(2,1)S(1)} %collective-permute-done.3.refs_0_, ...), custom_call_target="tpu_custom_call" | custom-call | flops 16777216 | bytes 262144 | tf_op jit(solution)/shard_map/pallas_call | solution.py:35
  28.3 2.4 %shard_map.78 = (bf16[1024,256]{1,0:T(8,128)(2,1)S(1)}, bf16[3072,128]{1,0:T(8,128)(2,1)S(1)}, bf16[3072,128]{1,0:T(8,128)(2,1)S(1)}, bf16[2,128,256]{2,1,0:T(8,128)(2,1)S(1)}, bf16[2,128,256]{2,1,0:T(8,128)(2,1)S(1)}) custom-call(s32[1]{0:T(128)} %bitcast.refs_0_, bf16[1024,256]{1,0:T(8,128)(2,1)S(1)} %collective-permute-done.refs_1_, ...), custom_call_target="tpu_custom_call" | custom-call | flops 16777216 | bytes 262144 | tf_op jit(solution)/shard_map/pallas_call | solution.py:35
  31.6 3.0 %collective-permute-start.4 = (bf16[3072,128]{1,0:T(8,128)(2,1)S(1)}, bf16[3072,128]{1,0:T(8,128)(2,1)S(1)}, u32[]{:S(2)}, u32[]{:S(2)}) collective-permute-start(bf16[3072,128]{1,0:T(8,128)(2,1)S(1)} %get-tuple-element.46), channel_id=1, source_target_pairs={{0,1},{1,0},{2,3},{3,2},{4,5},{5,4},{6,7},{7,6},{8,9},{9,8},{10,11... | collective-permute-start | bytes 2359304 | tf_op jit(solution)/shard_map/ppermute | solution.py:446
  34.5 3.6 %collective-permute-start.5 = (bf16[2,1024,256]{2,1,0:T(8,128)(2,1)}, bf16[2,1024,256]{2,1,0:T(8,128)(2,1)S(1)}, u32[]{:S(2)}, u32[]{:S(2)}) collective-permute-start(bf16[2,1024,256]{2,1,0:T(8,128)(2,1)} %get-tuple-element.47.refs_0_), channel_id=1, source_target_pairs={{0,8},{8,16},{16,24},{24,32},{32,40},{40,48},{48,56},{56,64},{64,7... | collective-permute-start | bytes 3145736 | tf_op jit(solution)/shard_map/ppermute | solution.py:399
  38.3 15.6 %all_to_all.20.refs_0_ = bf16[4,768,128]{2,1,0:T(8,128)(2,1)S(1)} all-to-all(bf16[4,768,128]{2,1,0:T(8,128)(2,1)S(1)} %bitcast.14), channel_id=1, replica_groups=mesh['clip'=2,'y'=4,'zl'=4,'x'=4,'core'=2] {'x'}, dimensions={0} | all-to-all | bytes 1572864 | tf_op jit(solution)/shard_map/all_to_all | solution.py:361
  54.7 6.3 %all-to-all-start.1 = ((bf16[4,192,128]{2,1,0:T(8,128)(2,1)}), bf16[4,192,128]{2,1,0:T(8,128)(2,1)S(1)}, u32[]{:S(2)}, u32[]{:S(2)}) async-start(bf16[4,192,128]{2,1,0:T(8,128)(2,1)} %bitcast.6), calls=%async_computation.1 | async-start | bytes 393216 | tf_op jit(solution)/shard_map/all_to_all | solution.py:361
  61.0 11.1 %all-to-all-done.1.refs_0_ = bf16[4,192,128]{2,1,0:T(8,128)(2,1)S(1)} async-done(((bf16[4,192,128]{2,1,0:T(8,128)(2,1)}), bf16[4,192,128]{2,1,0:T(8,128)(2,1)S(1)}, u32[]{:S(2)}, u32[]{:S(2)}) %all-to-all-start.1) | async-done | bytes 196640 | tf_op jit(solution)/shard_map/all_to_all | solution.py:361
  72.9 6.4 %all-to-all-start.2 = ((bf16[8,192,128]{2,1,0:T(8,128)(2,1)}), bf16[8,192,128]{2,1,0:T(8,128)(2,1)S(1)}, u32[]{:S(2)}, u32[]{:S(2)}) async-start(bf16[8,192,128]{2,1,0:T(8,128)(2,1)} %shard_map.81), calls=%async_computation.2 | async-start | bytes 786432 | tf_op jit(solution)/shard_map/all_to_all | solution.py:361
  79.3 3.8 %collective-permute-start.6 = (bf16[2,128,256]{2,1,0:T(8,128)(2,1)S(1)}, bf16[2,128,256]{2,1,0:T(8,128)(2,1)S(1)}, u32[]{:S(2)}, u32[]{:S(2)}) collective-permute-start(bf16[2,128,256]{2,1,0:T(8,128)(2,1)S(1)} %get-tuple-element.48), channel_id=1, source_target_pairs={{0,1},{1,2},{2,3},{3,4},{4,5},{5,6},{6,7},{8,9},{9,10},{10,11},{11... | collective-permute-start | bytes 393224 | tf_op jit(solution)/shard_map/ppermute | solution.py:365
  83.1 1.9 %collective-permute-start.7 = (bf16[2,128,256]{2,1,0:T(8,128)(2,1)S(1)}, bf16[2,128,256]{2,1,0:T(8,128)(2,1)S(1)}, u32[]{:S(2)}, u32[]{:S(2)}) collective-permute-start(bf16[2,128,256]{2,1,0:T(8,128)(2,1)S(1)} %get-tuple-element.49), channel_id=1, source_target_pairs={{1,0},{2,1},{3,2},{4,3},{5,4},{6,5},{7,6},{9,8},{10,9},{11,10},{12... | collective-permute-start | bytes 393224 | tf_op jit(solution)/shard_map/ppermute | solution.py:365
  85.0 4.6 %collective-permute-done.7.refs_3_ = bf16[2,128,256]{2,1,0:T(8,128)(2,1)S(1)} collective-permute-done((bf16[2,128,256]{2,1,0:T(8,128)(2,1)S(1)}, bf16[2,128,256]{2,1,0:T(8,128)(2,1)S(1)}, u32[]{:S(2)}, u32[]{:S(2)}) %collective-permute-start.7) | collective-permute-done | bytes 131104 | tf_op jit(solution)/shard_map/ppermute | solution.py:365
  89.7 4.7 %all-to-all-done.2.refs_0_ = bf16[8,192,128]{2,1,0:T(8,128)(2,1)S(1)} async-done(((bf16[8,192,128]{2,1,0:T(8,128)(2,1)}), bf16[8,192,128]{2,1,0:T(8,128)(2,1)S(1)}, u32[]{:S(2)}, u32[]{:S(2)}) %all-to-all-start.2) | async-done | bytes 393248 | tf_op jit(solution)/shard_map/all_to_all | solution.py:361
  95.3 3.8 %all-to-all-start.3 = ((bf16[16,192,128]{2,1,0:T(8,128)(2,1)}), bf16[16,192,128]{2,1,0:T(8,128)(2,1)S(1)}, u32[]{:S(2)}, u32[]{:S(2)}) async-start(bf16[16,192,128]{2,1,0:T(8,128)(2,1)} %shard_map.82), calls=%async_computation.3 | async-start | bytes 1572864 | tf_op jit(solution)/shard_map/all_to_all | solution.py:361
  99.2 5.2 %shard_map.83 = bf16[2,1024,256]{2,1,0:T(8,128)(2,1)} custom-call(bf16[2,1024,256]{2,1,0:T(8,128)(2,1)} %get-tuple-element.47.refs_0_, bf16[2,1024,256]{2,1,0:T(8,128)(2,1)} %copy-done, bf16[3,256,256]{2,1,0:T(8,128)(2,1)} %refs_2_.3, bf16[2,1024,256]{2,1,0:T(8,128)(2,1)} %bitcast.15), custom_call_target="tpu_custom_call" | custom-call | flops 805306368 | bytes 4194304 | tf_op jit(solution)/shard_map/pallas_call | solution.py:35
  104.4 5.8 %shard_map.84 = bf16[2,1024,256]{2,1,0:T(8,128)(2,1)} custom-call(bf16[1024,256]{1,0:T(8,128)(2,1)} %copy-done.5, bf16[1024,256]{1,0:T(8,128)(2,1)} %copy-done.6, bf16[2,128,256]{2,1,0:T(8,128)(2,1)} %copy-done.7, bf16[2,128,256]{2,1,0:T(8,128)(2,1)} %copy-done.8, bf16[3,3,256,256]{3,2,1,0:T(8,128)(2,1)} %refs_4_.1, bf16[2,1024,256]{2,1,0:T(8,128)(2,1)} %bitcast.19), custom_call_target="tpu_custom_call" | custom-call | flops 2415919104 | bytes 5242880 | tf_op jit(solution)/shard_map/pallas_call | solution.py:35
  110.2 1.8 %all-to-all-done.3 = bf16[16,192,128]{2,1,0:T(8,128)(2,1)S(1)} async-done(((bf16[16,192,128]{2,1,0:T(8,128)(2,1)}), bf16[16,192,128]{2,1,0:T(8,128)(2,1)S(1)}, u32[]{:S(2)}, u32[]{:S(2)}) %all-to-all-start.3) | async-done | bytes 786464 | tf_op jit(solution)/shard_map/all_to_all | solution.py:361
  111.9 2.6 %collective-permute-start.8 = (bf16[3072,128]{1,0:T(8,128)(2,1)S(1)}, bf16[3072,128]{1,0:T(8,128)(2,1)S(1)}, u32[]{:S(2)}, u32[]{:S(2)}) collective-permute-start(bf16[3072,128]{1,0:T(8,128)(2,1)S(1)} %bitcast.12), channel_id=1, source_target_pairs={{0,1},{1,0},{2,3},{3,2},{4,5},{5,4},{6,7},{7,6},{8,9},{9,8},{10,11... | collective-permute-start | bytes 2359304 | tf_op jit(solution)/shard_map/ppermute | solution.py:505
  (34 shorter events, 11.1 us)
Async XLA Ops:
  0.6 5.6 %copy-start.2 = (bf16[1,2,8,128,256]{4,3,2,1,0:T(8,128)(2,1)S(1)}, bf16[1,2,8,128,256]{4,3,2,1,0:T(8,128)(2,1)}, u32[]{:S(2)}) copy-start(bf16[1,2,8,128,256]{4,3,2,1,0:T(8,128)(2,1)} %param.4) | copy-start | bytes 3145732
  2.6 22.4 %collective-permute-start.3 = (bf16[1024,256]{1,0:T(8,128)(2,1)}, bf16[1024,256]{1,0:T(8,128)(2,1)S(1)}, u32[]{:S(2)}, u32[]{:S(2)}) collective-permute-start(bf16[1024,256]{1,0:T(8,128)(2,1)} %bitcast.1), channel_id=1, source_target_pairs={{8,0},{16,8},{24,16},{32,24},{40,32},{48,40},{56,48},{64,56},{72,6... | collective-permute-start | bytes 1572872 | tf_op jit(solution)/shard_map/ppermute | solution.py:377
  5.0 23.3 %collective-permute-start = (bf16[1024,256]{1,0:T(8,128)(2,1)S(1)}, bf16[1024,256]{1,0:T(8,128)(2,1)S(1)}, u32[]{:S(2)}, u32[]{:S(2)}) collective-permute-start(bf16[1024,256]{1,0:T(8,128)(2,1)S(1)} %slice_bitcast_fusion), channel_id=1, source_target_pairs={{8,0},{16,8},{24,16},{32,24},{40,32},{48,40},{56,48},{64,56},{72,6... | collective-permute-start | bytes 1572872 | tf_op jit(solution)/shard_map/ppermute | solution.py:377
  6.3 6.5 %collective-permute-start.1 = (bf16[2,128,256]{2,1,0:T(8,128)(2,1)S(1)}, bf16[2,128,256]{2,1,0:T(8,128)(2,1)S(1)}, u32[]{:S(2)}, u32[]{:S(2)}) collective-permute-start(bf16[2,128,256]{2,1,0:T(8,128)(2,1)S(1)} %get-tuple-element.63), channel_id=1, source_target_pairs={{0,1},{1,2},{2,3},{3,4},{4,5},{5,6},{6,7},{8,9},{9,10},{10,11},{11... | collective-permute-start | bytes 393224 | tf_op jit(solution)/shard_map/ppermute | solution.py:365
  10.8 6.6 %collective-permute-start.2 = (bf16[2,128,256]{2,1,0:T(8,128)(2,1)S(1)}, bf16[2,128,256]{2,1,0:T(8,128)(2,1)S(1)}, u32[]{:S(2)}, u32[]{:S(2)}) collective-permute-start(bf16[2,128,256]{2,1,0:T(8,128)(2,1)S(1)} %get-tuple-element.62), channel_id=1, source_target_pairs={{1,0},{2,1},{3,2},{4,3},{5,4},{6,5},{7,6},{9,8},{10,9},{11,10},{12... | collective-permute-start | bytes 393224 | tf_op jit(solution)/shard_map/ppermute | solution.py:365
  12.8 10.8 %copy-start.1 = (bf16[3,256,256]{2,1,0:T(8,128)(2,1)S(1)}, bf16[3,256,256]{2,1,0:T(8,128)(2,1)}, u32[]{:S(2)}) copy-start(bf16[3,256,256]{2,1,0:T(8,128)(2,1)} %refs_2_.3) | copy-start | bytes 1179652
  12.8 10.8 %copy-start.3 = (bf16[1,2,8,128,256]{4,3,2,1,0:T(8,128)(2,1)S(1)}, bf16[1,2,8,128,256]{4,3,2,1,0:T(8,128)(2,1)}, u32[]{:S(2)}) copy-start(bf16[1,2,8,128,256]{4,3,2,1,0:T(8,128)(2,1)} %param.5) | copy-start | bytes 3145732
  17.4 1.3 %copy-start.4 = (bf16[3,3,256,256]{3,2,1,0:T(8,128)(2,1)S(1)}, bf16[3,3,256,256]{3,2,1,0:T(8,128)(2,1)}, u32[]{:S(2)}) copy-start(bf16[3,3,256,256]{3,2,1,0:T(8,128)(2,1)} %refs_4_.1) | copy-start | bytes 3538948
  27.5 0.8 copy-start.5
  30.7 0.8 copy-start.6
  31.6 6.6 %collective-permute-start.4 = (bf16[3072,128]{1,0:T(8,128)(2,1)S(1)}, bf16[3072,128]{1,0:T(8,128)(2,1)S(1)}, u32[]{:S(2)}, u32[]{:S(2)}) collective-permute-start(bf16[3072,128]{1,0:T(8,128)(2,1)S(1)} %get-tuple-element.46), channel_id=1, source_target_pairs={{0,1},{1,0},{2,3},{3,2},{4,5},{5,4},{6,7},{7,6},{8,9},{9,8},{10,11... | collective-permute-start | bytes 2359304 | tf_op jit(solution)/shard_map/ppermute | solution.py:446
  34.5 26.5 %collective-permute-start.5 = (bf16[2,1024,256]{2,1,0:T(8,128)(2,1)}, bf16[2,1024,256]{2,1,0:T(8,128)(2,1)S(1)}, u32[]{:S(2)}, u32[]{:S(2)}) collective-permute-start(bf16[2,1024,256]{2,1,0:T(8,128)(2,1)} %get-tuple-element.47.refs_0_), channel_id=1, source_target_pairs={{0,8},{8,16},{16,24},{24,32},{32,40},{40,48},{48,56},{56,64},{64,7... | collective-permute-start | bytes 3145736 | tf_op jit(solution)/shard_map/ppermute | solution.py:399
  54.7 17.4 %all-to-all-start.1 = ((bf16[4,192,128]{2,1,0:T(8,128)(2,1)}), bf16[4,192,128]{2,1,0:T(8,128)(2,1)S(1)}, u32[]{:S(2)}, u32[]{:S(2)}) async-start(bf16[4,192,128]{2,1,0:T(8,128)(2,1)} %bitcast.6), calls=%async_computation.1 | async-start | bytes 393216 | tf_op jit(solution)/shard_map/all_to_all | solution.py:361
  61.0 34.4 %copy-start = (bf16[2,1024,256]{2,1,0:T(8,128)(2,1)}, bf16[2,1024,256]{2,1,0:T(8,128)(2,1)S(1)}, u32[]{:S(2)}) copy-start(bf16[2,1024,256]{2,1,0:T(8,128)(2,1)S(1)} %collective-permute-done.5.refs_1_) | copy-start | bytes 3145732
  72.9 21.5 %all-to-all-start.2 = ((bf16[8,192,128]{2,1,0:T(8,128)(2,1)}), bf16[8,192,128]{2,1,0:T(8,128)(2,1)S(1)}, u32[]{:S(2)}, u32[]{:S(2)}) async-start(bf16[8,192,128]{2,1,0:T(8,128)(2,1)} %shard_map.81), calls=%async_computation.2 | async-start | bytes 786432 | tf_op jit(solution)/shard_map/all_to_all | solution.py:361
  79.3 5.7 %collective-permute-start.6 = (bf16[2,128,256]{2,1,0:T(8,128)(2,1)S(1)}, bf16[2,128,256]{2,1,0:T(8,128)(2,1)S(1)}, u32[]{:S(2)}, u32[]{:S(2)}) collective-permute-start(bf16[2,128,256]{2,1,0:T(8,128)(2,1)S(1)} %get-tuple-element.48), channel_id=1, source_target_pairs={{0,1},{1,2},{2,3},{3,4},{4,5},{5,6},{6,7},{8,9},{9,10},{10,11},{11... | collective-permute-start | bytes 393224 | tf_op jit(solution)/shard_map/ppermute | solution.py:365
  83.1 6.6 %collective-permute-start.7 = (bf16[2,128,256]{2,1,0:T(8,128)(2,1)S(1)}, bf16[2,128,256]{2,1,0:T(8,128)(2,1)S(1)}, u32[]{:S(2)}, u32[]{:S(2)}) collective-permute-start(bf16[2,128,256]{2,1,0:T(8,128)(2,1)S(1)} %get-tuple-element.49), channel_id=1, source_target_pairs={{1,0},{2,1},{3,2},{4,3},{5,4},{6,5},{7,6},{9,8},{10,9},{11,10},{12... | collective-permute-start | bytes 393224 | tf_op jit(solution)/shard_map/ppermute | solution.py:365
  85.0 19.4 %copy-start.7 = (bf16[2,128,256]{2,1,0:T(8,128)(2,1)}, bf16[2,128,256]{2,1,0:T(8,128)(2,1)S(1)}, u32[]{:S(2)}) copy-start(bf16[2,128,256]{2,1,0:T(8,128)(2,1)S(1)} %collective-permute-done.6.refs_2_) | copy-start | bytes 393220
  89.7 14.8 %copy-start.8 = (bf16[2,128,256]{2,1,0:T(8,128)(2,1)}, bf16[2,128,256]{2,1,0:T(8,128)(2,1)S(1)}, u32[]{:S(2)}) copy-start(bf16[2,128,256]{2,1,0:T(8,128)(2,1)S(1)} %collective-permute-done.7.refs_3_) | copy-start | bytes 393220
  95.3 16.6 %all-to-all-start.3 = ((bf16[16,192,128]{2,1,0:T(8,128)(2,1)}), bf16[16,192,128]{2,1,0:T(8,128)(2,1)S(1)}, u32[]{:S(2)}, u32[]{:S(2)}) async-start(bf16[16,192,128]{2,1,0:T(8,128)(2,1)} %shard_map.82), calls=%async_computation.3 | async-start | bytes 1572864 | tf_op jit(solution)/shard_map/all_to_all | solution.py:361
  111.9 4.5 %collective-permute-start.8 = (bf16[3072,128]{1,0:T(8,128)(2,1)S(1)}, bf16[3072,128]{1,0:T(8,128)(2,1)S(1)}, u32[]{:S(2)}, u32[]{:S(2)}) collective-permute-start(bf16[3072,128]{1,0:T(8,128)(2,1)S(1)} %bitcast.12), channel_id=1, source_target_pairs={{0,1},{1,0},{2,3},{3,2},{4,5},{5,4},{6,7},{7,6},{8,9},{9,8},{10,11... | collective-permute-start | bytes 2359304 | tf_op jit(solution)/shard_map/ppermute | solution.py:505

commit v7 on v6

--- a/solution.py
+++ b/solution.py
@@ -122,55 +122,25 @@
     grad = (agrad.astype(BF).astype(F32) * slope[f, at, :]).astype(BF)
     full = grad.astype(F32)
     column = columns_of(CHUNK, full.shape[1])
-    wide[0, at, :] = shifted(full, column, -1).astype(BF)
-    wide[1, at, :] = grad
-    wide[2, at, :] = shifted(full, column, 1).astype(BF)
+    into = pl.ds(f * slope.shape[1] + start, CHUNK)
+    wide[0, into, :] = shifted(full, column, -1).astype(BF)
+    wide[1, into, :] = grad
+    wide[2, into, :] = shifted(full, column, 1).astype(BF)
 
 
 def windows_of(x_t, f, size):
     return jnp.concatenate([x_t[f, :, i * COLS : i * COLS + size] for i in range(3)], axis=0)
 
 
-def first_kernel(
-    ahead, weight, slope, x_t, act_t, partial, early, pgrad, rest, spatial, temporal, last, first, wide, sem
-):
-    size = ahead.shape[0]
-
-    @pl.loop(0, size // CHUNK)
-    def _(step):
-        start = pl.multiple_of(step * CHUNK, CHUNK)
-        at = pl.ds(start, CHUNK)
-        block = ahead[at, :]
-        more = lax.dot_general(block, weight[2], NT, preferred_element_type=F32)
-        finish(0, start, partial[0, at, :] + more, slope, wide)
-        more = lax.dot_general(block, weight[1], NT, preferred_element_type=F32)
-        rest[at, :] = partial[1, at, :] + more
-
-    store = pltpu.make_async_copy(wide.at[1], pgrad, sem)
-    store.start()
-    last[...] = wide[1, size - COLS :, :]
-    first[...] = wide[1, :COLS, :]
-    left = windows_of(x_t, 0, size)
-    for j in range(3):
-        spatial[j] = jnp.dot(left, wide[j], preferred_element_type=F32)
-    temporal[0] = early[1] + jnp.dot(act_t[1], ahead[...], preferred_element_type=F32)
-    temporal[1] = jnp.dot(act_t[0], ahead[...], preferred_element_type=F32)
-    store.wait()
-
-
-def second_kernel(
+def gradient_kernel(
     core,
     ahead,
     weight,
     slope,
     x_t,
     act_t,
-    rest,
+    partial,
     early,
-    spatial,
-    temporal,
-    last_0,
-    first_0,
     pgrad,
     keep,
     send,
@@ -178,37 +148,45 @@
     first,
     wide,
     terms,
-    sem,
+    sems,
 ):
-    size, chans = ahead.shape
+    frames, size, chans = ahead.shape
 
     @pl.loop(0, size // CHUNK)
     def _(step):
         start = pl.multiple_of(step * CHUNK, CHUNK)
         at = pl.ds(start, CHUNK)
-        more = lax.dot_general(ahead[at, :], weight[2], NT, preferred_element_type=F32)
-        finish(1, start, rest[at, :] + more, slope, wide)
-
-    store = pltpu.make_async_copy(wide.at[1], pgrad, sem)
-    store.start()
-    last[0] = last_0[...]
-    first[0] = first_0[...]
-    last[1] = wide[1, size - COLS :, :]
-    first[1] = wide[1, :COLS, :]
+        block = ahead[0, at, :]
+        more = lax.dot_general(block, weight[2], NT, preferred_element_type=F32)
+        finish(0, start, partial[0, at, :] + more, slope, wide)
+        both = jnp.concatenate([block, ahead[1, at, :]], axis=1)
+        taps = jnp.concatenate([weight[1], weight[2]], axis=1)
+        more = lax.dot_general(both, taps, NT, preferred_element_type=F32)
+        finish(1, start, partial[1, at, :] + more, slope, wide)
+
+    stores = []
+    for f in range(frames):
+        rows = pl.ds(f * size, size)
+        stores.append(pltpu.make_async_copy(wide.at[1, rows], pgrad.at[f], sems.at[f]))
+        stores[f].start()
+        last[f] = wide[1, (f + 1) * size - COLS : (f + 1) * size, :]
+        first[f] = wide[1, f * size : f * size + COLS, :]
 
     def put(tap, value):
         for h in range(2):
             at = (tap * 2 + h) * chans
             terms[at : at + chans, :] = value[:, h * 128 : (h + 1) * 128].astype(BF)
 
-    left = windows_of(x_t, 1, size)
+    left = jnp.concatenate([windows_of(x_t, f, size) for f in range(frames)], axis=1)
     for j in range(3):
-        out = spatial[j] + jnp.dot(left, wide[j], preferred_element_type=F32)
+        out = jnp.dot(left, wide[j], preferred_element_type=F32)
         for i in range(3):
             put(3 * i + j, out[i * chans : (i + 1) * chans])
     put(9, early[0])
-    put(10, temporal[0])
-    put(11, temporal[1] + jnp.dot(act_t[1], ahead[...], preferred_element_type=F32))
+    put(10, early[1] + jnp.dot(act_t[1], ahead[0], preferred_element_type=F32))
+    left_t = jnp.concatenate([act_t[0], act_t[1]], axis=1)
+    right = ahead[...].reshape(frames * size, chans)
+    put(11, jnp.dot(left_t, right, preferred_element_type=F32))
     half = terms.shape[0] // 2
     for c in range(2):
 
@@ -217,7 +195,8 @@
             keep[...] = terms[c * half : (c + 1) * half, :]
             send[...] = terms[(1 - c) * half : (2 - c) * half, :]
 
-    store.wait()
+    for store in stores:
+        store.wait()
 
 
 def add_kernel(a, b, out):
@@ -271,27 +250,30 @@
             write_half(c == 1, other, spatial, temporal, wide, sems)
 
 
-def back_kernel(
-    grad_0, grad_1, top, bottom, weight, dy, out, padded, taps, own, result, sems
-):
+def back_taps(taps, j):
+    return jnp.concatenate([taps[i, j] for i in range(3)], axis=1)
+
+
+def back_kernel(grad, weight, dy, out, edge, padded, taps, own, result, sems):
     frames, size, chans = own.shape
     whole = pltpu.make_async_copy(weight, taps, sems.at[0])
     whole.start()
     loads = []
-    for f, grad in enumerate((grad_0, grad_1)):
-        base = 1 + 5 * f
+    for f in range(frames):
+        base = 1 + 3 * f
         loads.append(
             [
-                pltpu.make_async_copy(top.at[f], padded.at[f, pl.ds(0, COLS)], sems.at[base]),
-                pltpu.make_async_copy(grad, padded.at[f, pl.ds(COLS, size)], sems.at[base + 1]),
                 pltpu.make_async_copy(
-                    bottom.at[f], padded.at[f, pl.ds(COLS + size, COLS)], sems.at[base + 2]
+                    grad.at[f], padded.at[f, pl.ds(COLS, size)], sems.at[base]
                 ),
-                pltpu.make_async_copy(dy.at[f], own.at[f], sems.at[base + 3]),
+                pltpu.make_async_copy(dy.at[f], own.at[f], sems.at[base + 1]),
             ]
         )
         for load in loads[f]:
             load.start()
+        blank = jnp.zeros((COLS, chans), BF)
+        padded[f, 0:COLS, :] = blank
+        padded[f, COLS + size :, :] = blank
     whole.wait()
     stores = []
     for f in range(frames):
@@ -305,46 +287,68 @@
             rows = window(padded, f, start, CHUNK, (2, 1, 0))
             column = columns_of(CHUNK, chans)
             z = [
-                lax.dot_general(
-                    rows,
-                    jnp.concatenate([taps[i, j] for i in range(3)], axis=1),
-                    NT,
-                    preferred_element_type=F32,
-                )
+                lax.dot_general(rows, back_taps(taps, j), NT, preferred_element_type=F32)
                 for j in range(3)
             ]
             back = shifted(z[0], column, -1) + z[1] + shifted(z[2], column, 1)
-            result[f, at, :] = (own[f, at, :].astype(F32) + back).astype(BF)
-
-        store = pltpu.make_async_copy(result.at[f], out.at[f], sems.at[5 + 5 * f])
+            total = own[f, at, :].astype(F32) + back
+            result[f, at, :] = total.astype(BF)
+
+            @pl.when(step == 0)
+            def _():
+                edge[f, 0] = total[:COLS]
+
+            @pl.when(step == size // CHUNK - 1)
+            def _():
+                edge[f, 1] = total[CHUNK - COLS :]
+
+        store = pltpu.make_async_copy(result.at[f], out.at[f], sems.at[3 + 3 * f])
         store.start()
         stores.append(store)
     for store in stores:
         store.wait()
 
 
+def edge_kernel(top, bottom, weight, edge, part, out, result, sems):
+    frames, size = part.shape[0], part.shape[1]
+    chans = part.shape[2]
+    column = columns_of(frames * COLS, chans)
+    stores = []
+    for e, (rim, i) in enumerate(((top, 2), (bottom, 0))):
+        rows = rim[...].reshape(frames * COLS, chans)
+        z = [
+            lax.dot_general(rows, weight[i, j], NT, preferred_element_type=F32) for j in range(3)
+        ]
+        more = shifted(z[0], column, -1) + z[1] + shifted(z[2], column, 1)
+        for f in range(frames):
+            total = edge[f, e] + more[f * COLS : (f + 1) * COLS]
+            result[f, e] = total.astype(BF)
+            target = out.at[f, pl.ds(e * (size - COLS), COLS)]
+            store = pltpu.make_async_copy(result.at[f, e], target, sems.at[2 * f + e])
+            store.start()
+            stores.append(store)
+    for store in stores:
+        store.wait()
+
+
 def mix_kernel(act, behind, weight, x, out, ext, own, result, sems):
     frames, size, chans = own.shape
-    loads = []
-    for f in range(frames):
-        loads.append(pltpu.make_async_copy(behind.at[f], ext.at[f], sems.at[f]))
-        loads.append(pltpu.make_async_copy(act.at[f], ext.at[frames + f], sems.at[frames + f]))
-        loads.append(pltpu.make_async_copy(x.at[f], own.at[f], sems.at[2 * frames + f]))
+    loads = [pltpu.make_async_copy(behind.at[f], ext.at[f], sems.at[f]) for f in range(frames)]
+    for f in range(frames):
+        loads.append(pltpu.make_async_copy(act.at[f], ext.at[frames + f], sems.at[frames + 2 * f]))
+        loads.append(pltpu.make_async_copy(x.at[f], own.at[f], sems.at[frames + 2 * f + 1]))
     for load in loads:
         load.start()
-    for load in loads:
+    for load in loads[:frames]:
         load.wait()
     stores = []
     for f in range(frames):
-
-        @pl.loop(0, size // CHUNK)
-        def _(step):
-            at = pl.ds(pl.multiple_of(step * CHUNK, CHUNK), CHUNK)
-            rows = jnp.concatenate([ext[f + 2 - k, at, :] for k in range(3)], axis=1)
-            taps = weight[...].reshape(3 * chans, chans)
-            mixed = jnp.dot(rows, taps, preferred_element_type=F32).astype(BF)
-            result[f, at, :] = (own[f, at, :].astype(F32) + mixed.astype(F32)).astype(BF)
-
+        for load in loads[frames + 2 * f : frames + 2 * f + 2]:
+            load.wait()
+        rows = jnp.concatenate([ext[f + 2 - k] for k in range(3)], axis=1)
+        taps = weight[...].reshape(3 * chans, chans)
+        mixed = jnp.dot(rows, taps, preferred_element_type=F32).astype(BF)
+        result[f] = (own[f].astype(F32) + mixed.astype(F32)).astype(BF)
         store = pltpu.make_async_copy(result.at[f], out.at[f], sems.at[3 * frames + f])
         store.start()
         stores.append(store)
@@ -373,8 +377,7 @@
     dy = cotangent.reshape(frames, size, chans)
     work = 2 * frames * size * chans * chans
     core = lax.axis_index("core").astype(jnp.int32).reshape(1)
-    dy_0, later = lax.optimization_barrier((dy[0], dy))
-    ahead = [lax.ppermute(frame, TM, steps(TM, -1)) for frame in (dy_0, later[1])]
+    ahead = lax.ppermute(dy, TM, steps(TM, -1))
     top, bottom = swap_rims(x[:, size - COLS :, :], x[:, :COLS, :])
     act, slope, x_t, act_t = call(
         forward_kernel,
@@ -399,47 +402,20 @@
     behind = lax.ppermute(act, TM, steps(TM, 1))
     flat = frames * size
     rows = 12 * chans
-    wide = pltpu.VMEM((3, size, chans), BF)
-    edge = shape((COLS, chans))
-    pgrad_0, rest, spatial, temporal, last_0, first_0 = call(
-        first_kernel,
+    edges = shape((frames, COLS, chans))
+    pgrad, keep, send, last, first = call(
+        gradient_kernel,
+        [shape((frames, size, chans)), shape((rows, 128)), shape((rows, 128)), edges, edges],
+        (core, ahead, temporal_weight, slope, x_t, act_t, partial, early),
         [
-            shape((size, chans)),
-            shape((size, chans), F32),
-            shape((3, 3 * chans, chans), F32),
-            shape((2, chans, chans), F32),
-            edge,
-            edge,
+            pltpu.VMEM((3, flat, chans), BF),
+            pltpu.VMEM((2 * rows, 128), BF),
+            pltpu.SemaphoreType.DMA((frames,)),
         ],
-        (ahead[0], temporal_weight, slope, x_t, act_t, partial, early),
-        [wide, pltpu.SemaphoreType.DMA],
         flops=work // 16,
         moved=1 << 18,
+        smem=(0,),
         out_hbm=(0,),
-    )
-    edges = shape((frames, COLS, chans))
-    pgrad_1, keep, send, last, first = call(
-        second_kernel,
-        [shape((size, chans)), shape((rows, 128)), shape((rows, 128)), edges, edges],
-        (
-            core,
-            ahead[1],
-            temporal_weight,
-            slope,
-            x_t,
-            act_t,
-            rest,
-            early,
-            spatial,
-            temporal,
-            last_0,
-            first_0,
-        ),
-        [wide, pltpu.VMEM((2 * rows, 128), BF), pltpu.SemaphoreType.DMA],
-        flops=work // 16,
-        moved=1 << 18,
-        out_hbm=(0,),
-        smem=(0,),
     )
     grad_top, grad_bottom = swap_rims(last, first)
     pair = [(0, 1), (1, 0)]
@@ -452,6 +428,24 @@
     first = exchange(half.reshape(line, share, 128), "x")
     part = call(sum_kernel, shape((share, 128)), (first,), moved=1 << 18)
     second = exchange(part.reshape(rank, share // rank, 128), "y")
+    inner, edge = call(
+        back_kernel,
+        [shape((frames, size, chans)), shape((frames, 2, COLS, chans), F32)],
+        (pgrad, spatial_weight, dy),
+        [
+            pltpu.VMEM((frames, size + 2 * COLS, chans), BF),
+            pltpu.VMEM((3, 3, chans, chans), BF),
+            block,
+            block,
+            pltpu.SemaphoreType.DMA((7,)),
+        ],
+        flops=9 * work,
+        moved=5 << 20,
+        hbm=range(3),
+        out_hbm=(0,),
+        limit=58,
+    )
+    second, edge = lax.optimization_barrier((second, edge))
     spread = call(
         functools.partial(spread_sum_kernel, 1.0),
         shape((column, share // rank, 128)),
@@ -478,21 +472,15 @@
     )
     third, grad_top, grad_bottom = lax.optimization_barrier((third, grad_top, grad_bottom))
     input_grad = call(
-        back_kernel,
+        edge_kernel,
         shape((frames, size, chans)),
-        (pgrad_0, pgrad_1, grad_top, grad_bottom, spatial_weight, dy),
-        [
-            pltpu.VMEM((frames, size + 2 * COLS, chans), BF),
-            pltpu.VMEM((3, 3, chans, chans), BF),
-            block,
-            block,
-            pltpu.SemaphoreType.DMA((11,)),
-        ],
-        flops=9 * work,
-        moved=5 << 20,
-        hbm=range(6),
+        (grad_top, grad_bottom, spatial_weight, edge, inner),
+        [pltpu.VMEM((frames, 2, COLS, chans), BF), pltpu.SemaphoreType.DMA((2 * frames,))],
+        flops=work,
+        moved=1 << 20,
+        hbm=(4,),
         out_hbm=True,
-        limit=58,
+        alias={4: 0},
     )
     wider = call(
         functools.partial(spread_sum_kernel, scale),

time: 118 us -> 117 us (level)
  starting transfers between devices: 40.4 us -> 37.3 us
  waiting for transfers between devices: 27.6 us -> 30.6 us
  local copies, waits for them, and re-layouts: 5.97 us -> 3.52 us
    ppermute x2 -> x1, waiting for transfers between devices: 0.01 us -> 3.84 us  [local(): ahead = lax.ppermute(dy, TM, steps(TM, -1))]
    all_to_all x3, starting transfers between devices: 16.5 us -> 14.4 us  [exchange(): return lax.all_to_all(value, axes, split_axis=0, concat_axis=0, tiled=True)]
    slice x1 -> x0, local copies, waits for them, and re-layouts: 1.96 us -> none  [local(): dy_0, later = lax.optimization_barrier((dy[0], dy))]
    ppermute x2 -> x1, starting transfers between devices: 2.57 us -> 1.29 us  [local(): ahead = lax.ppermute(dy, TM, steps(TM, -1))]
  transfers between devices with their start and end apart: 12 -> 11, of which waited for: 6 -> 7; matrix products, arithmetic and copies ran while one was open for 1% -> 1% of each run, Pallas kernels for 19% -> 18%
where the time goes in v7:
time: 117 us; the launch traced here: 116 us
  starting transfers between devices  37.3 us (32%)
  waiting for transfers between devices  30.6 us (26%)
  Pallas kernels  28.4 us (24%)
  blocking collectives  15.3 us (13%)
  local copies, waits for them, and re-layouts  3.52 us (3%)
    pallas_call x12, Pallas kernels, call(): pl.pallas_call(body, out_shape=outs, in_specs=specs, out_specs=placed if...  28.4 us
    all_to_all x3, waiting for transfers between devices, exchange(): return lax.all_to_all(value, axes, split_axis=0, concat_axis=0, tiled=True)  16.8 us
    all_to_all x1, blocking collectives, exchange(): return lax.all_to_all(value, axes, split_axis=0, concat_axis=0, tiled=True)  15.3 us
    all_to_all x3, starting transfers between devices, exchange(): return lax.all_to_all(value, axes, split_axis=0, concat_axis=0, tiled=True)  14.4 us
    ppermute x2, waiting for transfers between devices, swap_rims(): lax.ppermute(first, SPACE, steps(SPACE, -1))  9.26 us
    ppermute x2, starting transfers between devices, swap_rims(): lax.ppermute(last, SPACE, steps(SPACE, 1))  8.28 us
    ppermute x2, starting transfers between devices, swap_rims(): lax.ppermute(first, SPACE, steps(SPACE, -1))  3.86 us
    ppermute x1, waiting for transfers between devices, local(): ahead = lax.ppermute(dy, TM, steps(TM, -1))  3.84 us
  transfers between devices with their start and end apart: 11, of which 7 were waited for; matrix products, arithmetic and copies ran while one was open for 1% of the time, Pallas kernels for 18%

profile of v7, /device:TPU:1, one launch (start us, length us, event | category | flops | bytes accessed | tf_op | source)
XLA Modules:
  0.0 115.9 jit_solution(10169820097700085593)
XLA Ops:
  0.6 1.3 %collective-permute-start = (bf16[2,1024,256]{2,1,0:T(8,128)(2,1)}, bf16[2,1024,256]{2,1,0:T(8,128)(2,1)S(1)}, u32[]{:S(2)}, u32[]{:S(2)}) collective-permute-start(bf16[2,1024,256]{2,1,0:T(8,128)(2,1)} %bitcast.15), channel_id=1, source_target_pairs={{8,0},{16,8},{24,16},{32,24},{40,32},{48,40},{56,48},{64,56},{72,6... | collective-permute-start | bytes 3145736 | tf_op jit(solution)/shard_map/ppermute | solution.py:380
  2.9 4.5 %collective-permute-start.1 = (bf16[2,128,256]{2,1,0:T(8,128)(2,1)S(1)}, bf16[2,128,256]{2,1,0:T(8,128)(2,1)S(1)}, u32[]{:S(2)}, u32[]{:S(2)}) collective-permute-start(bf16[2,128,256]{2,1,0:T(8,128)(2,1)S(1)} %get-tuple-element.55), channel_id=1, source_target_pairs={{0,1},{1,2},{2,3},{3,4},{4,5},{5,6},{6,7},{8,9},{9,10},{10,11},{11... | collective-permute-start | bytes 393224 | tf_op jit(solution)/shard_map/ppermute | solution.py:369
  7.4 1.9 %collective-permute-start.2 = (bf16[2,128,256]{2,1,0:T(8,128)(2,1)S(1)}, bf16[2,128,256]{2,1,0:T(8,128)(2,1)S(1)}, u32[]{:S(2)}, u32[]{:S(2)}) collective-permute-start(bf16[2,128,256]{2,1,0:T(8,128)(2,1)S(1)} %get-tuple-element.54), channel_id=1, source_target_pairs={{1,0},{2,1},{3,2},{4,3},{5,4},{6,5},{7,6},{9,8},{10,9},{11,10},{12... | collective-permute-start | bytes 393224 | tf_op jit(solution)/shard_map/ppermute | solution.py:369
  9.4 4.6 %collective-permute-done.2.refs_2_ = bf16[2,128,256]{2,1,0:T(8,128)(2,1)S(1)} collective-permute-done((bf16[2,128,256]{2,1,0:T(8,128)(2,1)S(1)}, bf16[2,128,256]{2,1,0:T(8,128)(2,1)S(1)}, u32[]{:S(2)}, u32[]{:S(2)}) %collective-permute-start.2) | collective-permute-done | bytes 131104 | tf_op jit(solution)/shard_map/ppermute | solution.py:369
  15.3 1.3 %copy-done.3 = bf16[3,3,256,256]{3,2,1,0:T(8,128)(2,1)S(1)} copy-done((bf16[3,3,256,256]{3,2,1,0:T(8,128)(2,1)S(1)}, bf16[3,3,256,256]{3,2,1,0:T(8,128)(2,1)}, u32[]{:S(2)}) %copy-start.3) | copy-done | bytes 1179672
  16.5 4.4 %shard_map.75 = (bf16[2,1024,256]{2,1,0:T(8,128)(2,1)S(1)}, f32[2,1024,256]{2,1,0:T(8,128)S(1)}, bf16[2,256,1280]{2,1,0:T(8,128)(2,1)S(1)}, bf16[2,256,1024]{2,1,0:T(8,128)(2,1)S(1)}) custom-call(bf16[2,1024,256]{2,1,0:T(8,128)(2,1)S(1)} %bitcast.14, bf16[2,128,256]{2,1,0:T(8,128)(2,1)S(1)} %collective-permute-done.1.refs_1_, ...), custom_call_target="tpu_custom_call" | custom-call | flops 2415919104 | bytes 9437184 | tf_op jit(solution)/shard_map/pallas_call | solution.py:35
  20.9 1.4 %shard_map.76 = (f32[2,1024,256]{2,1,0:T(8,128)S(1)}, f32[2,256,256]{2,1,0:T(8,128)S(1)}) custom-call(bf16[2,1024,256]{2,1,0:T(8,128)(2,1)S(1)} %bitcast.17, bf16[3,256,256]{2,1,0:T(8,128)(2,1)S(1)} %copy-done.2, bf16[2,256,1024]{2,1,0:T(8,128)(2,1)S(1)} %get-tuple-element.31.refs_2_.refs_5_), custom_call_target="tpu_custom_call" | custom-call | flops 1610612736 | bytes 6291456 | tf_op jit(solution)/shard_map/pallas_call | solution.py:35
  22.3 3.8 %collective-permute-done.refs_1_ = bf16[2,1024,256]{2,1,0:T(8,128)(2,1)S(1)} collective-permute-done((bf16[2,1024,256]{2,1,0:T(8,128)(2,1)}, bf16[2,1024,256]{2,1,0:T(8,128)(2,1)S(1)}, u32[]{:S(2)}, u32[]{:S(2)}) %collective-permute-start) | collective-permute-done | bytes 1048608 | tf_op jit(solution)/shard_map/ppermute | solution.py:380
  26.2 4.4 %shard_map.77 = (bf16[2,1024,256]{2,1,0:T(8,128)(2,1)S(1)}, bf16[3072,128]{1,0:T(8,128)(2,1)S(1)}, bf16[3072,128]{1,0:T(8,128)(2,1)S(1)}, bf16[2,128,256]{2,1,0:T(8,128)(2,1)S(1)}, bf16[2,128,256]{2,1,0:T(8,128)(2,1)S(1)}) custom-call(s32[1]{0:T(128)} %bitcast.refs_0_, bf16[2,1024,256]{2,1,0:T(8,128)(2,1)S(1)} %collective-permute-done.refs_1_, ...), custom_call_target="tpu_custom_call" | custom-call | flops 16777216 | bytes 262144 | tf_op jit(solution)/shard_map/pallas_call | solution.py:35
  30.6 3.2 %collective-permute-start.3 = (bf16[3072,128]{1,0:T(8,128)(2,1)S(1)}, bf16[3072,128]{1,0:T(8,128)(2,1)S(1)}, u32[]{:S(2)}, u32[]{:S(2)}) collective-permute-start(bf16[3072,128]{1,0:T(8,128)(2,1)S(1)} %get-tuple-element.35), channel_id=1, source_target_pairs={{0,1},{1,0},{2,3},{3,2},{4,5},{5,4},{6,7},{7,6},{8,9},{9,8},{10,11... | collective-permute-start | bytes 2359304 | tf_op jit(solution)/shard_map/ppermute | solution.py:422
  33.8 3.6 %collective-permute-start.4 = (bf16[2,1024,256]{2,1,0:T(8,128)(2,1)S(1)}, bf16[2,1024,256]{2,1,0:T(8,128)(2,1)S(1)}, u32[]{:S(2)}, u32[]{:S(2)}) collective-permute-start(bf16[2,1024,256]{2,1,0:T(8,128)(2,1)S(1)} %get-tuple-element.39.refs_0_), channel_id=1, source_target_pairs={{0,8},{8,16},{16,24},{24,32},{32,40},{40,48},{48,56},{56,64},{64,7... | collective-permute-start | bytes 3145736 | tf_op jit(solution)/shard_map/ppermute | solution.py:402
  37.6 15.3 %all_to_all.20.refs_0_ = bf16[4,768,128]{2,1,0:T(8,128)(2,1)S(1)} all-to-all(bf16[4,768,128]{2,1,0:T(8,128)(2,1)S(1)} %bitcast.11), channel_id=1, replica_groups=mesh['clip'=2,'y'=4,'zl'=4,'x'=4,'core'=2] {'x'}, dimensions={0} | all-to-all | bytes 1572864 | tf_op jit(solution)/shard_map/all_to_all | solution.py:365
  53.7 4.8 %all-to-all-start.1 = ((bf16[4,192,128]{2,1,0:T(8,128)(2,1)}), bf16[4,192,128]{2,1,0:T(8,128)(2,1)S(1)}, u32[]{:S(2)}, u32[]{:S(2)}) async-start(bf16[4,192,128]{2,1,0:T(8,128)(2,1)} %bitcast.4), calls=%async_computation.1 | async-start | bytes 393216 | tf_op jit(solution)/shard_map/all_to_all | solution.py:365
  58.5 6.5 %shard_map.80 = (bf16[2,1024,256]{2,1,0:T(8,128)(2,1)}, f32[2,2,128,256]{3,2,1,0:T(8,128)}) custom-call(bf16[2,1024,256]{2,1,0:T(8,128)(2,1)} %copy-done.8, bf16[3,3,256,256]{3,2,1,0:T(8,128)(2,1)} %refs_2_.5, bf16[2,1024,256]{2,1,0:T(8,128)(2,1)} %bitcast.16), custom_call_target="tpu_custom_call" | custom-call | flops 2415919104 | bytes 5242880 | tf_op jit(solution)/shard_map/pallas_call | solution.py:35
  65.1 5.9 %all-to-all-done.1.refs_0_ = bf16[4,192,128]{2,1,0:T(8,128)(2,1)S(1)} async-done(((bf16[4,192,128]{2,1,0:T(8,128)(2,1)}), bf16[4,192,128]{2,1,0:T(8,128)(2,1)S(1)}, u32[]{:S(2)}, u32[]{:S(2)}) %all-to-all-start.1) | async-done | bytes 196640 | tf_op jit(solution)/shard_map/all_to_all | solution.py:365
  71.8 5.5 %all-to-all-start.2 = ((bf16[8,192,128]{2,1,0:T(8,128)(2,1)}), bf16[8,192,128]{2,1,0:T(8,128)(2,1)S(1)}, u32[]{:S(2)}, u32[]{:S(2)}) async-start(bf16[8,192,128]{2,1,0:T(8,128)(2,1)} %shard_map.81), calls=%async_computation.2 | async-start | bytes 786432 | tf_op jit(solution)/shard_map/all_to_all | solution.py:365
  77.3 3.8 %collective-permute-start.5 = (bf16[2,128,256]{2,1,0:T(8,128)(2,1)S(1)}, bf16[2,128,256]{2,1,0:T(8,128)(2,1)S(1)}, u32[]{:S(2)}, u32[]{:S(2)}) collective-permute-start(bf16[2,128,256]{2,1,0:T(8,128)(2,1)S(1)} %get-tuple-element.40), channel_id=1, source_target_pairs={{0,1},{1,2},{2,3},{3,4},{4,5},{5,6},{6,7},{8,9},{9,10},{10,11},{11... | collective-permute-start | bytes 393224 | tf_op jit(solution)/shard_map/ppermute | solution.py:369
  81.0 1.9 %collective-permute-start.6 = (bf16[2,128,256]{2,1,0:T(8,128)(2,1)S(1)}, bf16[2,128,256]{2,1,0:T(8,128)(2,1)S(1)}, u32[]{:S(2)}, u32[]{:S(2)}) collective-permute-start(bf16[2,128,256]{2,1,0:T(8,128)(2,1)S(1)} %get-tuple-element.41), channel_id=1, source_target_pairs={{1,0},{2,1},{3,2},{4,3},{5,4},{6,5},{7,6},{9,8},{10,9},{11,10},{12... | collective-permute-start | bytes 393224 | tf_op jit(solution)/shard_map/ppermute | solution.py:369
  83.0 4.6 %collective-permute-done.6.refs_1_ = bf16[2,128,256]{2,1,0:T(8,128)(2,1)S(1)} collective-permute-done((bf16[2,128,256]{2,1,0:T(8,128)(2,1)S(1)}, bf16[2,128,256]{2,1,0:T(8,128)(2,1)S(1)}, u32[]{:S(2)}, u32[]{:S(2)}) %collective-permute-start.6) | collective-permute-done | bytes 131104 | tf_op jit(solution)/shard_map/ppermute | solution.py:369
  87.6 4.7 %all-to-all-done.2.refs_0_ = bf16[8,192,128]{2,1,0:T(8,128)(2,1)S(1)} async-done(((bf16[8,192,128]{2,1,0:T(8,128)(2,1)}), bf16[8,192,128]{2,1,0:T(8,128)(2,1)S(1)}, u32[]{:S(2)}, u32[]{:S(2)}) %all-to-all-start.2) | async-done | bytes 393248 | tf_op jit(solution)/shard_map/all_to_all | solution.py:365
  93.3 4.1 %all-to-all-start.3 = ((bf16[16,192,128]{2,1,0:T(8,128)(2,1)}), bf16[16,192,128]{2,1,0:T(8,128)(2,1)S(1)}, u32[]{:S(2)}, u32[]{:S(2)}) async-start(bf16[16,192,128]{2,1,0:T(8,128)(2,1)} %shard_map.82), calls=%async_computation.3 | async-start | bytes 1572864 | tf_op jit(solution)/shard_map/all_to_all | solution.py:365
  97.5 5.4 %shard_map.83 = bf16[2,1024,256]{2,1,0:T(8,128)(2,1)} custom-call(bf16[2,1024,256]{2,1,0:T(8,128)(2,1)} %copy-done.5, bf16[2,1024,256]{2,1,0:T(8,128)(2,1)} %copy-done, bf16[3,256,256]{2,1,0:T(8,128)(2,1)} %refs_2_.4, bf16[2,1024,256]{2,1,0:T(8,128)(2,1)} %bitcast.13), custom_call_target="tpu_custom_call" | custom-call | flops 805306368 | bytes 4194304 | tf_op jit(solution)/shard_map/pallas_call | solution.py:35
  104.0 6.2 %all-to-all-done.3 = bf16[16,192,128]{2,1,0:T(8,128)(2,1)S(1)} async-done(((bf16[16,192,128]{2,1,0:T(8,128)(2,1)}), bf16[16,192,128]{2,1,0:T(8,128)(2,1)S(1)}, u32[]{:S(2)}, u32[]{:S(2)}) %all-to-all-start.3) | async-done | bytes 786464 | tf_op jit(solution)/shard_map/all_to_all | solution.py:365
  110.2 2.6 %collective-permute-start.7 = (bf16[3072,128]{1,0:T(8,128)(2,1)S(1)}, bf16[3072,128]{1,0:T(8,128)(2,1)S(1)}, u32[]{:S(2)}, u32[]{:S(2)}) collective-permute-start(bf16[3072,128]{1,0:T(8,128)(2,1)S(1)} %bitcast.9), channel_id=1, source_target_pairs={{0,1},{1,0},{2,3},{3,2},{4,5},{5,4},{6,7},{7,6},{8,9},{9,8},{10,11... | collective-permute-start | bytes 2359304 | tf_op jit(solution)/shard_map/ppermute | solution.py:493
  (30 shorter events, 9.2 us)
Async XLA Ops:
  0.6 25.5 %collective-permute-start = (bf16[2,1024,256]{2,1,0:T(8,128)(2,1)}, bf16[2,1024,256]{2,1,0:T(8,128)(2,1)S(1)}, u32[]{:S(2)}, u32[]{:S(2)}) collective-permute-start(bf16[2,1024,256]{2,1,0:T(8,128)(2,1)} %bitcast.15), channel_id=1, source_target_pairs={{8,0},{16,8},{24,16},{32,24},{40,32},{48,40},{56,48},{64,56},{72,6... | collective-permute-start | bytes 3145736 | tf_op jit(solution)/shard_map/ppermute | solution.py:380
  2.9 6.5 %collective-permute-start.1 = (bf16[2,128,256]{2,1,0:T(8,128)(2,1)S(1)}, bf16[2,128,256]{2,1,0:T(8,128)(2,1)S(1)}, u32[]{:S(2)}, u32[]{:S(2)}) collective-permute-start(bf16[2,128,256]{2,1,0:T(8,128)(2,1)S(1)} %get-tuple-element.55), channel_id=1, source_target_pairs={{0,1},{1,2},{2,3},{3,4},{4,5},{5,6},{6,7},{8,9},{9,10},{10,11},{11... | collective-permute-start | bytes 393224 | tf_op jit(solution)/shard_map/ppermute | solution.py:369
  7.4 6.6 %collective-permute-start.2 = (bf16[2,128,256]{2,1,0:T(8,128)(2,1)S(1)}, bf16[2,128,256]{2,1,0:T(8,128)(2,1)S(1)}, u32[]{:S(2)}, u32[]{:S(2)}) collective-permute-start(bf16[2,128,256]{2,1,0:T(8,128)(2,1)S(1)} %get-tuple-element.54), channel_id=1, source_target_pairs={{1,0},{2,1},{3,2},{4,3},{5,4},{6,5},{7,6},{9,8},{10,9},{11,10},{12... | collective-permute-start | bytes 393224 | tf_op jit(solution)/shard_map/ppermute | solution.py:369
  14.0 1.2 %copy-start.1 = (bf16[1,2,8,128,256]{4,3,2,1,0:T(8,128)(2,1)S(1)}, bf16[1,2,8,128,256]{4,3,2,1,0:T(8,128)(2,1)}, u32[]{:S(2)}) copy-start(bf16[1,2,8,128,256]{4,3,2,1,0:T(8,128)(2,1)} %param.4) | copy-start | bytes 3145732
  15.3 1.3 %copy-start.3 = (bf16[3,3,256,256]{3,2,1,0:T(8,128)(2,1)S(1)}, bf16[3,3,256,256]{3,2,1,0:T(8,128)(2,1)}, u32[]{:S(2)}) copy-start(bf16[3,3,256,256]{3,2,1,0:T(8,128)(2,1)} %refs_2_.5) | copy-start | bytes 3538948
  16.5 4.4 %copy-start.2 = (bf16[3,256,256]{2,1,0:T(8,128)(2,1)S(1)}, bf16[3,256,256]{2,1,0:T(8,128)(2,1)}, u32[]{:S(2)}) copy-start(bf16[3,256,256]{2,1,0:T(8,128)(2,1)} %refs_2_.4) | copy-start | bytes 1179652
  16.5 4.4 %copy-start.7 = (bf16[1,2,8,128,256]{4,3,2,1,0:T(8,128)(2,1)S(1)}, bf16[1,2,8,128,256]{4,3,2,1,0:T(8,128)(2,1)}, u32[]{:S(2)}) copy-start(bf16[1,2,8,128,256]{4,3,2,1,0:T(8,128)(2,1)} %param.5) | copy-start | bytes 3145732
  20.9 12.9 %copy-start.5 = (bf16[2,1024,256]{2,1,0:T(8,128)(2,1)}, bf16[2,1024,256]{2,1,0:T(8,128)(2,1)S(1)}, u32[]{:S(2)}) copy-start(bf16[2,1024,256]{2,1,0:T(8,128)(2,1)S(1)} %get-tuple-element.39.refs_0_) | copy-start | bytes 3145732
  30.6 23.1 %copy-start.8 = (bf16[2,1024,256]{2,1,0:T(8,128)(2,1)}, bf16[2,1024,256]{2,1,0:T(8,128)(2,1)S(1)}, u32[]{:S(2)}) copy-start(bf16[2,1024,256]{2,1,0:T(8,128)(2,1)S(1)} %get-tuple-element.36.refs_0_) | copy-start | bytes 3145732
  30.6 6.8 %collective-permute-start.3 = (bf16[3072,128]{1,0:T(8,128)(2,1)S(1)}, bf16[3072,128]{1,0:T(8,128)(2,1)S(1)}, u32[]{:S(2)}, u32[]{:S(2)}) collective-permute-start(bf16[3072,128]{1,0:T(8,128)(2,1)S(1)} %get-tuple-element.35), channel_id=1, source_target_pairs={{0,1},{1,0},{2,3},{3,2},{4,5},{5,4},{6,7},{7,6},{8,9},{9,8},{10,11... | collective-permute-start | bytes 2359304 | tf_op jit(solution)/shard_map/ppermute | solution.py:422
  33.8 37.1 %collective-permute-start.4 = (bf16[2,1024,256]{2,1,0:T(8,128)(2,1)S(1)}, bf16[2,1024,256]{2,1,0:T(8,128)(2,1)S(1)}, u32[]{:S(2)}, u32[]{:S(2)}) collective-permute-start(bf16[2,1024,256]{2,1,0:T(8,128)(2,1)S(1)} %get-tuple-element.39.refs_0_), channel_id=1, source_target_pairs={{0,8},{8,16},{16,24},{24,32},{32,40},{40,48},{48,56},{56,64},{64,7... | collective-permute-start | bytes 3145736 | tf_op jit(solution)/shard_map/ppermute | solution.py:402
  53.7 17.2 %all-to-all-start.1 = ((bf16[4,192,128]{2,1,0:T(8,128)(2,1)}), bf16[4,192,128]{2,1,0:T(8,128)(2,1)S(1)}, u32[]{:S(2)}, u32[]{:S(2)}) async-start(bf16[4,192,128]{2,1,0:T(8,128)(2,1)} %bitcast.4), calls=%async_computation.1 | async-start | bytes 393216 | tf_op jit(solution)/shard_map/all_to_all | solution.py:365
  70.9 22.4 %copy-start = (bf16[2,1024,256]{2,1,0:T(8,128)(2,1)}, bf16[2,1024,256]{2,1,0:T(8,128)(2,1)S(1)}, u32[]{:S(2)}) copy-start(bf16[2,1024,256]{2,1,0:T(8,128)(2,1)S(1)} %collective-permute-done.4.refs_1_) | copy-start | bytes 3145732
  71.8 20.6 %all-to-all-start.2 = ((bf16[8,192,128]{2,1,0:T(8,128)(2,1)}), bf16[8,192,128]{2,1,0:T(8,128)(2,1)S(1)}, u32[]{:S(2)}, u32[]{:S(2)}) async-start(bf16[8,192,128]{2,1,0:T(8,128)(2,1)} %shard_map.81), calls=%async_computation.2 | async-start | bytes 786432 | tf_op jit(solution)/shard_map/all_to_all | solution.py:365
  77.3 5.7 %collective-permute-start.5 = (bf16[2,128,256]{2,1,0:T(8,128)(2,1)S(1)}, bf16[2,128,256]{2,1,0:T(8,128)(2,1)S(1)}, u32[]{:S(2)}, u32[]{:S(2)}) collective-permute-start(bf16[2,128,256]{2,1,0:T(8,128)(2,1)S(1)} %get-tuple-element.40), channel_id=1, source_target_pairs={{0,1},{1,2},{2,3},{3,4},{4,5},{5,6},{6,7},{8,9},{9,10},{10,11},{11... | collective-permute-start | bytes 393224 | tf_op jit(solution)/shard_map/ppermute | solution.py:369
  81.0 6.6 %collective-permute-start.6 = (bf16[2,128,256]{2,1,0:T(8,128)(2,1)S(1)}, bf16[2,128,256]{2,1,0:T(8,128)(2,1)S(1)}, u32[]{:S(2)}, u32[]{:S(2)}) collective-permute-start(bf16[2,128,256]{2,1,0:T(8,128)(2,1)S(1)} %get-tuple-element.41), channel_id=1, source_target_pairs={{1,0},{2,1},{3,2},{4,3},{5,4},{6,5},{7,6},{9,8},{10,9},{11,10},{12... | collective-permute-start | bytes 393224 | tf_op jit(solution)/shard_map/ppermute | solution.py:369
  93.3 16.9 %all-to-all-start.3 = ((bf16[16,192,128]{2,1,0:T(8,128)(2,1)}), bf16[16,192,128]{2,1,0:T(8,128)(2,1)S(1)}, u32[]{:S(2)}, u32[]{:S(2)}) async-start(bf16[16,192,128]{2,1,0:T(8,128)(2,1)} %shard_map.82), calls=%async_computation.3 | async-start | bytes 1572864 | tf_op jit(solution)/shard_map/all_to_all | solution.py:365
  97.4 5.5 %copy-start.4 = (bf16[3,3,256,256]{3,2,1,0:T(8,128)(2,1)S(1)}, bf16[3,3,256,256]{3,2,1,0:T(8,128)(2,1)}, u32[]{:S(2)}) copy-start(bf16[3,3,256,256]{3,2,1,0:T(8,128)(2,1)} %refs_2_.5) | copy-start | bytes 3538948
  97.5 5.5 %copy-start.6 = (f32[2,2,128,256]{3,2,1,0:T(8,128)S(1)}, f32[2,2,128,256]{3,2,1,0:T(8,128)}, u32[]{:S(2)}) copy-start(f32[2,2,128,256]{3,2,1,0:T(8,128)} %get-tuple-element.45.refs_3_) | copy-start | bytes 1572868
  110.2 4.5 %collective-permute-start.7 = (bf16[3072,128]{1,0:T(8,128)(2,1)S(1)}, bf16[3072,128]{1,0:T(8,128)(2,1)S(1)}, u32[]{:S(2)}, u32[]{:S(2)}) collective-permute-start(bf16[3072,128]{1,0:T(8,128)(2,1)S(1)} %bitcast.9), channel_id=1, source_target_pairs={{0,1},{1,0},{2,3},{3,2},{4,5},{5,4},{6,7},{7,6},{8,9},{9,8},{10,11... | collective-permute-start | bytes 2359304 | tf_op jit(solution)/shard_map/ppermute | solution.py:493

commit v8 on v7

--- a/solution.py
+++ b/solution.py
@@ -64,6 +64,7 @@
 
 
 CHUNK = 512
+SWAPS = 4
 
 
 def fill(padded, block, top, bottom, frame):
@@ -143,13 +144,11 @@
     early,
     pgrad,
     keep,
-    send,
     last,
     first,
-    wide,
-    terms,
-    sems,
+    *rest,
 ):
+    *sends, wide, terms, sems = rest
     frames, size, chans = ahead.shape
 
     @pl.loop(0, size // CHUNK)
@@ -193,14 +192,21 @@
         @pl.when(core[0] == c)
         def _():
             keep[...] = terms[c * half : (c + 1) * half, :]
-            send[...] = terms[(1 - c) * half : (2 - c) * half, :]
+            cut = sends[0].shape[0]
+            for n, send in enumerate(sends):
+                at = (1 - c) * half + n * cut
+                send[...] = terms[at : at + cut, :]
 
     for store in stores:
         store.wait()
 
 
-def add_kernel(a, b, out):
-    out[...] = (a[...].astype(F32) + b[...].astype(F32)).astype(BF)
+def add_kernel(a, *refs):
+    out = refs[-1]
+    cut = refs[0].shape[0]
+    for n, b in enumerate(refs[:-1]):
+        rows = pl.ds(n * cut, cut)
+        out[rows, :] = (a[rows, :].astype(F32) + b[...].astype(F32)).astype(BF)
 
 
 def sum_kernel(parts, out):
@@ -399,35 +405,34 @@
         flops=6 * work,
         moved=6 << 20,
     )
+    act, ahead = lax.optimization_barrier((act, ahead))
     behind = lax.ppermute(act, TM, steps(TM, 1))
     flat = frames * size
     rows = 12 * chans
     edges = shape((frames, COLS, chans))
-    pgrad, keep, send, last, first = call(
+    pgrad, keep, last, first, *send = call(
         gradient_kernel,
-        [shape((frames, size, chans)), shape((rows, 128)), shape((rows, 128)), edges, edges],
+        [shape((frames, size, chans)), shape((rows, 128)), edges, edges]
+        + [shape((rows // SWAPS, 128))] * SWAPS,
         (core, ahead, temporal_weight, slope, x_t, act_t, partial, early),
         [
             pltpu.VMEM((3, flat, chans), BF),
             pltpu.VMEM((2 * rows, 128), BF),
             pltpu.SemaphoreType.DMA((frames,)),
         ],
-        flops=work // 16,
-        moved=1 << 18,
+        flops=1 << 10,
+        moved=1 << 12,
         smem=(0,),
         out_hbm=(0,),
     )
     grad_top, grad_bottom = swap_rims(last, first)
     pair = [(0, 1), (1, 0)]
-    got = lax.ppermute(send, "core", pair)
-    half = call(add_kernel, shape((rows, 128)), (keep, got), moved=3 << 20)
+    got = [lax.ppermute(part, "core", pair) for part in send]
+    half = call(add_kernel, shape((rows, 128)), (keep, *got), moved=1 << 12)
     block = pltpu.VMEM((frames, size, chans), BF)
-    line, rank = lax.axis_size("x"), lax.axis_size("y")
     column, plane = lax.axis_size(COLUMN), lax.axis_size(PLANE)
-    share = rows // line
-    first = exchange(half.reshape(line, share, 128), "x")
-    part = call(sum_kernel, shape((share, 128)), (first,), moved=1 << 18)
-    second = exchange(part.reshape(rank, share // rank, 128), "y")
+    share = rows // plane
+    first = exchange(half.reshape(plane, share, 128), PLANE)
     inner, edge = call(
         back_kernel,
         [shape((frames, size, chans)), shape((frames, 2, COLS, chans), F32)],
@@ -445,12 +450,12 @@
         out_hbm=(0,),
         limit=58,
     )
-    second, edge = lax.optimization_barrier((second, edge))
+    first, edge = lax.optimization_barrier((first, edge))
     spread = call(
         functools.partial(spread_sum_kernel, 1.0),
-        shape((column, share // rank, 128)),
-        (second,),
-        moved=1 << 18,
+        shape((column, share, 128)),
+        (first,),
+        moved=1 << 12,
         after=(behind,),
     )
     third = exchange(spread, COLUMN)
@@ -484,9 +489,9 @@
     )
     wider = call(
         functools.partial(spread_sum_kernel, scale),
-        shape((plane, share // rank, 128)),
+        shape((plane, share, 128)),
         (third,),
-        moved=1 << 18,
+        moved=1 << 12,
     )
     own = exchange(wider, PLANE).reshape(rows, 128)
     own, block_out, input_grad = lax.optimization_barrier((own, block_out, input_grad))

time: 117 us -> 117 us (level)
  blocking collectives: 15.3 us -> 0 us
  waiting for transfers between devices: 30.6 us -> 41 us
  starting transfers between devices: 37.3 us -> 42 us
    all_to_all x1 -> x0, blocking collectives: 15.3 us -> none  [exchange(): return lax.all_to_all(value, axes, split_axis=0, concat_axis=0, tiled=True)]
    all_to_all x3, waiting for transfers between devices: 16.8 us -> 24.9 us  [exchange(): return lax.all_to_all(value, axes, split_axis=0, concat_axis=0, tiled=True)]
    all_to_all x3, starting transfers between devices: 14.4 us -> 18.1 us  [exchange(): return lax.all_to_all(value, axes, split_axis=0, concat_axis=0, tiled=True)]
    ppermute x1, starting transfers between devices: 3.59 us -> 5.41 us  [local(): behind = lax.ppermute(act, TM, steps(TM, 1))]
    ppermute x1 -> x4, waiting for transfers between devices: 0.01 us -> 1.39 us  [local(): got = [lax.ppermute(part, 'core', pair) for part in send]]
    ppermute x1 -> x4, starting transfers between devices: 3.22 us -> 2.31 us  [local(): got = [lax.ppermute(part, 'core', pair) for part in send]]
    pallas_call x12 -> x11, Pallas kernels: 28.4 us -> 29.2 us  [call(): pl.pallas_call(body, out_shape=outs, in_specs=specs, out_specs=placed if...]
    unnamed x18 -> x16, local copies, waits for them, and re-layouts: 2.53 us -> 2.52 us
  transfers between devices with their start and end apart: 11 -> 14, of which waited for: 7 -> 11; matrix products, arithmetic and copies ran while one was open for 1% -> 1% of each run, Pallas kernels for 18% -> 22%
where the time goes in v8:
time: 117 us
  starting transfers between devices  42 us (36%)
  waiting for transfers between devices  41 us (35%)
  Pallas kernels  29.2 us (25%)
  local copies, waits for them, and re-layouts  3.52 us (3%)
    pallas_call x11, Pallas kernels, call(): pl.pallas_call(body, out_shape=outs, in_specs=specs, out_specs=placed if...  29.2 us
    all_to_all x3, waiting for transfers between devices, exchange(): return lax.all_to_all(value, axes, split_axis=0, concat_axis=0, tiled=True)  24.9 us
    all_to_all x3, starting transfers between devices, exchange(): return lax.all_to_all(value, axes, split_axis=0, concat_axis=0, tiled=True)  18.1 us
    ppermute x2, waiting for transfers between devices, swap_rims(): lax.ppermute(first, SPACE, steps(SPACE, -1))  9.26 us
    ppermute x2, starting transfers between devices, swap_rims(): lax.ppermute(last, SPACE, steps(SPACE, 1))  8.37 us
    ppermute x1, starting transfers between devices, local(): behind = lax.ppermute(act, TM, steps(TM, 1))  5.41 us
    ppermute x1, waiting for transfers between devices, local(): ahead = lax.ppermute(dy, TM, steps(TM, -1))  4.72 us
    ppermute x2, starting transfers between devices, swap_rims(): lax.ppermute(first, SPACE, steps(SPACE, -1))  3.86 us
  transfers between devices with their start and end apart: 14, of which 11 were waited for; matrix products, arithmetic and copies ran while one was open for 1% of the time, Pallas kernels for 22%

profile of v8, /device:TPU:1, one launch (start us, length us, event | category | flops | bytes accessed | tf_op | source)
XLA Modules:
  0.0 116.6 jit_solution(16382749218374521379)
XLA Ops:
  0.6 1.3 %collective-permute-start.2 = (bf16[2,1024,256]{2,1,0:T(8,128)(2,1)}, bf16[2,1024,256]{2,1,0:T(8,128)(2,1)S(1)}, u32[]{:S(2)}, u32[]{:S(2)}) collective-permute-start(bf16[2,1024,256]{2,1,0:T(8,128)(2,1)} %bitcast.13), channel_id=1, source_target_pairs={{8,0},{16,8},{24,16},{32,24},{40,32},{48,40},{56,48},{64,56},{72,6... | collective-permute-start | bytes 3145736 | tf_op jit(solution)/shard_map/ppermute | solution.py:386
  2.9 4.5 %collective-permute-start = (bf16[2,128,256]{2,1,0:T(8,128)(2,1)S(1)}, bf16[2,128,256]{2,1,0:T(8,128)(2,1)S(1)}, u32[]{:S(2)}, u32[]{:S(2)}) collective-permute-start(bf16[2,128,256]{2,1,0:T(8,128)(2,1)S(1)} %get-tuple-element.65), channel_id=1, source_target_pairs={{0,1},{1,2},{2,3},{3,4},{4,5},{5,6},{6,7},{8,9},{9,10},{10,11},{11... | collective-permute-start | bytes 393224 | tf_op jit(solution)/shard_map/ppermute | solution.py:375
  7.4 1.9 %collective-permute-start.1 = (bf16[2,128,256]{2,1,0:T(8,128)(2,1)S(1)}, bf16[2,128,256]{2,1,0:T(8,128)(2,1)S(1)}, u32[]{:S(2)}, u32[]{:S(2)}) collective-permute-start(bf16[2,128,256]{2,1,0:T(8,128)(2,1)S(1)} %get-tuple-element.64), channel_id=1, source_target_pairs={{1,0},{2,1},{3,2},{4,3},{5,4},{6,5},{7,6},{9,8},{10,9},{11,10},{12... | collective-permute-start | bytes 393224 | tf_op jit(solution)/shard_map/ppermute | solution.py:375
  9.4 4.6 %collective-permute-done.1.refs_2_ = bf16[2,128,256]{2,1,0:T(8,128)(2,1)S(1)} collective-permute-done((bf16[2,128,256]{2,1,0:T(8,128)(2,1)S(1)}, bf16[2,128,256]{2,1,0:T(8,128)(2,1)S(1)}, u32[]{:S(2)}, u32[]{:S(2)}) %collective-permute-start.1) | collective-permute-done | bytes 131104 | tf_op jit(solution)/shard_map/ppermute | solution.py:375
  14.0 1.2 %copy-done.1 = bf16[1,2,8,128,256]{4,3,2,1,0:T(8,128)(2,1)S(1)} copy-done((bf16[1,2,8,128,256]{4,3,2,1,0:T(8,128)(2,1)S(1)}, bf16[1,2,8,128,256]{4,3,2,1,0:T(8,128)(2,1)}, u32[]{:S(2)}) %copy-start.1) | copy-done | bytes 1048600
  15.3 1.3 %copy-done.3 = bf16[3,3,256,256]{3,2,1,0:T(8,128)(2,1)S(1)} copy-done((bf16[3,3,256,256]{3,2,1,0:T(8,128)(2,1)S(1)}, bf16[3,3,256,256]{3,2,1,0:T(8,128)(2,1)}, u32[]{:S(2)}) %copy-start.3) | copy-done | bytes 1179672
  16.5 4.9 %shard_map.75 = (bf16[2,1024,256]{2,1,0:T(8,128)(2,1)}, f32[2,1024,256]{2,1,0:T(8,128)S(1)}, bf16[2,256,1280]{2,1,0:T(8,128)(2,1)S(1)}, bf16[2,256,1024]{2,1,0:T(8,128)(2,1)S(1)}) custom-call(bf16[2,1024,256]{2,1,0:T(8,128)(2,1)S(1)} %bitcast.12, bf16[2,128,256]{2,1,0:T(8,128)(2,1)S(1)} %collective-permute-done.refs_1_, ...), custom_call_target="tpu_custom_call" | custom-call | flops 2415919104 | bytes 9437184 | tf_op jit(solution)/shard_map/pallas_call | solution.py:35
  21.5 4.7 %collective-permute-done.2.refs_1_ = bf16[2,1024,256]{2,1,0:T(8,128)(2,1)S(1)} collective-permute-done((bf16[2,1024,256]{2,1,0:T(8,128)(2,1)}, bf16[2,1024,256]{2,1,0:T(8,128)(2,1)S(1)}, u32[]{:S(2)}, u32[]{:S(2)}) %collective-permute-start.2) | collective-permute-done | bytes 1048608 | tf_op jit(solution)/shard_map/ppermute | solution.py:386
  26.2 5.4 %collective-permute-start.7 = (bf16[2,1024,256]{2,1,0:T(8,128)(2,1)}, bf16[2,1024,256]{2,1,0:T(8,128)(2,1)S(1)}, u32[]{:S(2)}, u32[]{:S(2)}) collective-permute-start(bf16[2,1024,256]{2,1,0:T(8,128)(2,1)} %get-tuple-element.49.refs_0_), channel_id=1, source_target_pairs={{0,8},{8,16},{16,24},{24,32},{32,40},{40,48},{48,56},{56,64},{64,7... | collective-permute-start | bytes 3145736 | tf_op jit(solution)/shard_map/ppermute | solution.py:409
  31.6 1.4 %shard_map.76 = (f32[2,1024,256]{2,1,0:T(8,128)S(1)}, f32[2,256,256]{2,1,0:T(8,128)S(1)}) custom-call(bf16[2,1024,256]{2,1,0:T(8,128)(2,1)S(1)} %bitcast.15, bf16[3,256,256]{2,1,0:T(8,128)(2,1)S(1)} %copy-done.2, bf16[2,256,1024]{2,1,0:T(8,128)(2,1)S(1)} %get-tuple-element.38.refs_2_.refs_5_), custom_call_target="tpu_custom_call" | custom-call | flops 1610612736 | bytes 6291456 | tf_op jit(solution)/shard_map/pallas_call | solution.py:35
  33.0 4.4 %shard_map.77 = (bf16[2,1024,256]{2,1,0:T(8,128)(2,1)S(1)}, bf16[3072,128]{1,0:T(8,128)(2,1)S(1)}, bf16[2,128,256]{2,1,0:T(8,128)(2,1)S(1)}, bf16[2,128,256]{2,1...) custom-call(s32[1]{0:T(128)} %bitcast.refs_0_, ...), custom_call_target="tpu_custom_call" | custom-call | flops 1024 | bytes 4096 | tf_op jit(solution)/shard_map/pallas_call | solution.py:35
  37.4 1.7 %collective-permute-start.3 = (bf16[768,128]{1,0:T(8,128)(2,1)S(1)}, bf16[768,128]{1,0:T(8,128)(2,1)S(1)}, u32[]{:S(2)}, u32[]{:S(2)}) collective-permute-start(bf16[768,128]{1,0:T(8,128)(2,1)S(1)} %get-tuple-element.42), channel_id=1, source_target_pairs={{0,1},{1,0},{2,3},{3,2},{4,5},{5,4},{6,7},{7,6},{8,9},{9,8},{10,11... | collective-permute-start | bytes 589832 | tf_op jit(solution)/shard_map/ppermute | solution.py:430
  42.2 6.9 %all-to-all-start = ((bf16[16,192,128]{2,1,0:T(8,128)(2,1)}), bf16[16,192,128]{2,1,0:T(8,128)(2,1)S(1)}, u32[]{:S(2)}, u32[]{:S(2)}) async-start(bf16[16,192,128]{2,1,0:T(8,128)(2,1)} %bitcast.3), calls=%async_computation | async-start | bytes 1572864 | tf_op jit(solution)/shard_map/all_to_all | solution.py:371
  49.0 6.5 %shard_map.79 = (bf16[2,1024,256]{2,1,0:T(8,128)(2,1)}, f32[2,2,128,256]{3,2,1,0:T(8,128)}) custom-call(bf16[2,1024,256]{2,1,0:T(8,128)(2,1)} %copy-done.7, bf16[3,3,256,256]{3,2,1,0:T(8,128)(2,1)} %refs_2_.5, bf16[2,1024,256]{2,1,0:T(8,128)(2,1)} %bitcast.14), custom_call_target="tpu_custom_call" | custom-call | flops 2415919104 | bytes 5242880 | tf_op jit(solution)/shard_map/pallas_call | solution.py:35
  55.6 14.8 %all-to-all-done.refs_0_ = bf16[16,192,128]{2,1,0:T(8,128)(2,1)S(1)} async-done(((bf16[16,192,128]{2,1,0:T(8,128)(2,1)}), bf16[16,192,128]{2,1,0:T(8,128)(2,1)S(1)}, u32[]{:S(2)}, u32[]{:S(2)}) %all-to-all-start) | async-done | bytes 786464 | tf_op jit(solution)/shard_map/all_to_all | solution.py:371
  71.3 5.5 %all-to-all-start.1 = ((bf16[8,192,128]{2,1,0:T(8,128)(2,1)}), bf16[8,192,128]{2,1,0:T(8,128)(2,1)S(1)}, u32[]{:S(2)}, u32[]{:S(2)}) async-start(bf16[8,192,128]{2,1,0:T(8,128)(2,1)} %shard_map.80), calls=%async_computation.1 | async-start | bytes 786432 | tf_op jit(solution)/shard_map/all_to_all | solution.py:371
  76.8 3.9 %collective-permute-start.8 = (bf16[2,128,256]{2,1,0:T(8,128)(2,1)S(1)}, bf16[2,128,256]{2,1,0:T(8,128)(2,1)S(1)}, u32[]{:S(2)}, u32[]{:S(2)}) collective-permute-start(bf16[2,128,256]{2,1,0:T(8,128)(2,1)S(1)} %get-tuple-element.50), channel_id=1, source_target_pairs={{0,1},{1,2},{2,3},{3,4},{4,5},{5,6},{6,7},{8,9},{9,10},{10,11},{11... | collective-permute-start | bytes 393224 | tf_op jit(solution)/shard_map/ppermute | solution.py:375
  80.7 1.9 %collective-permute-start.9 = (bf16[2,128,256]{2,1,0:T(8,128)(2,1)S(1)}, bf16[2,128,256]{2,1,0:T(8,128)(2,1)S(1)}, u32[]{:S(2)}, u32[]{:S(2)}) collective-permute-start(bf16[2,128,256]{2,1,0:T(8,128)(2,1)S(1)} %get-tuple-element.51), channel_id=1, source_target_pairs={{1,0},{2,1},{3,2},{4,3},{5,4},{6,5},{7,6},{9,8},{10,9},{11,10},{12... | collective-permute-start | bytes 393224 | tf_op jit(solution)/shard_map/ppermute | solution.py:375
  82.6 4.6 %collective-permute-done.9.refs_1_ = bf16[2,128,256]{2,1,0:T(8,128)(2,1)S(1)} collective-permute-done((bf16[2,128,256]{2,1,0:T(8,128)(2,1)S(1)}, bf16[2,128,256]{2,1,0:T(8,128)(2,1)S(1)}, u32[]{:S(2)}, u32[]{:S(2)}) %collective-permute-start.9) | collective-permute-done | bytes 131104 | tf_op jit(solution)/shard_map/ppermute | solution.py:375
  87.3 4.0 %all-to-all-done.1.refs_0_ = bf16[8,192,128]{2,1,0:T(8,128)(2,1)S(1)} async-done(((bf16[8,192,128]{2,1,0:T(8,128)(2,1)}), bf16[8,192,128]{2,1,0:T(8,128)(2,1)S(1)}, u32[]{:S(2)}, u32[]{:S(2)}) %all-to-all-start.1) | async-done | bytes 393248 | tf_op jit(solution)/shard_map/all_to_all | solution.py:371
  92.3 5.8 %all-to-all-start.2 = ((bf16[16,192,128]{2,1,0:T(8,128)(2,1)}), bf16[16,192,128]{2,1,0:T(8,128)(2,1)S(1)}, u32[]{:S(2)}, u32[]{:S(2)}) async-start(bf16[16,192,128]{2,1,0:T(8,128)(2,1)} %shard_map.81), calls=%async_computation.2 | async-start | bytes 1572864 | tf_op jit(solution)/shard_map/all_to_all | solution.py:371
  98.1 5.4 %shard_map.82 = bf16[2,1024,256]{2,1,0:T(8,128)(2,1)} custom-call(bf16[2,1024,256]{2,1,0:T(8,128)(2,1)} %get-tuple-element.49.refs_0_, bf16[2,1024,256]{2,1,0:T(8,128)(2,1)} %copy-done, bf16[3,256,256]{2,1,0:T(8,128)(2,1)} %refs_2_.4, bf16[2,1024,256]{2,1,0:T(8,128)(2,1)} %bitcast.11), custom_call_target="tpu_custom_call" | custom-call | flops 805306368 | bytes 4194304 | tf_op jit(solution)/shard_map/pallas_call | solution.py:35
  104.7 6.2 %all-to-all-done.2 = bf16[16,192,128]{2,1,0:T(8,128)(2,1)S(1)} async-done(((bf16[16,192,128]{2,1,0:T(8,128)(2,1)}), bf16[16,192,128]{2,1,0:T(8,128)(2,1)S(1)}, u32[]{:S(2)}, u32[]{:S(2)}) %all-to-all-start.2) | async-done | bytes 786464 | tf_op jit(solution)/shard_map/all_to_all | solution.py:371
  110.8 2.6 %collective-permute-start.10 = (bf16[3072,128]{1,0:T(8,128)(2,1)S(1)}, bf16[3072,128]{1,0:T(8,128)(2,1)S(1)}, u32[]{:S(2)}, u32[]{:S(2)}) collective-permute-start(bf16[3072,128]{1,0:T(8,128)(2,1)S(1)} %bitcast.8), channel_id=1, source_target_pairs={{0,1},{1,0},{2,3},{3,2},{4,5},{5,4},{6,7},{7,6},{8,9},{9,8},{10,11... | collective-permute-start | bytes 2359304 | tf_op jit(solution)/shard_map/ppermute | solution.py:498
  (32 shorter events, 10.3 us)
Async XLA Ops:
  0.6 25.5 %collective-permute-start.2 = (bf16[2,1024,256]{2,1,0:T(8,128)(2,1)}, bf16[2,1024,256]{2,1,0:T(8,128)(2,1)S(1)}, u32[]{:S(2)}, u32[]{:S(2)}) collective-permute-start(bf16[2,1024,256]{2,1,0:T(8,128)(2,1)} %bitcast.13), channel_id=1, source_target_pairs={{8,0},{16,8},{24,16},{32,24},{40,32},{48,40},{56,48},{64,56},{72,6... | collective-permute-start | bytes 3145736 | tf_op jit(solution)/shard_map/ppermute | solution.py:386
  2.9 6.5 %collective-permute-start = (bf16[2,128,256]{2,1,0:T(8,128)(2,1)S(1)}, bf16[2,128,256]{2,1,0:T(8,128)(2,1)S(1)}, u32[]{:S(2)}, u32[]{:S(2)}) collective-permute-start(bf16[2,128,256]{2,1,0:T(8,128)(2,1)S(1)} %get-tuple-element.65), channel_id=1, source_target_pairs={{0,1},{1,2},{2,3},{3,4},{4,5},{5,6},{6,7},{8,9},{9,10},{10,11},{11... | collective-permute-start | bytes 393224 | tf_op jit(solution)/shard_map/ppermute | solution.py:375
  7.4 6.6 %collective-permute-start.1 = (bf16[2,128,256]{2,1,0:T(8,128)(2,1)S(1)}, bf16[2,128,256]{2,1,0:T(8,128)(2,1)S(1)}, u32[]{:S(2)}, u32[]{:S(2)}) collective-permute-start(bf16[2,128,256]{2,1,0:T(8,128)(2,1)S(1)} %get-tuple-element.64), channel_id=1, source_target_pairs={{1,0},{2,1},{3,2},{4,3},{5,4},{6,5},{7,6},{9,8},{10,9},{11,10},{12... | collective-permute-start | bytes 393224 | tf_op jit(solution)/shard_map/ppermute | solution.py:375
  14.0 1.2 %copy-start.1 = (bf16[1,2,8,128,256]{4,3,2,1,0:T(8,128)(2,1)S(1)}, bf16[1,2,8,128,256]{4,3,2,1,0:T(8,128)(2,1)}, u32[]{:S(2)}) copy-start(bf16[1,2,8,128,256]{4,3,2,1,0:T(8,128)(2,1)} %param.4) | copy-start | bytes 3145732
  15.3 1.3 %copy-start.3 = (bf16[3,3,256,256]{3,2,1,0:T(8,128)(2,1)S(1)}, bf16[3,3,256,256]{3,2,1,0:T(8,128)(2,1)}, u32[]{:S(2)}) copy-start(bf16[3,3,256,256]{3,2,1,0:T(8,128)(2,1)} %refs_2_.5) | copy-start | bytes 3538948
  16.5 15.1 %copy-start.2 = (bf16[3,256,256]{2,1,0:T(8,128)(2,1)S(1)}, bf16[3,256,256]{2,1,0:T(8,128)(2,1)}, u32[]{:S(2)}) copy-start(bf16[3,256,256]{2,1,0:T(8,128)(2,1)} %refs_2_.4) | copy-start | bytes 1179652
  16.5 15.1 %copy-start.6 = (bf16[1,2,8,128,256]{4,3,2,1,0:T(8,128)(2,1)S(1)}, bf16[1,2,8,128,256]{4,3,2,1,0:T(8,128)(2,1)}, u32[]{:S(2)}) copy-start(bf16[1,2,8,128,256]{4,3,2,1,0:T(8,128)(2,1)} %param.5) | copy-start | bytes 3145732
  26.2 44.2 %collective-permute-start.7 = (bf16[2,1024,256]{2,1,0:T(8,128)(2,1)}, bf16[2,1024,256]{2,1,0:T(8,128)(2,1)S(1)}, u32[]{:S(2)}, u32[]{:S(2)}) collective-permute-start(bf16[2,1024,256]{2,1,0:T(8,128)(2,1)} %get-tuple-element.49.refs_0_), channel_id=1, source_target_pairs={{0,8},{8,16},{16,24},{24,32},{32,40},{40,48},{48,56},{56,64},{64,7... | collective-permute-start | bytes 3145736 | tf_op jit(solution)/shard_map/ppermute | solution.py:409
  37.4 4.8 %copy-start.7 = (bf16[2,1024,256]{2,1,0:T(8,128)(2,1)}, bf16[2,1024,256]{2,1,0:T(8,128)(2,1)S(1)}, u32[]{:S(2)}) copy-start(bf16[2,1024,256]{2,1,0:T(8,128)(2,1)S(1)} %get-tuple-element.46.refs_0_) | copy-start | bytes 3145732
  37.4 2.8 %collective-permute-start.3 = (bf16[768,128]{1,0:T(8,128)(2,1)S(1)}, bf16[768,128]{1,0:T(8,128)(2,1)S(1)}, u32[]{:S(2)}, u32[]{:S(2)}) collective-permute-start(bf16[768,128]{1,0:T(8,128)(2,1)S(1)} %get-tuple-element.42), channel_id=1, source_target_pairs={{0,1},{1,0},{2,3},{3,2},{4,5},{5,4},{6,7},{7,6},{8,9},{9,8},{10,11... | collective-permute-start | bytes 589832 | tf_op jit(solution)/shard_map/ppermute | solution.py:430
  39.1 1.4 %collective-permute-start.4 = (bf16[768,128]{1,0:T(8,128)(2,1)S(1)}, bf16[768,128]{1,0:T(8,128)(2,1)S(1)}, u32[]{:S(2)}, u32[]{:S(2)}) collective-permute-start(bf16[768,128]{1,0:T(8,128)(2,1)S(1)} %get-tuple-element.43), channel_id=1, source_target_pairs={{0,1},{1,0},{2,3},{3,2},{4,5},{5,4},{6,7},{7,6},{8,9},{9,8},{10,11... | collective-permute-start | bytes 589832 | tf_op jit(solution)/shard_map/ppermute | solution.py:430
  39.2 1.6 %collective-permute-start.5 = (bf16[768,128]{1,0:T(8,128)(2,1)S(1)}, bf16[768,128]{1,0:T(8,128)(2,1)S(1)}, u32[]{:S(2)}, u32[]{:S(2)}) collective-permute-start(bf16[768,128]{1,0:T(8,128)(2,1)S(1)} %get-tuple-element.44), channel_id=1, source_target_pairs={{0,1},{1,0},{2,3},{3,2},{4,5},{5,4},{6,7},{7,6},{8,9},{9,8},{10,11... | collective-permute-start | bytes 589832 | tf_op jit(solution)/shard_map/ppermute | solution.py:430
  39.6 1.5 %collective-permute-start.6 = (bf16[768,128]{1,0:T(8,128)(2,1)S(1)}, bf16[768,128]{1,0:T(8,128)(2,1)S(1)}, u32[]{:S(2)}, u32[]{:S(2)}) collective-permute-start(bf16[768,128]{1,0:T(8,128)(2,1)S(1)} %get-tuple-element.45), channel_id=1, source_target_pairs={{0,1},{1,0},{2,3},{3,2},{4,5},{5,4},{6,7},{7,6},{8,9},{9,8},{10,11... | collective-permute-start | bytes 589832 | tf_op jit(solution)/shard_map/ppermute | solution.py:430
  42.2 28.2 %all-to-all-start = ((bf16[16,192,128]{2,1,0:T(8,128)(2,1)}), bf16[16,192,128]{2,1,0:T(8,128)(2,1)S(1)}, u32[]{:S(2)}, u32[]{:S(2)}) async-start(bf16[16,192,128]{2,1,0:T(8,128)(2,1)} %bitcast.3), calls=%async_computation | async-start | bytes 1572864 | tf_op jit(solution)/shard_map/all_to_all | solution.py:371
  70.4 21.9 %copy-start = (bf16[2,1024,256]{2,1,0:T(8,128)(2,1)}, bf16[2,1024,256]{2,1,0:T(8,128)(2,1)S(1)}, u32[]{:S(2)}) copy-start(bf16[2,1024,256]{2,1,0:T(8,128)(2,1)S(1)} %collective-permute-done.7.refs_1_) | copy-start | bytes 3145732
  71.3 19.9 %all-to-all-start.1 = ((bf16[8,192,128]{2,1,0:T(8,128)(2,1)}), bf16[8,192,128]{2,1,0:T(8,128)(2,1)S(1)}, u32[]{:S(2)}, u32[]{:S(2)}) async-start(bf16[8,192,128]{2,1,0:T(8,128)(2,1)} %shard_map.80), calls=%async_computation.1 | async-start | bytes 786432 | tf_op jit(solution)/shard_map/all_to_all | solution.py:371
  76.8 5.8 %collective-permute-start.8 = (bf16[2,128,256]{2,1,0:T(8,128)(2,1)S(1)}, bf16[2,128,256]{2,1,0:T(8,128)(2,1)S(1)}, u32[]{:S(2)}, u32[]{:S(2)}) collective-permute-start(bf16[2,128,256]{2,1,0:T(8,128)(2,1)S(1)} %get-tuple-element.50), channel_id=1, source_target_pairs={{0,1},{1,2},{2,3},{3,4},{4,5},{5,6},{6,7},{8,9},{9,10},{10,11},{11... | collective-permute-start | bytes 393224 | tf_op jit(solution)/shard_map/ppermute | solution.py:375
  80.7 6.6 %collective-permute-start.9 = (bf16[2,128,256]{2,1,0:T(8,128)(2,1)S(1)}, bf16[2,128,256]{2,1,0:T(8,128)(2,1)S(1)}, u32[]{:S(2)}, u32[]{:S(2)}) collective-permute-start(bf16[2,128,256]{2,1,0:T(8,128)(2,1)S(1)} %get-tuple-element.51), channel_id=1, source_target_pairs={{1,0},{2,1},{3,2},{4,3},{5,4},{6,5},{7,6},{9,8},{10,9},{11,10},{12... | collective-permute-start | bytes 393224 | tf_op jit(solution)/shard_map/ppermute | solution.py:375
  92.3 18.6 %all-to-all-start.2 = ((bf16[16,192,128]{2,1,0:T(8,128)(2,1)}), bf16[16,192,128]{2,1,0:T(8,128)(2,1)S(1)}, u32[]{:S(2)}, u32[]{:S(2)}) async-start(bf16[16,192,128]{2,1,0:T(8,128)(2,1)} %shard_map.81), calls=%async_computation.2 | async-start | bytes 1572864 | tf_op jit(solution)/shard_map/all_to_all | solution.py:371
  98.1 5.5 %copy-start.4 = (bf16[3,3,256,256]{3,2,1,0:T(8,128)(2,1)S(1)}, bf16[3,3,256,256]{3,2,1,0:T(8,128)(2,1)}, u32[]{:S(2)}) copy-start(bf16[3,3,256,256]{3,2,1,0:T(8,128)(2,1)} %refs_2_.5) | copy-start | bytes 3538948
  98.1 5.5 %copy-start.5 = (f32[2,2,128,256]{3,2,1,0:T(8,128)S(1)}, f32[2,2,128,256]{3,2,1,0:T(8,128)}, u32[]{:S(2)}) copy-start(f32[2,2,128,256]{3,2,1,0:T(8,128)} %get-tuple-element.55.refs_3_) | copy-start | bytes 1572868
  110.8 4.5 %collective-permute-start.10 = (bf16[3072,128]{1,0:T(8,128)(2,1)S(1)}, bf16[3072,128]{1,0:T(8,128)(2,1)S(1)}, u32[]{:S(2)}, u32[]{:S(2)}) collective-permute-start(bf16[3072,128]{1,0:T(8,128)(2,1)S(1)} %bitcast.8), channel_id=1, source_target_pairs={{0,1},{1,0},{2,3},{3,2},{4,5},{5,4},{6,7},{7,6},{8,9},{9,8},{10,11... | collective-permute-start | bytes 2359304 | tf_op jit(solution)/shard_map/ppermute | solution.py:498

commit v9 on v8

--- a/solution.py
+++ b/solution.py
@@ -405,7 +405,6 @@
         flops=6 * work,
         moved=6 << 20,
     )
-    act, ahead = lax.optimization_barrier((act, ahead))
     behind = lax.ppermute(act, TM, steps(TM, 1))
     flat = frames * size
     rows = 12 * chans

time: 117 us -> 112 us (0.957)
  waiting for transfers between devices: 41 us -> 31.3 us
  starting transfers between devices: 42 us -> 46.9 us
    all_to_all x3, waiting for transfers between devices: 24.9 us -> 20.1 us  [exchange(): return lax.all_to_all(value, axes, split_axis=0, concat_axis=0, tiled=True)]
    ppermute x1, waiting for transfers between devices: 4.72 us -> 0.01 us  [local(): ahead = lax.ppermute(dy, TM, steps(TM, -1))]
    all_to_all x3, starting transfers between devices: 18.1 us -> 22.8 us  [exchange(): return lax.all_to_all(value, axes, split_axis=0, concat_axis=0, tiled=True)]
  transfers between devices with their start and end apart: 14 -> 14, of which waited for: 11 -> 10; matrix products, arithmetic and copies ran while one was open for 1% -> 1% of each run, Pallas kernels for 22% -> 23%
where the time goes in v9:
time: 112 us
  starting transfers between devices  46.9 us (42%)
  waiting for transfers between devices  31.3 us (28%)
  Pallas kernels  29.2 us (26%)
  local copies, waits for them, and re-layouts  3.52 us (3%)
    pallas_call x11, Pallas kernels, call(): pl.pallas_call(body, out_shape=outs, in_specs=specs, out_specs=placed if...  29.2 us
    all_to_all x3, starting transfers between devices, exchange(): return lax.all_to_all(value, axes, split_axis=0, concat_axis=0, tiled=True)  22.8 us
    all_to_all x3, waiting for transfers between devices, exchange(): return lax.all_to_all(value, axes, split_axis=0, concat_axis=0, tiled=True)  20.1 us
    ppermute x2, waiting for transfers between devices, swap_rims(): lax.ppermute(first, SPACE, steps(SPACE, -1))  9.16 us
    ppermute x2, starting transfers between devices, swap_rims(): lax.ppermute(last, SPACE, steps(SPACE, 1))  9.16 us
    ppermute x1, starting transfers between devices, local(): behind = lax.ppermute(act, TM, steps(TM, 1))  4.32 us
    ppermute x2, starting transfers between devices, swap_rims(): lax.ppermute(first, SPACE, steps(SPACE, -1))  3.86 us
    ppermute x4, starting transfers between devices, local(): got = [lax.ppermute(part, 'core', pair) for part in send]  2.82 us
  transfers between devices with their start and end apart: 14, of which 10 were waited for; matrix products, arithmetic and copies ran while one was open for 1% of the time, Pallas kernels for 23%

profile of v9, /device:TPU:1, one launch (start us, length us, event | category | flops | bytes accessed | tf_op | source)
XLA Modules:
  0.0 111.7 jit_solution(2239200848611934928)
XLA Ops:
  0.6 1.3 %collective-permute-start = (bf16[2,1024,256]{2,1,0:T(8,128)(2,1)}, bf16[2,1024,256]{2,1,0:T(8,128)(2,1)S(1)}, u32[]{:S(2)}, u32[]{:S(2)}) collective-permute-start(bf16[2,1024,256]{2,1,0:T(8,128)(2,1)} %bitcast.13), channel_id=1, source_target_pairs={{8,0},{16,8},{24,16},{32,24},{40,32},{48,40},{56,48},{64,56},{72,6... | collective-permute-start | bytes 3145736 | tf_op jit(solution)/shard_map/ppermute | solution.py:386
  2.9 4.5 %collective-permute-start.1 = (bf16[2,128,256]{2,1,0:T(8,128)(2,1)S(1)}, bf16[2,128,256]{2,1,0:T(8,128)(2,1)S(1)}, u32[]{:S(2)}, u32[]{:S(2)}) collective-permute-start(bf16[2,128,256]{2,1,0:T(8,128)(2,1)S(1)} %get-tuple-element.61), channel_id=1, source_target_pairs={{0,1},{1,2},{2,3},{3,4},{4,5},{5,6},{6,7},{8,9},{9,10},{10,11},{11... | collective-permute-start | bytes 393224 | tf_op jit(solution)/shard_map/ppermute | solution.py:375
  7.4 1.9 %collective-permute-start.2 = (bf16[2,128,256]{2,1,0:T(8,128)(2,1)S(1)}, bf16[2,128,256]{2,1,0:T(8,128)(2,1)S(1)}, u32[]{:S(2)}, u32[]{:S(2)}) collective-permute-start(bf16[2,128,256]{2,1,0:T(8,128)(2,1)S(1)} %get-tuple-element.60), channel_id=1, source_target_pairs={{1,0},{2,1},{3,2},{4,3},{5,4},{6,5},{7,6},{9,8},{10,9},{11,10},{12... | collective-permute-start | bytes 393224 | tf_op jit(solution)/shard_map/ppermute | solution.py:375
  9.4 4.6 %collective-permute-done.2.refs_2_ = bf16[2,128,256]{2,1,0:T(8,128)(2,1)S(1)} collective-permute-done((bf16[2,128,256]{2,1,0:T(8,128)(2,1)S(1)}, bf16[2,128,256]{2,1,0:T(8,128)(2,1)S(1)}, u32[]{:S(2)}, u32[]{:S(2)}) %collective-permute-start.2) | collective-permute-done | bytes 131104 | tf_op jit(solution)/shard_map/ppermute | solution.py:375
  14.0 1.2 %copy-done.1 = bf16[1,2,8,128,256]{4,3,2,1,0:T(8,128)(2,1)S(1)} copy-done((bf16[1,2,8,128,256]{4,3,2,1,0:T(8,128)(2,1)S(1)}, bf16[1,2,8,128,256]{4,3,2,1,0:T(8,128)(2,1)}, u32[]{:S(2)}) %copy-start.1) | copy-done | bytes 1048600
  15.3 1.3 %copy-done.3 = bf16[3,3,256,256]{3,2,1,0:T(8,128)(2,1)S(1)} copy-done((bf16[3,3,256,256]{3,2,1,0:T(8,128)(2,1)S(1)}, bf16[3,3,256,256]{3,2,1,0:T(8,128)(2,1)}, u32[]{:S(2)}) %copy-start.3) | copy-done | bytes 1179672
  16.5 4.9 %shard_map.75 = (bf16[2,1024,256]{2,1,0:T(8,128)(2,1)}, f32[2,1024,256]{2,1,0:T(8,128)S(1)}, bf16[2,256,1280]{2,1,0:T(8,128)(2,1)S(1)}, bf16[2,256,1024]{2,1,0:T(8,128)(2,1)S(1)}) custom-call(bf16[2,1024,256]{2,1,0:T(8,128)(2,1)S(1)} %bitcast.12, bf16[2,128,256]{2,1,0:T(8,128)(2,1)S(1)} %collective-permute-done.1.refs_1_, ...), custom_call_target="tpu_custom_call" | custom-call | flops 2415919104 | bytes 9437184 | tf_op jit(solution)/shard_map/pallas_call | solution.py:35
  21.5 4.3 %collective-permute-start.7 = (bf16[2,1024,256]{2,1,0:T(8,128)(2,1)}, bf16[2,1024,256]{2,1,0:T(8,128)(2,1)S(1)}, u32[]{:S(2)}, u32[]{:S(2)}) collective-permute-start(bf16[2,1024,256]{2,1,0:T(8,128)(2,1)} %get-tuple-element.45.refs_0_), channel_id=1, source_target_pairs={{0,8},{8,16},{16,24},{24,32},{32,40},{40,48},{48,56},{56,64},{64,7... | collective-permute-start | bytes 3145736 | tf_op jit(solution)/shard_map/ppermute | solution.py:408
  25.8 1.4 %shard_map.76 = (f32[2,1024,256]{2,1,0:T(8,128)S(1)}, f32[2,256,256]{2,1,0:T(8,128)S(1)}) custom-call(bf16[2,1024,256]{2,1,0:T(8,128)(2,1)S(1)} %bitcast.15, bf16[3,256,256]{2,1,0:T(8,128)(2,1)S(1)} %copy-done.2, bf16[2,256,1024]{2,1,0:T(8,128)(2,1)S(1)} %get-tuple-element.34.refs_2_.refs_5_), custom_call_target="tpu_custom_call" | custom-call | flops 1610612736 | bytes 6291456 | tf_op jit(solution)/shard_map/pallas_call | solution.py:35
  27.2 4.4 %shard_map.77 = (bf16[2,1024,256]{2,1,0:T(8,128)(2,1)S(1)}, bf16[3072,128]{1,0:T(8,128)(2,1)S(1)}, bf16[2,128,256]{2,1,0:T(8,128)(2,1)S(1)}, bf16[2,128,256]{2,1...) custom-call(s32[1]{0:T(128)} %bitcast.refs_0_, ...), custom_call_target="tpu_custom_call" | custom-call | flops 1024 | bytes 4096 | tf_op jit(solution)/shard_map/pallas_call | solution.py:35
  31.6 2.2 %collective-permute-start.3 = (bf16[768,128]{1,0:T(8,128)(2,1)S(1)}, bf16[768,128]{1,0:T(8,128)(2,1)S(1)}, u32[]{:S(2)}, u32[]{:S(2)}) collective-permute-start(bf16[768,128]{1,0:T(8,128)(2,1)S(1)} %get-tuple-element.38), channel_id=1, source_target_pairs={{0,1},{1,0},{2,3},{3,2},{4,5},{5,4},{6,7},{7,6},{8,9},{9,8},{10,11... | collective-permute-start | bytes 589832 | tf_op jit(solution)/shard_map/ppermute | solution.py:429
  36.9 10.0 %all-to-all-start = ((bf16[16,192,128]{2,1,0:T(8,128)(2,1)}), bf16[16,192,128]{2,1,0:T(8,128)(2,1)S(1)}, u32[]{:S(2)}, u32[]{:S(2)}) async-start(bf16[16,192,128]{2,1,0:T(8,128)(2,1)} %bitcast.3), calls=%async_computation | async-start | bytes 1572864 | tf_op jit(solution)/shard_map/all_to_all | solution.py:371
  46.9 6.5 %shard_map.79 = (bf16[2,1024,256]{2,1,0:T(8,128)(2,1)}, f32[2,2,128,256]{3,2,1,0:T(8,128)}) custom-call(bf16[2,1024,256]{2,1,0:T(8,128)(2,1)} %copy-done.7, bf16[3,3,256,256]{3,2,1,0:T(8,128)(2,1)} %refs_2_.5, bf16[2,1024,256]{2,1,0:T(8,128)(2,1)} %bitcast.14), custom_call_target="tpu_custom_call" | custom-call | flops 2415919104 | bytes 5242880 | tf_op jit(solution)/shard_map/pallas_call | solution.py:35
  53.4 10.6 %all-to-all-done.refs_0_ = bf16[16,192,128]{2,1,0:T(8,128)(2,1)S(1)} async-done(((bf16[16,192,128]{2,1,0:T(8,128)(2,1)}), bf16[16,192,128]{2,1,0:T(8,128)(2,1)S(1)}, u32[]{:S(2)}, u32[]{:S(2)}) %all-to-all-start) | async-done | bytes 786464 | tf_op jit(solution)/shard_map/all_to_all | solution.py:371
  65.0 6.2 %all-to-all-start.1 = ((bf16[8,192,128]{2,1,0:T(8,128)(2,1)}), bf16[8,192,128]{2,1,0:T(8,128)(2,1)S(1)}, u32[]{:S(2)}, u32[]{:S(2)}) async-start(bf16[8,192,128]{2,1,0:T(8,128)(2,1)} %shard_map.80), calls=%async_computation.1 | async-start | bytes 786432 | tf_op jit(solution)/shard_map/all_to_all | solution.py:371
  71.2 4.6 %collective-permute-start.8 = (bf16[2,128,256]{2,1,0:T(8,128)(2,1)S(1)}, bf16[2,128,256]{2,1,0:T(8,128)(2,1)S(1)}, u32[]{:S(2)}, u32[]{:S(2)}) collective-permute-start(bf16[2,128,256]{2,1,0:T(8,128)(2,1)S(1)} %get-tuple-element.46), channel_id=1, source_target_pairs={{0,1},{1,2},{2,3},{3,4},{4,5},{5,6},{6,7},{8,9},{9,10},{10,11},{11... | collective-permute-start | bytes 393224 | tf_op jit(solution)/shard_map/ppermute | solution.py:375
  75.9 1.9 %collective-permute-start.9 = (bf16[2,128,256]{2,1,0:T(8,128)(2,1)S(1)}, bf16[2,128,256]{2,1,0:T(8,128)(2,1)S(1)}, u32[]{:S(2)}, u32[]{:S(2)}) collective-permute-start(bf16[2,128,256]{2,1,0:T(8,128)(2,1)S(1)} %get-tuple-element.47), channel_id=1, source_target_pairs={{1,0},{2,1},{3,2},{4,3},{5,4},{6,5},{7,6},{9,8},{10,9},{11,10},{12... | collective-permute-start | bytes 393224 | tf_op jit(solution)/shard_map/ppermute | solution.py:375
  77.8 4.5 %collective-permute-done.9.refs_1_ = bf16[2,128,256]{2,1,0:T(8,128)(2,1)S(1)} collective-permute-done((bf16[2,128,256]{2,1,0:T(8,128)(2,1)S(1)}, bf16[2,128,256]{2,1,0:T(8,128)(2,1)S(1)}, u32[]{:S(2)}, u32[]{:S(2)}) %collective-permute-start.9) | collective-permute-done | bytes 131104 | tf_op jit(solution)/shard_map/ppermute | solution.py:375
  82.3 3.3 %all-to-all-done.1.refs_0_ = bf16[8,192,128]{2,1,0:T(8,128)(2,1)S(1)} async-done(((bf16[8,192,128]{2,1,0:T(8,128)(2,1)}), bf16[8,192,128]{2,1,0:T(8,128)(2,1)S(1)}, u32[]{:S(2)}, u32[]{:S(2)}) %all-to-all-start.1) | async-done | bytes 393248 | tf_op jit(solution)/shard_map/all_to_all | solution.py:371
  86.6 6.6 %all-to-all-start.2 = ((bf16[16,192,128]{2,1,0:T(8,128)(2,1)}), bf16[16,192,128]{2,1,0:T(8,128)(2,1)S(1)}, u32[]{:S(2)}, u32[]{:S(2)}) async-start(bf16[16,192,128]{2,1,0:T(8,128)(2,1)} %shard_map.81), calls=%async_computation.2 | async-start | bytes 1572864 | tf_op jit(solution)/shard_map/all_to_all | solution.py:371
  93.3 5.4 %shard_map.82 = bf16[2,1024,256]{2,1,0:T(8,128)(2,1)} custom-call(bf16[2,1024,256]{2,1,0:T(8,128)(2,1)} %get-tuple-element.45.refs_0_, bf16[2,1024,256]{2,1,0:T(8,128)(2,1)} %copy-done, bf16[3,256,256]{2,1,0:T(8,128)(2,1)} %refs_2_.4, bf16[2,1024,256]{2,1,0:T(8,128)(2,1)} %bitcast.11), custom_call_target="tpu_custom_call" | custom-call | flops 805306368 | bytes 4194304 | tf_op jit(solution)/shard_map/pallas_call | solution.py:35
  99.8 6.2 %all-to-all-done.2 = bf16[16,192,128]{2,1,0:T(8,128)(2,1)S(1)} async-done(((bf16[16,192,128]{2,1,0:T(8,128)(2,1)}), bf16[16,192,128]{2,1,0:T(8,128)(2,1)S(1)}, u32[]{:S(2)}, u32[]{:S(2)}) %all-to-all-start.2) | async-done | bytes 786464 | tf_op jit(solution)/shard_map/all_to_all | solution.py:371
  106.0 2.6 %collective-permute-start.10 = (bf16[3072,128]{1,0:T(8,128)(2,1)S(1)}, bf16[3072,128]{1,0:T(8,128)(2,1)S(1)}, u32[]{:S(2)}, u32[]{:S(2)}) collective-permute-start(bf16[3072,128]{1,0:T(8,128)(2,1)S(1)} %bitcast.8), channel_id=1, source_target_pairs={{0,1},{1,0},{2,3},{3,2},{4,5},{5,4},{6,7},{7,6},{8,9},{9,8},{10,11... | collective-permute-start | bytes 2359304 | tf_op jit(solution)/shard_map/ppermute | solution.py:497
  108.6 1.2 %shard_map.84 = (f32[9,256,256]{2,1,0:T(8,128)}, f32[3,256,256]{2,1,0:T(8,128)}) custom-call(s32[1]{0:T(128)} %bitcast.refs_0_, bf16[3072,128]{1,0:T(8,128)(2,1)S(1)} %bitcast.9), custom_call_target="tpu_custom_call" | custom-call | bytes 3145728 | tf_op jit(solution)/shard_map/pallas_call | solution.py:35
  (32 shorter events, 9.1 us)
Async XLA Ops:
  0.6 26.5 %collective-permute-start = (bf16[2,1024,256]{2,1,0:T(8,128)(2,1)}, bf16[2,1024,256]{2,1,0:T(8,128)(2,1)S(1)}, u32[]{:S(2)}, u32[]{:S(2)}) collective-permute-start(bf16[2,1024,256]{2,1,0:T(8,128)(2,1)} %bitcast.13), channel_id=1, source_target_pairs={{8,0},{16,8},{24,16},{32,24},{40,32},{48,40},{56,48},{64,56},{72,6... | collective-permute-start | bytes 3145736 | tf_op jit(solution)/shard_map/ppermute | solution.py:386
  2.9 6.5 %collective-permute-start.1 = (bf16[2,128,256]{2,1,0:T(8,128)(2,1)S(1)}, bf16[2,128,256]{2,1,0:T(8,128)(2,1)S(1)}, u32[]{:S(2)}, u32[]{:S(2)}) collective-permute-start(bf16[2,128,256]{2,1,0:T(8,128)(2,1)S(1)} %get-tuple-element.61), channel_id=1, source_target_pairs={{0,1},{1,2},{2,3},{3,4},{4,5},{5,6},{6,7},{8,9},{9,10},{10,11},{11... | collective-permute-start | bytes 393224 | tf_op jit(solution)/shard_map/ppermute | solution.py:375
  7.4 6.6 %collective-permute-start.2 = (bf16[2,128,256]{2,1,0:T(8,128)(2,1)S(1)}, bf16[2,128,256]{2,1,0:T(8,128)(2,1)S(1)}, u32[]{:S(2)}, u32[]{:S(2)}) collective-permute-start(bf16[2,128,256]{2,1,0:T(8,128)(2,1)S(1)} %get-tuple-element.60), channel_id=1, source_target_pairs={{1,0},{2,1},{3,2},{4,3},{5,4},{6,5},{7,6},{9,8},{10,9},{11,10},{12... | collective-permute-start | bytes 393224 | tf_op jit(solution)/shard_map/ppermute | solution.py:375
  14.0 1.2 %copy-start.1 = (bf16[1,2,8,128,256]{4,3,2,1,0:T(8,128)(2,1)S(1)}, bf16[1,2,8,128,256]{4,3,2,1,0:T(8,128)(2,1)}, u32[]{:S(2)}) copy-start(bf16[1,2,8,128,256]{4,3,2,1,0:T(8,128)(2,1)} %param.4) | copy-start | bytes 3145732
  15.3 1.3 %copy-start.3 = (bf16[3,3,256,256]{3,2,1,0:T(8,128)(2,1)S(1)}, bf16[3,3,256,256]{3,2,1,0:T(8,128)(2,1)}, u32[]{:S(2)}) copy-start(bf16[3,3,256,256]{3,2,1,0:T(8,128)(2,1)} %refs_2_.5) | copy-start | bytes 3538948
  16.5 9.3 %copy-start.2 = (bf16[3,256,256]{2,1,0:T(8,128)(2,1)S(1)}, bf16[3,256,256]{2,1,0:T(8,128)(2,1)}, u32[]{:S(2)}) copy-start(bf16[3,256,256]{2,1,0:T(8,128)(2,1)} %refs_2_.4) | copy-start | bytes 1179652
  16.5 9.3 %copy-start.6 = (bf16[1,2,8,128,256]{4,3,2,1,0:T(8,128)(2,1)S(1)}, bf16[1,2,8,128,256]{4,3,2,1,0:T(8,128)(2,1)}, u32[]{:S(2)}) copy-start(bf16[1,2,8,128,256]{4,3,2,1,0:T(8,128)(2,1)} %param.5) | copy-start | bytes 3145732
  21.5 42.6 %collective-permute-start.7 = (bf16[2,1024,256]{2,1,0:T(8,128)(2,1)}, bf16[2,1024,256]{2,1,0:T(8,128)(2,1)S(1)}, u32[]{:S(2)}, u32[]{:S(2)}) collective-permute-start(bf16[2,1024,256]{2,1,0:T(8,128)(2,1)} %get-tuple-element.45.refs_0_), channel_id=1, source_target_pairs={{0,8},{8,16},{16,24},{24,32},{32,40},{40,48},{48,56},{56,64},{64,7... | collective-permute-start | bytes 3145736 | tf_op jit(solution)/shard_map/ppermute | solution.py:408
  31.6 5.3 %copy-start.7 = (bf16[2,1024,256]{2,1,0:T(8,128)(2,1)}, bf16[2,1024,256]{2,1,0:T(8,128)(2,1)S(1)}, u32[]{:S(2)}) copy-start(bf16[2,1024,256]{2,1,0:T(8,128)(2,1)S(1)} %get-tuple-element.42.refs_0_) | copy-start | bytes 3145732
  31.6 3.3 %collective-permute-start.3 = (bf16[768,128]{1,0:T(8,128)(2,1)S(1)}, bf16[768,128]{1,0:T(8,128)(2,1)S(1)}, u32[]{:S(2)}, u32[]{:S(2)}) collective-permute-start(bf16[768,128]{1,0:T(8,128)(2,1)S(1)} %get-tuple-element.38), channel_id=1, source_target_pairs={{0,1},{1,0},{2,3},{3,2},{4,5},{5,4},{6,7},{7,6},{8,9},{9,8},{10,11... | collective-permute-start | bytes 589832 | tf_op jit(solution)/shard_map/ppermute | solution.py:429
  33.8 1.4 %collective-permute-start.4 = (bf16[768,128]{1,0:T(8,128)(2,1)S(1)}, bf16[768,128]{1,0:T(8,128)(2,1)S(1)}, u32[]{:S(2)}, u32[]{:S(2)}) collective-permute-start(bf16[768,128]{1,0:T(8,128)(2,1)S(1)} %get-tuple-element.39), channel_id=1, source_target_pairs={{0,1},{1,0},{2,3},{3,2},{4,5},{5,4},{6,7},{7,6},{8,9},{9,8},{10,11... | collective-permute-start | bytes 589832 | tf_op jit(solution)/shard_map/ppermute | solution.py:429
  33.9 1.6 %collective-permute-start.5 = (bf16[768,128]{1,0:T(8,128)(2,1)S(1)}, bf16[768,128]{1,0:T(8,128)(2,1)S(1)}, u32[]{:S(2)}, u32[]{:S(2)}) collective-permute-start(bf16[768,128]{1,0:T(8,128)(2,1)S(1)} %get-tuple-element.40), channel_id=1, source_target_pairs={{0,1},{1,0},{2,3},{3,2},{4,5},{5,4},{6,7},{7,6},{8,9},{9,8},{10,11... | collective-permute-start | bytes 589832 | tf_op jit(solution)/shard_map/ppermute | solution.py:429
  34.3 1.5 %collective-permute-start.6 = (bf16[768,128]{1,0:T(8,128)(2,1)S(1)}, bf16[768,128]{1,0:T(8,128)(2,1)S(1)}, u32[]{:S(2)}, u32[]{:S(2)}) collective-permute-start(bf16[768,128]{1,0:T(8,128)(2,1)S(1)} %get-tuple-element.41), channel_id=1, source_target_pairs={{0,1},{1,0},{2,3},{3,2},{4,5},{5,4},{6,7},{7,6},{8,9},{9,8},{10,11... | collective-permute-start | bytes 589832 | tf_op jit(solution)/shard_map/ppermute | solution.py:429
  36.9 27.1 %all-to-all-start = ((bf16[16,192,128]{2,1,0:T(8,128)(2,1)}), bf16[16,192,128]{2,1,0:T(8,128)(2,1)S(1)}, u32[]{:S(2)}, u32[]{:S(2)}) async-start(bf16[16,192,128]{2,1,0:T(8,128)(2,1)} %bitcast.3), calls=%async_computation | async-start | bytes 1572864 | tf_op jit(solution)/shard_map/all_to_all | solution.py:371
  64.0 22.6 %copy-start = (bf16[2,1024,256]{2,1,0:T(8,128)(2,1)}, bf16[2,1024,256]{2,1,0:T(8,128)(2,1)S(1)}, u32[]{:S(2)}) copy-start(bf16[2,1024,256]{2,1,0:T(8,128)(2,1)S(1)} %collective-permute-done.7.refs_1_) | copy-start | bytes 3145732
  65.0 20.6 %all-to-all-start.1 = ((bf16[8,192,128]{2,1,0:T(8,128)(2,1)}), bf16[8,192,128]{2,1,0:T(8,128)(2,1)S(1)}, u32[]{:S(2)}, u32[]{:S(2)}) async-start(bf16[8,192,128]{2,1,0:T(8,128)(2,1)} %shard_map.80), calls=%async_computation.1 | async-start | bytes 786432 | tf_op jit(solution)/shard_map/all_to_all | solution.py:371
  71.2 6.6 %collective-permute-start.8 = (bf16[2,128,256]{2,1,0:T(8,128)(2,1)S(1)}, bf16[2,128,256]{2,1,0:T(8,128)(2,1)S(1)}, u32[]{:S(2)}, u32[]{:S(2)}) collective-permute-start(bf16[2,128,256]{2,1,0:T(8,128)(2,1)S(1)} %get-tuple-element.46), channel_id=1, source_target_pairs={{0,1},{1,2},{2,3},{3,4},{4,5},{5,6},{6,7},{8,9},{9,10},{10,11},{11... | collective-permute-start | bytes 393224 | tf_op jit(solution)/shard_map/ppermute | solution.py:375
  75.9 6.5 %collective-permute-start.9 = (bf16[2,128,256]{2,1,0:T(8,128)(2,1)S(1)}, bf16[2,128,256]{2,1,0:T(8,128)(2,1)S(1)}, u32[]{:S(2)}, u32[]{:S(2)}) collective-permute-start(bf16[2,128,256]{2,1,0:T(8,128)(2,1)S(1)} %get-tuple-element.47), channel_id=1, source_target_pairs={{1,0},{2,1},{3,2},{4,3},{5,4},{6,5},{7,6},{9,8},{10,9},{11,10},{12... | collective-permute-start | bytes 393224 | tf_op jit(solution)/shard_map/ppermute | solution.py:375
  86.6 19.4 %all-to-all-start.2 = ((bf16[16,192,128]{2,1,0:T(8,128)(2,1)}), bf16[16,192,128]{2,1,0:T(8,128)(2,1)S(1)}, u32[]{:S(2)}, u32[]{:S(2)}) async-start(bf16[16,192,128]{2,1,0:T(8,128)(2,1)} %shard_map.81), calls=%async_computation.2 | async-start | bytes 1572864 | tf_op jit(solution)/shard_map/all_to_all | solution.py:371
  93.2 5.5 %copy-start.4 = (bf16[3,3,256,256]{3,2,1,0:T(8,128)(2,1)S(1)}, bf16[3,3,256,256]{3,2,1,0:T(8,128)(2,1)}, u32[]{:S(2)}) copy-start(bf16[3,3,256,256]{3,2,1,0:T(8,128)(2,1)} %refs_2_.5) | copy-start | bytes 3538948
  93.2 5.5 %copy-start.5 = (f32[2,2,128,256]{3,2,1,0:T(8,128)S(1)}, f32[2,2,128,256]{3,2,1,0:T(8,128)}, u32[]{:S(2)}) copy-start(f32[2,2,128,256]{3,2,1,0:T(8,128)} %get-tuple-element.51.refs_3_) | copy-start | bytes 1572868
  106.0 4.5 %collective-permute-start.10 = (bf16[3072,128]{1,0:T(8,128)(2,1)S(1)}, bf16[3072,128]{1,0:T(8,128)(2,1)S(1)}, u32[]{:S(2)}, u32[]{:S(2)}) collective-permute-start(bf16[3072,128]{1,0:T(8,128)(2,1)S(1)} %bitcast.8), channel_id=1, source_target_pairs={{0,1},{1,0},{2,3},{3,2},{4,5},{5,4},{6,7},{7,6},{8,9},{9,8},{10,11... | collective-permute-start | bytes 2359304 | tf_op jit(solution)/shard_map/ppermute | solution.py:497

commit v10 on v9

--- a/solution.py
+++ b/solution.py
@@ -74,7 +74,12 @@
     padded[frame, COLS + size :, :] = bottom[frame]
 
 
-def forward_kernel(x, top, bottom, weight, act, slope, x_t, act_t, padded):
+def turn_kernel(x, weight, x_t):
+    for f in range(x.shape[0]):
+        x_t[f] = x[f].T
+
+
+def forward_kernel(x, top, bottom, weight, act, slope, top_t, bottom_t, act_t, padded):
     frames, size, chans = x.shape
     for f in range(frames):
         fill(padded, x, top, bottom, f)
@@ -97,7 +102,8 @@
         act_t[f, :, pl.ds(start, CHUNK)] = active.T
 
     for f in range(frames):
-        x_t[f] = padded[f].T
+        top_t[f] = top[f].T
+        bottom_t[f] = bottom[f].T
 
 
 def early_kernel(dy, weight, act_t, partial, terms):
@@ -129,8 +135,10 @@
     wide[2, into, :] = shifted(full, column, 1).astype(BF)
 
 
-def windows_of(x_t, f, size):
-    return jnp.concatenate([x_t[f, :, i * COLS : i * COLS + size] for i in range(3)], axis=0)
+def windows_of(x_t, top_t, bottom_t, f, size):
+    above = jnp.concatenate([top_t[f], x_t[f, :, : size - COLS]], axis=1)
+    below = jnp.concatenate([x_t[f, :, COLS:], bottom_t[f]], axis=1)
+    return jnp.concatenate([above, x_t[f], below], axis=0)
 
 
 def gradient_kernel(
@@ -139,6 +147,8 @@
     weight,
     slope,
     x_t,
+    top_t,
+    bottom_t,
     act_t,
     partial,
     early,
@@ -176,7 +186,7 @@
             at = (tap * 2 + h) * chans
             terms[at : at + chans, :] = value[:, h * 128 : (h + 1) * 128].astype(BF)
 
-    left = jnp.concatenate([windows_of(x_t, f, size) for f in range(frames)], axis=1)
+    left = jnp.concatenate([windows_of(x_t, top_t, bottom_t, f, size) for f in range(frames)], axis=1)
     for j in range(3):
         out = jnp.dot(left, wide[j], preferred_element_type=F32)
         for i in range(3):
@@ -216,13 +226,18 @@
     out[...] = total.astype(out.dtype)
 
 
-def spread_sum_kernel(scale, parts, out):
+def spread_sum_kernel(scale, parts, out, sent, sems):
     total = parts[0].astype(F32)
     for i in range(1, parts.shape[0]):
         total = total + parts[i].astype(F32)
-    total = (total * scale).astype(out.dtype)
-    for i in range(out.shape[0]):
-        out[i] = total
+    sent[...] = (total * scale).astype(sent.dtype)
+    copies = [
+        pltpu.make_async_copy(sent, out.at[i], sems.at[i]) for i in range(out.shape[0])
+    ]
+    for copy in copies:
+        copy.start()
+    for copy in copies:
+        copy.wait()
 
 
 def write_half(first, source, spatial, temporal, wide, sems):
@@ -385,12 +400,20 @@
     core = lax.axis_index("core").astype(jnp.int32).reshape(1)
     ahead = lax.ppermute(dy, TM, steps(TM, -1))
     top, bottom = swap_rims(x[:, size - COLS :, :], x[:, :COLS, :])
-    act, slope, x_t, act_t = call(
+    x_t = call(
+        turn_kernel,
+        shape((frames, chans, size)),
+        (x, spatial_weight),
+        flops=1 << 20,
+        moved=2 << 20,
+    )
+    act, slope, top_t, bottom_t, act_t = call(
         forward_kernel,
         [
             shape((frames, size, chans)),
             shape((frames, size, chans), F32),
-            shape((frames, chans, size + 2 * COLS)),
+            shape((frames, chans, COLS)),
+            shape((frames, chans, COLS)),
             shape((frames, chans, size)),
         ],
         (x, top, bottom, spatial_weight),
@@ -413,7 +436,18 @@
         gradient_kernel,
         [shape((frames, size, chans)), shape((rows, 128)), edges, edges]
         + [shape((rows // SWAPS, 128))] * SWAPS,
-        (core, ahead, temporal_weight, slope, x_t, act_t, partial, early),
+        (
+            core,
+            ahead,
+            temporal_weight,
+            slope,
+            x_t,
+            top_t,
+            bottom_t,
+            act_t,
+            partial,
+            early,
+        ),
         [
             pltpu.VMEM((3, flat, chans), BF),
             pltpu.VMEM((2 * rows, 128), BF),
@@ -454,7 +488,9 @@
         functools.partial(spread_sum_kernel, 1.0),
         shape((column, share, 128)),
         (first,),
+        [pltpu.VMEM((share, 128), BF), pltpu.SemaphoreType.DMA((column,))],
         moved=1 << 12,
+        out_hbm=(0,),
         after=(behind,),
     )
     third = exchange(spread, COLUMN)
@@ -490,7 +526,9 @@
         functools.partial(spread_sum_kernel, scale),
         shape((plane, share, 128)),
         (third,),
+        [pltpu.VMEM((share, 128), BF), pltpu.SemaphoreType.DMA((plane,))],
         moved=1 << 12,
+        out_hbm=(0,),
     )
     own = exchange(wider, PLANE).reshape(rows, 128)
     own, block_out, input_grad = lax.optimization_barrier((own, block_out, input_grad))

time: 112 us -> 112 us (level)
  waiting for transfers between devices: 31.3 us -> 29.9 us
    ppermute x2, waiting for transfers between devices: 9.16 us -> 6.4 us  [swap_rims(): lax.ppermute(first, SPACE, steps(SPACE, -1))]
    ppermute x1, waiting for transfers between devices: 0.01 us -> 1.44 us  [local(): ahead = lax.ppermute(dy, TM, steps(TM, -1))]
    unnamed x16 -> x18, local copies, waits for them, and re-layouts: 2.52 us -> 3.49 us
    pallas_call x11 -> x12, Pallas kernels: 29.2 us -> 29.7 us  [call(): pl.pallas_call(body, out_shape=outs, in_specs=specs, out_specs=placed if...]
  transfers between devices with their start and end apart: 14 -> 14, of which waited for: 10 -> 11; matrix products, arithmetic and copies ran while one was open for 1% -> 1% of each run, Pallas kernels for 23% -> 24%
where the time goes in v10:
time: 112 us; the launch traced here: 111 us
  starting transfers between devices  46.2 us (41%)
  waiting for transfers between devices  29.9 us (27%)
  Pallas kernels  29.7 us (27%)
  local copies, waits for them, and re-layouts  4.48 us (4%)
    pallas_call x12, Pallas kernels, call(): pl.pallas_call(body, out_shape=outs, in_specs=specs, out_specs=placed if...  29.7 us
    all_to_all x3, starting transfers between devices, exchange(): return lax.all_to_all(value, axes, split_axis=0, concat_axis=0, tiled=True)  22 us
    all_to_all x3, waiting for transfers between devices, exchange(): return lax.all_to_all(value, axes, split_axis=0, concat_axis=0, tiled=True)  19.9 us
    ppermute x2, starting transfers between devices, swap_rims(): lax.ppermute(last, SPACE, steps(SPACE, 1))  8.37 us
    ppermute x2, waiting for transfers between devices, swap_rims(): lax.ppermute(first, SPACE, steps(SPACE, -1))  6.4 us
    ppermute x1, starting transfers between devices, local(): behind = lax.ppermute(act, TM, steps(TM, 1))  4.32 us
    ppermute x2, starting transfers between devices, swap_rims(): lax.ppermute(first, SPACE, steps(SPACE, -1))  3.86 us
    ppermute x4, starting transfers between devices, local(): got = [lax.ppermute(part, 'core', pair) for part in send]  3.65 us
  transfers between devices with their start and end apart: 14, of which 11 were waited for; matrix products, arithmetic and copies ran while one was open for 1% of the time, Pallas kernels for 24%

profile of v10, /device:TPU:1, one launch (start us, length us, event | category | flops | bytes accessed | tf_op | source)
XLA Modules:
  0.0 111.1 jit_solution(16979798671421668637)
XLA Ops:
  0.6 1.3 %collective-permute-start = (bf16[2,1024,256]{2,1,0:T(8,128)(2,1)}, bf16[2,1024,256]{2,1,0:T(8,128)(2,1)S(1)}, u32[]{:S(2)}, u32[]{:S(2)}) collective-permute-start(bf16[2,1024,256]{2,1,0:T(8,128)(2,1)} %bitcast.14), channel_id=1, source_target_pairs={{8,0},{16,8},{24,16},{32,24},{40,32},{48,40},{56,48},{64,56},{72,6... | collective-permute-start | bytes 3145736 | tf_op jit(solution)/shard_map/ppermute | solution.py:401
  2.9 4.5 %collective-permute-start.1 = (bf16[2,128,256]{2,1,0:T(8,128)(2,1)S(1)}, bf16[2,128,256]{2,1,0:T(8,128)(2,1)S(1)}, u32[]{:S(2)}, u32[]{:S(2)}) collective-permute-start(bf16[2,128,256]{2,1,0:T(8,128)(2,1)S(1)} %get-tuple-element.63), channel_id=1, source_target_pairs={{0,1},{1,2},{2,3},{3,4},{4,5},{5,6},{6,7},{8,9},{9,10},{10,11},{11... | collective-permute-start | bytes 393224 | tf_op jit(solution)/shard_map/ppermute | solution.py:390
  7.4 1.9 %collective-permute-start.2 = (bf16[2,128,256]{2,1,0:T(8,128)(2,1)S(1)}, bf16[2,128,256]{2,1,0:T(8,128)(2,1)S(1)}, u32[]{:S(2)}, u32[]{:S(2)}) collective-permute-start(bf16[2,128,256]{2,1,0:T(8,128)(2,1)S(1)} %get-tuple-element.62), channel_id=1, source_target_pairs={{1,0},{2,1},{3,2},{4,3},{5,4},{6,5},{7,6},{9,8},{10,9},{11,10},{12... | collective-permute-start | bytes 393224 | tf_op jit(solution)/shard_map/ppermute | solution.py:390
  9.4 1.2 %copy-done = bf16[1,2,8,128,256]{4,3,2,1,0:T(8,128)(2,1)S(1)} copy-done((bf16[1,2,8,128,256]{4,3,2,1,0:T(8,128)(2,1)S(1)}, bf16[1,2,8,128,256]{4,3,2,1,0:T(8,128)(2,1)}, u32[]{:S(2)}) %copy-start) | copy-done | bytes 1048600
  10.6 1.3 %copy-done.1 = bf16[3,3,256,256]{3,2,1,0:T(8,128)(2,1)S(1)} copy-done((bf16[3,3,256,256]{3,2,1,0:T(8,128)(2,1)S(1)}, bf16[3,3,256,256]{3,2,1,0:T(8,128)(2,1)}, u32[]{:S(2)}) %copy-start.1) | copy-done | bytes 1179672
  12.3 1.8 %collective-permute-done.2.refs_2_ = bf16[2,128,256]{2,1,0:T(8,128)(2,1)S(1)} collective-permute-done((bf16[2,128,256]{2,1,0:T(8,128)(2,1)S(1)}, bf16[2,128,256]{2,1,0:T(8,128)(2,1)S(1)}, u32[]{:S(2)}, u32[]{:S(2)}) %collective-permute-start.2) | collective-permute-done | bytes 131104 | tf_op jit(solution)/shard_map/ppermute | solution.py:390
  14.0 5.0 %shard_map.75 = (bf16[2,1024,256]{2,1,0:T(8,128)(2,1)}, f32[2,1024,256]{2,1,0:T(8,128)S(1)}, bf16[2,256,128]{2,1,0:T(8,128)(2,1)S(1)}, bf16[2,256,128]{2,1,0:T(8,128)(2,1)S(1)}, bf16[2,256,1024]{2,1,0:T(8,128)(2,1)S(1)}) custom-call(bf16[2,1024,256]{2,1,0:T(8,128)(2,1)S(1)} %bitcast.11, bf16[2,128,256]{2,1,0:T(8,128)(2,1)S(1)} %collective-permute-done.1.refs_1_, ...), custom_call_target="tpu_custom_call" | custom-call | flops 2415919104 | bytes 9437184 | tf_op jit(solution)/shard_map/pallas_call | solution.py:35
  19.0 4.3 %collective-permute-start.7 = (bf16[2,1024,256]{2,1,0:T(8,128)(2,1)}, bf16[2,1024,256]{2,1,0:T(8,128)(2,1)S(1)}, u32[]{:S(2)}, u32[]{:S(2)}) collective-permute-start(bf16[2,1024,256]{2,1,0:T(8,128)(2,1)} %get-tuple-element.47.refs_0_), channel_id=1, source_target_pairs={{0,8},{8,16},{16,24},{24,32},{32,40},{40,48},{48,56},{56,64},{64,7... | collective-permute-start | bytes 3145736 | tf_op jit(solution)/shard_map/ppermute | solution.py:431
  23.4 1.4 %shard_map.77 = (f32[2,1024,256]{2,1,0:T(8,128)S(1)}, f32[2,256,256]{2,1,0:T(8,128)S(1)}) custom-call(bf16[2,1024,256]{2,1,0:T(8,128)(2,1)S(1)} %bitcast.16, bf16[3,256,256]{2,1,0:T(8,128)(2,1)S(1)} %copy-done.5, bf16[2,256,1024]{2,1,0:T(8,128)(2,1)S(1)} %get-tuple-element.36.refs_2_.refs_7_), custom_call_target="tpu_custom_call" | custom-call | flops 1610612736 | bytes 6291456 | tf_op jit(solution)/shard_map/pallas_call | solution.py:35
  24.7 1.4 %collective-permute-done.refs_1_ = bf16[2,1024,256]{2,1,0:T(8,128)(2,1)S(1)} collective-permute-done((bf16[2,1024,256]{2,1,0:T(8,128)(2,1)}, bf16[2,1024,256]{2,1,0:T(8,128)(2,1)S(1)}, u32[]{:S(2)}, u32[]{:S(2)}) %collective-permute-start) | collective-permute-done | bytes 1048608 | tf_op jit(solution)/shard_map/ppermute | solution.py:401
  26.2 4.4 %shard_map.78 = (bf16[2,1024,256]{2,1,0:T(8,128)(2,1)S(1)}, bf16[3072,128]{1,0:T(8,128)(2,1)S(1)}, bf16[2,128,256]{2,1,0:T(8,128)(2,1)S(1)}, bf16[2,128,256]{2,1...) custom-call(s32[1]{0:T(128)} %bitcast.refs_0_, ...), custom_call_target="tpu_custom_call" | custom-call | flops 1024 | bytes 4096 | tf_op jit(solution)/shard_map/pallas_call | solution.py:35
  31.6 3.1 %collective-permute-start.3 = (bf16[768,128]{1,0:T(8,128)(2,1)S(1)}, bf16[768,128]{1,0:T(8,128)(2,1)S(1)}, u32[]{:S(2)}, u32[]{:S(2)}) collective-permute-start(bf16[768,128]{1,0:T(8,128)(2,1)S(1)} %get-tuple-element.40), channel_id=1, source_target_pairs={{0,1},{1,0},{2,3},{3,2},{4,5},{5,4},{6,7},{7,6},{8,9},{9,8},{10,11... | collective-permute-start | bytes 589832 | tf_op jit(solution)/shard_map/ppermute | solution.py:463
  37.8 10.0 %all-to-all-start = ((bf16[16,192,128]{2,1,0:T(8,128)(2,1)}), bf16[16,192,128]{2,1,0:T(8,128)(2,1)S(1)}, u32[]{:S(2)}, u32[]{:S(2)}) async-start(bf16[16,192,128]{2,1,0:T(8,128)(2,1)} %bitcast.3), calls=%async_computation | async-start | bytes 1572864 | tf_op jit(solution)/shard_map/all_to_all | solution.py:386
  47.8 6.5 %shard_map.80 = (bf16[2,1024,256]{2,1,0:T(8,128)(2,1)}, f32[2,2,128,256]{3,2,1,0:T(8,128)}) custom-call(bf16[2,1024,256]{2,1,0:T(8,128)(2,1)} %copy-done.8, bf16[3,3,256,256]{3,2,1,0:T(8,128)(2,1)} %refs_2_.5, bf16[2,1024,256]{2,1,0:T(8,128)(2,1)} %bitcast.15), custom_call_target="tpu_custom_call" | custom-call | flops 2415919104 | bytes 5242880 | tf_op jit(solution)/shard_map/pallas_call | solution.py:35
  54.3 9.7 %all-to-all-done.refs_0_ = bf16[16,192,128]{2,1,0:T(8,128)(2,1)S(1)} async-done(((bf16[16,192,128]{2,1,0:T(8,128)(2,1)}), bf16[16,192,128]{2,1,0:T(8,128)(2,1)S(1)}, u32[]{:S(2)}, u32[]{:S(2)}) %all-to-all-start) | async-done | bytes 786464 | tf_op jit(solution)/shard_map/all_to_all | solution.py:386
  65.1 6.2 %all-to-all-start.1 = ((bf16[8,192,128]{2,1,0:T(8,128)(2,1)}), bf16[8,192,128]{2,1,0:T(8,128)(2,1)S(1)}, u32[]{:S(2)}, u32[]{:S(2)}) async-start(bf16[8,192,128]{2,1,0:T(8,128)(2,1)} %shard_map.81), calls=%async_computation.1 | async-start | bytes 786432 | tf_op jit(solution)/shard_map/all_to_all | solution.py:386
  71.3 3.9 %collective-permute-start.8 = (bf16[2,128,256]{2,1,0:T(8,128)(2,1)S(1)}, bf16[2,128,256]{2,1,0:T(8,128)(2,1)S(1)}, u32[]{:S(2)}, u32[]{:S(2)}) collective-permute-start(bf16[2,128,256]{2,1,0:T(8,128)(2,1)S(1)} %get-tuple-element.48), channel_id=1, source_target_pairs={{0,1},{1,2},{2,3},{3,4},{4,5},{5,6},{6,7},{8,9},{9,10},{10,11},{11... | collective-permute-start | bytes 393224 | tf_op jit(solution)/shard_map/ppermute | solution.py:390
  75.2 1.9 %collective-permute-start.9 = (bf16[2,128,256]{2,1,0:T(8,128)(2,1)S(1)}, bf16[2,128,256]{2,1,0:T(8,128)(2,1)S(1)}, u32[]{:S(2)}, u32[]{:S(2)}) collective-permute-start(bf16[2,128,256]{2,1,0:T(8,128)(2,1)S(1)} %get-tuple-element.49), channel_id=1, source_target_pairs={{1,0},{2,1},{3,2},{4,3},{5,4},{6,5},{7,6},{9,8},{10,9},{11,10},{12... | collective-permute-start | bytes 393224 | tf_op jit(solution)/shard_map/ppermute | solution.py:390
  77.1 4.6 %collective-permute-done.9.refs_1_ = bf16[2,128,256]{2,1,0:T(8,128)(2,1)S(1)} collective-permute-done((bf16[2,128,256]{2,1,0:T(8,128)(2,1)S(1)}, bf16[2,128,256]{2,1,0:T(8,128)(2,1)S(1)}, u32[]{:S(2)}, u32[]{:S(2)}) %collective-permute-start.9) | collective-permute-done | bytes 131104 | tf_op jit(solution)/shard_map/ppermute | solution.py:390
  81.7 4.0 %all-to-all-done.1.refs_0_ = bf16[8,192,128]{2,1,0:T(8,128)(2,1)S(1)} async-done(((bf16[8,192,128]{2,1,0:T(8,128)(2,1)}), bf16[8,192,128]{2,1,0:T(8,128)(2,1)S(1)}, u32[]{:S(2)}, u32[]{:S(2)}) %all-to-all-start.1) | async-done | bytes 393248 | tf_op jit(solution)/shard_map/all_to_all | solution.py:386
  86.8 5.8 %all-to-all-start.2 = ((bf16[16,192,128]{2,1,0:T(8,128)(2,1)}), bf16[16,192,128]{2,1,0:T(8,128)(2,1)S(1)}, u32[]{:S(2)}, u32[]{:S(2)}) async-start(bf16[16,192,128]{2,1,0:T(8,128)(2,1)} %shard_map.82), calls=%async_computation.2 | async-start | bytes 1572864 | tf_op jit(solution)/shard_map/all_to_all | solution.py:386
  92.7 5.4 %shard_map.83 = bf16[2,1024,256]{2,1,0:T(8,128)(2,1)} custom-call(bf16[2,1024,256]{2,1,0:T(8,128)(2,1)} %get-tuple-element.47.refs_0_, bf16[2,1024,256]{2,1,0:T(8,128)(2,1)} %copy-done.4, bf16[3,256,256]{2,1,0:T(8,128)(2,1)} %refs_2_.4, bf16[2,1024,256]{2,1,0:T(8,128)(2,1)} %bitcast.9), custom_call_target="tpu_custom_call" | custom-call | flops 805306368 | bytes 4194304 | tf_op jit(solution)/shard_map/pallas_call | solution.py:35
  99.2 6.2 %all-to-all-done.2 = bf16[16,192,128]{2,1,0:T(8,128)(2,1)S(1)} async-done(((bf16[16,192,128]{2,1,0:T(8,128)(2,1)}), bf16[16,192,128]{2,1,0:T(8,128)(2,1)S(1)}, u32[]{:S(2)}, u32[]{:S(2)}) %all-to-all-start.2) | async-done | bytes 786464 | tf_op jit(solution)/shard_map/all_to_all | solution.py:386
  105.4 2.6 %collective-permute-start.10 = (bf16[3072,128]{1,0:T(8,128)(2,1)S(1)}, bf16[3072,128]{1,0:T(8,128)(2,1)S(1)}, u32[]{:S(2)}, u32[]{:S(2)}) collective-permute-start(bf16[3072,128]{1,0:T(8,128)(2,1)S(1)} %bitcast.12), channel_id=1, source_target_pairs={{0,1},{1,0},{2,3},{3,2},{4,5},{5,4},{6,7},{7,6},{8,9},{9,8},{10,11... | collective-permute-start | bytes 2359304 | tf_op jit(solution)/shard_map/ppermute | solution.py:535
  (35 shorter events, 11.7 us)
Async XLA Ops:
  0.6 25.5 %collective-permute-start = (bf16[2,1024,256]{2,1,0:T(8,128)(2,1)}, bf16[2,1024,256]{2,1,0:T(8,128)(2,1)S(1)}, u32[]{:S(2)}, u32[]{:S(2)}) collective-permute-start(bf16[2,1024,256]{2,1,0:T(8,128)(2,1)} %bitcast.14), channel_id=1, source_target_pairs={{8,0},{16,8},{24,16},{32,24},{40,32},{48,40},{56,48},{64,56},{72,6... | collective-permute-start | bytes 3145736 | tf_op jit(solution)/shard_map/ppermute | solution.py:401
  2.9 9.3 %collective-permute-start.1 = (bf16[2,128,256]{2,1,0:T(8,128)(2,1)S(1)}, bf16[2,128,256]{2,1,0:T(8,128)(2,1)S(1)}, u32[]{:S(2)}, u32[]{:S(2)}) collective-permute-start(bf16[2,128,256]{2,1,0:T(8,128)(2,1)S(1)} %get-tuple-element.63), channel_id=1, source_target_pairs={{0,1},{1,2},{2,3},{3,4},{4,5},{5,6},{6,7},{8,9},{9,10},{10,11},{11... | collective-permute-start | bytes 393224 | tf_op jit(solution)/shard_map/ppermute | solution.py:390
  7.4 6.6 %collective-permute-start.2 = (bf16[2,128,256]{2,1,0:T(8,128)(2,1)S(1)}, bf16[2,128,256]{2,1,0:T(8,128)(2,1)S(1)}, u32[]{:S(2)}, u32[]{:S(2)}) collective-permute-start(bf16[2,128,256]{2,1,0:T(8,128)(2,1)S(1)} %get-tuple-element.62), channel_id=1, source_target_pairs={{1,0},{2,1},{3,2},{4,3},{5,4},{6,5},{7,6},{9,8},{10,9},{11,10},{12... | collective-permute-start | bytes 393224 | tf_op jit(solution)/shard_map/ppermute | solution.py:390
  9.4 1.2 %copy-start = (bf16[1,2,8,128,256]{4,3,2,1,0:T(8,128)(2,1)S(1)}, bf16[1,2,8,128,256]{4,3,2,1,0:T(8,128)(2,1)}, u32[]{:S(2)}) copy-start(bf16[1,2,8,128,256]{4,3,2,1,0:T(8,128)(2,1)} %param.4) | copy-start | bytes 3145732
  10.6 1.3 %copy-start.1 = (bf16[3,3,256,256]{3,2,1,0:T(8,128)(2,1)S(1)}, bf16[3,3,256,256]{3,2,1,0:T(8,128)(2,1)}, u32[]{:S(2)}) copy-start(bf16[3,3,256,256]{3,2,1,0:T(8,128)(2,1)} %refs_2_.5) | copy-start | bytes 3538948
  11.9 2.1 %copy-start.2 = (bf16[3,3,256,256]{3,2,1,0:T(8,128)(2,1)S(1)}, bf16[3,3,256,256]{3,2,1,0:T(8,128)(2,1)}, u32[]{:S(2)}) copy-start(bf16[3,3,256,256]{3,2,1,0:T(8,128)(2,1)} %refs_2_.5) | copy-start | bytes 3538948
  12.2 11.1 %copy-start.5 = (bf16[3,256,256]{2,1,0:T(8,128)(2,1)S(1)}, bf16[3,256,256]{2,1,0:T(8,128)(2,1)}, u32[]{:S(2)}) copy-start(bf16[3,256,256]{2,1,0:T(8,128)(2,1)} %refs_2_.4) | copy-start | bytes 1179652
  12.2 11.1 %copy-start.7 = (bf16[1,2,8,128,256]{4,3,2,1,0:T(8,128)(2,1)S(1)}, bf16[1,2,8,128,256]{4,3,2,1,0:T(8,128)(2,1)}, u32[]{:S(2)}) copy-start(bf16[1,2,8,128,256]{4,3,2,1,0:T(8,128)(2,1)} %param.5) | copy-start | bytes 3145732
  19.0 45.0 %collective-permute-start.7 = (bf16[2,1024,256]{2,1,0:T(8,128)(2,1)}, bf16[2,1024,256]{2,1,0:T(8,128)(2,1)S(1)}, u32[]{:S(2)}, u32[]{:S(2)}) collective-permute-start(bf16[2,1024,256]{2,1,0:T(8,128)(2,1)} %get-tuple-element.47.refs_0_), channel_id=1, source_target_pairs={{0,8},{8,16},{16,24},{24,32},{32,40},{40,48},{48,56},{56,64},{64,7... | collective-permute-start | bytes 3145736 | tf_op jit(solution)/shard_map/ppermute | solution.py:431
  30.6 1.0 copy-start.8
  31.6 4.2 %collective-permute-start.3 = (bf16[768,128]{1,0:T(8,128)(2,1)S(1)}, bf16[768,128]{1,0:T(8,128)(2,1)S(1)}, u32[]{:S(2)}, u32[]{:S(2)}) collective-permute-start(bf16[768,128]{1,0:T(8,128)(2,1)S(1)} %get-tuple-element.40), channel_id=1, source_target_pairs={{0,1},{1,0},{2,3},{3,2},{4,5},{5,4},{6,7},{7,6},{8,9},{9,8},{10,11... | collective-permute-start | bytes 589832 | tf_op jit(solution)/shard_map/ppermute | solution.py:463
  34.7 1.4 %collective-permute-start.4 = (bf16[768,128]{1,0:T(8,128)(2,1)S(1)}, bf16[768,128]{1,0:T(8,128)(2,1)S(1)}, u32[]{:S(2)}, u32[]{:S(2)}) collective-permute-start(bf16[768,128]{1,0:T(8,128)(2,1)S(1)} %get-tuple-element.41), channel_id=1, source_target_pairs={{0,1},{1,0},{2,3},{3,2},{4,5},{5,4},{6,7},{7,6},{8,9},{9,8},{10,11... | collective-permute-start | bytes 589832 | tf_op jit(solution)/shard_map/ppermute | solution.py:463
  34.7 1.7 %collective-permute-start.5 = (bf16[768,128]{1,0:T(8,128)(2,1)S(1)}, bf16[768,128]{1,0:T(8,128)(2,1)S(1)}, u32[]{:S(2)}, u32[]{:S(2)}) collective-permute-start(bf16[768,128]{1,0:T(8,128)(2,1)S(1)} %get-tuple-element.42), channel_id=1, source_target_pairs={{0,1},{1,0},{2,3},{3,2},{4,5},{5,4},{6,7},{7,6},{8,9},{9,8},{10,11... | collective-permute-start | bytes 589832 | tf_op jit(solution)/shard_map/ppermute | solution.py:463
  35.2 1.5 %collective-permute-start.6 = (bf16[768,128]{1,0:T(8,128)(2,1)S(1)}, bf16[768,128]{1,0:T(8,128)(2,1)S(1)}, u32[]{:S(2)}, u32[]{:S(2)}) collective-permute-start(bf16[768,128]{1,0:T(8,128)(2,1)S(1)} %get-tuple-element.43), channel_id=1, source_target_pairs={{0,1},{1,0},{2,3},{3,2},{4,5},{5,4},{6,7},{7,6},{8,9},{9,8},{10,11... | collective-permute-start | bytes 589832 | tf_op jit(solution)/shard_map/ppermute | solution.py:463
  37.8 26.3 %all-to-all-start = ((bf16[16,192,128]{2,1,0:T(8,128)(2,1)}), bf16[16,192,128]{2,1,0:T(8,128)(2,1)S(1)}, u32[]{:S(2)}, u32[]{:S(2)}) async-start(bf16[16,192,128]{2,1,0:T(8,128)(2,1)} %bitcast.3), calls=%async_computation | async-start | bytes 1572864 | tf_op jit(solution)/shard_map/all_to_all | solution.py:386
  64.0 22.8 %copy-start.4 = (bf16[2,1024,256]{2,1,0:T(8,128)(2,1)}, bf16[2,1024,256]{2,1,0:T(8,128)(2,1)S(1)}, u32[]{:S(2)}) copy-start(bf16[2,1024,256]{2,1,0:T(8,128)(2,1)S(1)} %collective-permute-done.7.refs_1_) | copy-start | bytes 3145732
  65.1 20.7 %all-to-all-start.1 = ((bf16[8,192,128]{2,1,0:T(8,128)(2,1)}), bf16[8,192,128]{2,1,0:T(8,128)(2,1)S(1)}, u32[]{:S(2)}, u32[]{:S(2)}) async-start(bf16[8,192,128]{2,1,0:T(8,128)(2,1)} %shard_map.81), calls=%async_computation.1 | async-start | bytes 786432 | tf_op jit(solution)/shard_map/all_to_all | solution.py:386
  71.3 5.8 %collective-permute-start.8 = (bf16[2,128,256]{2,1,0:T(8,128)(2,1)S(1)}, bf16[2,128,256]{2,1,0:T(8,128)(2,1)S(1)}, u32[]{:S(2)}, u32[]{:S(2)}) collective-permute-start(bf16[2,128,256]{2,1,0:T(8,128)(2,1)S(1)} %get-tuple-element.48), channel_id=1, source_target_pairs={{0,1},{1,2},{2,3},{3,4},{4,5},{5,6},{6,7},{8,9},{9,10},{10,11},{11... | collective-permute-start | bytes 393224 | tf_op jit(solution)/shard_map/ppermute | solution.py:390
  75.2 6.6 %collective-permute-start.9 = (bf16[2,128,256]{2,1,0:T(8,128)(2,1)S(1)}, bf16[2,128,256]{2,1,0:T(8,128)(2,1)S(1)}, u32[]{:S(2)}, u32[]{:S(2)}) collective-permute-start(bf16[2,128,256]{2,1,0:T(8,128)(2,1)S(1)} %get-tuple-element.49), channel_id=1, source_target_pairs={{1,0},{2,1},{3,2},{4,3},{5,4},{6,5},{7,6},{9,8},{10,9},{11,10},{12... | collective-permute-start | bytes 393224 | tf_op jit(solution)/shard_map/ppermute | solution.py:390
  86.8 18.6 %all-to-all-start.2 = ((bf16[16,192,128]{2,1,0:T(8,128)(2,1)}), bf16[16,192,128]{2,1,0:T(8,128)(2,1)S(1)}, u32[]{:S(2)}, u32[]{:S(2)}) async-start(bf16[16,192,128]{2,1,0:T(8,128)(2,1)} %shard_map.82), calls=%async_computation.2 | async-start | bytes 1572864 | tf_op jit(solution)/shard_map/all_to_all | solution.py:386
  92.6 5.5 %copy-start.3 = (bf16[3,3,256,256]{3,2,1,0:T(8,128)(2,1)S(1)}, bf16[3,3,256,256]{3,2,1,0:T(8,128)(2,1)}, u32[]{:S(2)}) copy-start(bf16[3,3,256,256]{3,2,1,0:T(8,128)(2,1)} %refs_2_.5) | copy-start | bytes 3538948
  92.7 5.5 %copy-start.6 = (f32[2,2,128,256]{3,2,1,0:T(8,128)S(1)}, f32[2,2,128,256]{3,2,1,0:T(8,128)}, u32[]{:S(2)}) copy-start(f32[2,2,128,256]{3,2,1,0:T(8,128)} %get-tuple-element.53.refs_3_) | copy-start | bytes 1572868
  105.4 4.5 %collective-permute-start.10 = (bf16[3072,128]{1,0:T(8,128)(2,1)S(1)}, bf16[3072,128]{1,0:T(8,128)(2,1)S(1)}, u32[]{:S(2)}, u32[]{:S(2)}) collective-permute-start(bf16[3072,128]{1,0:T(8,128)(2,1)S(1)} %bitcast.12), channel_id=1, source_target_pairs={{0,1},{1,0},{2,3},{3,2},{4,5},{5,4},{6,7},{7,6},{8,9},{9,8},{10,11... | collective-permute-start | bytes 2359304 | tf_op jit(solution)/shard_map/ppermute | solution.py:535

commit v11 on v10

--- a/solution.py
+++ b/solution.py
@@ -11,7 +11,6 @@
 F32 = jnp.float32
 TM = ("y", "zl")
 SPACE = ("x", "core")
-PLANE = ("x", "y")
 COLUMN = ("clip", "zl")
 COLS = 128
 NT = (((1,), (1,)), ((), ()))
@@ -74,7 +73,7 @@
     padded[frame, COLS + size :, :] = bottom[frame]
 
 
-def turn_kernel(x, weight, x_t):
+def turn_kernel(x, x_t):
     for f in range(x.shape[0]):
         x_t[f] = x[f].T
 
@@ -211,33 +210,54 @@
         store.wait()
 
 
-def add_kernel(a, *refs):
-    out = refs[-1]
-    cut = refs[0].shape[0]
-    for n, b in enumerate(refs[:-1]):
+def deal(place, total, own, outs):
+    size = own.shape[0]
+    count = len(outs) + 1
+    for d in range(count):
+        at = pl.multiple_of(lax.rem(place[0] + d, count) * size, size)
+        block = total[pl.ds(at, size), :]
+        if d:
+            outs[d - 1][...] = block.astype(BF)
+        else:
+            own[...] = block
+
+
+def add_kernel(place, a, *refs):
+    parts, (own, *outs), total = refs[:SWAPS], refs[SWAPS:-1], refs[-1]
+    cut = parts[0].shape[0]
+    for n, b in enumerate(parts):
         rows = pl.ds(n * cut, cut)
-        out[rows, :] = (a[rows, :].astype(F32) + b[...].astype(F32)).astype(BF)
-
-
-def sum_kernel(parts, out):
+        total[rows, :] = a[rows, :].astype(F32) + b[...].astype(F32)
+    deal(place, total, own, outs)
+
+
+def sum_deal_kernel(place, a, b, c, d, own, *refs):
+    outs, total = refs[:-1], refs[-1]
+    total[...] = a[...] + b[...].astype(F32) + c[...].astype(F32) + d[...].astype(F32)
+    deal(place, total, own, outs)
+
+
+def sum_spread_kernel(a, b, c, d, out):
+    total = a[...] + b[...].astype(F32) + c[...].astype(F32) + d[...].astype(F32)
+    total = total.astype(BF)
+    for i in range(out.shape[0]):
+        out[i] = total
+
+
+def sum_kernel(scale, parts, out):
     total = parts[0].astype(F32)
     for i in range(1, parts.shape[0]):
         total = total + parts[i].astype(F32)
-    out[...] = total.astype(out.dtype)
-
-
-def spread_sum_kernel(scale, parts, out, sent, sems):
-    total = parts[0].astype(F32)
-    for i in range(1, parts.shape[0]):
-        total = total + parts[i].astype(F32)
-    sent[...] = (total * scale).astype(sent.dtype)
-    copies = [
-        pltpu.make_async_copy(sent, out.at[i], sems.at[i]) for i in range(out.shape[0])
-    ]
-    for copy in copies:
-        copy.start()
-    for copy in copies:
-        copy.wait()
+    out[...] = (total * scale).astype(out.dtype)
+
+
+def collect_kernel(place, *refs):
+    blocks, out = refs[:-1], refs[-1]
+    size = blocks[0].shape[0]
+    count = len(blocks)
+    for d, block in enumerate(blocks):
+        at = pl.multiple_of(lax.rem(place[0] + count - d, count) * size, size)
+        out[pl.ds(at, size), :] = block[...]
 
 
 def write_half(first, source, spatial, temporal, wide, sems):
@@ -382,6 +402,15 @@
     return [(i, i + by) for i in range(count) if 0 <= i + by < count]
 
 
+def ring(value, axis):
+    count = lax.axis_size(axis)
+    values = value if isinstance(value, list) else [value] * (count - 1)
+    return [
+        lax.ppermute(part, axis, [(i, (i + d) % count) for i in range(count)])
+        for d, part in enumerate(values, 1)
+    ]
+
+
 def exchange(value, axes):
     return lax.all_to_all(value, axes, split_axis=0, concat_axis=0, tiled=True)
 
@@ -400,13 +429,7 @@
     core = lax.axis_index("core").astype(jnp.int32).reshape(1)
     ahead = lax.ppermute(dy, TM, steps(TM, -1))
     top, bottom = swap_rims(x[:, size - COLS :, :], x[:, :COLS, :])
-    x_t = call(
-        turn_kernel,
-        shape((frames, chans, size)),
-        (x, spatial_weight),
-        flops=1 << 20,
-        moved=2 << 20,
-    )
+    x_t = call(turn_kernel, shape((frames, chans, size)), (x,), flops=1 << 20, moved=2 << 20)
     act, slope, top_t, bottom_t, act_t = call(
         forward_kernel,
         [
@@ -461,11 +484,17 @@
     grad_top, grad_bottom = swap_rims(last, first)
     pair = [(0, 1), (1, 0)]
     got = [lax.ppermute(part, "core", pair) for part in send]
-    half = call(add_kernel, shape((rows, 128)), (keep, *got), moved=1 << 12)
+    at_x = lax.axis_index("x").astype(jnp.int32).reshape(1)
+    at_y = lax.axis_index("y").astype(jnp.int32).reshape(1)
     block = pltpu.VMEM((frames, size, chans), BF)
-    column, plane = lax.axis_size(COLUMN), lax.axis_size(PLANE)
-    share = rows // plane
-    first = exchange(half.reshape(plane, share, 128), PLANE)
+    column = lax.axis_size(COLUMN)
+    quarter = rows // lax.axis_size("x")
+    share = quarter // lax.axis_size("y")
+    dealt = [shape((quarter, 128), F32)] + [shape((quarter, 128))] * 3
+    own, *out = call(
+        add_kernel, dealt, (at_x, keep, *got), [pltpu.VMEM((rows, 128), F32)], moved=1 << 12, smem=(0,)
+    )
+    first = ring(out, "x")
     inner, edge = call(
         back_kernel,
         [shape((frames, size, chans)), shape((frames, 2, COLS, chans), F32)],
@@ -477,23 +506,38 @@
             block,
             pltpu.SemaphoreType.DMA((7,)),
         ],
-        flops=9 * work,
-        moved=5 << 20,
+        flops=1 << 10,
+        moved=1 << 12,
         hbm=range(3),
         out_hbm=(0,),
         limit=58,
     )
-    first, edge = lax.optimization_barrier((first, edge))
+    first[0], edge = lax.optimization_barrier((first[0], edge))
+    dealt = [shape((share, 128), F32)] + [shape((share, 128))] * 3
+    own, *out = call(
+        sum_deal_kernel,
+        dealt,
+        (at_y, own, *first),
+        [pltpu.VMEM((quarter, 128), F32)],
+        moved=1 << 12,
+        smem=(0,),
+    )
+    second = ring(out, "y")
+    second[0], grad_top, grad_bottom = lax.optimization_barrier((second[0], grad_top, grad_bottom))
     spread = call(
-        functools.partial(spread_sum_kernel, 1.0),
+        sum_spread_kernel,
         shape((column, share, 128)),
-        (first,),
-        [pltpu.VMEM((share, 128), BF), pltpu.SemaphoreType.DMA((column,))],
+        (own, *second),
         moved=1 << 12,
-        out_hbm=(0,),
         after=(behind,),
     )
     third = exchange(spread, COLUMN)
+    total = call(functools.partial(sum_kernel, scale), shape((share, 128)), (third,), moved=1 << 12)
+    fourth = ring(total, "y")
+    wider = call(
+        collect_kernel, shape((quarter, 128)), (at_y, total, *fourth), moved=1 << 12, smem=(0,)
+    )
+    fifth = ring(wider, "x")
     block_out = call(
         mix_kernel,
         shape((frames, size, chans)),
@@ -510,7 +554,6 @@
         out_hbm=True,
         limit=58,
     )
-    third, grad_top, grad_bottom = lax.optimization_barrier((third, grad_top, grad_bottom))
     input_grad = call(
         edge_kernel,
         shape((frames, size, chans)),
@@ -522,16 +565,10 @@
         out_hbm=True,
         alias={4: 0},
     )
-    wider = call(
-        functools.partial(spread_sum_kernel, scale),
-        shape((plane, share, 128)),
-        (third,),
-        [pltpu.VMEM((share, 128), BF), pltpu.SemaphoreType.DMA((plane,))],
-        moved=1 << 12,
-        out_hbm=(0,),
-    )
-    own = exchange(wider, PLANE).reshape(rows, 128)
-    own, block_out, input_grad = lax.optimization_barrier((own, block_out, input_grad))
+    fifth[0], block_out, input_grad = lax.optimization_barrier((fifth[0], block_out, input_grad))
+    own = call(
+        collect_kernel, shape((rows, 128)), (at_x, wider, *fifth), moved=1 << 12, smem=(0,)
+    )
     other = lax.ppermute(own, "core", pair)
     grads = [shape((9, chans, chans), F32), shape((3, chans, chans), F32)]
     room = [pltpu.VMEM((6, chans, chans), F32), pltpu.SemaphoreType.DMA((6,))]

time: 112 us -> 119 us (1.062)
  blocking collectives: 0 us -> 19 us
  waiting for transfers between devices: 29.9 us -> 12.6 us
  local copies, waits for them, and re-layouts: 4.48 us -> 9.69 us
    all_to_all x3 -> x0, starting transfers between devices: 22 us -> none  [exchange(): return lax.all_to_all(value, axes, split_axis=0, concat_axis=0, tiled=True)]
    ppermute x0 -> x12, starting transfers between devices: none -> 20.2 us  [ring(): lax.ppermute(part, axis, [(i, (i + d) % count) for i in range(count)])]
    all_to_all x3 -> x0, waiting for transfers between devices: 19.9 us -> none  [exchange(): return lax.all_to_all(value, axes, split_axis=0, concat_axis=0, tiled=True)]
    all_to_all x0 -> x1, blocking collectives: none -> 19 us  [exchange(): return lax.all_to_all(value, axes, split_axis=0, concat_axis=0, tiled=True)]
    ppermute x0 -> x12, waiting for transfers between devices: none -> 5.86 us  [ring(): lax.ppermute(part, axis, [(i, (i + d) % count) for i in range(count)])]
    unnamed x18 -> x38, local copies, waits for them, and re-layouts: 3.49 us -> 8.7 us
    ppermute x2, starting transfers between devices: 3.86 us -> 8.94 us  [swap_rims(): lax.ppermute(first, SPACE, steps(SPACE, -1))]
    ppermute x4, starting transfers between devices: 3.65 us -> 0.85 us  [local(): got = [lax.ppermute(part, 'core', pair) for part in send]]
  transfers between devices with their start and end apart: 14 -> 23, of which waited for: 11 -> 10; matrix products, arithmetic and copies ran while one was open for 1% -> 1% of each run, Pallas kernels for 24% -> 23%
where the time goes in v11:
time: 119 us; the launch traced here: 118 us
  starting transfers between devices  47 us (39%)
  Pallas kernels  29 us (24%)
  blocking collectives  19 us (16%)
  waiting for transfers between devices  12.6 us (11%)
  local copies, waits for them, and re-layouts  9.69 us (8%)
    pallas_call x15, Pallas kernels, call(): pl.pallas_call(body, out_shape=outs, in_specs=specs, out_specs=placed if...  29 us
    ppermute x12, starting transfers between devices, ring(): lax.ppermute(part, axis, [(i, (i + d) % count) for i in range(count)])  20.2 us
    all_to_all x1, blocking collectives, exchange(): return lax.all_to_all(value, axes, split_axis=0, concat_axis=0, tiled=True)  19 us
    ppermute x2, starting transfers between devices, swap_rims(): lax.ppermute(first, SPACE, steps(SPACE, -1))  8.94 us
    unnamed x38, local copies, waits for them, and re-layouts  8.7 us
    ppermute x2, starting transfers between devices, swap_rims(): lax.ppermute(last, SPACE, steps(SPACE, 1))  6.57 us
    ppermute x12, waiting for transfers between devices, ring(): lax.ppermute(part, axis, [(i, (i + d) % count) for i in range(count)])  5.86 us
    ppermute x2, waiting for transfers between devices, swap_rims(): lax.ppermute(first, SPACE, steps(SPACE, -1))  4.73 us
  transfers between devices with their start and end apart: 23, of which 10 were waited for; matrix products, arithmetic and copies ran while one was open for 1% of the time, Pallas kernels for 23%

profile of v11, /device:TPU:1, one launch (start us, length us, event | category | flops | bytes accessed | tf_op | source)
XLA Modules:
  0.0 118.4 jit_solution(15248749612246885303)
XLA Ops:
  0.6 1.3 %collective-permute-start = (bf16[2,1024,256]{2,1,0:T(8,128)(2,1)}, bf16[2,1024,256]{2,1,0:T(8,128)(2,1)}, u32[]{:S(2)}, u32[]{:S(2)}) collective-permute-start(bf16[2,1024,256]{2,1,0:T(8,128)(2,1)} %bitcast.12), channel_id=1, source_target_pairs={{8,0},{16,8},{24,16},{32,24},{40,32},{48,40},{56,48},{64,56},{72,6... | collective-permute-start | bytes 3145736 | tf_op jit(solution)/shard_map/ppermute | solution.py:430
  2.9 4.5 %collective-permute-start.1 = (bf16[2,128,256]{2,1,0:T(8,128)(2,1)S(1)}, bf16[2,128,256]{2,1,0:T(8,128)(2,1)S(1)}, u32[]{:S(2)}, u32[]{:S(2)}) collective-permute-start(bf16[2,128,256]{2,1,0:T(8,128)(2,1)S(1)} %get-tuple-element.79), channel_id=1, source_target_pairs={{0,1},{1,2},{2,3},{3,4},{4,5},{5,6},{6,7},{8,9},{9,10},{10,11},{11... | collective-permute-start | bytes 393224 | tf_op jit(solution)/shard_map/ppermute | solution.py:419
  7.4 1.9 %collective-permute-start.2 = (bf16[2,128,256]{2,1,0:T(8,128)(2,1)S(1)}, bf16[2,128,256]{2,1,0:T(8,128)(2,1)S(1)}, u32[]{:S(2)}, u32[]{:S(2)}) collective-permute-start(bf16[2,128,256]{2,1,0:T(8,128)(2,1)S(1)} %get-tuple-element.78), channel_id=1, source_target_pairs={{1,0},{2,1},{3,2},{4,3},{5,4},{6,5},{7,6},{9,8},{10,9},{11,10},{12... | collective-permute-start | bytes 393224 | tf_op jit(solution)/shard_map/ppermute | solution.py:419
  9.4 4.7 %collective-permute-done.2.refs_2_ = bf16[2,128,256]{2,1,0:T(8,128)(2,1)S(1)} collective-permute-done((bf16[2,128,256]{2,1,0:T(8,128)(2,1)S(1)}, bf16[2,128,256]{2,1,0:T(8,128)(2,1)S(1)}, u32[]{:S(2)}, u32[]{:S(2)}) %collective-permute-start.2) | collective-permute-done | bytes 131104 | tf_op jit(solution)/shard_map/ppermute | solution.py:419
  16.6 5.0 %shard_map.75 = (bf16[2,1024,256]{2,1,0:T(8,128)(2,1)}, f32[2,1024,256]{2,1,0:T(8,128)S(1)}, bf16[2,256,128]{2,1,0:T(8,128)(2,1)S(1)}, bf16[2,256,128]{2,1,0:T(8,128)(2,1)S(1)}, bf16[2,256,1024]{2,1,0:T(8,128)(2,1)S(1)}) custom-call(bf16[2,1024,256]{2,1,0:T(8,128)(2,1)S(1)} %bitcast.10, bf16[2,128,256]{2,1,0:T(8,128)(2,1)S(1)} %collective-permute-done.1.refs_1_, ...), custom_call_target="tpu_custom_call" | custom-call | flops 2415919104 | bytes 9437184 | tf_op jit(solution)/shard_map/pallas_call | solution.py:34
  21.6 1.3 %copy-done.5 = f32[2,1024,256]{2,1,0:T(8,128)} copy-done((f32[2,1024,256]{2,1,0:T(8,128)}, f32[2,1024,256]{2,1,0:T(8,128)S(1)}, u32[]{:S(2)}) %copy-start.5) | copy-done | bytes 2097176
  25.2 4.5 %collective-permute-start.15 = (bf16[2,1024,256]{2,1,0:T(8,128)(2,1)}, bf16[2,1024,256]{2,1,0:T(8,128)(2,1)S(1)}, u32[]{:S(2)}, u32[]{:S(2)}) collective-permute-start(bf16[2,1024,256]{2,1,0:T(8,128)(2,1)} %get-tuple-element.66.refs_0_), channel_id=1, source_target_pairs={{0,8},{8,16},{16,24},{24,32},{32,40},{40,48},{48,56},{56,64},{64,7... | collective-permute-start | bytes 3145736 | tf_op jit(solution)/shard_map/ppermute | solution.py:454
  31.3 1.4 %shard_map.77 = (f32[2,1024,256]{2,1,0:T(8,128)S(1)}, f32[2,256,256]{2,1,0:T(8,128)S(1)}) custom-call(bf16[2,1024,256]{2,1,0:T(8,128)(2,1)S(1)} %bitcast.14, bf16[3,256,256]{2,1,0:T(8,128)(2,1)S(1)} %copy-done.7, bf16[2,256,1024]{2,1,0:T(8,128)(2,1)S(1)} %copy-done.11), custom_call_target="tpu_custom_call" | custom-call | flops 1610612736 | bytes 6291456 | tf_op jit(solution)/shard_map/pallas_call | solution.py:34
  32.9 6.4 %shard_map.78 = (bf16[2,1024,256]{2,1,0:T(8,128)(2,1)S(1)}, bf16[3072,128]{1,0:T(8,128)(2,1)S(1)}, bf16[2,128,256]{2,1,0:T(8,128)(2,1)S(1)}, bf16[2,128,256]{2,1...) custom-call(s32[1]{0:T(128)} %bitcast.2.refs_0_, ...), custom_call_target="tpu_custom_call" | custom-call | flops 1024 | bytes 4096 | tf_op jit(solution)/shard_map/pallas_call | solution.py:34
  42.9 1.3 %collective-permute-start.7 = (bf16[768,128]{1,0:T(8,128)(2,1)S(1)}, bf16[768,128]{1,0:T(8,128)(2,1)S(1)}, u32[]{:S(2)}, u32[]{:S(2)}) collective-permute-start(bf16[768,128]{1,0:T(8,128)(2,1)S(1)} %get-tuple-element.53), channel_id=1, source_target_pairs={{0,2},{2,4},{4,6},{6,0},{1,3},{3,5},{5,7},{7,1},{8,10},{10,12},{12... | collective-permute-start | bytes 589832 | tf_op jit(solution)/shard_map/ppermute | solution.py:409
  44.2 1.3 %collective-permute-start.8 = (bf16[768,128]{1,0:T(8,128)(2,1)S(1)}, bf16[768,128]{1,0:T(8,128)(2,1)S(1)}, u32[]{:S(2)}, u32[]{:S(2)}) collective-permute-start(bf16[768,128]{1,0:T(8,128)(2,1)S(1)} %get-tuple-element.57), channel_id=1, source_target_pairs={{0,4},{2,6},{4,0},{6,2},{1,5},{3,7},{5,1},{7,3},{8,12},{10,14},{12... | collective-permute-start | bytes 589832 | tf_op jit(solution)/shard_map/ppermute | solution.py:409
  45.5 2.0 %collective-permute-start.9 = (bf16[768,128]{1,0:T(8,128)(2,1)S(1)}, bf16[768,128]{1,0:T(8,128)(2,1)S(1)}, u32[]{:S(2)}, u32[]{:S(2)}) collective-permute-start(bf16[768,128]{1,0:T(8,128)(2,1)S(1)} %get-tuple-element.58), channel_id=1, source_target_pairs={{0,6},{2,0},{4,2},{6,4},{1,7},{3,1},{5,3},{7,5},{8,14},{10,8},{12,... | collective-permute-start | bytes 589832 | tf_op jit(solution)/shard_map/ppermute | solution.py:409
  47.5 2.1 %collective-permute-start.11 = (bf16[2,128,256]{2,1,0:T(8,128)(2,1)}, bf16[2,128,256]{2,1,0:T(8,128)(2,1)S(1)}, u32[]{:S(2)}, u32[]{:S(2)}) collective-permute-start(bf16[2,128,256]{2,1,0:T(8,128)(2,1)} %copy-done.18), channel_id=1, source_target_pairs={{0,1},{1,2},{2,3},{3,4},{4,5},{5,6},{6,7},{8,9},{9,10},{10,11},{11... | collective-permute-start | bytes 393224 | tf_op jit(solution)/shard_map/ppermute | solution.py:419
  50.4 7.0 %collective-permute-start.12 = (bf16[2,128,256]{2,1,0:T(8,128)(2,1)}, bf16[2,128,256]{2,1,0:T(8,128)(2,1)S(1)}, u32[]{:S(2)}, u32[]{:S(2)}) collective-permute-start(bf16[2,128,256]{2,1,0:T(8,128)(2,1)} %copy-done.17), channel_id=1, source_target_pairs={{1,0},{2,1},{3,2},{4,3},{5,4},{6,5},{7,6},{9,8},{10,9},{11,10},{12... | collective-permute-start | bytes 393224 | tf_op jit(solution)/shard_map/ppermute | solution.py:419
  57.5 6.5 %shard_map.80 = (bf16[2,1024,256]{2,1,0:T(8,128)(2,1)}, f32[2,2,128,256]{3,2,1,0:T(8,128)}) custom-call(bf16[2,1024,256]{2,1,0:T(8,128)(2,1)} %copy-done.9, bf16[3,3,256,256]{3,2,1,0:T(8,128)(2,1)} %refs_2_.5, bf16[2,1024,256]{2,1,0:T(8,128)(2,1)} %bitcast.13), custom_call_target="tpu_custom_call" | custom-call | flops 1024 | bytes 4096 | tf_op jit(solution)/shard_map/pallas_call | solution.py:34
  64.1 4.3 %collective-permute-start.10 = (bf16[192,128]{1,0:T(8,128)(2,1)S(1)}, bf16[192,128]{1,0:T(8,128)(2,1)S(1)}, u32[]{:S(2)}, u32[]{:S(2)}) collective-permute-start(bf16[192,128]{1,0:T(8,128)(2,1)S(1)} %get-tuple-element.60), channel_id=1, source_target_pairs={{0,32},{32,64},{64,96},{96,0},{1,33},{33,65},{65,97},{97,1},{2,34}... | collective-permute-start | bytes 147464 | tf_op jit(solution)/shard_map/ppermute | solution.py:409
  68.4 2.9 %collective-permute-start.13 = (bf16[192,128]{1,0:T(8,128)(2,1)S(1)}, bf16[192,128]{1,0:T(8,128)(2,1)S(1)}, u32[]{:S(2)}, u32[]{:S(2)}) collective-permute-start(bf16[192,128]{1,0:T(8,128)(2,1)S(1)} %get-tuple-element.64), channel_id=1, source_target_pairs={{0,64},{32,96},{64,0},{96,32},{1,65},{33,97},{65,1},{97,33},{2,66}... | collective-permute-start | bytes 147464 | tf_op jit(solution)/shard_map/ppermute | solution.py:409
  72.1 2.2 %collective-permute-done.13.refs_2_ = bf16[192,128]{1,0:T(8,128)(2,1)S(1)} collective-permute-done((bf16[192,128]{1,0:T(8,128)(2,1)S(1)}, bf16[192,128]{1,0:T(8,128)(2,1)S(1)}, u32[]{:S(2)}, u32[]{:S(2)}) %collective-permute-start.13) | collective-permute-done | bytes 49184 | tf_op jit(solution)/shard_map/ppermute | solution.py:409
  74.8 19.0 %all_to_all.5.refs_0_ = bf16[8,192,128]{2,1,0:T(8,128)(2,1)S(1)} all-to-all(bf16[8,192,128]{2,1,0:T(8,128)(2,1)S(1)} %shard_map.82), channel_id=1, replica_groups=mesh['clip'=2,'y'=4,'zl'=4,'x'=4,'core'=2] {'clip','zl'}, dimensions={0} | all-to-all | bytes 786432 | tf_op jit(solution)/shard_map/all_to_all | solution.py:415
  95.0 3.1 %collective-permute-start.17 = (bf16[192,128]{1,0:T(8,128)(2,1)S(1)}, bf16[192,128]{1,0:T(8,128)(2,1)S(1)}, u32[]{:S(2)}, u32[]{:S(2)}) collective-permute-start(bf16[192,128]{1,0:T(8,128)(2,1)S(1)} %shard_map.83.refs_1_), channel_id=1, source_target_pairs={{0,64},{32,96},{64,0},{96,32},{1,65},{33,97},{65,1},{97,33},{2,66}... | collective-permute-start | bytes 147464 | tf_op jit(solution)/shard_map/ppermute | solution.py:409
  98.8 1.3 %collective-permute-done.17.refs_3_ = bf16[192,128]{1,0:T(8,128)(2,1)S(1)} collective-permute-done((bf16[192,128]{1,0:T(8,128)(2,1)S(1)}, bf16[192,128]{1,0:T(8,128)(2,1)S(1)}, u32[]{:S(2)}, u32[]{:S(2)}) %collective-permute-start.17) | collective-permute-done | bytes 49184 | tf_op jit(solution)/shard_map/ppermute | solution.py:409
  101.3 2.6 %collective-permute-start.21 = (bf16[768,128]{1,0:T(8,128)(2,1)S(1)}, bf16[768,128]{1,0:T(8,128)(2,1)S(1)}, u32[]{:S(2)}, u32[]{:S(2)}) collective-permute-start(bf16[768,128]{1,0:T(8,128)(2,1)S(1)} %shard_map.84.refs_1_), channel_id=1, source_target_pairs={{0,6},{2,0},{4,2},{6,4},{1,7},{3,1},{5,3},{7,5},{8,14},{10,8},{12,... | collective-permute-start | bytes 589832 | tf_op jit(solution)/shard_map/ppermute | solution.py:409
  103.9 5.3 %shard_map.85 = bf16[2,1024,256]{2,1,0:T(8,128)(2,1)} custom-call(bf16[2,1024,256]{2,1,0:T(8,128)(2,1)} %get-tuple-element.66.refs_0_, bf16[2,1024,256]{2,1,0:T(8,128)(2,1)} %copy-done.4, bf16[3,256,256]{2,1,0:T(8,128)(2,1)} %refs_2_.4, bf16[2,1024,256]{2,1,0:T(8,128)(2,1)} %bitcast.9), custom_call_target="tpu_custom_call" | custom-call | flops 805306368 | bytes 4194304 | tf_op jit(solution)/shard_map/pallas_call | solution.py:34
  110.4 4.7 %collective-permute-start.22 = (bf16[3072,128]{1,0:T(8,128)(2,1)S(1)}, bf16[3072,128]{1,0:T(8,128)(2,1)S(1)}, u32[]{:S(2)}, u32[]{:S(2)}) collective-permute-start(bf16[3072,128]{1,0:T(8,128)(2,1)S(1)} %shard_map.87.refs_1_), channel_id=1, source_target_pairs={{0,1},{1,0},{2,3},{3,2},{4,5},{5,4},{6,7},{7,6},{8,9},{9,8},{10,11... | collective-permute-start | bytes 2359304 | tf_op jit(solution)/shard_map/ppermute | solution.py:572
  (77 shorter events, 20.7 us)
Async XLA Ops:
  0.6 32.1 %collective-permute-start = (bf16[2,1024,256]{2,1,0:T(8,128)(2,1)}, bf16[2,1024,256]{2,1,0:T(8,128)(2,1)}, u32[]{:S(2)}, u32[]{:S(2)}) collective-permute-start(bf16[2,1024,256]{2,1,0:T(8,128)(2,1)} %bitcast.12), channel_id=1, source_target_pairs={{8,0},{16,8},{24,16},{32,24},{40,32},{48,40},{56,48},{64,56},{72,6... | collective-permute-start | bytes 3145736 | tf_op jit(solution)/shard_map/ppermute | solution.py:430
  2.9 6.5 %collective-permute-start.1 = (bf16[2,128,256]{2,1,0:T(8,128)(2,1)S(1)}, bf16[2,128,256]{2,1,0:T(8,128)(2,1)S(1)}, u32[]{:S(2)}, u32[]{:S(2)}) collective-permute-start(bf16[2,128,256]{2,1,0:T(8,128)(2,1)S(1)} %get-tuple-element.79), channel_id=1, source_target_pairs={{0,1},{1,2},{2,3},{3,4},{4,5},{5,6},{6,7},{8,9},{9,10},{10,11},{11... | collective-permute-start | bytes 393224 | tf_op jit(solution)/shard_map/ppermute | solution.py:419
  7.4 6.7 %collective-permute-start.2 = (bf16[2,128,256]{2,1,0:T(8,128)(2,1)S(1)}, bf16[2,128,256]{2,1,0:T(8,128)(2,1)S(1)}, u32[]{:S(2)}, u32[]{:S(2)}) collective-permute-start(bf16[2,128,256]{2,1,0:T(8,128)(2,1)S(1)} %get-tuple-element.78), channel_id=1, source_target_pairs={{1,0},{2,1},{3,2},{4,3},{5,4},{6,5},{7,6},{9,8},{10,9},{11,10},{12... | collective-permute-start | bytes 393224 | tf_op jit(solution)/shard_map/ppermute | solution.py:419
  25.2 46.9 %collective-permute-start.15 = (bf16[2,1024,256]{2,1,0:T(8,128)(2,1)}, bf16[2,1024,256]{2,1,0:T(8,128)(2,1)S(1)}, u32[]{:S(2)}, u32[]{:S(2)}) collective-permute-start(bf16[2,1024,256]{2,1,0:T(8,128)(2,1)} %get-tuple-element.66.refs_0_), channel_id=1, source_target_pairs={{0,8},{8,16},{16,24},{24,32},{32,40},{40,48},{48,56},{56,64},{64,7... | collective-permute-start | bytes 3145736 | tf_op jit(solution)/shard_map/ppermute | solution.py:454
  40.3 1.7 %collective-permute-start.3 = (bf16[768,128]{1,0:T(8,128)(2,1)}, bf16[768,128]{1,0:T(8,128)(2,1)S(1)}, u32[]{:S(2)}, u32[]{:S(2)}) collective-permute-start(bf16[768,128]{1,0:T(8,128)(2,1)} %get-tuple-element.48), channel_id=1, source_target_pairs={{0,1},{1,0},{2,3},{3,2},{4,5},{5,4},{6,7},{7,6},{8,9},{9,8},{10,11... | collective-permute-start | bytes 589832 | tf_op jit(solution)/shard_map/ppermute | solution.py:486
  40.3 2.0 %collective-permute-start.4 = (bf16[768,128]{1,0:T(8,128)(2,1)}, bf16[768,128]{1,0:T(8,128)(2,1)S(1)}, u32[]{:S(2)}, u32[]{:S(2)}) collective-permute-start(bf16[768,128]{1,0:T(8,128)(2,1)} %get-tuple-element.49), channel_id=1, source_target_pairs={{0,1},{1,0},{2,3},{3,2},{4,5},{5,4},{6,7},{7,6},{8,9},{9,8},{10,11... | collective-permute-start | bytes 589832 | tf_op jit(solution)/shard_map/ppermute | solution.py:486
  40.8 1.5 %collective-permute-start.5 = (bf16[768,128]{1,0:T(8,128)(2,1)S(1)}, bf16[768,128]{1,0:T(8,128)(2,1)S(1)}, u32[]{:S(2)}, u32[]{:S(2)}) collective-permute-start(bf16[768,128]{1,0:T(8,128)(2,1)S(1)} %get-tuple-element.50), channel_id=1, source_target_pairs={{0,1},{1,0},{2,3},{3,2},{4,5},{5,4},{6,7},{7,6},{8,9},{9,8},{10,11... | collective-permute-start | bytes 589832 | tf_op jit(solution)/shard_map/ppermute | solution.py:486
  41.0 1.6 %collective-permute-start.6 = (bf16[768,128]{1,0:T(8,128)(2,1)S(1)}, bf16[768,128]{1,0:T(8,128)(2,1)S(1)}, u32[]{:S(2)}, u32[]{:S(2)}) collective-permute-start(bf16[768,128]{1,0:T(8,128)(2,1)S(1)} %get-tuple-element.51), channel_id=1, source_target_pairs={{0,1},{1,0},{2,3},{3,2},{4,5},{5,4},{6,7},{7,6},{8,9},{9,8},{10,11... | collective-permute-start | bytes 589832 | tf_op jit(solution)/shard_map/ppermute | solution.py:486
  42.9 7.6 %collective-permute-start.7 = (bf16[768,128]{1,0:T(8,128)(2,1)S(1)}, bf16[768,128]{1,0:T(8,128)(2,1)S(1)}, u32[]{:S(2)}, u32[]{:S(2)}) collective-permute-start(bf16[768,128]{1,0:T(8,128)(2,1)S(1)} %get-tuple-element.53), channel_id=1, source_target_pairs={{0,2},{2,4},{4,6},{6,0},{1,3},{3,5},{5,7},{7,1},{8,10},{10,12},{12... | collective-permute-start | bytes 589832 | tf_op jit(solution)/shard_map/ppermute | solution.py:409
  44.2 19.8 %collective-permute-start.8 = (bf16[768,128]{1,0:T(8,128)(2,1)S(1)}, bf16[768,128]{1,0:T(8,128)(2,1)S(1)}, u32[]{:S(2)}, u32[]{:S(2)}) collective-permute-start(bf16[768,128]{1,0:T(8,128)(2,1)S(1)} %get-tuple-element.57), channel_id=1, source_target_pairs={{0,4},{2,6},{4,0},{6,2},{1,5},{3,7},{5,1},{7,3},{8,12},{10,14},{12... | collective-permute-start | bytes 589832 | tf_op jit(solution)/shard_map/ppermute | solution.py:409
  45.5 18.5 %collective-permute-start.9 = (bf16[768,128]{1,0:T(8,128)(2,1)S(1)}, bf16[768,128]{1,0:T(8,128)(2,1)S(1)}, u32[]{:S(2)}, u32[]{:S(2)}) collective-permute-start(bf16[768,128]{1,0:T(8,128)(2,1)S(1)} %get-tuple-element.58), channel_id=1, source_target_pairs={{0,6},{2,0},{4,2},{6,4},{1,7},{3,1},{5,3},{7,5},{8,14},{10,8},{12,... | collective-permute-start | bytes 589832 | tf_op jit(solution)/shard_map/ppermute | solution.py:409
  47.5 23.8 %collective-permute-start.11 = (bf16[2,128,256]{2,1,0:T(8,128)(2,1)}, bf16[2,128,256]{2,1,0:T(8,128)(2,1)S(1)}, u32[]{:S(2)}, u32[]{:S(2)}) collective-permute-start(bf16[2,128,256]{2,1,0:T(8,128)(2,1)} %copy-done.18), channel_id=1, source_target_pairs={{0,1},{1,2},{2,3},{3,4},{4,5},{5,6},{6,7},{8,9},{9,10},{10,11},{11... | collective-permute-start | bytes 393224 | tf_op jit(solution)/shard_map/ppermute | solution.py:419
  50.4 21.7 %collective-permute-start.12 = (bf16[2,128,256]{2,1,0:T(8,128)(2,1)}, bf16[2,128,256]{2,1,0:T(8,128)(2,1)S(1)}, u32[]{:S(2)}, u32[]{:S(2)}) collective-permute-start(bf16[2,128,256]{2,1,0:T(8,128)(2,1)} %copy-done.17), channel_id=1, source_target_pairs={{1,0},{2,1},{3,2},{4,3},{5,4},{6,5},{7,6},{9,8},{10,9},{11,10},{12... | collective-permute-start | bytes 393224 | tf_op jit(solution)/shard_map/ppermute | solution.py:419
  64.1 8.0 %collective-permute-start.10 = (bf16[192,128]{1,0:T(8,128)(2,1)S(1)}, bf16[192,128]{1,0:T(8,128)(2,1)S(1)}, u32[]{:S(2)}, u32[]{:S(2)}) collective-permute-start(bf16[192,128]{1,0:T(8,128)(2,1)S(1)} %get-tuple-element.60), channel_id=1, source_target_pairs={{0,32},{32,64},{64,96},{96,0},{1,33},{33,65},{65,97},{97,1},{2,34}... | collective-permute-start | bytes 147464 | tf_op jit(solution)/shard_map/ppermute | solution.py:409
  68.4 6.0 %collective-permute-start.13 = (bf16[192,128]{1,0:T(8,128)(2,1)S(1)}, bf16[192,128]{1,0:T(8,128)(2,1)S(1)}, u32[]{:S(2)}, u32[]{:S(2)}) collective-permute-start(bf16[192,128]{1,0:T(8,128)(2,1)S(1)} %get-tuple-element.64), channel_id=1, source_target_pairs={{0,64},{32,96},{64,0},{96,32},{1,65},{33,97},{65,1},{97,33},{2,66}... | collective-permute-start | bytes 147464 | tf_op jit(solution)/shard_map/ppermute | solution.py:409
  71.3 3.4 %collective-permute-start.14 = (bf16[192,128]{1,0:T(8,128)(2,1)S(1)}, bf16[192,128]{1,0:T(8,128)(2,1)S(1)}, u32[]{:S(2)}, u32[]{:S(2)}) collective-permute-start(bf16[192,128]{1,0:T(8,128)(2,1)S(1)} %get-tuple-element.65), channel_id=1, source_target_pairs={{0,96},{32,0},{64,32},{96,64},{1,97},{33,1},{65,33},{97,65},{2,98}... | collective-permute-start | bytes 147464 | tf_op jit(solution)/shard_map/ppermute | solution.py:409
  72.1 31.8 %copy-start.4 = (bf16[2,1024,256]{2,1,0:T(8,128)(2,1)}, bf16[2,1024,256]{2,1,0:T(8,128)(2,1)S(1)}, u32[]{:S(2)}) copy-start(bf16[2,1024,256]{2,1,0:T(8,128)(2,1)S(1)} %collective-permute-done.15.refs_4_.refs_1_) | copy-start | bytes 3145732
  93.9 4.9 %collective-permute-start.16 = (bf16[192,128]{1,0:T(8,128)(2,1)S(1)}, bf16[192,128]{1,0:T(8,128)(2,1)S(1)}, u32[]{:S(2)}, u32[]{:S(2)}) collective-permute-start(bf16[192,128]{1,0:T(8,128)(2,1)S(1)} %shard_map.83.refs_1_), channel_id=1, source_target_pairs={{0,32},{32,64},{64,96},{96,0},{1,33},{33,65},{65,97},{97,1},{2,34}... | collective-permute-start | bytes 147464 | tf_op jit(solution)/shard_map/ppermute | solution.py:409
  95.0 5.1 %collective-permute-start.17 = (bf16[192,128]{1,0:T(8,128)(2,1)S(1)}, bf16[192,128]{1,0:T(8,128)(2,1)S(1)}, u32[]{:S(2)}, u32[]{:S(2)}) collective-permute-start(bf16[192,128]{1,0:T(8,128)(2,1)S(1)} %shard_map.83.refs_1_), channel_id=1, source_target_pairs={{0,64},{32,96},{64,0},{96,32},{1,65},{33,97},{65,1},{97,33},{2,66}... | collective-permute-start | bytes 147464 | tf_op jit(solution)/shard_map/ppermute | solution.py:409
  98.1 3.0 %collective-permute-start.18 = (bf16[192,128]{1,0:T(8,128)(2,1)S(1)}, bf16[192,128]{1,0:T(8,128)(2,1)S(1)}, u32[]{:S(2)}, u32[]{:S(2)}) collective-permute-start(bf16[192,128]{1,0:T(8,128)(2,1)S(1)} %shard_map.83.refs_1_), channel_id=1, source_target_pairs={{0,96},{32,0},{64,32},{96,64},{1,97},{33,1},{65,33},{97,65},{2,98}... | collective-permute-start | bytes 147464 | tf_op jit(solution)/shard_map/ppermute | solution.py:409
  101.1 9.2 %collective-permute-start.19 = (bf16[768,128]{1,0:T(8,128)(2,1)S(1)}, bf16[768,128]{1,0:T(8,128)(2,1)S(1)}, u32[]{:S(2)}, u32[]{:S(2)}) collective-permute-start(bf16[768,128]{1,0:T(8,128)(2,1)S(1)} %shard_map.84.refs_1_), channel_id=1, source_target_pairs={{0,2},{2,4},{4,6},{6,0},{1,3},{3,5},{5,7},{7,1},{8,10},{10,12},{12... | collective-permute-start | bytes 589832 | tf_op jit(solution)/shard_map/ppermute | solution.py:409
  101.2 9.1 %collective-permute-start.20 = (bf16[768,128]{1,0:T(8,128)(2,1)S(1)}, bf16[768,128]{1,0:T(8,128)(2,1)S(1)}, u32[]{:S(2)}, u32[]{:S(2)}) collective-permute-start(bf16[768,128]{1,0:T(8,128)(2,1)S(1)} %shard_map.84.refs_1_), channel_id=1, source_target_pairs={{0,4},{2,6},{4,0},{6,2},{1,5},{3,7},{5,1},{7,3},{8,12},{10,14},{12... | collective-permute-start | bytes 589832 | tf_op jit(solution)/shard_map/ppermute | solution.py:409
  101.3 9.0 %collective-permute-start.21 = (bf16[768,128]{1,0:T(8,128)(2,1)S(1)}, bf16[768,128]{1,0:T(8,128)(2,1)S(1)}, u32[]{:S(2)}, u32[]{:S(2)}) collective-permute-start(bf16[768,128]{1,0:T(8,128)(2,1)S(1)} %shard_map.84.refs_1_), channel_id=1, source_target_pairs={{0,6},{2,0},{4,2},{6,4},{1,7},{3,1},{5,3},{7,5},{8,14},{10,8},{12,... | collective-permute-start | bytes 589832 | tf_op jit(solution)/shard_map/ppermute | solution.py:409
  110.4 6.6 %collective-permute-start.22 = (bf16[3072,128]{1,0:T(8,128)(2,1)S(1)}, bf16[3072,128]{1,0:T(8,128)(2,1)S(1)}, u32[]{:S(2)}, u32[]{:S(2)}) collective-permute-start(bf16[3072,128]{1,0:T(8,128)(2,1)S(1)} %shard_map.87.refs_1_), channel_id=1, source_target_pairs={{0,1},{1,0},{2,3},{3,2},{4,5},{5,4},{6,7},{7,6},{8,9},{9,8},{10,11... | collective-permute-start | bytes 2359304 | tf_op jit(solution)/shard_map/ppermute | solution.py:572
  (18 other events, 53.4 us)

commit v12 on v9

--- a/solution.py
+++ b/solution.py
@@ -260,26 +260,27 @@
     return jnp.concatenate([taps[i, j] for i in range(3)], axis=1)
 
 
-def back_kernel(grad, weight, dy, out, edge, padded, taps, own, result, sems):
+def back_kernel(grad, top, bottom, weight, dy, out, padded, taps, own, result, sems):
     frames, size, chans = own.shape
     whole = pltpu.make_async_copy(weight, taps, sems.at[0])
     whole.start()
     loads = []
     for f in range(frames):
-        base = 1 + 3 * f
+        base = 1 + 5 * f
         loads.append(
             [
+                pltpu.make_async_copy(top.at[f], padded.at[f, pl.ds(0, COLS)], sems.at[base]),
                 pltpu.make_async_copy(
-                    grad.at[f], padded.at[f, pl.ds(COLS, size)], sems.at[base]
+                    grad.at[f], padded.at[f, pl.ds(COLS, size)], sems.at[base + 1]
                 ),
-                pltpu.make_async_copy(dy.at[f], own.at[f], sems.at[base + 1]),
+                pltpu.make_async_copy(
+                    bottom.at[f], padded.at[f, pl.ds(COLS + size, COLS)], sems.at[base + 2]
+                ),
+                pltpu.make_async_copy(dy.at[f], own.at[f], sems.at[base + 3]),
             ]
         )
         for load in loads[f]:
             load.start()
-        blank = jnp.zeros((COLS, chans), BF)
-        padded[f, 0:COLS, :] = blank
-        padded[f, COLS + size :, :] = blank
     whole.wait()
     stores = []
     for f in range(frames):
@@ -297,69 +298,30 @@
                 for j in range(3)
             ]
             back = shifted(z[0], column, -1) + z[1] + shifted(z[2], column, 1)
-            total = own[f, at, :].astype(F32) + back
-            result[f, at, :] = total.astype(BF)
-
-            @pl.when(step == 0)
-            def _():
-                edge[f, 0] = total[:COLS]
-
-            @pl.when(step == size // CHUNK - 1)
-            def _():
-                edge[f, 1] = total[CHUNK - COLS :]
-
-        store = pltpu.make_async_copy(result.at[f], out.at[f], sems.at[3 + 3 * f])
+            result[f, at, :] = (own[f, at, :].astype(F32) + back).astype(BF)
+
+        store = pltpu.make_async_copy(result.at[f], out.at[f], sems.at[5 + 5 * f])
         store.start()
         stores.append(store)
     for store in stores:
         store.wait()
 
 
-def edge_kernel(top, bottom, weight, edge, part, out, result, sems):
-    frames, size = part.shape[0], part.shape[1]
-    chans = part.shape[2]
-    column = columns_of(frames * COLS, chans)
-    stores = []
-    for e, (rim, i) in enumerate(((top, 2), (bottom, 0))):
-        rows = rim[...].reshape(frames * COLS, chans)
-        z = [
-            lax.dot_general(rows, weight[i, j], NT, preferred_element_type=F32) for j in range(3)
-        ]
-        more = shifted(z[0], column, -1) + z[1] + shifted(z[2], column, 1)
-        for f in range(frames):
-            total = edge[f, e] + more[f * COLS : (f + 1) * COLS]
-            result[f, e] = total.astype(BF)
-            target = out.at[f, pl.ds(e * (size - COLS), COLS)]
-            store = pltpu.make_async_copy(result.at[f, e], target, sems.at[2 * f + e])
-            store.start()
-            stores.append(store)
-    for store in stores:
-        store.wait()
-
-
-def mix_kernel(act, behind, weight, x, out, ext, own, result, sems):
-    frames, size, chans = own.shape
-    loads = [pltpu.make_async_copy(behind.at[f], ext.at[f], sems.at[f]) for f in range(frames)]
-    for f in range(frames):
-        loads.append(pltpu.make_async_copy(act.at[f], ext.at[frames + f], sems.at[frames + 2 * f]))
-        loads.append(pltpu.make_async_copy(x.at[f], own.at[f], sems.at[frames + 2 * f + 1]))
-    for load in loads:
-        load.start()
-    for load in loads[:frames]:
-        load.wait()
-    stores = []
-    for f in range(frames):
-        for load in loads[frames + 2 * f : frames + 2 * f + 2]:
-            load.wait()
-        rows = jnp.concatenate([ext[f + 2 - k] for k in range(3)], axis=1)
-        taps = weight[...].reshape(3 * chans, chans)
-        mixed = jnp.dot(rows, taps, preferred_element_type=F32).astype(BF)
-        result[f] = (own[f].astype(F32) + mixed.astype(F32)).astype(BF)
-        store = pltpu.make_async_copy(result.at[f], out.at[f], sems.at[3 * frames + f])
-        store.start()
-        stores.append(store)
-    for store in stores:
-        store.wait()
+def mix_kernel(act, behind, weight, x, out, ext):
+    frames, size, chans = act.shape
+    for f in range(frames):
+        ext[f * size : (f + 1) * size, :] = behind[f]
+        ext[(frames + f) * size : (frames + f + 1) * size, :] = act[f]
+
+    @pl.loop(0, frames * (size // CHUNK))
+    def _(step):
+        start = pl.multiple_of(step * CHUNK, CHUNK)
+        rows = jnp.concatenate(
+            [ext[pl.ds(start + (2 - k) * size, CHUNK), :] for k in range(3)], axis=1
+        )
+        mixed = jnp.dot(rows, weight[...].reshape(3 * chans, chans), preferred_element_type=F32)
+        own = x[pl.ds(start, CHUNK), :].astype(F32)
+        out[pl.ds(start, CHUNK), :] = (own + mixed.astype(BF).astype(F32)).astype(BF)
 
 
 def steps(axes, by):
@@ -432,24 +394,7 @@
     column, plane = lax.axis_size(COLUMN), lax.axis_size(PLANE)
     share = rows // plane
     first = exchange(half.reshape(plane, share, 128), PLANE)
-    inner, edge = call(
-        back_kernel,
-        [shape((frames, size, chans)), shape((frames, 2, COLS, chans), F32)],
-        (pgrad, spatial_weight, dy),
-        [
-            pltpu.VMEM((frames, size + 2 * COLS, chans), BF),
-            pltpu.VMEM((3, 3, chans, chans), BF),
-            block,
-            block,
-            pltpu.SemaphoreType.DMA((7,)),
-        ],
-        flops=9 * work,
-        moved=5 << 20,
-        hbm=range(3),
-        out_hbm=(0,),
-        limit=58,
-    )
-    first, edge = lax.optimization_barrier((first, edge))
+    first, grad_top, grad_bottom = lax.optimization_barrier((first, grad_top, grad_bottom))
     spread = call(
         functools.partial(spread_sum_kernel, 1.0),
         shape((column, share, 128)),
@@ -460,31 +405,28 @@
     third = exchange(spread, COLUMN)
     block_out = call(
         mix_kernel,
+        shape((flat, chans)),
+        (act, behind, temporal_weight, x.reshape(flat, chans)),
+        [pltpu.VMEM((2 * flat, chans), BF)],
+        flops=3 * work,
+        moved=4 << 20,
+    )
+    input_grad = call(
+        back_kernel,
         shape((frames, size, chans)),
-        (act, behind, temporal_weight, x),
+        (pgrad, grad_top, grad_bottom, spatial_weight, dy),
         [
-            pltpu.VMEM((2 * frames, size, chans), BF),
+            pltpu.VMEM((frames, size + 2 * COLS, chans), BF),
+            pltpu.VMEM((3, 3, chans, chans), BF),
             block,
             block,
-            pltpu.SemaphoreType.DMA((4 * frames,)),
+            pltpu.SemaphoreType.DMA((11,)),
         ],
-        flops=3 * work,
-        moved=4 << 20,
-        hbm=(0, 1, 3),
+        flops=9 * work,
+        moved=5 << 20,
+        hbm=range(5),
         out_hbm=True,
         limit=58,
-    )
-    third, grad_top, grad_bottom = lax.optimization_barrier((third, grad_top, grad_bottom))
-    input_grad = call(
-        edge_kernel,
-        shape((frames, size, chans)),
-        (grad_top, grad_bottom, spatial_weight, edge, inner),
-        [pltpu.VMEM((frames, 2, COLS, chans), BF), pltpu.SemaphoreType.DMA((2 * frames,))],
-        flops=work,
-        moved=1 << 20,
-        hbm=(4,),
-        out_hbm=True,
-        alias={4: 0},
     )
     wider = call(
         functools.partial(spread_sum_kernel, scale),

time: 112 us -> 110 us (0.982)
  blocking collectives: 0 us -> 19.7 us
  waiting for transfers between devices: 31.3 us -> 18.6 us
  starting transfers between devices: 46.9 us -> 41.6 us
  Pallas kernels: 29.2 us -> 24.8 us
    all_to_all x0 -> x1, blocking collectives: none -> 19.7 us  [exchange(): return lax.all_to_all(value, axes, split_axis=0, concat_axis=0, tiled=True)]
    all_to_all x3 -> x2, waiting for transfers between devices: 20.1 us -> 4.58 us  [exchange(): return lax.all_to_all(value, axes, split_axis=0, concat_axis=0, tiled=True)]
    all_to_all x3 -> x2, starting transfers between devices: 22.8 us -> 15.9 us  [exchange(): return lax.all_to_all(value, axes, split_axis=0, concat_axis=0, tiled=True)]
    ppermute x2, waiting for transfers between devices: 0.01 us -> 4.7 us  [swap_rims(): lax.ppermute(last, SPACE, steps(SPACE, 1))]
    pallas_call x11 -> x10, Pallas kernels: 29.2 us -> 24.8 us  [call(): pl.pallas_call(body, out_shape=outs, in_specs=specs, out_specs=placed if...]
    ppermute x1, starting transfers between devices: 2.63 us -> 4.92 us  [local(): other = lax.ppermute(own, 'core', pair)]
    ppermute x2, waiting for transfers between devices: 9.16 us -> 7.24 us  [swap_rims(): lax.ppermute(first, SPACE, steps(SPACE, -1))]
  transfers between devices with their start and end apart: 14 -> 13, of which waited for: 10 -> 10; matrix products, arithmetic and copies ran while one was open for 1% -> 1% of each run, Pallas kernels for 23% -> 21%
where the time goes in v12:
time: 110 us; the launch traced here: 109 us
  starting transfers between devices  41.6 us (38%)
  Pallas kernels  24.8 us (23%)
  blocking collectives  19.7 us (18%)
  waiting for transfers between devices  18.6 us (17%)
  local copies, waits for them, and re-layouts  3.51 us (3%)
    pallas_call x10, Pallas kernels, call(): pl.pallas_call(body, out_shape=outs, in_specs=specs, out_specs=placed if...  24.8 us
    all_to_all x1, blocking collectives, exchange(): return lax.all_to_all(value, axes, split_axis=0, concat_axis=0, tiled=True)  19.7 us
    all_to_all x2, starting transfers between devices, exchange(): return lax.all_to_all(value, axes, split_axis=0, concat_axis=0, tiled=True)  15.9 us
    ppermute x2, starting transfers between devices, swap_rims(): lax.ppermute(last, SPACE, steps(SPACE, 1))  8.5 us
    ppermute x2, waiting for transfers between devices, swap_rims(): lax.ppermute(first, SPACE, steps(SPACE, -1))  7.24 us
    ppermute x1, starting transfers between devices, local(): other = lax.ppermute(own, 'core', pair)  4.92 us
    ppermute x2, waiting for transfers between devices, swap_rims(): lax.ppermute(last, SPACE, steps(SPACE, 1))  4.7 us
    all_to_all x2, waiting for transfers between devices, exchange(): return lax.all_to_all(value, axes, split_axis=0, concat_axis=0, tiled=True)  4.58 us
  transfers between devices with their start and end apart: 13, of which 10 were waited for; matrix products, arithmetic and copies ran while one was open for 1% of the time, Pallas kernels for 21%

profile of v12, /device:TPU:1, one launch (start us, length us, event | category | flops | bytes accessed | tf_op | source)
XLA Modules:
  0.0 109.1 jit_solution(12371942543106135828)
XLA Ops:
  0.6 1.3 %collective-permute-start = (bf16[2,1024,256]{2,1,0:T(8,128)(2,1)}, bf16[2,1024,256]{2,1,0:T(8,128)(2,1)S(1)}, u32[]{:S(2)}, u32[]{:S(2)}) collective-permute-start(bf16[2,1024,256]{2,1,0:T(8,128)(2,1)} %bitcast.14), channel_id=1, source_target_pairs={{8,0},{16,8},{24,16},{32,24},{40,32},{48,40},{56,48},{64,56},{72,6... | collective-permute-start | bytes 3145736 | tf_op jit(solution)/shard_map/ppermute | solution.py:348
  2.9 4.5 %collective-permute-start.1 = (bf16[2,128,256]{2,1,0:T(8,128)(2,1)S(1)}, bf16[2,128,256]{2,1,0:T(8,128)(2,1)S(1)}, u32[]{:S(2)}, u32[]{:S(2)}) collective-permute-start(bf16[2,128,256]{2,1,0:T(8,128)(2,1)S(1)} %get-tuple-element.53), channel_id=1, source_target_pairs={{0,1},{1,2},{2,3},{3,4},{4,5},{5,6},{6,7},{8,9},{9,10},{10,11},{11... | collective-permute-start | bytes 393224 | tf_op jit(solution)/shard_map/ppermute | solution.py:337
  7.4 1.9 %collective-permute-start.2 = (bf16[2,128,256]{2,1,0:T(8,128)(2,1)S(1)}, bf16[2,128,256]{2,1,0:T(8,128)(2,1)S(1)}, u32[]{:S(2)}, u32[]{:S(2)}) collective-permute-start(bf16[2,128,256]{2,1,0:T(8,128)(2,1)S(1)} %get-tuple-element.52), channel_id=1, source_target_pairs={{1,0},{2,1},{3,2},{4,3},{5,4},{6,5},{7,6},{9,8},{10,9},{11,10},{12... | collective-permute-start | bytes 393224 | tf_op jit(solution)/shard_map/ppermute | solution.py:337
  9.4 4.6 %collective-permute-done.2.refs_2_ = bf16[2,128,256]{2,1,0:T(8,128)(2,1)S(1)} collective-permute-done((bf16[2,128,256]{2,1,0:T(8,128)(2,1)S(1)}, bf16[2,128,256]{2,1,0:T(8,128)(2,1)S(1)}, u32[]{:S(2)}, u32[]{:S(2)}) %collective-permute-start.2) | collective-permute-done | bytes 131104 | tf_op jit(solution)/shard_map/ppermute | solution.py:337
  14.0 1.2 %copy-done = bf16[1,2,8,128,256]{4,3,2,1,0:T(8,128)(2,1)S(1)} copy-done((bf16[1,2,8,128,256]{4,3,2,1,0:T(8,128)(2,1)S(1)}, bf16[1,2,8,128,256]{4,3,2,1,0:T(8,128)(2,1)}, u32[]{:S(2)}) %copy-start) | copy-done | bytes 1048600
  15.3 1.3 %copy-done.3 = bf16[3,3,256,256]{3,2,1,0:T(8,128)(2,1)S(1)} copy-done((bf16[3,3,256,256]{3,2,1,0:T(8,128)(2,1)S(1)}, bf16[3,3,256,256]{3,2,1,0:T(8,128)(2,1)}, u32[]{:S(2)}) %copy-start.3) | copy-done | bytes 1179672
  16.5 4.9 %shard_map.75 = (bf16[2,1024,256]{2,1,0:T(8,128)(2,1)}, f32[2,1024,256]{2,1,0:T(8,128)S(1)}, bf16[2,256,1280]{2,1,0:T(8,128)(2,1)S(1)}, bf16[2,256,1024]{2,1,0:T(8,128)(2,1)S(1)}) custom-call(bf16[2,1024,256]{2,1,0:T(8,128)(2,1)S(1)} %bitcast.12, bf16[2,128,256]{2,1,0:T(8,128)(2,1)S(1)} %collective-permute-done.1.refs_1_, ...), custom_call_target="tpu_custom_call" | custom-call | flops 2415919104 | bytes 9437184 | tf_op jit(solution)/shard_map/pallas_call | solution.py:35
  21.5 4.3 %collective-permute-start.9 = (bf16[2,1024,256]{2,1,0:T(8,128)(2,1)}, bf16[2,1024,256]{2,1,0:T(8,128)(2,1)S(1)}, u32[]{:S(2)}, u32[]{:S(2)}) collective-permute-start(bf16[2,1024,256]{2,1,0:T(8,128)(2,1)} %get-tuple-element.41.refs_0_), channel_id=1, source_target_pairs={{0,8},{8,16},{16,24},{24,32},{32,40},{40,48},{48,56},{56,64},{64,7... | collective-permute-start | bytes 3145736 | tf_op jit(solution)/shard_map/ppermute | solution.py:370
  25.8 1.4 %shard_map.76 = (f32[2,1024,256]{2,1,0:T(8,128)S(1)}, f32[2,256,256]{2,1,0:T(8,128)S(1)}) custom-call(bf16[2,1024,256]{2,1,0:T(8,128)(2,1)S(1)} %bitcast.16, bf16[3,256,256]{2,1,0:T(8,128)(2,1)S(1)} %copy-done.2, bf16[2,256,1024]{2,1,0:T(8,128)(2,1)S(1)} %get-tuple-element.30.refs_2_.refs_5_), custom_call_target="tpu_custom_call" | custom-call | flops 1610612736 | bytes 6291456 | tf_op jit(solution)/shard_map/pallas_call | solution.py:35
  27.2 4.4 %shard_map.77 = (bf16[2,1024,256]{2,1,0:T(8,128)(2,1)S(1)}, bf16[3072,128]{1,0:T(8,128)(2,1)S(1)}, bf16[2,128,256]{2,1,0:T(8,128)(2,1)S(1)}, bf16[2,128,256]{2,1...) custom-call(s32[1]{0:T(128)} %bitcast.refs_0_, ...), custom_call_target="tpu_custom_call" | custom-call | flops 1024 | bytes 4096 | tf_op jit(solution)/shard_map/pallas_call | solution.py:35
  31.6 2.2 %collective-permute-start.3 = (bf16[768,128]{1,0:T(8,128)(2,1)S(1)}, bf16[768,128]{1,0:T(8,128)(2,1)S(1)}, u32[]{:S(2)}, u32[]{:S(2)}) collective-permute-start(bf16[768,128]{1,0:T(8,128)(2,1)S(1)} %get-tuple-element.34), channel_id=1, source_target_pairs={{0,1},{1,0},{2,3},{3,2},{4,5},{5,4},{6,7},{7,6},{8,9},{9,8},{10,11... | collective-permute-start | bytes 589832 | tf_op jit(solution)/shard_map/ppermute | solution.py:391
  36.9 10.0 %all-to-all-start = ((bf16[16,192,128]{2,1,0:T(8,128)(2,1)}), bf16[16,192,128]{2,1,0:T(8,128)(2,1)S(1)}, u32[]{:S(2)}, u32[]{:S(2)}) async-start(bf16[16,192,128]{2,1,0:T(8,128)(2,1)} %bitcast.3), calls=%async_computation | async-start | bytes 1572864 | tf_op jit(solution)/shard_map/all_to_all | solution.py:333
  46.9 4.0 %collective-permute-start.7 = (bf16[2,128,256]{2,1,0:T(8,128)(2,1)S(1)}, bf16[2,128,256]{2,1,0:T(8,128)(2,1)S(1)}, u32[]{:S(2)}, u32[]{:S(2)}) collective-permute-start(bf16[2,128,256]{2,1,0:T(8,128)(2,1)S(1)} %get-tuple-element.38), channel_id=1, source_target_pairs={{0,1},{1,2},{2,3},{3,4},{4,5},{5,6},{6,7},{8,9},{9,10},{10,11},{11... | collective-permute-start | bytes 393224 | tf_op jit(solution)/shard_map/ppermute | solution.py:337
  50.9 1.9 %collective-permute-start.8 = (bf16[2,128,256]{2,1,0:T(8,128)(2,1)S(1)}, bf16[2,128,256]{2,1,0:T(8,128)(2,1)S(1)}, u32[]{:S(2)}, u32[]{:S(2)}) collective-permute-start(bf16[2,128,256]{2,1,0:T(8,128)(2,1)S(1)} %get-tuple-element.39), channel_id=1, source_target_pairs={{1,0},{2,1},{3,2},{4,3},{5,4},{6,5},{7,6},{9,8},{10,9},{11,10},{12... | collective-permute-start | bytes 393224 | tf_op jit(solution)/shard_map/ppermute | solution.py:337
  52.8 4.7 %collective-permute-done.7.refs_1_ = bf16[2,128,256]{2,1,0:T(8,128)(2,1)S(1)} collective-permute-done((bf16[2,128,256]{2,1,0:T(8,128)(2,1)S(1)}, bf16[2,128,256]{2,1,0:T(8,128)(2,1)S(1)}, u32[]{:S(2)}, u32[]{:S(2)}) %collective-permute-start.7) | collective-permute-done | bytes 131104 | tf_op jit(solution)/shard_map/ppermute | solution.py:337
  57.5 2.6 %collective-permute-done.8.refs_2_ = bf16[2,128,256]{2,1,0:T(8,128)(2,1)S(1)} collective-permute-done((bf16[2,128,256]{2,1,0:T(8,128)(2,1)S(1)}, bf16[2,128,256]{2,1,0:T(8,128)(2,1)S(1)}, u32[]{:S(2)}, u32[]{:S(2)}) %collective-permute-start.8) | collective-permute-done | bytes 131104 | tf_op jit(solution)/shard_map/ppermute | solution.py:337
  60.2 3.9 %all-to-all-done.refs_0_ = bf16[16,192,128]{2,1,0:T(8,128)(2,1)S(1)} async-done(((bf16[16,192,128]{2,1,0:T(8,128)(2,1)}), bf16[16,192,128]{2,1,0:T(8,128)(2,1)S(1)}, u32[]{:S(2)}, u32[]{:S(2)}) %all-to-all-start) | async-done | bytes 786464 | tf_op jit(solution)/shard_map/all_to_all | solution.py:333
  64.1 19.7 %all_to_all.15.refs_0_ = bf16[8,192,128]{2,1,0:T(8,128)(2,1)S(1)} all-to-all(bf16[8,192,128]{2,1,0:T(8,128)(2,1)S(1)} %shard_map.79), channel_id=1, replica_groups=mesh['clip'=2,'y'=4,'zl'=4,'x'=4,'core'=2] {'clip','zl'}, dimensions={0} | all-to-all | bytes 786432 | tf_op jit(solution)/shard_map/all_to_all | solution.py:333
  84.8 5.9 %all-to-all-start.2 = ((bf16[16,192,128]{2,1,0:T(8,128)(2,1)}), bf16[16,192,128]{2,1,0:T(8,128)(2,1)S(1)}, u32[]{:S(2)}, u32[]{:S(2)}) async-start(bf16[16,192,128]{2,1,0:T(8,128)(2,1)} %shard_map.80), calls=%async_computation.2 | async-start | bytes 1572864 | tf_op jit(solution)/shard_map/all_to_all | solution.py:333
  90.7 3.8 %shard_map.81 = bf16[2048,256]{1,0:T(8,128)(2,1)} custom-call(bf16[2,1024,256]{2,1,0:T(8,128)(2,1)} %get-tuple-element.41.refs_0_, bf16[2,1024,256]{2,1,0:T(8,128)(2,1)S(1)} %collective-permute-done.9.refs_1_, bf16[3,256,256]{2,1,0:T(8,128)(2,1)S(1)} %copy-done.2, bf16[2048,256]{1,0:T(8,128)(2,1)S(1)} %bitcast.13), custom_call_target="tpu_custom_call" | custom-call | flops 805306368 | bytes 4194304 | tf_op jit(solution)/shard_map/pallas_call | solution.py:35
  94.6 5.7 %shard_map.82 = bf16[2,1024,256]{2,1,0:T(8,128)(2,1)} custom-call(bf16[2,1024,256]{2,1,0:T(8,128)(2,1)} %copy-done.5, bf16[2,128,256]{2,1,0:T(8,128)(2,1)} %copy-done.6, bf16[2,128,256]{2,1,0:T(8,128)(2,1)} %copy-done.7, bf16[3,3,256,256]{3,2,1,0:T(8,128)(2,1)} %refs_3_.3, bf16[2,1024,256]{2,1,0:T(8,128)(2,1)} %bitcast.15), custom_call_target="tpu_custom_call" | custom-call | flops 2415919104 | bytes 5242880 | tf_op jit(solution)/shard_map/pallas_call | solution.py:35
  101.1 4.9 %collective-permute-start.10 = (bf16[3072,128]{1,0:T(8,128)(2,1)S(1)}, bf16[3072,128]{1,0:T(8,128)(2,1)S(1)}, u32[]{:S(2)}, u32[]{:S(2)}) collective-permute-start(bf16[3072,128]{1,0:T(8,128)(2,1)S(1)} %bitcast.9), channel_id=1, source_target_pairs={{0,1},{1,0},{2,3},{3,2},{4,5},{5,4},{6,7},{7,6},{8,9},{9,8},{10,11... | collective-permute-start | bytes 2359304 | tf_op jit(solution)/shard_map/ppermute | solution.py:439
  106.0 1.2 %shard_map.83 = (f32[9,256,256]{2,1,0:T(8,128)}, f32[3,256,256]{2,1,0:T(8,128)}) custom-call(s32[1]{0:T(128)} %bitcast.refs_0_, bf16[3072,128]{1,0:T(8,128)(2,1)S(1)} %bitcast.10), custom_call_target="tpu_custom_call" | custom-call | bytes 3145728 | tf_op jit(solution)/shard_map/pallas_call | solution.py:35
  107.9 1.2 %shard_map.84 = (f32[9,256,256]{2,1,0:T(8,128)}, f32[3,256,256]{2,1,0:T(8,128)}) custom-call(s32[1]{0:T(128)} %bitcast.refs_0_, bf16[3072,128]{1,0:T(8,128)(2,1)S(1)} %collective-permute-done.10.refs_1_, f32[9,256,256]{2,1,0:T(8,128)} %get-tuple-element.48.refs_2_, ...), custom_call_target="tpu_custom_call", output_to_operand_aliasing={{0}: (2, {}), {1}: (3, {})} | custom-call | bytes 3145728 | tf_op jit(solution)/shard_map/pallas_call | solution.py:35
  (30 shorter events, 6.6 us)
Async XLA Ops:
  0.6 26.5 %collective-permute-start = (bf16[2,1024,256]{2,1,0:T(8,128)(2,1)}, bf16[2,1024,256]{2,1,0:T(8,128)(2,1)S(1)}, u32[]{:S(2)}, u32[]{:S(2)}) collective-permute-start(bf16[2,1024,256]{2,1,0:T(8,128)(2,1)} %bitcast.14), channel_id=1, source_target_pairs={{8,0},{16,8},{24,16},{32,24},{40,32},{48,40},{56,48},{64,56},{72,6... | collective-permute-start | bytes 3145736 | tf_op jit(solution)/shard_map/ppermute | solution.py:348
  2.9 6.5 %collective-permute-start.1 = (bf16[2,128,256]{2,1,0:T(8,128)(2,1)S(1)}, bf16[2,128,256]{2,1,0:T(8,128)(2,1)S(1)}, u32[]{:S(2)}, u32[]{:S(2)}) collective-permute-start(bf16[2,128,256]{2,1,0:T(8,128)(2,1)S(1)} %get-tuple-element.53), channel_id=1, source_target_pairs={{0,1},{1,2},{2,3},{3,4},{4,5},{5,6},{6,7},{8,9},{9,10},{10,11},{11... | collective-permute-start | bytes 393224 | tf_op jit(solution)/shard_map/ppermute | solution.py:337
  7.4 6.6 %collective-permute-start.2 = (bf16[2,128,256]{2,1,0:T(8,128)(2,1)S(1)}, bf16[2,128,256]{2,1,0:T(8,128)(2,1)S(1)}, u32[]{:S(2)}, u32[]{:S(2)}) collective-permute-start(bf16[2,128,256]{2,1,0:T(8,128)(2,1)S(1)} %get-tuple-element.52), channel_id=1, source_target_pairs={{1,0},{2,1},{3,2},{4,3},{5,4},{6,5},{7,6},{9,8},{10,9},{11,10},{12... | collective-permute-start | bytes 393224 | tf_op jit(solution)/shard_map/ppermute | solution.py:337
  14.0 1.2 %copy-start = (bf16[1,2,8,128,256]{4,3,2,1,0:T(8,128)(2,1)S(1)}, bf16[1,2,8,128,256]{4,3,2,1,0:T(8,128)(2,1)}, u32[]{:S(2)}) copy-start(bf16[1,2,8,128,256]{4,3,2,1,0:T(8,128)(2,1)} %param.4) | copy-start | bytes 3145732
  15.3 1.3 %copy-start.3 = (bf16[3,3,256,256]{3,2,1,0:T(8,128)(2,1)S(1)}, bf16[3,3,256,256]{3,2,1,0:T(8,128)(2,1)}, u32[]{:S(2)}) copy-start(bf16[3,3,256,256]{3,2,1,0:T(8,128)(2,1)} %refs_3_.3) | copy-start | bytes 3538948
  16.5 9.3 %copy-start.2 = (bf16[3,256,256]{2,1,0:T(8,128)(2,1)S(1)}, bf16[3,256,256]{2,1,0:T(8,128)(2,1)}, u32[]{:S(2)}) copy-start(bf16[3,256,256]{2,1,0:T(8,128)(2,1)} %refs_2_.3) | copy-start | bytes 1179652
  16.5 9.3 %copy-start.4 = (bf16[1,2,8,128,256]{4,3,2,1,0:T(8,128)(2,1)S(1)}, bf16[1,2,8,128,256]{4,3,2,1,0:T(8,128)(2,1)}, u32[]{:S(2)}) copy-start(bf16[1,2,8,128,256]{4,3,2,1,0:T(8,128)(2,1)} %param.5) | copy-start | bytes 3145732
  21.5 42.6 %collective-permute-start.9 = (bf16[2,1024,256]{2,1,0:T(8,128)(2,1)}, bf16[2,1024,256]{2,1,0:T(8,128)(2,1)S(1)}, u32[]{:S(2)}, u32[]{:S(2)}) collective-permute-start(bf16[2,1024,256]{2,1,0:T(8,128)(2,1)} %get-tuple-element.41.refs_0_), channel_id=1, source_target_pairs={{0,8},{8,16},{16,24},{24,32},{32,40},{40,48},{48,56},{56,64},{64,7... | collective-permute-start | bytes 3145736 | tf_op jit(solution)/shard_map/ppermute | solution.py:370
  31.6 5.3 %copy-start.5 = (bf16[2,1024,256]{2,1,0:T(8,128)(2,1)}, bf16[2,1024,256]{2,1,0:T(8,128)(2,1)S(1)}, u32[]{:S(2)}) copy-start(bf16[2,1024,256]{2,1,0:T(8,128)(2,1)S(1)} %get-tuple-element.42.refs_0_) | copy-start | bytes 3145732
  31.6 3.3 %collective-permute-start.3 = (bf16[768,128]{1,0:T(8,128)(2,1)S(1)}, bf16[768,128]{1,0:T(8,128)(2,1)S(1)}, u32[]{:S(2)}, u32[]{:S(2)}) collective-permute-start(bf16[768,128]{1,0:T(8,128)(2,1)S(1)} %get-tuple-element.34), channel_id=1, source_target_pairs={{0,1},{1,0},{2,3},{3,2},{4,5},{5,4},{6,7},{7,6},{8,9},{9,8},{10,11... | collective-permute-start | bytes 589832 | tf_op jit(solution)/shard_map/ppermute | solution.py:391
  33.8 1.4 %collective-permute-start.4 = (bf16[768,128]{1,0:T(8,128)(2,1)S(1)}, bf16[768,128]{1,0:T(8,128)(2,1)S(1)}, u32[]{:S(2)}, u32[]{:S(2)}) collective-permute-start(bf16[768,128]{1,0:T(8,128)(2,1)S(1)} %get-tuple-element.35), channel_id=1, source_target_pairs={{0,1},{1,0},{2,3},{3,2},{4,5},{5,4},{6,7},{7,6},{8,9},{9,8},{10,11... | collective-permute-start | bytes 589832 | tf_op jit(solution)/shard_map/ppermute | solution.py:391
  33.9 1.6 %collective-permute-start.5 = (bf16[768,128]{1,0:T(8,128)(2,1)S(1)}, bf16[768,128]{1,0:T(8,128)(2,1)S(1)}, u32[]{:S(2)}, u32[]{:S(2)}) collective-permute-start(bf16[768,128]{1,0:T(8,128)(2,1)S(1)} %get-tuple-element.36), channel_id=1, source_target_pairs={{0,1},{1,0},{2,3},{3,2},{4,5},{5,4},{6,7},{7,6},{8,9},{9,8},{10,11... | collective-permute-start | bytes 589832 | tf_op jit(solution)/shard_map/ppermute | solution.py:391
  34.3 1.5 %collective-permute-start.6 = (bf16[768,128]{1,0:T(8,128)(2,1)S(1)}, bf16[768,128]{1,0:T(8,128)(2,1)S(1)}, u32[]{:S(2)}, u32[]{:S(2)}) collective-permute-start(bf16[768,128]{1,0:T(8,128)(2,1)S(1)} %get-tuple-element.37), channel_id=1, source_target_pairs={{0,1},{1,0},{2,3},{3,2},{4,5},{5,4},{6,7},{7,6},{8,9},{9,8},{10,11... | collective-permute-start | bytes 589832 | tf_op jit(solution)/shard_map/ppermute | solution.py:391
  36.9 27.1 %all-to-all-start = ((bf16[16,192,128]{2,1,0:T(8,128)(2,1)}), bf16[16,192,128]{2,1,0:T(8,128)(2,1)S(1)}, u32[]{:S(2)}, u32[]{:S(2)}) async-start(bf16[16,192,128]{2,1,0:T(8,128)(2,1)} %bitcast.3), calls=%async_computation | async-start | bytes 1572864 | tf_op jit(solution)/shard_map/all_to_all | solution.py:333
  46.9 10.6 %collective-permute-start.7 = (bf16[2,128,256]{2,1,0:T(8,128)(2,1)S(1)}, bf16[2,128,256]{2,1,0:T(8,128)(2,1)S(1)}, u32[]{:S(2)}, u32[]{:S(2)}) collective-permute-start(bf16[2,128,256]{2,1,0:T(8,128)(2,1)S(1)} %get-tuple-element.38), channel_id=1, source_target_pairs={{0,1},{1,2},{2,3},{3,4},{4,5},{5,6},{6,7},{8,9},{9,10},{10,11},{11... | collective-permute-start | bytes 393224 | tf_op jit(solution)/shard_map/ppermute | solution.py:337
  50.9 9.3 %collective-permute-start.8 = (bf16[2,128,256]{2,1,0:T(8,128)(2,1)S(1)}, bf16[2,128,256]{2,1,0:T(8,128)(2,1)S(1)}, u32[]{:S(2)}, u32[]{:S(2)}) collective-permute-start(bf16[2,128,256]{2,1,0:T(8,128)(2,1)S(1)} %get-tuple-element.39), channel_id=1, source_target_pairs={{1,0},{2,1},{3,2},{4,3},{5,4},{6,5},{7,6},{9,8},{10,9},{11,10},{12... | collective-permute-start | bytes 393224 | tf_op jit(solution)/shard_map/ppermute | solution.py:337
  57.5 27.3 %copy-start.6 = (bf16[2,128,256]{2,1,0:T(8,128)(2,1)}, bf16[2,128,256]{2,1,0:T(8,128)(2,1)S(1)}, u32[]{:S(2)}) copy-start(bf16[2,128,256]{2,1,0:T(8,128)(2,1)S(1)} %collective-permute-done.7.refs_1_) | copy-start | bytes 393220
  60.2 24.6 %copy-start.7 = (bf16[2,128,256]{2,1,0:T(8,128)(2,1)}, bf16[2,128,256]{2,1,0:T(8,128)(2,1)S(1)}, u32[]{:S(2)}) copy-start(bf16[2,128,256]{2,1,0:T(8,128)(2,1)S(1)} %collective-permute-done.8.refs_2_) | copy-start | bytes 393220
  64.1 26.6 %copy-start.1 = (bf16[1,2,8,128,256]{4,3,2,1,0:T(8,128)(2,1)S(1)}, bf16[1,2,8,128,256]{4,3,2,1,0:T(8,128)(2,1)}, u32[]{:S(2)}) copy-start(bf16[1,2,8,128,256]{4,3,2,1,0:T(8,128)(2,1)} %param.4) | copy-start | bytes 3145732
  84.8 16.3 %all-to-all-start.2 = ((bf16[16,192,128]{2,1,0:T(8,128)(2,1)}), bf16[16,192,128]{2,1,0:T(8,128)(2,1)S(1)}, u32[]{:S(2)}, u32[]{:S(2)}) async-start(bf16[16,192,128]{2,1,0:T(8,128)(2,1)} %shard_map.80), calls=%async_computation.2 | async-start | bytes 1572864 | tf_op jit(solution)/shard_map/all_to_all | solution.py:333
  101.1 6.8 %collective-permute-start.10 = (bf16[3072,128]{1,0:T(8,128)(2,1)S(1)}, bf16[3072,128]{1,0:T(8,128)(2,1)S(1)}, u32[]{:S(2)}, u32[]{:S(2)}) collective-permute-start(bf16[3072,128]{1,0:T(8,128)(2,1)S(1)} %bitcast.9), channel_id=1, source_target_pairs={{0,1},{1,0},{2,3},{3,2},{4,5},{5,4},{6,7},{7,6},{8,9},{9,8},{10,11... | collective-permute-start | bytes 2359304 | tf_op jit(solution)/shard_map/ppermute | solution.py:439

commit v13 on v12

--- a/solution.py
+++ b/solution.py
@@ -74,7 +74,13 @@
     padded[frame, COLS + size :, :] = bottom[frame]
 
 
-def forward_kernel(x, top, bottom, weight, act, slope, x_t, act_t, padded):
+def turn_kernel(x, weight, x_t, held):
+    for f in range(x.shape[0]):
+        x_t[f] = x[f].T
+    held[...] = weight[...]
+
+
+def forward_kernel(x, top, bottom, weight, act, slope, top_t, bottom_t, act_t, padded):
     frames, size, chans = x.shape
     for f in range(frames):
         fill(padded, x, top, bottom, f)
@@ -97,7 +103,8 @@
         act_t[f, :, pl.ds(start, CHUNK)] = active.T
 
     for f in range(frames):
-        x_t[f] = padded[f].T
+        top_t[f] = top[f].T
+        bottom_t[f] = bottom[f].T
 
 
 def early_kernel(dy, weight, act_t, partial, terms):
@@ -129,8 +136,10 @@
     wide[2, into, :] = shifted(full, column, 1).astype(BF)
 
 
-def windows_of(x_t, f, size):
-    return jnp.concatenate([x_t[f, :, i * COLS : i * COLS + size] for i in range(3)], axis=0)
+def windows_of(x_t, top_t, bottom_t, f, size):
+    above = jnp.concatenate([top_t[f], x_t[f, :, : size - COLS]], axis=1)
+    below = jnp.concatenate([x_t[f, :, COLS:], bottom_t[f]], axis=1)
+    return jnp.concatenate([above, x_t[f], below], axis=0)
 
 
 def gradient_kernel(
@@ -139,6 +148,8 @@
     weight,
     slope,
     x_t,
+    top_t,
+    bottom_t,
     act_t,
     partial,
     early,
@@ -176,7 +187,7 @@
             at = (tap * 2 + h) * chans
             terms[at : at + chans, :] = value[:, h * 128 : (h + 1) * 128].astype(BF)
 
-    left = jnp.concatenate([windows_of(x_t, f, size) for f in range(frames)], axis=1)
+    left = jnp.concatenate([windows_of(x_t, top_t, bottom_t, f, size) for f in range(frames)], axis=1)
     for j in range(3):
         out = jnp.dot(left, wide[j], preferred_element_type=F32)
         for i in range(3):
@@ -347,15 +358,23 @@
     core = lax.axis_index("core").astype(jnp.int32).reshape(1)
     ahead = lax.ppermute(dy, TM, steps(TM, -1))
     top, bottom = swap_rims(x[:, size - COLS :, :], x[:, :COLS, :])
-    act, slope, x_t, act_t = call(
+    x_t, held = call(
+        turn_kernel,
+        [shape((frames, chans, size)), shape(spatial_weight.shape)],
+        (x, spatial_weight),
+        flops=1 << 20,
+        moved=2 << 20,
+    )
+    act, slope, top_t, bottom_t, act_t = call(
         forward_kernel,
         [
             shape((frames, size, chans)),
             shape((frames, size, chans), F32),
-            shape((frames, chans, size + 2 * COLS)),
+            shape((frames, chans, COLS)),
+            shape((frames, chans, COLS)),
             shape((frames, chans, size)),
         ],
-        (x, top, bottom, spatial_weight),
+        (x, top, bottom, held),
         [pltpu.VMEM((frames, size + 2 * COLS, chans), BF)],
         flops=9 * work,
         moved=9 << 20,
@@ -375,7 +394,18 @@
         gradient_kernel,
         [shape((frames, size, chans)), shape((rows, 128)), edges, edges]
         + [shape((rows // SWAPS, 128))] * SWAPS,
-        (core, ahead, temporal_weight, slope, x_t, act_t, partial, early),
+        (
+            core,
+            ahead,
+            temporal_weight,
+            slope,
+            x_t,
+            top_t,
+            bottom_t,
+            act_t,
+            partial,
+            early,
+        ),
         [
             pltpu.VMEM((3, flat, chans), BF),
             pltpu.VMEM((2 * rows, 128), BF),

time: 110 us -> 109 us (level)
  waiting for transfers between devices: 18.6 us -> 17.2 us
    ppermute x2, waiting for transfers between devices: 7.24 us -> 4.4 us  [swap_rims(): lax.ppermute(first, SPACE, steps(SPACE, -1))]
    ppermute x1, waiting for transfers between devices: 0.01 us -> 1.45 us  [local(): ahead = lax.ppermute(dy, TM, steps(TM, -1))]
    unnamed x16 -> x18, local copies, waits for them, and re-layouts: 2.52 us -> 3.39 us
    pallas_call x10 -> x11, Pallas kernels: 24.8 us -> 24.3 us  [call(): pl.pallas_call(body, out_shape=outs, in_specs=specs, out_specs=placed if...]
  transfers between devices with their start and end apart: 13 -> 13, of which waited for: 10 -> 11; matrix products, arithmetic and copies ran while one was open for 1% -> 1% of each run, Pallas kernels for 21% -> 21%
where the time goes in v13:
time: 109 us; the launch traced here: 108 us
  starting transfers between devices  41.9 us (38%)
  Pallas kernels  24.3 us (22%)
  blocking collectives  19.7 us (18%)
  waiting for transfers between devices  17.2 us (16%)
  local copies, waits for them, and re-layouts  4.38 us (4%)
    pallas_call x11, Pallas kernels, call(): pl.pallas_call(body, out_shape=outs, in_specs=specs, out_specs=placed if...  24.3 us
    all_to_all x1, blocking collectives, exchange(): return lax.all_to_all(value, axes, split_axis=0, concat_axis=0, tiled=True)  19.7 us
    all_to_all x2, starting transfers between devices, exchange(): return lax.all_to_all(value, axes, split_axis=0, concat_axis=0, tiled=True)  15.1 us
    ppermute x2, starting transfers between devices, swap_rims(): lax.ppermute(last, SPACE, steps(SPACE, 1))  8.5 us
    ppermute x1, starting transfers between devices, local(): other = lax.ppermute(own, 'core', pair)  4.92 us
    ppermute x2, waiting for transfers between devices, swap_rims(): lax.ppermute(last, SPACE, steps(SPACE, 1))  4.7 us
    all_to_all x2, waiting for transfers between devices, exchange(): return lax.all_to_all(value, axes, split_axis=0, concat_axis=0, tiled=True)  4.59 us
    ppermute x2, waiting for transfers between devices, swap_rims(): lax.ppermute(first, SPACE, steps(SPACE, -1))  4.4 us
  transfers between devices with their start and end apart: 13, of which 11 were waited for; matrix products, arithmetic and copies ran while one was open for 1% of the time, Pallas kernels for 21%

profile of v13, /device:TPU:1, one launch (start us, length us, event | category | flops | bytes accessed | tf_op | source)
XLA Modules:
  0.0 108.3 jit_solution(16602095758395595289)
XLA Ops:
  0.6 1.3 %collective-permute-start = (bf16[2,1024,256]{2,1,0:T(8,128)(2,1)}, bf16[2,1024,256]{2,1,0:T(8,128)(2,1)S(1)}, u32[]{:S(2)}, u32[]{:S(2)}) collective-permute-start(bf16[2,1024,256]{2,1,0:T(8,128)(2,1)} %bitcast.15), channel_id=1, source_target_pairs={{8,0},{16,8},{24,16},{32,24},{40,32},{48,40},{56,48},{64,56},{72,6... | collective-permute-start | bytes 3145736 | tf_op jit(solution)/shard_map/ppermute | solution.py:359
  2.9 4.5 %collective-permute-start.1 = (bf16[2,128,256]{2,1,0:T(8,128)(2,1)S(1)}, bf16[2,128,256]{2,1,0:T(8,128)(2,1)S(1)}, u32[]{:S(2)}, u32[]{:S(2)}) collective-permute-start(bf16[2,128,256]{2,1,0:T(8,128)(2,1)S(1)} %get-tuple-element.59), channel_id=1, source_target_pairs={{0,1},{1,2},{2,3},{3,4},{4,5},{5,6},{6,7},{8,9},{9,10},{10,11},{11... | collective-permute-start | bytes 393224 | tf_op jit(solution)/shard_map/ppermute | solution.py:348
  7.4 1.9 %collective-permute-start.2 = (bf16[2,128,256]{2,1,0:T(8,128)(2,1)S(1)}, bf16[2,128,256]{2,1,0:T(8,128)(2,1)S(1)}, u32[]{:S(2)}, u32[]{:S(2)}) collective-permute-start(bf16[2,128,256]{2,1,0:T(8,128)(2,1)S(1)} %get-tuple-element.58), channel_id=1, source_target_pairs={{1,0},{2,1},{3,2},{4,3},{5,4},{6,5},{7,6},{9,8},{10,9},{11,10},{12... | collective-permute-start | bytes 393224 | tf_op jit(solution)/shard_map/ppermute | solution.py:348
  9.4 1.2 %copy-done = bf16[1,2,8,128,256]{4,3,2,1,0:T(8,128)(2,1)S(1)} copy-done((bf16[1,2,8,128,256]{4,3,2,1,0:T(8,128)(2,1)S(1)}, bf16[1,2,8,128,256]{4,3,2,1,0:T(8,128)(2,1)}, u32[]{:S(2)}) %copy-start) | copy-done | bytes 1048600
  10.6 1.3 %copy-done.4 = bf16[3,3,256,256]{3,2,1,0:T(8,128)(2,1)S(1)} copy-done((bf16[3,3,256,256]{3,2,1,0:T(8,128)(2,1)S(1)}, bf16[3,3,256,256]{3,2,1,0:T(8,128)(2,1)}, u32[]{:S(2)}) %copy-start.4) | copy-done | bytes 1179672
  12.3 1.8 %collective-permute-done.2.refs_2_ = bf16[2,128,256]{2,1,0:T(8,128)(2,1)S(1)} collective-permute-done((bf16[2,128,256]{2,1,0:T(8,128)(2,1)S(1)}, bf16[2,128,256]{2,1,0:T(8,128)(2,1)S(1)}, u32[]{:S(2)}, u32[]{:S(2)}) %collective-permute-start.2) | collective-permute-done | bytes 131104 | tf_op jit(solution)/shard_map/ppermute | solution.py:348
  14.0 5.0 %shard_map.76 = (bf16[2,1024,256]{2,1,0:T(8,128)(2,1)}, f32[2,1024,256]{2,1,0:T(8,128)S(1)}, bf16[2,256,128]{2,1,0:T(8,128)(2,1)S(1)}, bf16[2,256,128]{2,1,0:T(8,128)(2,1)S(1)}, bf16[2,256,1024]{2,1,0:T(8,128)(2,1)S(1)}) custom-call(bf16[2,1024,256]{2,1,0:T(8,128)(2,1)S(1)} %bitcast.11, bf16[2,128,256]{2,1,0:T(8,128)(2,1)S(1)} %collective-permute-done.1.refs_1_, ...), custom_call_target="tpu_custom_call" | custom-call | flops 2415919104 | bytes 9437184 | tf_op jit(solution)/shard_map/pallas_call | solution.py:35
  19.0 4.3 %collective-permute-start.9 = (bf16[2,1024,256]{2,1,0:T(8,128)(2,1)}, bf16[2,1024,256]{2,1,0:T(8,128)(2,1)S(1)}, u32[]{:S(2)}, u32[]{:S(2)}) collective-permute-start(bf16[2,1024,256]{2,1,0:T(8,128)(2,1)} %get-tuple-element.47.refs_0_), channel_id=1, source_target_pairs={{0,8},{8,16},{16,24},{24,32},{32,40},{40,48},{48,56},{56,64},{64,7... | collective-permute-start | bytes 3145736 | tf_op jit(solution)/shard_map/ppermute | solution.py:389
  23.4 1.4 %shard_map.77 = (f32[2,1024,256]{2,1,0:T(8,128)S(1)}, f32[2,256,256]{2,1,0:T(8,128)S(1)}) custom-call(bf16[2,1024,256]{2,1,0:T(8,128)(2,1)S(1)} %bitcast.17, bf16[3,256,256]{2,1,0:T(8,128)(2,1)S(1)} %copy-done.3, bf16[2,256,1024]{2,1,0:T(8,128)(2,1)S(1)} %get-tuple-element.36.refs_2_.refs_7_), custom_call_target="tpu_custom_call" | custom-call | flops 1610612736 | bytes 6291456 | tf_op jit(solution)/shard_map/pallas_call | solution.py:35
  24.7 1.5 %collective-permute-done.refs_1_ = bf16[2,1024,256]{2,1,0:T(8,128)(2,1)S(1)} collective-permute-done((bf16[2,1024,256]{2,1,0:T(8,128)(2,1)}, bf16[2,1024,256]{2,1,0:T(8,128)(2,1)S(1)}, u32[]{:S(2)}, u32[]{:S(2)}) %collective-permute-start) | collective-permute-done | bytes 1048608 | tf_op jit(solution)/shard_map/ppermute | solution.py:359
  26.2 4.4 %shard_map.78 = (bf16[2,1024,256]{2,1,0:T(8,128)(2,1)S(1)}, bf16[3072,128]{1,0:T(8,128)(2,1)S(1)}, bf16[2,128,256]{2,1,0:T(8,128)(2,1)S(1)}, bf16[2,128,256]{2,1...) custom-call(s32[1]{0:T(128)} %bitcast.refs_0_, ...), custom_call_target="tpu_custom_call" | custom-call | flops 1024 | bytes 4096 | tf_op jit(solution)/shard_map/pallas_call | solution.py:35
  30.6 3.2 %collective-permute-start.3 = (bf16[768,128]{1,0:T(8,128)(2,1)S(1)}, bf16[768,128]{1,0:T(8,128)(2,1)S(1)}, u32[]{:S(2)}, u32[]{:S(2)}) collective-permute-start(bf16[768,128]{1,0:T(8,128)(2,1)S(1)} %get-tuple-element.40), channel_id=1, source_target_pairs={{0,1},{1,0},{2,3},{3,2},{4,5},{5,4},{6,7},{7,6},{8,9},{9,8},{10,11... | collective-permute-start | bytes 589832 | tf_op jit(solution)/shard_map/ppermute | solution.py:421
  36.9 10.0 %all-to-all-start = ((bf16[16,192,128]{2,1,0:T(8,128)(2,1)}), bf16[16,192,128]{2,1,0:T(8,128)(2,1)S(1)}, u32[]{:S(2)}, u32[]{:S(2)}) async-start(bf16[16,192,128]{2,1,0:T(8,128)(2,1)} %bitcast.3), calls=%async_computation | async-start | bytes 1572864 | tf_op jit(solution)/shard_map/all_to_all | solution.py:344
  46.9 4.0 %collective-permute-start.7 = (bf16[2,128,256]{2,1,0:T(8,128)(2,1)S(1)}, bf16[2,128,256]{2,1,0:T(8,128)(2,1)S(1)}, u32[]{:S(2)}, u32[]{:S(2)}) collective-permute-start(bf16[2,128,256]{2,1,0:T(8,128)(2,1)S(1)} %get-tuple-element.44), channel_id=1, source_target_pairs={{0,1},{1,2},{2,3},{3,4},{4,5},{5,6},{6,7},{8,9},{9,10},{10,11},{11... | collective-permute-start | bytes 393224 | tf_op jit(solution)/shard_map/ppermute | solution.py:348
  50.9 1.9 %collective-permute-start.8 = (bf16[2,128,256]{2,1,0:T(8,128)(2,1)S(1)}, bf16[2,128,256]{2,1,0:T(8,128)(2,1)S(1)}, u32[]{:S(2)}, u32[]{:S(2)}) collective-permute-start(bf16[2,128,256]{2,1,0:T(8,128)(2,1)S(1)} %get-tuple-element.45), channel_id=1, source_target_pairs={{1,0},{2,1},{3,2},{4,3},{5,4},{6,5},{7,6},{9,8},{10,9},{11,10},{12... | collective-permute-start | bytes 393224 | tf_op jit(solution)/shard_map/ppermute | solution.py:348
  52.8 4.7 %collective-permute-done.7.refs_1_ = bf16[2,128,256]{2,1,0:T(8,128)(2,1)S(1)} collective-permute-done((bf16[2,128,256]{2,1,0:T(8,128)(2,1)S(1)}, bf16[2,128,256]{2,1,0:T(8,128)(2,1)S(1)}, u32[]{:S(2)}, u32[]{:S(2)}) %collective-permute-start.7) | collective-permute-done | bytes 131104 | tf_op jit(solution)/shard_map/ppermute | solution.py:348
  57.5 2.6 %collective-permute-done.8.refs_2_ = bf16[2,128,256]{2,1,0:T(8,128)(2,1)S(1)} collective-permute-done((bf16[2,128,256]{2,1,0:T(8,128)(2,1)S(1)}, bf16[2,128,256]{2,1,0:T(8,128)(2,1)S(1)}, u32[]{:S(2)}, u32[]{:S(2)}) %collective-permute-start.8) | collective-permute-done | bytes 131104 | tf_op jit(solution)/shard_map/ppermute | solution.py:348
  60.2 3.9 %all-to-all-done.refs_0_ = bf16[16,192,128]{2,1,0:T(8,128)(2,1)S(1)} async-done(((bf16[16,192,128]{2,1,0:T(8,128)(2,1)}), bf16[16,192,128]{2,1,0:T(8,128)(2,1)S(1)}, u32[]{:S(2)}, u32[]{:S(2)}) %all-to-all-start) | async-done | bytes 786464 | tf_op jit(solution)/shard_map/all_to_all | solution.py:344
  64.2 19.7 %all_to_all.15.refs_0_ = bf16[8,192,128]{2,1,0:T(8,128)(2,1)S(1)} all-to-all(bf16[8,192,128]{2,1,0:T(8,128)(2,1)S(1)} %shard_map.80), channel_id=1, replica_groups=mesh['clip'=2,'y'=4,'zl'=4,'x'=4,'core'=2] {'clip','zl'}, dimensions={0} | all-to-all | bytes 786432 | tf_op jit(solution)/shard_map/all_to_all | solution.py:344
  84.8 5.1 %all-to-all-start.2 = ((bf16[16,192,128]{2,1,0:T(8,128)(2,1)}), bf16[16,192,128]{2,1,0:T(8,128)(2,1)S(1)}, u32[]{:S(2)}, u32[]{:S(2)}) async-start(bf16[16,192,128]{2,1,0:T(8,128)(2,1)} %copy-done.2), calls=%async_computation.2 | async-start | bytes 1572864 | tf_op jit(solution)/shard_map/all_to_all | solution.py:344
  90.0 3.8 %shard_map.82 = bf16[2048,256]{1,0:T(8,128)(2,1)} custom-call(bf16[2,1024,256]{2,1,0:T(8,128)(2,1)} %get-tuple-element.47.refs_0_, bf16[2,1024,256]{2,1,0:T(8,128)(2,1)S(1)} %collective-permute-done.9.refs_1_, bf16[3,256,256]{2,1,0:T(8,128)(2,1)S(1)} %copy-done.3, bf16[2048,256]{1,0:T(8,128)(2,1)S(1)} %bitcast.12), custom_call_target="tpu_custom_call" | custom-call | flops 805306368 | bytes 4194304 | tf_op jit(solution)/shard_map/pallas_call | solution.py:35
  93.8 5.7 %shard_map.83 = bf16[2,1024,256]{2,1,0:T(8,128)(2,1)} custom-call(bf16[2,1024,256]{2,1,0:T(8,128)(2,1)} %copy-done.6, bf16[2,128,256]{2,1,0:T(8,128)(2,1)} %copy-done.7, bf16[2,128,256]{2,1,0:T(8,128)(2,1)} %copy-done.8, bf16[3,3,256,256]{3,2,1,0:T(8,128)(2,1)} %refs_3_.1, bf16[2,1024,256]{2,1,0:T(8,128)(2,1)} %bitcast.16), custom_call_target="tpu_custom_call" | custom-call | flops 2415919104 | bytes 5242880 | tf_op jit(solution)/shard_map/pallas_call | solution.py:35
  100.3 4.9 %collective-permute-start.10 = (bf16[3072,128]{1,0:T(8,128)(2,1)S(1)}, bf16[3072,128]{1,0:T(8,128)(2,1)S(1)}, u32[]{:S(2)}, u32[]{:S(2)}) collective-permute-start(bf16[3072,128]{1,0:T(8,128)(2,1)S(1)} %bitcast.13), channel_id=1, source_target_pairs={{0,1},{1,0},{2,3},{3,2},{4,5},{5,4},{6,7},{7,6},{8,9},{9,8},{10,11... | collective-permute-start | bytes 2359304 | tf_op jit(solution)/shard_map/ppermute | solution.py:469
  105.2 1.2 %shard_map.84 = (f32[9,256,256]{2,1,0:T(8,128)}, f32[3,256,256]{2,1,0:T(8,128)}) custom-call(s32[1]{0:T(128)} %bitcast.refs_0_, bf16[3072,128]{1,0:T(8,128)(2,1)S(1)} %bitcast.14), custom_call_target="tpu_custom_call" | custom-call | bytes 3145728 | tf_op jit(solution)/shard_map/pallas_call | solution.py:35
  (33 shorter events, 8.2 us)
Async XLA Ops:
  0.6 25.5 %collective-permute-start = (bf16[2,1024,256]{2,1,0:T(8,128)(2,1)}, bf16[2,1024,256]{2,1,0:T(8,128)(2,1)S(1)}, u32[]{:S(2)}, u32[]{:S(2)}) collective-permute-start(bf16[2,1024,256]{2,1,0:T(8,128)(2,1)} %bitcast.15), channel_id=1, source_target_pairs={{8,0},{16,8},{24,16},{32,24},{40,32},{48,40},{56,48},{64,56},{72,6... | collective-permute-start | bytes 3145736 | tf_op jit(solution)/shard_map/ppermute | solution.py:359
  2.9 9.3 %collective-permute-start.1 = (bf16[2,128,256]{2,1,0:T(8,128)(2,1)S(1)}, bf16[2,128,256]{2,1,0:T(8,128)(2,1)S(1)}, u32[]{:S(2)}, u32[]{:S(2)}) collective-permute-start(bf16[2,128,256]{2,1,0:T(8,128)(2,1)S(1)} %get-tuple-element.59), channel_id=1, source_target_pairs={{0,1},{1,2},{2,3},{3,4},{4,5},{5,6},{6,7},{8,9},{9,10},{10,11},{11... | collective-permute-start | bytes 393224 | tf_op jit(solution)/shard_map/ppermute | solution.py:348
  7.4 6.6 %collective-permute-start.2 = (bf16[2,128,256]{2,1,0:T(8,128)(2,1)S(1)}, bf16[2,128,256]{2,1,0:T(8,128)(2,1)S(1)}, u32[]{:S(2)}, u32[]{:S(2)}) collective-permute-start(bf16[2,128,256]{2,1,0:T(8,128)(2,1)S(1)} %get-tuple-element.58), channel_id=1, source_target_pairs={{1,0},{2,1},{3,2},{4,3},{5,4},{6,5},{7,6},{9,8},{10,9},{11,10},{12... | collective-permute-start | bytes 393224 | tf_op jit(solution)/shard_map/ppermute | solution.py:348
  9.4 1.2 %copy-start = (bf16[1,2,8,128,256]{4,3,2,1,0:T(8,128)(2,1)S(1)}, bf16[1,2,8,128,256]{4,3,2,1,0:T(8,128)(2,1)}, u32[]{:S(2)}) copy-start(bf16[1,2,8,128,256]{4,3,2,1,0:T(8,128)(2,1)} %param.4) | copy-start | bytes 3145732
  10.6 1.3 %copy-start.4 = (bf16[3,3,256,256]{3,2,1,0:T(8,128)(2,1)S(1)}, bf16[3,3,256,256]{3,2,1,0:T(8,128)(2,1)}, u32[]{:S(2)}) copy-start(bf16[3,3,256,256]{3,2,1,0:T(8,128)(2,1)} %refs_3_.1) | copy-start | bytes 3538948
  14.0 9.3 %copy-start.3 = (bf16[3,256,256]{2,1,0:T(8,128)(2,1)S(1)}, bf16[3,256,256]{2,1,0:T(8,128)(2,1)}, u32[]{:S(2)}) copy-start(bf16[3,256,256]{2,1,0:T(8,128)(2,1)} %refs_2_.3) | copy-start | bytes 1179652
  14.0 9.3 %copy-start.5 = (bf16[1,2,8,128,256]{4,3,2,1,0:T(8,128)(2,1)S(1)}, bf16[1,2,8,128,256]{4,3,2,1,0:T(8,128)(2,1)}, u32[]{:S(2)}) copy-start(bf16[1,2,8,128,256]{4,3,2,1,0:T(8,128)(2,1)} %param.5) | copy-start | bytes 3145732
  19.0 45.0 %collective-permute-start.9 = (bf16[2,1024,256]{2,1,0:T(8,128)(2,1)}, bf16[2,1024,256]{2,1,0:T(8,128)(2,1)S(1)}, u32[]{:S(2)}, u32[]{:S(2)}) collective-permute-start(bf16[2,1024,256]{2,1,0:T(8,128)(2,1)} %get-tuple-element.47.refs_0_), channel_id=1, source_target_pairs={{0,8},{8,16},{16,24},{24,32},{32,40},{40,48},{48,56},{56,64},{64,7... | collective-permute-start | bytes 3145736 | tf_op jit(solution)/shard_map/ppermute | solution.py:389
  30.6 6.3 %copy-start.6 = (bf16[2,1024,256]{2,1,0:T(8,128)(2,1)}, bf16[2,1024,256]{2,1,0:T(8,128)(2,1)S(1)}, u32[]{:S(2)}) copy-start(bf16[2,1024,256]{2,1,0:T(8,128)(2,1)S(1)} %get-tuple-element.48.refs_0_) | copy-start | bytes 3145732
  30.6 4.3 %collective-permute-start.3 = (bf16[768,128]{1,0:T(8,128)(2,1)S(1)}, bf16[768,128]{1,0:T(8,128)(2,1)S(1)}, u32[]{:S(2)}, u32[]{:S(2)}) collective-permute-start(bf16[768,128]{1,0:T(8,128)(2,1)S(1)} %get-tuple-element.40), channel_id=1, source_target_pairs={{0,1},{1,0},{2,3},{3,2},{4,5},{5,4},{6,7},{7,6},{8,9},{9,8},{10,11... | collective-permute-start | bytes 589832 | tf_op jit(solution)/shard_map/ppermute | solution.py:421
  33.8 1.4 %collective-permute-start.4 = (bf16[768,128]{1,0:T(8,128)(2,1)S(1)}, bf16[768,128]{1,0:T(8,128)(2,1)S(1)}, u32[]{:S(2)}, u32[]{:S(2)}) collective-permute-start(bf16[768,128]{1,0:T(8,128)(2,1)S(1)} %get-tuple-element.41), channel_id=1, source_target_pairs={{0,1},{1,0},{2,3},{3,2},{4,5},{5,4},{6,7},{7,6},{8,9},{9,8},{10,11... | collective-permute-start | bytes 589832 | tf_op jit(solution)/shard_map/ppermute | solution.py:421
  33.9 1.6 %collective-permute-start.5 = (bf16[768,128]{1,0:T(8,128)(2,1)S(1)}, bf16[768,128]{1,0:T(8,128)(2,1)S(1)}, u32[]{:S(2)}, u32[]{:S(2)}) collective-permute-start(bf16[768,128]{1,0:T(8,128)(2,1)S(1)} %get-tuple-element.42), channel_id=1, source_target_pairs={{0,1},{1,0},{2,3},{3,2},{4,5},{5,4},{6,7},{7,6},{8,9},{9,8},{10,11... | collective-permute-start | bytes 589832 | tf_op jit(solution)/shard_map/ppermute | solution.py:421
  34.3 1.5 %collective-permute-start.6 = (bf16[768,128]{1,0:T(8,128)(2,1)S(1)}, bf16[768,128]{1,0:T(8,128)(2,1)S(1)}, u32[]{:S(2)}, u32[]{:S(2)}) collective-permute-start(bf16[768,128]{1,0:T(8,128)(2,1)S(1)} %get-tuple-element.43), channel_id=1, source_target_pairs={{0,1},{1,0},{2,3},{3,2},{4,5},{5,4},{6,7},{7,6},{8,9},{9,8},{10,11... | collective-permute-start | bytes 589832 | tf_op jit(solution)/shard_map/ppermute | solution.py:421
  36.9 27.2 %all-to-all-start = ((bf16[16,192,128]{2,1,0:T(8,128)(2,1)}), bf16[16,192,128]{2,1,0:T(8,128)(2,1)S(1)}, u32[]{:S(2)}, u32[]{:S(2)}) async-start(bf16[16,192,128]{2,1,0:T(8,128)(2,1)} %bitcast.3), calls=%async_computation | async-start | bytes 1572864 | tf_op jit(solution)/shard_map/all_to_all | solution.py:344
  46.9 10.6 %collective-permute-start.7 = (bf16[2,128,256]{2,1,0:T(8,128)(2,1)S(1)}, bf16[2,128,256]{2,1,0:T(8,128)(2,1)S(1)}, u32[]{:S(2)}, u32[]{:S(2)}) collective-permute-start(bf16[2,128,256]{2,1,0:T(8,128)(2,1)S(1)} %get-tuple-element.44), channel_id=1, source_target_pairs={{0,1},{1,2},{2,3},{3,4},{4,5},{5,6},{6,7},{8,9},{9,10},{10,11},{11... | collective-permute-start | bytes 393224 | tf_op jit(solution)/shard_map/ppermute | solution.py:348
  50.9 9.3 %collective-permute-start.8 = (bf16[2,128,256]{2,1,0:T(8,128)(2,1)S(1)}, bf16[2,128,256]{2,1,0:T(8,128)(2,1)S(1)}, u32[]{:S(2)}, u32[]{:S(2)}) collective-permute-start(bf16[2,128,256]{2,1,0:T(8,128)(2,1)S(1)} %get-tuple-element.45), channel_id=1, source_target_pairs={{1,0},{2,1},{3,2},{4,3},{5,4},{6,5},{7,6},{9,8},{10,9},{11,10},{12... | collective-permute-start | bytes 393224 | tf_op jit(solution)/shard_map/ppermute | solution.py:348
  57.5 6.5 %copy-start.7 = (bf16[2,128,256]{2,1,0:T(8,128)(2,1)}, bf16[2,128,256]{2,1,0:T(8,128)(2,1)S(1)}, u32[]{:S(2)}) copy-start(bf16[2,128,256]{2,1,0:T(8,128)(2,1)S(1)} %collective-permute-done.7.refs_1_) | copy-start | bytes 393220
  60.2 3.9 %copy-start.8 = (bf16[2,128,256]{2,1,0:T(8,128)(2,1)}, bf16[2,128,256]{2,1,0:T(8,128)(2,1)S(1)}, u32[]{:S(2)}) copy-start(bf16[2,128,256]{2,1,0:T(8,128)(2,1)S(1)} %collective-permute-done.8.refs_2_) | copy-start | bytes 393220
  64.1 25.8 %copy-start.1 = (bf16[1,2,8,128,256]{4,3,2,1,0:T(8,128)(2,1)S(1)}, bf16[1,2,8,128,256]{4,3,2,1,0:T(8,128)(2,1)}, u32[]{:S(2)}) copy-start(bf16[1,2,8,128,256]{4,3,2,1,0:T(8,128)(2,1)} %param.4) | copy-start | bytes 3145732
  83.9 0.9 copy-start.2
  84.8 15.5 %all-to-all-start.2 = ((bf16[16,192,128]{2,1,0:T(8,128)(2,1)}), bf16[16,192,128]{2,1,0:T(8,128)(2,1)S(1)}, u32[]{:S(2)}, u32[]{:S(2)}) async-start(bf16[16,192,128]{2,1,0:T(8,128)(2,1)} %copy-done.2), calls=%async_computation.2 | async-start | bytes 1572864 | tf_op jit(solution)/shard_map/all_to_all | solution.py:344
  100.3 6.8 %collective-permute-start.10 = (bf16[3072,128]{1,0:T(8,128)(2,1)S(1)}, bf16[3072,128]{1,0:T(8,128)(2,1)S(1)}, u32[]{:S(2)}, u32[]{:S(2)}) collective-permute-start(bf16[3072,128]{1,0:T(8,128)(2,1)S(1)} %bitcast.13), channel_id=1, source_target_pairs={{0,1},{1,0},{2,3},{3,2},{4,5},{5,4},{6,7},{7,6},{8,9},{9,8},{10,11... | collective-permute-start | bytes 2359304 | tf_op jit(solution)/shard_map/ppermute | solution.py:469

commit v14 on v13

--- a/solution.py
+++ b/solution.py
@@ -271,32 +271,70 @@
     return jnp.concatenate([taps[i, j] for i in range(3)], axis=1)
 
 
-def back_kernel(grad, top, bottom, weight, dy, out, padded, taps, own, result, sems):
+def last_kernel(
+    behind,
+    act,
+    x,
+    grad,
+    top,
+    bottom,
+    dy,
+    weight,
+    mix,
+    block_out,
+    input_grad,
+    ext,
+    own,
+    mixed,
+    padded,
+    taps,
+    up,
+    result,
+    sems,
+):
     frames, size, chans = own.shape
-    whole = pltpu.make_async_copy(weight, taps, sems.at[0])
-    whole.start()
-    loads = []
+    used = iter(range(sems.shape[0]))
+
+    def begin(source, target):
+        copy = pltpu.make_async_copy(source, target, sems.at[next(used)])
+        copy.start()
+        return copy
+
+    old = [begin(behind.at[f], ext.at[f]) for f in range(frames)]
+    new = [
+        [begin(act.at[f], ext.at[frames + f]), begin(x.at[f], own.at[f])] for f in range(frames)
+    ]
+    whole = begin(weight, taps)
+    loads = [
+        [
+            begin(top.at[f], padded.at[f, pl.ds(0, COLS)]),
+            begin(grad.at[f], padded.at[f, pl.ds(COLS, size)]),
+            begin(bottom.at[f], padded.at[f, pl.ds(COLS + size, COLS)]),
+            begin(dy.at[f], up.at[f]),
+        ]
+        for f in range(frames)
+    ]
+    stores = []
+    for copy in old:
+        copy.wait()
     for f in range(frames):
-        base = 1 + 5 * f
-        loads.append(
-            [
-                pltpu.make_async_copy(top.at[f], padded.at[f, pl.ds(0, COLS)], sems.at[base]),
-                pltpu.make_async_copy(
-                    grad.at[f], padded.at[f, pl.ds(COLS, size)], sems.at[base + 1]
-                ),
-                pltpu.make_async_copy(
-                    bottom.at[f], padded.at[f, pl.ds(COLS + size, COLS)], sems.at[base + 2]
-                ),
-                pltpu.make_async_copy(dy.at[f], own.at[f], sems.at[base + 3]),
-            ]
-        )
-        for load in loads[f]:
-            load.start()
+        for copy in new[f]:
+            copy.wait()
+
+        @pl.loop(0, size // CHUNK)
+        def _(step):
+            at = pl.ds(pl.multiple_of(step * CHUNK, CHUNK), CHUNK)
+            rows = jnp.concatenate([ext[f + 2 - k, at, :] for k in range(3)], axis=1)
+            total = jnp.dot(
+                rows, mix[...].reshape(3 * chans, chans), preferred_element_type=F32
+            ).astype(BF)
+            mixed[f, at, :] = (own[f, at, :].astype(F32) + total.astype(F32)).astype(BF)
+
+        stores.append(begin(mixed.at[f], block_out.at[f]))
     whole.wait()
-    stores = []
     for f in range(frames):
-        for load in loads[f]:
-            load.wait()
+        for copy in loads[f]:
+            copy.wait()
 
         @pl.loop(0, size // CHUNK)
         def _(step):
@@ -309,30 +347,11 @@
                 for j in range(3)
             ]
             back = shifted(z[0], column, -1) + z[1] + shifted(z[2], column, 1)
-            result[f, at, :] = (own[f, at, :].astype(F32) + back).astype(BF)
-
-        store = pltpu.make_async_copy(result.at[f], out.at[f], sems.at[5 + 5 * f])
-        store.start()
-        stores.append(store)
+            result[f, at, :] = (up[f, at, :].astype(F32) + back).astype(BF)
+
+        stores.append(begin(result.at[f], input_grad.at[f]))
     for store in stores:
         store.wait()
-
-
-def mix_kernel(act, behind, weight, x, out, ext):
-    frames, size, chans = act.shape
-    for f in range(frames):
-        ext[f * size : (f + 1) * size, :] = behind[f]
-        ext[(frames + f) * size : (frames + f + 1) * size, :] = act[f]
-
-    @pl.loop(0, frames * (size // CHUNK))
-    def _(step):
-        start = pl.multiple_of(step * CHUNK, CHUNK)
-        rows = jnp.concatenate(
-            [ext[pl.ds(start + (2 - k) * size, CHUNK), :] for k in range(3)], axis=1
-        )
-        mixed = jnp.dot(rows, weight[...].reshape(3 * chans, chans), preferred_element_type=F32)
-        own = x[pl.ds(start, CHUNK), :].astype(F32)
-        out[pl.ds(start, CHUNK), :] = (own + mixed.astype(BF).astype(F32)).astype(BF)
 
 
 def steps(axes, by):
@@ -433,28 +452,23 @@
         after=(behind,),
     )
     third = exchange(spread, COLUMN)
-    block_out = call(
-        mix_kernel,
-        shape((flat, chans)),
-        (act, behind, temporal_weight, x.reshape(flat, chans)),
-        [pltpu.VMEM((2 * flat, chans), BF)],
-        flops=3 * work,
-        moved=4 << 20,
-    )
-    input_grad = call(
-        back_kernel,
-        shape((frames, size, chans)),
-        (pgrad, grad_top, grad_bottom, spatial_weight, dy),
+    block_out, input_grad = call(
+        last_kernel,
+        [shape((frames, size, chans)), shape((frames, size, chans))],
+        (behind, act, x, pgrad, grad_top, grad_bottom, dy, spatial_weight, temporal_weight),
         [
+            pltpu.VMEM((2 * frames, size, chans), BF),
+            block,
+            block,
             pltpu.VMEM((frames, size + 2 * COLS, chans), BF),
             pltpu.VMEM((3, 3, chans, chans), BF),
             block,
             block,
-            pltpu.SemaphoreType.DMA((11,)),
+            pltpu.SemaphoreType.DMA((3 * frames + 1 + 4 * frames + 2 * frames,)),
         ],
-        flops=9 * work,
-        moved=5 << 20,
-        hbm=range(5),
+        flops=12 * work,
+        moved=9 << 20,
+        hbm=range(8),
         out_hbm=True,
         limit=58,
     )

time: 109 us -> 109 us (level)
  waiting for transfers between devices: 17.2 us -> 18.5 us
    all_to_all x2, waiting for transfers between devices: 4.59 us -> 5.92 us  [exchange(): return lax.all_to_all(value, axes, split_axis=0, concat_axis=0, tiled=True)]
    unnamed x18 -> x16, local copies, waits for them, and re-layouts: 3.39 us -> 2.51 us
    pallas_call x11 -> x10, Pallas kernels: 24.3 us -> 24 us  [call(): pl.pallas_call(body, out_shape=outs, in_specs=specs, out_specs=placed if...]
  transfers between devices with their start and end apart: 13 -> 13, of which waited for: 11 -> 11; matrix products, arithmetic and copies ran while one was open for 1% -> 1% of each run, Pallas kernels for 21% -> 20%
where the time goes in v14:
time: 109 us; the launch traced here: 108 us
  starting transfers between devices  41.9 us (38%)
  Pallas kernels  24 us (22%)
  blocking collectives  19.6 us (18%)
  waiting for transfers between devices  18.5 us (17%)
  local copies, waits for them, and re-layouts  3.51 us (3%)
    pallas_call x10, Pallas kernels, call(): pl.pallas_call(body, out_shape=outs, in_specs=specs, out_specs=placed if...  24 us
    all_to_all x1, blocking collectives, exchange(): return lax.all_to_all(value, axes, split_axis=0, concat_axis=0, tiled=True)  19.6 us
    all_to_all x2, starting transfers between devices, exchange(): return lax.all_to_all(value, axes, split_axis=0, concat_axis=0, tiled=True)  15.1 us
    ppermute x2, starting transfers between devices, swap_rims(): lax.ppermute(last, SPACE, steps(SPACE, 1))  8.5 us
    all_to_all x2, waiting for transfers between devices, exchange(): return lax.all_to_all(value, axes, split_axis=0, concat_axis=0, tiled=True)  5.92 us
    ppermute x1, starting transfers between devices, local(): other = lax.ppermute(own, 'core', pair)  4.92 us
    ppermute x2, waiting for transfers between devices, swap_rims(): lax.ppermute(last, SPACE, steps(SPACE, 1))  4.7 us
    ppermute x2, waiting for transfers between devices, swap_rims(): lax.ppermute(first, SPACE, steps(SPACE, -1))  4.37 us
  transfers between devices with their start and end apart: 13, of which 11 were waited for; matrix products, arithmetic and copies ran while one was open for 1% of the time, Pallas kernels for 20%

profile of v14, /device:TPU:1, one launch (start us, length us, event | category | flops | bytes accessed | tf_op | source)
XLA Modules:
  0.0 108.2 jit_solution(5932213829876608467)
XLA Ops:
  0.6 1.3 %collective-permute-start = (bf16[2,1024,256]{2,1,0:T(8,128)(2,1)}, bf16[2,1024,256]{2,1,0:T(8,128)(2,1)S(1)}, u32[]{:S(2)}, u32[]{:S(2)}) collective-permute-start(bf16[2,1024,256]{2,1,0:T(8,128)(2,1)} %bitcast.14), channel_id=1, source_target_pairs={{8,0},{16,8},{24,16},{32,24},{40,32},{48,40},{56,48},{64,56},{72,6... | collective-permute-start | bytes 3145736 | tf_op jit(solution)/shard_map/ppermute | solution.py:378
  2.9 4.5 %collective-permute-start.1 = (bf16[2,128,256]{2,1,0:T(8,128)(2,1)S(1)}, bf16[2,128,256]{2,1,0:T(8,128)(2,1)S(1)}, u32[]{:S(2)}, u32[]{:S(2)}) collective-permute-start(bf16[2,128,256]{2,1,0:T(8,128)(2,1)S(1)} %get-tuple-element.63), channel_id=1, source_target_pairs={{0,1},{1,2},{2,3},{3,4},{4,5},{5,6},{6,7},{8,9},{9,10},{10,11},{11... | collective-permute-start | bytes 393224 | tf_op jit(solution)/shard_map/ppermute | solution.py:367
  7.4 1.9 %collective-permute-start.2 = (bf16[2,128,256]{2,1,0:T(8,128)(2,1)S(1)}, bf16[2,128,256]{2,1,0:T(8,128)(2,1)S(1)}, u32[]{:S(2)}, u32[]{:S(2)}) collective-permute-start(bf16[2,128,256]{2,1,0:T(8,128)(2,1)S(1)} %get-tuple-element.62), channel_id=1, source_target_pairs={{1,0},{2,1},{3,2},{4,3},{5,4},{6,5},{7,6},{9,8},{10,9},{11,10},{12... | collective-permute-start | bytes 393224 | tf_op jit(solution)/shard_map/ppermute | solution.py:367
  9.4 1.2 %copy-done = bf16[1,2,8,128,256]{4,3,2,1,0:T(8,128)(2,1)S(1)} copy-done((bf16[1,2,8,128,256]{4,3,2,1,0:T(8,128)(2,1)S(1)}, bf16[1,2,8,128,256]{4,3,2,1,0:T(8,128)(2,1)}, u32[]{:S(2)}) %copy-start) | copy-done | bytes 1048600
  10.6 1.3 %copy-done.1 = bf16[3,3,256,256]{3,2,1,0:T(8,128)(2,1)S(1)} copy-done((bf16[3,3,256,256]{3,2,1,0:T(8,128)(2,1)S(1)}, bf16[3,3,256,256]{3,2,1,0:T(8,128)(2,1)}, u32[]{:S(2)}) %copy-start.1) | copy-done | bytes 1179672
  12.3 1.8 %collective-permute-done.2.refs_2_ = bf16[2,128,256]{2,1,0:T(8,128)(2,1)S(1)} collective-permute-done((bf16[2,128,256]{2,1,0:T(8,128)(2,1)S(1)}, bf16[2,128,256]{2,1,0:T(8,128)(2,1)S(1)}, u32[]{:S(2)}, u32[]{:S(2)}) %collective-permute-start.2) | collective-permute-done | bytes 131104 | tf_op jit(solution)/shard_map/ppermute | solution.py:367
  14.0 5.0 %shard_map.76 = (bf16[2,1024,256]{2,1,0:T(8,128)(2,1)}, f32[2,1024,256]{2,1,0:T(8,128)S(1)}, bf16[2,256,128]{2,1,0:T(8,128)(2,1)S(1)}, bf16[2,256,128]{2,1,0:T(8,128)(2,1)S(1)}, bf16[2,256,1024]{2,1,0:T(8,128)(2,1)S(1)}) custom-call(bf16[2,1024,256]{2,1,0:T(8,128)(2,1)S(1)} %bitcast.13, bf16[2,128,256]{2,1,0:T(8,128)(2,1)S(1)} %collective-permute-done.1.refs_1_, ...), custom_call_target="tpu_custom_call" | custom-call | flops 2415919104 | bytes 9437184 | tf_op jit(solution)/shard_map/pallas_call | solution.py:35
  19.1 4.3 %collective-permute-start.9 = (bf16[2,1024,256]{2,1,0:T(8,128)(2,1)}, bf16[2,1024,256]{2,1,0:T(8,128)(2,1)S(1)}, u32[]{:S(2)}, u32[]{:S(2)}) collective-permute-start(bf16[2,1024,256]{2,1,0:T(8,128)(2,1)} %get-tuple-element.49.refs_1_), channel_id=1, source_target_pairs={{0,8},{8,16},{16,24},{24,32},{32,40},{40,48},{48,56},{56,64},{64,7... | collective-permute-start | bytes 3145736 | tf_op jit(solution)/shard_map/ppermute | solution.py:408
  23.4 1.4 %shard_map.77 = (f32[2,1024,256]{2,1,0:T(8,128)S(1)}, f32[2,256,256]{2,1,0:T(8,128)S(1)}) custom-call(bf16[2,1024,256]{2,1,0:T(8,128)(2,1)S(1)} %bitcast.16, bf16[3,256,256]{2,1,0:T(8,128)(2,1)S(1)} %copy-done.3, bf16[2,256,1024]{2,1,0:T(8,128)(2,1)S(1)} %get-tuple-element.38.refs_2_.refs_7_), custom_call_target="tpu_custom_call" | custom-call | flops 1610612736 | bytes 6291456 | tf_op jit(solution)/shard_map/pallas_call | solution.py:35
  24.8 1.4 %collective-permute-done.refs_1_ = bf16[2,1024,256]{2,1,0:T(8,128)(2,1)S(1)} collective-permute-done((bf16[2,1024,256]{2,1,0:T(8,128)(2,1)}, bf16[2,1024,256]{2,1,0:T(8,128)(2,1)S(1)}, u32[]{:S(2)}, u32[]{:S(2)}) %collective-permute-start) | collective-permute-done | bytes 1048608 | tf_op jit(solution)/shard_map/ppermute | solution.py:378
  26.2 4.4 %shard_map.78 = (bf16[2,1024,256]{2,1,0:T(8,128)(2,1)S(1)}, bf16[3072,128]{1,0:T(8,128)(2,1)S(1)}, bf16[2,128,256]{2,1,0:T(8,128)(2,1)S(1)}, bf16[2,128,256]{2,1...) custom-call(s32[1]{0:T(128)} %bitcast.refs_0_, ...), custom_call_target="tpu_custom_call" | custom-call | flops 1024 | bytes 4096 | tf_op jit(solution)/shard_map/pallas_call | solution.py:35
  30.6 3.2 %collective-permute-start.3 = (bf16[768,128]{1,0:T(8,128)(2,1)S(1)}, bf16[768,128]{1,0:T(8,128)(2,1)S(1)}, u32[]{:S(2)}, u32[]{:S(2)}) collective-permute-start(bf16[768,128]{1,0:T(8,128)(2,1)S(1)} %get-tuple-element.42), channel_id=1, source_target_pairs={{0,1},{1,0},{2,3},{3,2},{4,5},{5,4},{6,7},{7,6},{8,9},{9,8},{10,11... | collective-permute-start | bytes 589832 | tf_op jit(solution)/shard_map/ppermute | solution.py:440
  36.9 10.0 %all-to-all-start = ((bf16[16,192,128]{2,1,0:T(8,128)(2,1)}), bf16[16,192,128]{2,1,0:T(8,128)(2,1)S(1)}, u32[]{:S(2)}, u32[]{:S(2)}) async-start(bf16[16,192,128]{2,1,0:T(8,128)(2,1)} %bitcast.3), calls=%async_computation | async-start | bytes 1572864 | tf_op jit(solution)/shard_map/all_to_all | solution.py:363
  46.9 4.0 %collective-permute-start.7 = (bf16[2,128,256]{2,1,0:T(8,128)(2,1)S(1)}, bf16[2,128,256]{2,1,0:T(8,128)(2,1)S(1)}, u32[]{:S(2)}, u32[]{:S(2)}) collective-permute-start(bf16[2,128,256]{2,1,0:T(8,128)(2,1)S(1)} %get-tuple-element.46), channel_id=1, source_target_pairs={{0,1},{1,2},{2,3},{3,4},{4,5},{5,6},{6,7},{8,9},{9,10},{10,11},{11... | collective-permute-start | bytes 393224 | tf_op jit(solution)/shard_map/ppermute | solution.py:367
  50.9 1.9 %collective-permute-start.8 = (bf16[2,128,256]{2,1,0:T(8,128)(2,1)S(1)}, bf16[2,128,256]{2,1,0:T(8,128)(2,1)S(1)}, u32[]{:S(2)}, u32[]{:S(2)}) collective-permute-start(bf16[2,128,256]{2,1,0:T(8,128)(2,1)S(1)} %get-tuple-element.47), channel_id=1, source_target_pairs={{1,0},{2,1},{3,2},{4,3},{5,4},{6,5},{7,6},{9,8},{10,9},{11,10},{12... | collective-permute-start | bytes 393224 | tf_op jit(solution)/shard_map/ppermute | solution.py:367
  52.8 4.7 %collective-permute-done.7.refs_4_ = bf16[2,128,256]{2,1,0:T(8,128)(2,1)S(1)} collective-permute-done((bf16[2,128,256]{2,1,0:T(8,128)(2,1)S(1)}, bf16[2,128,256]{2,1,0:T(8,128)(2,1)S(1)}, u32[]{:S(2)}, u32[]{:S(2)}) %collective-permute-start.7) | collective-permute-done | bytes 131104 | tf_op jit(solution)/shard_map/ppermute | solution.py:367
  57.5 2.6 %collective-permute-done.8.refs_5_ = bf16[2,128,256]{2,1,0:T(8,128)(2,1)S(1)} collective-permute-done((bf16[2,128,256]{2,1,0:T(8,128)(2,1)S(1)}, bf16[2,128,256]{2,1,0:T(8,128)(2,1)S(1)}, u32[]{:S(2)}, u32[]{:S(2)}) %collective-permute-start.8) | collective-permute-done | bytes 131104 | tf_op jit(solution)/shard_map/ppermute | solution.py:367
  60.2 3.9 %all-to-all-done.refs_0_ = bf16[16,192,128]{2,1,0:T(8,128)(2,1)S(1)} async-done(((bf16[16,192,128]{2,1,0:T(8,128)(2,1)}), bf16[16,192,128]{2,1,0:T(8,128)(2,1)S(1)}, u32[]{:S(2)}, u32[]{:S(2)}) %all-to-all-start) | async-done | bytes 786464 | tf_op jit(solution)/shard_map/all_to_all | solution.py:363
  64.1 19.6 %all_to_all.15.refs_0_ = bf16[8,192,128]{2,1,0:T(8,128)(2,1)S(1)} all-to-all(bf16[8,192,128]{2,1,0:T(8,128)(2,1)S(1)} %shard_map.80), channel_id=1, replica_groups=mesh['clip'=2,'y'=4,'zl'=4,'x'=4,'core'=2] {'clip','zl'}, dimensions={0} | all-to-all | bytes 786432 | tf_op jit(solution)/shard_map/all_to_all | solution.py:363
  84.7 5.1 %all-to-all-start.2 = ((bf16[16,192,128]{2,1,0:T(8,128)(2,1)}), bf16[16,192,128]{2,1,0:T(8,128)(2,1)S(1)}, u32[]{:S(2)}, u32[]{:S(2)}) async-start(bf16[16,192,128]{2,1,0:T(8,128)(2,1)} %shard_map.81), calls=%async_computation.2 | async-start | bytes 1572864 | tf_op jit(solution)/shard_map/all_to_all | solution.py:363
  89.8 8.3 %shard_map.82 = (bf16[2,1024,256]{2,1,0:T(8,128)(2,1)}, bf16[2,1024,256]{2,1,0:T(8,128)(2,1)}) custom-call(bf16[2,1024,256]{2,1,0:T(8,128)(2,1)} %copy-done.2, bf16[2,1024,256]{2,1,0:T(8,128)(2,1)} %get-tuple-element.49.refs_1_, bf16[2,1024,256]{2,1,0:T(8,128)(2,1)} %bitcast.11, bf16[2,1024,256]{2,1,0:T(8,128)(2,1)} %copy-done.5, ...), custom_call_target="tpu_custom_call" | custom-call | flops 3221225472 | bytes 9437184 | tf_op jit(solution)/shard_map/pallas_call | solution.py:35
  98.1 2.1 %all-to-all-done.2 = bf16[16,192,128]{2,1,0:T(8,128)(2,1)S(1)} async-done(((bf16[16,192,128]{2,1,0:T(8,128)(2,1)}), bf16[16,192,128]{2,1,0:T(8,128)(2,1)S(1)}, u32[]{:S(2)}, u32[]{:S(2)}) %all-to-all-start.2) | async-done | bytes 786464 | tf_op jit(solution)/shard_map/all_to_all | solution.py:363
  100.1 4.9 %collective-permute-start.10 = (bf16[3072,128]{1,0:T(8,128)(2,1)S(1)}, bf16[3072,128]{1,0:T(8,128)(2,1)S(1)}, u32[]{:S(2)}, u32[]{:S(2)}) collective-permute-start(bf16[3072,128]{1,0:T(8,128)(2,1)S(1)} %bitcast.8), channel_id=1, source_target_pairs={{0,1},{1,0},{2,3},{3,2},{4,5},{5,4},{6,7},{7,6},{8,9},{9,8},{10,11... | collective-permute-start | bytes 2359304 | tf_op jit(solution)/shard_map/ppermute | solution.py:483
  105.1 1.2 %shard_map.83 = (f32[9,256,256]{2,1,0:T(8,128)}, f32[3,256,256]{2,1,0:T(8,128)}) custom-call(s32[1]{0:T(128)} %bitcast.refs_0_, bf16[3072,128]{1,0:T(8,128)(2,1)S(1)} %bitcast.9), custom_call_target="tpu_custom_call" | custom-call | bytes 3145728 | tf_op jit(solution)/shard_map/pallas_call | solution.py:35
  (30 shorter events, 7.4 us)
Async XLA Ops:
  0.6 25.5 %collective-permute-start = (bf16[2,1024,256]{2,1,0:T(8,128)(2,1)}, bf16[2,1024,256]{2,1,0:T(8,128)(2,1)S(1)}, u32[]{:S(2)}, u32[]{:S(2)}) collective-permute-start(bf16[2,1024,256]{2,1,0:T(8,128)(2,1)} %bitcast.14), channel_id=1, source_target_pairs={{8,0},{16,8},{24,16},{32,24},{40,32},{48,40},{56,48},{64,56},{72,6... | collective-permute-start | bytes 3145736 | tf_op jit(solution)/shard_map/ppermute | solution.py:378
  2.9 9.3 %collective-permute-start.1 = (bf16[2,128,256]{2,1,0:T(8,128)(2,1)S(1)}, bf16[2,128,256]{2,1,0:T(8,128)(2,1)S(1)}, u32[]{:S(2)}, u32[]{:S(2)}) collective-permute-start(bf16[2,128,256]{2,1,0:T(8,128)(2,1)S(1)} %get-tuple-element.63), channel_id=1, source_target_pairs={{0,1},{1,2},{2,3},{3,4},{4,5},{5,6},{6,7},{8,9},{9,10},{10,11},{11... | collective-permute-start | bytes 393224 | tf_op jit(solution)/shard_map/ppermute | solution.py:367
  7.4 6.6 %collective-permute-start.2 = (bf16[2,128,256]{2,1,0:T(8,128)(2,1)S(1)}, bf16[2,128,256]{2,1,0:T(8,128)(2,1)S(1)}, u32[]{:S(2)}, u32[]{:S(2)}) collective-permute-start(bf16[2,128,256]{2,1,0:T(8,128)(2,1)S(1)} %get-tuple-element.62), channel_id=1, source_target_pairs={{1,0},{2,1},{3,2},{4,3},{5,4},{6,5},{7,6},{9,8},{10,9},{11,10},{12... | collective-permute-start | bytes 393224 | tf_op jit(solution)/shard_map/ppermute | solution.py:367
  9.4 1.2 %copy-start = (bf16[1,2,8,128,256]{4,3,2,1,0:T(8,128)(2,1)S(1)}, bf16[1,2,8,128,256]{4,3,2,1,0:T(8,128)(2,1)}, u32[]{:S(2)}) copy-start(bf16[1,2,8,128,256]{4,3,2,1,0:T(8,128)(2,1)} %param.4) | copy-start | bytes 3145732
  10.6 1.3 %copy-start.1 = (bf16[3,3,256,256]{3,2,1,0:T(8,128)(2,1)S(1)}, bf16[3,3,256,256]{3,2,1,0:T(8,128)(2,1)}, u32[]{:S(2)}) copy-start(bf16[3,3,256,256]{3,2,1,0:T(8,128)(2,1)} %refs_7_.1) | copy-start | bytes 3538948
  14.0 9.4 %copy-start.3 = (bf16[3,256,256]{2,1,0:T(8,128)(2,1)S(1)}, bf16[3,256,256]{2,1,0:T(8,128)(2,1)}, u32[]{:S(2)}) copy-start(bf16[3,256,256]{2,1,0:T(8,128)(2,1)} %refs_8_.1) | copy-start | bytes 1179652
  14.0 9.4 %copy-start.4 = (bf16[1,2,8,128,256]{4,3,2,1,0:T(8,128)(2,1)S(1)}, bf16[1,2,8,128,256]{4,3,2,1,0:T(8,128)(2,1)}, u32[]{:S(2)}) copy-start(bf16[1,2,8,128,256]{4,3,2,1,0:T(8,128)(2,1)} %param.5) | copy-start | bytes 3145732
  19.1 45.0 %collective-permute-start.9 = (bf16[2,1024,256]{2,1,0:T(8,128)(2,1)}, bf16[2,1024,256]{2,1,0:T(8,128)(2,1)S(1)}, u32[]{:S(2)}, u32[]{:S(2)}) collective-permute-start(bf16[2,1024,256]{2,1,0:T(8,128)(2,1)} %get-tuple-element.49.refs_1_), channel_id=1, source_target_pairs={{0,8},{8,16},{16,24},{24,32},{32,40},{40,48},{48,56},{56,64},{64,7... | collective-permute-start | bytes 3145736 | tf_op jit(solution)/shard_map/ppermute | solution.py:408
  30.6 6.3 %copy-start.5 = (bf16[2,1024,256]{2,1,0:T(8,128)(2,1)}, bf16[2,1024,256]{2,1,0:T(8,128)(2,1)S(1)}, u32[]{:S(2)}) copy-start(bf16[2,1024,256]{2,1,0:T(8,128)(2,1)S(1)} %get-tuple-element.50.refs_3_) | copy-start | bytes 3145732
  30.6 4.3 %collective-permute-start.3 = (bf16[768,128]{1,0:T(8,128)(2,1)S(1)}, bf16[768,128]{1,0:T(8,128)(2,1)S(1)}, u32[]{:S(2)}, u32[]{:S(2)}) collective-permute-start(bf16[768,128]{1,0:T(8,128)(2,1)S(1)} %get-tuple-element.42), channel_id=1, source_target_pairs={{0,1},{1,0},{2,3},{3,2},{4,5},{5,4},{6,7},{7,6},{8,9},{9,8},{10,11... | collective-permute-start | bytes 589832 | tf_op jit(solution)/shard_map/ppermute | solution.py:440
  33.8 1.4 %collective-permute-start.4 = (bf16[768,128]{1,0:T(8,128)(2,1)S(1)}, bf16[768,128]{1,0:T(8,128)(2,1)S(1)}, u32[]{:S(2)}, u32[]{:S(2)}) collective-permute-start(bf16[768,128]{1,0:T(8,128)(2,1)S(1)} %get-tuple-element.43), channel_id=1, source_target_pairs={{0,1},{1,0},{2,3},{3,2},{4,5},{5,4},{6,7},{7,6},{8,9},{9,8},{10,11... | collective-permute-start | bytes 589832 | tf_op jit(solution)/shard_map/ppermute | solution.py:440
  33.9 1.6 %collective-permute-start.5 = (bf16[768,128]{1,0:T(8,128)(2,1)S(1)}, bf16[768,128]{1,0:T(8,128)(2,1)S(1)}, u32[]{:S(2)}, u32[]{:S(2)}) collective-permute-start(bf16[768,128]{1,0:T(8,128)(2,1)S(1)} %get-tuple-element.44), channel_id=1, source_target_pairs={{0,1},{1,0},{2,3},{3,2},{4,5},{5,4},{6,7},{7,6},{8,9},{9,8},{10,11... | collective-permute-start | bytes 589832 | tf_op jit(solution)/shard_map/ppermute | solution.py:440
  34.3 1.5 %collective-permute-start.6 = (bf16[768,128]{1,0:T(8,128)(2,1)S(1)}, bf16[768,128]{1,0:T(8,128)(2,1)S(1)}, u32[]{:S(2)}, u32[]{:S(2)}) collective-permute-start(bf16[768,128]{1,0:T(8,128)(2,1)S(1)} %get-tuple-element.45), channel_id=1, source_target_pairs={{0,1},{1,0},{2,3},{3,2},{4,5},{5,4},{6,7},{7,6},{8,9},{9,8},{10,11... | collective-permute-start | bytes 589832 | tf_op jit(solution)/shard_map/ppermute | solution.py:440
  36.9 27.1 %all-to-all-start = ((bf16[16,192,128]{2,1,0:T(8,128)(2,1)}), bf16[16,192,128]{2,1,0:T(8,128)(2,1)S(1)}, u32[]{:S(2)}, u32[]{:S(2)}) async-start(bf16[16,192,128]{2,1,0:T(8,128)(2,1)} %bitcast.3), calls=%async_computation | async-start | bytes 1572864 | tf_op jit(solution)/shard_map/all_to_all | solution.py:363
  46.9 10.6 %collective-permute-start.7 = (bf16[2,128,256]{2,1,0:T(8,128)(2,1)S(1)}, bf16[2,128,256]{2,1,0:T(8,128)(2,1)S(1)}, u32[]{:S(2)}, u32[]{:S(2)}) collective-permute-start(bf16[2,128,256]{2,1,0:T(8,128)(2,1)S(1)} %get-tuple-element.46), channel_id=1, source_target_pairs={{0,1},{1,2},{2,3},{3,4},{4,5},{5,6},{6,7},{8,9},{9,10},{10,11},{11... | collective-permute-start | bytes 393224 | tf_op jit(solution)/shard_map/ppermute | solution.py:367
  50.9 9.2 %collective-permute-start.8 = (bf16[2,128,256]{2,1,0:T(8,128)(2,1)S(1)}, bf16[2,128,256]{2,1,0:T(8,128)(2,1)S(1)}, u32[]{:S(2)}, u32[]{:S(2)}) collective-permute-start(bf16[2,128,256]{2,1,0:T(8,128)(2,1)S(1)} %get-tuple-element.47), channel_id=1, source_target_pairs={{1,0},{2,1},{3,2},{4,3},{5,4},{6,5},{7,6},{9,8},{10,9},{11,10},{12... | collective-permute-start | bytes 393224 | tf_op jit(solution)/shard_map/ppermute | solution.py:367
  57.5 27.1 %copy-start.6 = (bf16[2,128,256]{2,1,0:T(8,128)(2,1)}, bf16[2,128,256]{2,1,0:T(8,128)(2,1)S(1)}, u32[]{:S(2)}) copy-start(bf16[2,128,256]{2,1,0:T(8,128)(2,1)S(1)} %collective-permute-done.7.refs_4_) | copy-start | bytes 393220
  60.2 24.5 %copy-start.7 = (bf16[2,128,256]{2,1,0:T(8,128)(2,1)}, bf16[2,128,256]{2,1,0:T(8,128)(2,1)S(1)}, u32[]{:S(2)}) copy-start(bf16[2,128,256]{2,1,0:T(8,128)(2,1)S(1)} %collective-permute-done.8.refs_5_) | copy-start | bytes 393220
  64.0 20.6 %copy-start.2 = (bf16[2,1024,256]{2,1,0:T(8,128)(2,1)}, bf16[2,1024,256]{2,1,0:T(8,128)(2,1)S(1)}, u32[]{:S(2)}) copy-start(bf16[2,1024,256]{2,1,0:T(8,128)(2,1)S(1)} %collective-permute-done.9.refs_1_.refs_0_) | copy-start | bytes 3145732
  84.7 15.5 %all-to-all-start.2 = ((bf16[16,192,128]{2,1,0:T(8,128)(2,1)}), bf16[16,192,128]{2,1,0:T(8,128)(2,1)S(1)}, u32[]{:S(2)}, u32[]{:S(2)}) async-start(bf16[16,192,128]{2,1,0:T(8,128)(2,1)} %shard_map.81), calls=%async_computation.2 | async-start | bytes 1572864 | tf_op jit(solution)/shard_map/all_to_all | solution.py:363
  100.1 6.8 %collective-permute-start.10 = (bf16[3072,128]{1,0:T(8,128)(2,1)S(1)}, bf16[3072,128]{1,0:T(8,128)(2,1)S(1)}, u32[]{:S(2)}, u32[]{:S(2)}) collective-permute-start(bf16[3072,128]{1,0:T(8,128)(2,1)S(1)} %bitcast.8), channel_id=1, source_target_pairs={{0,1},{1,0},{2,3},{3,2},{4,5},{5,4},{6,7},{7,6},{8,9},{9,8},{10,11... | collective-permute-start | bytes 2359304 | tf_op jit(solution)/shard_map/ppermute | solution.py:483

commit v15 on v14

--- a/solution.py
+++ b/solution.py
@@ -12,7 +12,7 @@
 TM = ("y", "zl")
 SPACE = ("x", "core")
 PLANE = ("x", "y")
-COLUMN = ("clip", "zl")
+COLUMN = ("zl", "clip")
 COLS = 128
 NT = (((1,), (1,)), ((), ()))
 
@@ -64,6 +64,7 @@
 
 
 CHUNK = 512
+BLOCK = 1024
 SWAPS = 4
 
 
@@ -85,12 +86,12 @@
     for f in range(frames):
         fill(padded, x, top, bottom, f)
 
-    @pl.loop(0, frames * (size // CHUNK))
+    @pl.loop(0, frames * (size // BLOCK))
     def _(step):
-        f = step // (size // CHUNK)
-        start = pl.multiple_of((step % (size // CHUNK)) * CHUNK, CHUNK)
-        rows = window(padded, f, start, CHUNK, (0, 1, 2))
-        column = columns_of(CHUNK, chans)
+        f = step // (size // BLOCK)
+        start = pl.multiple_of((step % (size // BLOCK)) * BLOCK, BLOCK)
+        rows = window(padded, f, start, BLOCK, (0, 1, 2))
+        column = columns_of(BLOCK, chans)
         z = [
             jnp.dot(rows, weight[:, j].reshape(3 * chans, chans), preferred_element_type=F32)
             for j in range(3)
@@ -98,9 +99,9 @@
         pre = shifted(z[0], column, 1) + z[1] + shifted(z[2], column, -1)
         sigma = 1.0 / (1.0 + jnp.exp(-pre))
         active = (pre * sigma).astype(BF)
-        act[f, pl.ds(start, CHUNK), :] = active
-        slope[f, pl.ds(start, CHUNK), :] = sigma * (1.0 + pre * (1.0 - sigma))
-        act_t[f, :, pl.ds(start, CHUNK)] = active.T
+        act[f, pl.ds(start, BLOCK), :] = active
+        slope[f, pl.ds(start, BLOCK), :] = sigma * (1.0 + pre * (1.0 - sigma))
+        act_t[f, :, pl.ds(start, BLOCK)] = active.T
 
     for f in range(frames):
         top_t[f] = top[f].T
@@ -110,9 +111,9 @@
 def early_kernel(dy, weight, act_t, partial, terms):
     frames, size, chans = dy.shape
 
-    @pl.loop(0, size // CHUNK)
+    @pl.loop(0, size // BLOCK)
     def _(step):
-        at = pl.ds(pl.multiple_of(step * CHUNK, CHUNK), CHUNK)
+        at = pl.ds(pl.multiple_of(step * BLOCK, BLOCK), BLOCK)
         second = dy[1, at, :]
         both = jnp.concatenate([dy[0, at, :], second], axis=1)
         taps = jnp.concatenate([weight[0], weight[1]], axis=1)

time: 109 us -> 108 us (level)
  the two profiles are of different devices: /device:TPU:1 before, /device:TPU:33 now
where the time goes in v15:
time: 108 us
  starting transfers between devices  33.7 us (31%)
  blocking collectives  27.3 us (25%)
  Pallas kernels  23.1 us (21%)
  waiting for transfers between devices  19.2 us (18%)
  local copies, waits for them, and re-layouts  3.51 us (3%)
    all_to_all x1, blocking collectives, exchange(): return lax.all_to_all(value, axes, split_axis=0, concat_axis=0, tiled=True)  27.3 us
    pallas_call x10, Pallas kernels, call(): pl.pallas_call(body, out_shape=outs, in_specs=specs, out_specs=placed if...  23.1 us
    all_to_all x2, starting transfers between devices, exchange(): return lax.all_to_all(value, axes, split_axis=0, concat_axis=0, tiled=True)  11.9 us
    ppermute x2, starting transfers between devices, swap_rims(): lax.ppermute(last, SPACE, steps(SPACE, 1))  7.77 us
    ppermute x2, waiting for transfers between devices, swap_rims(): lax.ppermute(last, SPACE, steps(SPACE, 1))  4.53 us
    all_to_all x2, waiting for transfers between devices, exchange(): return lax.all_to_all(value, axes, split_axis=0, concat_axis=0, tiled=True)  4.48 us
    ppermute x1, waiting for transfers between devices, local(): ahead = lax.ppermute(dy, TM, steps(TM, -1))  4.1 us
    ppermute x2, waiting for transfers between devices, swap_rims(): lax.ppermute(first, SPACE, steps(SPACE, -1))  3.99 us
  transfers between devices with their start and end apart: 13, of which 10 were waited for; matrix products, arithmetic and copies ran while one was open for 1% of the time, Pallas kernels for 19%

profile of v15, /device:TPU:33, one launch (start us, length us, event | category | flops | bytes accessed | tf_op | source)
XLA Modules:
  0.0 107.6 jit_solution(1688641513810608749)
XLA Ops:
  0.6 1.9 %collective-permute-start = (bf16[2,1024,256]{2,1,0:T(8,128)(2,1)}, bf16[2,1024,256]{2,1,0:T(8,128)(2,1)S(1)}, u32[]{:S(2)}, u32[]{:S(2)}) collective-permute-start(bf16[2,1024,256]{2,1,0:T(8,128)(2,1)} %bitcast.14), channel_id=1, source_target_pairs={{8,0},{16,8},{24,16},{32,24},{40,32},{48,40},{56,48},{64,56},{72,6... | collective-permute-start | bytes 3145736 | tf_op jit(solution)/shard_map/ppermute | solution.py:379
  3.6 3.8 %collective-permute-start.1 = (bf16[2,128,256]{2,1,0:T(8,128)(2,1)S(1)}, bf16[2,128,256]{2,1,0:T(8,128)(2,1)S(1)}, u32[]{:S(2)}, u32[]{:S(2)}) collective-permute-start(bf16[2,128,256]{2,1,0:T(8,128)(2,1)S(1)} %get-tuple-element.63), channel_id=1, source_target_pairs={{0,1},{1,2},{2,3},{3,4},{4,5},{5,6},{6,7},{8,9},{9,10},{10,11},{11... | collective-permute-start | bytes 393224 | tf_op jit(solution)/shard_map/ppermute | solution.py:368
  7.3 1.9 %collective-permute-start.2 = (bf16[2,128,256]{2,1,0:T(8,128)(2,1)S(1)}, bf16[2,128,256]{2,1,0:T(8,128)(2,1)S(1)}, u32[]{:S(2)}, u32[]{:S(2)}) collective-permute-start(bf16[2,128,256]{2,1,0:T(8,128)(2,1)S(1)} %get-tuple-element.62), channel_id=1, source_target_pairs={{1,0},{2,1},{3,2},{4,3},{5,4},{6,5},{7,6},{9,8},{10,9},{11,10},{12... | collective-permute-start | bytes 393224 | tf_op jit(solution)/shard_map/ppermute | solution.py:368
  9.3 1.2 %copy-done = bf16[1,2,8,128,256]{4,3,2,1,0:T(8,128)(2,1)S(1)} copy-done((bf16[1,2,8,128,256]{4,3,2,1,0:T(8,128)(2,1)S(1)}, bf16[1,2,8,128,256]{4,3,2,1,0:T(8,128)(2,1)}, u32[]{:S(2)}) %copy-start) | copy-done | bytes 1048600
  10.5 1.3 %copy-done.1 = bf16[3,3,256,256]{3,2,1,0:T(8,128)(2,1)S(1)} copy-done((bf16[3,3,256,256]{3,2,1,0:T(8,128)(2,1)S(1)}, bf16[3,3,256,256]{3,2,1,0:T(8,128)(2,1)}, u32[]{:S(2)}) %copy-start.1) | copy-done | bytes 1179672
  12.2 1.8 %collective-permute-done.2.refs_2_ = bf16[2,128,256]{2,1,0:T(8,128)(2,1)S(1)} collective-permute-done((bf16[2,128,256]{2,1,0:T(8,128)(2,1)S(1)}, bf16[2,128,256]{2,1,0:T(8,128)(2,1)S(1)}, u32[]{:S(2)}, u32[]{:S(2)}) %collective-permute-start.2) | collective-permute-done | bytes 131104 | tf_op jit(solution)/shard_map/ppermute | solution.py:368
  13.9 4.6 %shard_map.76 = (bf16[2,1024,256]{2,1,0:T(8,128)(2,1)}, f32[2,1024,256]{2,1,0:T(8,128)S(1)}, bf16[2,256,128]{2,1,0:T(8,128)(2,1)S(1)}, bf16[2,256,128]{2,1,0:T(8,128)(2,1)S(1)}, bf16[2,256,1024]{2,1,0:T(8,128)(2,1)S(1)}) custom-call(bf16[2,1024,256]{2,1,0:T(8,128)(2,1)S(1)} %bitcast.13, bf16[2,128,256]{2,1,0:T(8,128)(2,1)S(1)} %collective-permute-done.1.refs_1_, ...), custom_call_target="tpu_custom_call" | custom-call | flops 2415919104 | bytes 9437184 | tf_op jit(solution)/shard_map/pallas_call | solution.py:35
  18.5 3.5 %collective-permute-start.9 = (bf16[2,1024,256]{2,1,0:T(8,128)(2,1)}, bf16[2,1024,256]{2,1,0:T(8,128)(2,1)S(1)}, u32[]{:S(2)}, u32[]{:S(2)}) collective-permute-start(bf16[2,1024,256]{2,1,0:T(8,128)(2,1)} %get-tuple-element.49.refs_1_), channel_id=1, source_target_pairs={{0,8},{8,16},{16,24},{24,32},{32,40},{40,48},{48,56},{56,64},{64,7... | collective-permute-start | bytes 3145736 | tf_op jit(solution)/shard_map/ppermute | solution.py:409
  23.1 4.1 %collective-permute-done.refs_1_ = bf16[2,1024,256]{2,1,0:T(8,128)(2,1)S(1)} collective-permute-done((bf16[2,1024,256]{2,1,0:T(8,128)(2,1)}, bf16[2,1024,256]{2,1,0:T(8,128)(2,1)S(1)}, u32[]{:S(2)}, u32[]{:S(2)}) %collective-permute-start) | collective-permute-done | bytes 1048608 | tf_op jit(solution)/shard_map/ppermute | solution.py:379
  27.2 4.4 %shard_map.78 = (bf16[2,1024,256]{2,1,0:T(8,128)(2,1)S(1)}, bf16[3072,128]{1,0:T(8,128)(2,1)S(1)}, bf16[2,128,256]{2,1,0:T(8,128)(2,1)S(1)}, bf16[2,128,256]{2,1...) custom-call(s32[1]{0:T(128)} %bitcast.refs_0_, ...), custom_call_target="tpu_custom_call" | custom-call | flops 1024 | bytes 4096 | tf_op jit(solution)/shard_map/pallas_call | solution.py:35
  31.6 1.4 %collective-permute-start.3 = (bf16[768,128]{1,0:T(8,128)(2,1)S(1)}, bf16[768,128]{1,0:T(8,128)(2,1)S(1)}, u32[]{:S(2)}, u32[]{:S(2)}) collective-permute-start(bf16[768,128]{1,0:T(8,128)(2,1)S(1)} %get-tuple-element.42), channel_id=1, source_target_pairs={{0,1},{1,0},{2,3},{3,2},{4,5},{5,4},{6,7},{7,6},{8,9},{9,8},{10,11... | collective-permute-start | bytes 589832 | tf_op jit(solution)/shard_map/ppermute | solution.py:441
  35.0 1.1 shard_map.79
  36.1 6.8 %all-to-all-start = ((bf16[16,192,128]{2,1,0:T(8,128)(2,1)}), bf16[16,192,128]{2,1,0:T(8,128)(2,1)S(1)}, u32[]{:S(2)}, u32[]{:S(2)}) async-start(bf16[16,192,128]{2,1,0:T(8,128)(2,1)} %bitcast.3), calls=%async_computation | async-start | bytes 1572864 | tf_op jit(solution)/shard_map/all_to_all | solution.py:364
  42.8 4.0 %collective-permute-start.7 = (bf16[2,128,256]{2,1,0:T(8,128)(2,1)S(1)}, bf16[2,128,256]{2,1,0:T(8,128)(2,1)S(1)}, u32[]{:S(2)}, u32[]{:S(2)}) collective-permute-start(bf16[2,128,256]{2,1,0:T(8,128)(2,1)S(1)} %get-tuple-element.46), channel_id=1, source_target_pairs={{0,1},{1,2},{2,3},{3,4},{4,5},{5,6},{6,7},{8,9},{9,10},{10,11},{11... | collective-permute-start | bytes 393224 | tf_op jit(solution)/shard_map/ppermute | solution.py:368
  46.8 1.9 %collective-permute-start.8 = (bf16[2,128,256]{2,1,0:T(8,128)(2,1)S(1)}, bf16[2,128,256]{2,1,0:T(8,128)(2,1)S(1)}, u32[]{:S(2)}, u32[]{:S(2)}) collective-permute-start(bf16[2,128,256]{2,1,0:T(8,128)(2,1)S(1)} %get-tuple-element.47), channel_id=1, source_target_pairs={{1,0},{2,1},{3,2},{4,3},{5,4},{6,5},{7,6},{9,8},{10,9},{11,10},{12... | collective-permute-start | bytes 393224 | tf_op jit(solution)/shard_map/ppermute | solution.py:368
  48.8 4.5 %collective-permute-done.7.refs_4_ = bf16[2,128,256]{2,1,0:T(8,128)(2,1)S(1)} collective-permute-done((bf16[2,128,256]{2,1,0:T(8,128)(2,1)S(1)}, bf16[2,128,256]{2,1,0:T(8,128)(2,1)S(1)}, u32[]{:S(2)}, u32[]{:S(2)}) %collective-permute-start.7) | collective-permute-done | bytes 131104 | tf_op jit(solution)/shard_map/ppermute | solution.py:368
  53.3 2.2 %collective-permute-done.8.refs_5_ = bf16[2,128,256]{2,1,0:T(8,128)(2,1)S(1)} collective-permute-done((bf16[2,128,256]{2,1,0:T(8,128)(2,1)S(1)}, bf16[2,128,256]{2,1,0:T(8,128)(2,1)S(1)}, u32[]{:S(2)}, u32[]{:S(2)}) %collective-permute-start.8) | collective-permute-done | bytes 131104 | tf_op jit(solution)/shard_map/ppermute | solution.py:368
  55.7 27.3 %all_to_all.15.refs_0_ = bf16[8,192,128]{2,1,0:T(8,128)(2,1)S(1)} all-to-all(bf16[8,192,128]{2,1,0:T(8,128)(2,1)S(1)} %shard_map.80), channel_id=1, replica_groups=mesh['clip'=2,'y'=4,'zl'=4,'x'=4,'core'=2] {'zl','clip'}, dimensions={0} | all-to-all | bytes 786432 | tf_op jit(solution)/shard_map/all_to_all | solution.py:364
  83.9 5.2 %all-to-all-start.2 = ((bf16[16,192,128]{2,1,0:T(8,128)(2,1)}), bf16[16,192,128]{2,1,0:T(8,128)(2,1)S(1)}, u32[]{:S(2)}, u32[]{:S(2)}) async-start(bf16[16,192,128]{2,1,0:T(8,128)(2,1)} %shard_map.81), calls=%async_computation.2 | async-start | bytes 1572864 | tf_op jit(solution)/shard_map/all_to_all | solution.py:364
  89.1 8.3 %shard_map.82 = (bf16[2,1024,256]{2,1,0:T(8,128)(2,1)}, bf16[2,1024,256]{2,1,0:T(8,128)(2,1)}) custom-call(bf16[2,1024,256]{2,1,0:T(8,128)(2,1)} %copy-done.2, bf16[2,1024,256]{2,1,0:T(8,128)(2,1)} %get-tuple-element.49.refs_1_, bf16[2,1024,256]{2,1,0:T(8,128)(2,1)} %bitcast.11, bf16[2,1024,256]{2,1,0:T(8,128)(2,1)} %copy-done.5, ...), custom_call_target="tpu_custom_call" | custom-call | flops 3221225472 | bytes 9437184 | tf_op jit(solution)/shard_map/pallas_call | solution.py:35
  97.3 4.5 %all-to-all-done.2 = bf16[16,192,128]{2,1,0:T(8,128)(2,1)S(1)} async-done(((bf16[16,192,128]{2,1,0:T(8,128)(2,1)}), bf16[16,192,128]{2,1,0:T(8,128)(2,1)S(1)}, u32[]{:S(2)}, u32[]{:S(2)}) %all-to-all-start.2) | async-done | bytes 786464 | tf_op jit(solution)/shard_map/all_to_all | solution.py:364
  101.8 2.7 %collective-permute-start.10 = (bf16[3072,128]{1,0:T(8,128)(2,1)S(1)}, bf16[3072,128]{1,0:T(8,128)(2,1)S(1)}, u32[]{:S(2)}, u32[]{:S(2)}) collective-permute-start(bf16[3072,128]{1,0:T(8,128)(2,1)S(1)} %bitcast.8), channel_id=1, source_target_pairs={{0,1},{1,0},{2,3},{3,2},{4,5},{5,4},{6,7},{7,6},{8,9},{9,8},{10,11... | collective-permute-start | bytes 2359304 | tf_op jit(solution)/shard_map/ppermute | solution.py:484
  104.5 1.2 %shard_map.83 = (f32[9,256,256]{2,1,0:T(8,128)}, f32[3,256,256]{2,1,0:T(8,128)}) custom-call(s32[1]{0:T(128)} %bitcast.refs_0_, bf16[3072,128]{1,0:T(8,128)(2,1)S(1)} %bitcast.9), custom_call_target="tpu_custom_call" | custom-call | bytes 3145728 | tf_op jit(solution)/shard_map/pallas_call | solution.py:35
  106.4 1.2 %shard_map.84 = (f32[9,256,256]{2,1,0:T(8,128)}, f32[3,256,256]{2,1,0:T(8,128)}) custom-call(s32[1]{0:T(128)} %bitcast.refs_0_, bf16[3072,128]{1,0:T(8,128)(2,1)S(1)} %collective-permute-done.10.refs_1_, f32[9,256,256]{2,1,0:T(8,128)} %get-tuple-element.58.refs_2_, ...), custom_call_target="tpu_custom_call", output_to_operand_aliasing={{0}: (2, {}), {1}: (3, {})} | custom-call | bytes 3145728 | tf_op jit(solution)/shard_map/pallas_call | solution.py:35
  (30 shorter events, 6.2 us)
Async XLA Ops:
  0.6 26.5 %collective-permute-start = (bf16[2,1024,256]{2,1,0:T(8,128)(2,1)}, bf16[2,1024,256]{2,1,0:T(8,128)(2,1)S(1)}, u32[]{:S(2)}, u32[]{:S(2)}) collective-permute-start(bf16[2,1024,256]{2,1,0:T(8,128)(2,1)} %bitcast.14), channel_id=1, source_target_pairs={{8,0},{16,8},{24,16},{32,24},{40,32},{48,40},{56,48},{64,56},{72,6... | collective-permute-start | bytes 3145736 | tf_op jit(solution)/shard_map/ppermute | solution.py:379
  3.6 8.6 %collective-permute-start.1 = (bf16[2,128,256]{2,1,0:T(8,128)(2,1)S(1)}, bf16[2,128,256]{2,1,0:T(8,128)(2,1)S(1)}, u32[]{:S(2)}, u32[]{:S(2)}) collective-permute-start(bf16[2,128,256]{2,1,0:T(8,128)(2,1)S(1)} %get-tuple-element.63), channel_id=1, source_target_pairs={{0,1},{1,2},{2,3},{3,4},{4,5},{5,6},{6,7},{8,9},{9,10},{10,11},{11... | collective-permute-start | bytes 393224 | tf_op jit(solution)/shard_map/ppermute | solution.py:368
  7.3 6.6 %collective-permute-start.2 = (bf16[2,128,256]{2,1,0:T(8,128)(2,1)S(1)}, bf16[2,128,256]{2,1,0:T(8,128)(2,1)S(1)}, u32[]{:S(2)}, u32[]{:S(2)}) collective-permute-start(bf16[2,128,256]{2,1,0:T(8,128)(2,1)S(1)} %get-tuple-element.62), channel_id=1, source_target_pairs={{1,0},{2,1},{3,2},{4,3},{5,4},{6,5},{7,6},{9,8},{10,9},{11,10},{12... | collective-permute-start | bytes 393224 | tf_op jit(solution)/shard_map/ppermute | solution.py:368
  9.3 1.2 %copy-start = (bf16[1,2,8,128,256]{4,3,2,1,0:T(8,128)(2,1)S(1)}, bf16[1,2,8,128,256]{4,3,2,1,0:T(8,128)(2,1)}, u32[]{:S(2)}) copy-start(bf16[1,2,8,128,256]{4,3,2,1,0:T(8,128)(2,1)} %param.4) | copy-start | bytes 3145732
  10.5 1.3 %copy-start.1 = (bf16[3,3,256,256]{3,2,1,0:T(8,128)(2,1)S(1)}, bf16[3,3,256,256]{3,2,1,0:T(8,128)(2,1)}, u32[]{:S(2)}) copy-start(bf16[3,3,256,256]{3,2,1,0:T(8,128)(2,1)} %refs_7_.1) | copy-start | bytes 3538948
  13.9 8.1 %copy-start.3 = (bf16[3,256,256]{2,1,0:T(8,128)(2,1)S(1)}, bf16[3,256,256]{2,1,0:T(8,128)(2,1)}, u32[]{:S(2)}) copy-start(bf16[3,256,256]{2,1,0:T(8,128)(2,1)} %refs_8_.1) | copy-start | bytes 1179652
  13.9 8.1 %copy-start.4 = (bf16[1,2,8,128,256]{4,3,2,1,0:T(8,128)(2,1)S(1)}, bf16[1,2,8,128,256]{4,3,2,1,0:T(8,128)(2,1)}, u32[]{:S(2)}) copy-start(bf16[1,2,8,128,256]{4,3,2,1,0:T(8,128)(2,1)} %param.5) | copy-start | bytes 3145732
  18.5 37.0 %collective-permute-start.9 = (bf16[2,1024,256]{2,1,0:T(8,128)(2,1)}, bf16[2,1024,256]{2,1,0:T(8,128)(2,1)S(1)}, u32[]{:S(2)}, u32[]{:S(2)}) collective-permute-start(bf16[2,1024,256]{2,1,0:T(8,128)(2,1)} %get-tuple-element.49.refs_1_), channel_id=1, source_target_pairs={{0,8},{8,16},{16,24},{24,32},{32,40},{40,48},{48,56},{56,64},{64,7... | collective-permute-start | bytes 3145736 | tf_op jit(solution)/shard_map/ppermute | solution.py:409
  31.6 4.5 %copy-start.5 = (bf16[2,1024,256]{2,1,0:T(8,128)(2,1)}, bf16[2,1024,256]{2,1,0:T(8,128)(2,1)S(1)}, u32[]{:S(2)}) copy-start(bf16[2,1024,256]{2,1,0:T(8,128)(2,1)S(1)} %get-tuple-element.50.refs_3_) | copy-start | bytes 3145732
  31.6 2.5 %collective-permute-start.3 = (bf16[768,128]{1,0:T(8,128)(2,1)S(1)}, bf16[768,128]{1,0:T(8,128)(2,1)S(1)}, u32[]{:S(2)}, u32[]{:S(2)}) collective-permute-start(bf16[768,128]{1,0:T(8,128)(2,1)S(1)} %get-tuple-element.42), channel_id=1, source_target_pairs={{0,1},{1,0},{2,3},{3,2},{4,5},{5,4},{6,7},{7,6},{8,9},{9,8},{10,11... | collective-permute-start | bytes 589832 | tf_op jit(solution)/shard_map/ppermute | solution.py:441
  33.0 1.4 %collective-permute-start.4 = (bf16[768,128]{1,0:T(8,128)(2,1)S(1)}, bf16[768,128]{1,0:T(8,128)(2,1)S(1)}, u32[]{:S(2)}, u32[]{:S(2)}) collective-permute-start(bf16[768,128]{1,0:T(8,128)(2,1)S(1)} %get-tuple-element.43), channel_id=1, source_target_pairs={{0,1},{1,0},{2,3},{3,2},{4,5},{5,4},{6,7},{7,6},{8,9},{9,8},{10,11... | collective-permute-start | bytes 589832 | tf_op jit(solution)/shard_map/ppermute | solution.py:441
  33.1 1.6 %collective-permute-start.5 = (bf16[768,128]{1,0:T(8,128)(2,1)S(1)}, bf16[768,128]{1,0:T(8,128)(2,1)S(1)}, u32[]{:S(2)}, u32[]{:S(2)}) collective-permute-start(bf16[768,128]{1,0:T(8,128)(2,1)S(1)} %get-tuple-element.44), channel_id=1, source_target_pairs={{0,1},{1,0},{2,3},{3,2},{4,5},{5,4},{6,7},{7,6},{8,9},{9,8},{10,11... | collective-permute-start | bytes 589832 | tf_op jit(solution)/shard_map/ppermute | solution.py:441
  33.5 1.5 %collective-permute-start.6 = (bf16[768,128]{1,0:T(8,128)(2,1)S(1)}, bf16[768,128]{1,0:T(8,128)(2,1)S(1)}, u32[]{:S(2)}, u32[]{:S(2)}) collective-permute-start(bf16[768,128]{1,0:T(8,128)(2,1)S(1)} %get-tuple-element.45), channel_id=1, source_target_pairs={{0,1},{1,0},{2,3},{3,2},{4,5},{5,4},{6,7},{7,6},{8,9},{9,8},{10,11... | collective-permute-start | bytes 589832 | tf_op jit(solution)/shard_map/ppermute | solution.py:441
  36.1 19.5 %all-to-all-start = ((bf16[16,192,128]{2,1,0:T(8,128)(2,1)}), bf16[16,192,128]{2,1,0:T(8,128)(2,1)S(1)}, u32[]{:S(2)}, u32[]{:S(2)}) async-start(bf16[16,192,128]{2,1,0:T(8,128)(2,1)} %bitcast.3), calls=%async_computation | async-start | bytes 1572864 | tf_op jit(solution)/shard_map/all_to_all | solution.py:364
  42.8 10.5 %collective-permute-start.7 = (bf16[2,128,256]{2,1,0:T(8,128)(2,1)S(1)}, bf16[2,128,256]{2,1,0:T(8,128)(2,1)S(1)}, u32[]{:S(2)}, u32[]{:S(2)}) collective-permute-start(bf16[2,128,256]{2,1,0:T(8,128)(2,1)S(1)} %get-tuple-element.46), channel_id=1, source_target_pairs={{0,1},{1,2},{2,3},{3,4},{4,5},{5,6},{6,7},{8,9},{9,10},{10,11},{11... | collective-permute-start | bytes 393224 | tf_op jit(solution)/shard_map/ppermute | solution.py:368
  46.8 8.7 %collective-permute-start.8 = (bf16[2,128,256]{2,1,0:T(8,128)(2,1)S(1)}, bf16[2,128,256]{2,1,0:T(8,128)(2,1)S(1)}, u32[]{:S(2)}, u32[]{:S(2)}) collective-permute-start(bf16[2,128,256]{2,1,0:T(8,128)(2,1)S(1)} %get-tuple-element.47), channel_id=1, source_target_pairs={{1,0},{2,1},{3,2},{4,3},{5,4},{6,5},{7,6},{9,8},{10,9},{11,10},{12... | collective-permute-start | bytes 393224 | tf_op jit(solution)/shard_map/ppermute | solution.py:368
  53.3 30.6 %copy-start.6 = (bf16[2,128,256]{2,1,0:T(8,128)(2,1)}, bf16[2,128,256]{2,1,0:T(8,128)(2,1)S(1)}, u32[]{:S(2)}) copy-start(bf16[2,128,256]{2,1,0:T(8,128)(2,1)S(1)} %collective-permute-done.7.refs_4_) | copy-start | bytes 393220
  55.5 28.4 %copy-start.7 = (bf16[2,128,256]{2,1,0:T(8,128)(2,1)}, bf16[2,128,256]{2,1,0:T(8,128)(2,1)S(1)}, u32[]{:S(2)}) copy-start(bf16[2,128,256]{2,1,0:T(8,128)(2,1)S(1)} %collective-permute-done.8.refs_5_) | copy-start | bytes 393220
  55.5 28.4 %copy-start.2 = (bf16[2,1024,256]{2,1,0:T(8,128)(2,1)}, bf16[2,1024,256]{2,1,0:T(8,128)(2,1)S(1)}, u32[]{:S(2)}) copy-start(bf16[2,1024,256]{2,1,0:T(8,128)(2,1)S(1)} %collective-permute-done.9.refs_1_.refs_0_) | copy-start | bytes 3145732
  83.9 17.9 %all-to-all-start.2 = ((bf16[16,192,128]{2,1,0:T(8,128)(2,1)}), bf16[16,192,128]{2,1,0:T(8,128)(2,1)S(1)}, u32[]{:S(2)}, u32[]{:S(2)}) async-start(bf16[16,192,128]{2,1,0:T(8,128)(2,1)} %shard_map.81), calls=%async_computation.2 | async-start | bytes 1572864 | tf_op jit(solution)/shard_map/all_to_all | solution.py:364
  101.8 4.6 %collective-permute-start.10 = (bf16[3072,128]{1,0:T(8,128)(2,1)S(1)}, bf16[3072,128]{1,0:T(8,128)(2,1)S(1)}, u32[]{:S(2)}, u32[]{:S(2)}) collective-permute-start(bf16[3072,128]{1,0:T(8,128)(2,1)S(1)} %bitcast.8), channel_id=1, source_target_pairs={{0,1},{1,0},{2,3},{3,2},{4,5},{5,4},{6,7},{7,6},{8,9},{9,8},{10,11... | collective-permute-start | bytes 2359304 | tf_op jit(solution)/shard_map/ppermute | solution.py:484
